TPU v7x, 32 devices: a whole 2x2x4 slice. The times are simulated.
32 devices in a mesh: dp: 4 (over y, core), rows: 4 (over z), cols: 2 (over x).
Axes of the slice: x: 2, y: 2, z: 4, core: 2. Of those that a mesh axis runs over, the one named last changes fastest.
Arguments:
- image_in: bfloat16 [8, 64, 64, 1280], P('dp', 'rows', 'cols'), may hold values from -6 to 6
- ln1_gain: bfloat16 [1280], P(('dp', 'rows', 'cols')), may hold values from 0.5 to 1.5
- ln1_bias: bfloat16 [1280], P(('dp', 'rows', 'cols')), may hold values from -1.1953125 to 1.1953125
- w_qkv: bfloat16 [1280, 3840], P(('dp', 'rows', 'cols')), may hold values from -0.15625 to 0.15625
- qv_bias: bfloat16 [1280, 2], P(('dp', 'rows', 'cols')), may hold values from -1.1953125 to 1.1953125
- rel_rows: bfloat16 [27, 80], replicated, may hold values from -0.59765625 to 0.59765625
- rel_cols: bfloat16 [27, 80], replicated, may hold values from -0.59765625 to 0.59765625
- w_proj: bfloat16 [1280, 1280], P(('dp', 'rows', 'cols')), may hold values from -0.625 to 0.625
- proj_bias: bfloat16 [1280], P(('dp', 'rows', 'cols')), may hold values from -1.1953125 to 1.1953125
- ln2_gain: bfloat16 [1280], P(('dp', 'rows', 'cols')), may hold values from 0.5 to 1.5
- ln2_bias: bfloat16 [1280], P(('dp', 'rows', 'cols')), may hold values from -1.1953125 to 1.1953125
- w_fc1: bfloat16 [1280, 5120], P(('dp', 'rows', 'cols')), may hold values from -0.15625 to 0.15625
- fc1_bias: bfloat16 [5120], P(('dp', 'rows', 'cols')), may hold values from -1.1953125 to 1.1953125
- w_fc2: bfloat16 [5120, 1280], P(('dp', 'rows', 'cols')), may hold values from -0.078125 to 0.078125
- fc2_bias: bfloat16 [1280], P(('dp', 'rows', 'cols')), may hold values from -1.1953125 to 1.1953125
- cotangent: bfloat16 [8, 64, 64, 1280], P('dp', 'rows', 'cols'), may hold values from -6 to 6
Outputs:
- block_out: bfloat16 [8, 64, 64, 1280], P('dp', 'rows', 'cols')
- grad_in: float32 [8, 64, 64, 1280], P('dp', 'rows', 'cols')
- grad_ln1_gain: float32 [1280], P(('dp', 'rows', 'cols'))
- grad_ln1_bias: float32 [1280], P(('dp', 'rows', 'cols'))
- grad_w_qkv: float32 [1280, 3840], P(('dp', 'rows', 'cols'))
- grad_qv_bias: float32 [1280, 2], P(('dp', 'rows', 'cols'))
- grad_rel_rows: float32 [27, 80], replicated
- grad_rel_cols: float32 [27, 80], replicated
- grad_w_proj: float32 [1280, 1280], P(('dp', 'rows', 'cols'))
- grad_proj_bias: float32 [1280], P(('dp', 'rows', 'cols'))
- grad_ln2_gain: float32 [1280], P(('dp', 'rows', 'cols'))
- grad_ln2_bias: float32 [1280], P(('dp', 'rows', 'cols'))
- grad_w_fc1: float32 [1280, 5120], P(('dp', 'rows', 'cols'))
- grad_fc1_bias: float32 [5120], P(('dp', 'rows', 'cols'))
- grad_w_fc2: float32 [5120, 1280], P(('dp', 'rows', 'cols'))
- grad_fc2_bias: float32 [1280], P(('dp', 'rows', 'cols'))
All inputs are finite; a program needn't handle non-finite values.
Results may differ from a plain program's by a relative error of at most 0.013.
Values may be sent and summed in bfloat16 or wider, within the bound.
No kernel may reach another device: no remote copies, remote signals or barrier semaphores. Data moves between devices by JAX's collectives and lax.ppermute only.
A program may use at most 488 MiB of HBM per device.

v0:
```python
import jax
import jax.numpy as jnp
from jax import lax
from jax.sharding import PartitionSpec as P

HEADS = 16
WIN = 14
NWIN = 5


eps = 1e-06
highest = lax.Precision.HIGHEST


def passed_along(value, axis, steps):
    count = lax.axis_size(axis)
    first, last = (max(0, -steps), min(count, count - steps))
    return lax.ppermute(value, axis, [(source, source + steps) for source in range(first, last)])


def layer_norm(values, gain, shift):
    average = jnp.mean(values, axis=-1, keepdims=True)
    centered = values - average
    variance = jnp.mean(centered * centered, axis=-1, keepdims=True)
    return centered * lax.rsqrt(variance + eps) * gain + shift


def exact_gelu(values):
    return jax.nn.gelu(values, approximate=False)


def position_onehot(dtype):
    query_pos = lax.broadcasted_iota(jnp.int32, (WIN, WIN, 2 * WIN - 1), 0)
    key_pos = lax.broadcasted_iota(jnp.int32, (WIN, WIN, 2 * WIN - 1), 1)
    offset = lax.broadcasted_iota(jnp.int32, (WIN, WIN, 2 * WIN - 1), 2)
    return (offset == query_pos - key_pos + WIN - 1).astype(dtype)


def scores_of(query, key, table_rows, table_cols):
    width, _, heads, head_size = query.shape
    scores = jnp.einsum(
        "abhc,ijhc->habij", query, key, preferred_element_type=jnp.float32
    ) * head_size ** (-0.5)
    along_rows = jnp.einsum("abhc,aic->habi", query, table_rows, preferred_element_type=jnp.float32)
    along_cols = jnp.einsum("abhc,bjc->habj", query, table_cols, preferred_element_type=jnp.float32)
    scores = scores + along_rows[:, :, :, :, None] + along_cols[:, :, :, None, :]
    return scores.reshape(heads, width * width, width * width)


def split_project(project, width, model):
    head_size = model // HEADS
    query = project[:, :model].reshape(width, width, HEADS, head_size)
    key = project[:, model : 2 * model].reshape(width, width, HEADS, head_size)
    value = project[:, 2 * model :].reshape(width * width, HEADS, head_size)
    return (query, key, value)


def window_forward(window, w_full, bias_row, table_rows, table_cols):
    width = window.shape[0]
    model = window.shape[2]
    tokens = window.reshape(width * width, model)
    project = (jnp.dot(tokens, w_full, preferred_element_type=jnp.float32) + bias_row).astype(
        jnp.bfloat16
    )
    query, key, value = split_project(project, width, model)
    scores = scores_of(query, key, table_rows, table_cols)
    maxima = jnp.max(scores, axis=-1, keepdims=True)
    weights = jnp.exp(scores - maxima)
    totals = jnp.sum(weights, axis=-1, keepdims=True)
    probs = (weights / totals).astype(jnp.bfloat16)
    attended = jnp.einsum("hqk,khc->qhc", probs, value, preferred_element_type=jnp.float32)
    return (
        attended.reshape(width, width, model).astype(jnp.bfloat16),
        project,
        maxima + jnp.log(totals),
    )


def window_backward(window, project, log_total, grad_window, w_full, table_rows, table_cols):
    width = window.shape[0]
    model = window.shape[2]
    count = width * width
    head_size = model // HEADS
    scale = head_size ** (-0.5)
    query, key, value = split_project(project, width, model)
    scores = scores_of(query, key, table_rows, table_cols)
    probs = jnp.exp(scores - log_total)
    grad_heads = grad_window.reshape(count, HEADS, head_size)
    grad_probs = jnp.einsum("qhc,khc->hqk", grad_heads, value, preferred_element_type=jnp.float32)
    inner = jnp.sum(probs * grad_probs, axis=-1, keepdims=True)
    grad_scores = (probs * (grad_probs - inner)).astype(jnp.bfloat16)
    grad_value = jnp.einsum(
        "hqk,qhc->khc", probs.astype(jnp.bfloat16), grad_heads, preferred_element_type=jnp.float32
    )
    grid = grad_scores.reshape(HEADS, width, width, width, width)
    grad_query = (
        jnp.einsum("habij,ijhc->abhc", grid, key, preferred_element_type=jnp.float32) * scale
    )
    grad_key = (
        jnp.einsum("habij,abhc->ijhc", grid, query, preferred_element_type=jnp.float32) * scale
    )
    rows_grad = jnp.sum(grid, axis=4, dtype=jnp.float32)
    cols_grad = jnp.sum(grid, axis=3, dtype=jnp.float32)
    grad_query = grad_query + jnp.einsum(
        "habi,aic->abhc", rows_grad, table_rows.astype(jnp.float32), precision=highest
    )
    grad_query = grad_query + jnp.einsum(
        "habj,bjc->abhc", cols_grad, table_cols.astype(jnp.float32), precision=highest
    )
    query_float = query.astype(jnp.float32)
    grad_table_rows = jnp.einsum("habi,abhc->aic", rows_grad, query_float, precision=highest)
    grad_table_cols = jnp.einsum("habj,abhc->bjc", cols_grad, query_float, precision=highest)
    grad_project = jnp.concatenate(
        [
            grad_query.reshape(count, model),
            grad_key.reshape(count, model),
            grad_value.reshape(count, model),
        ],
        axis=1,
    ).astype(jnp.bfloat16)
    tokens = window.reshape(count, model)
    grad_tokens = lax.dot_general(
        grad_project, w_full, (((1,), (1,)), ((), ())), preferred_element_type=jnp.float32
    )
    grad_weight = lax.dot_general(
        tokens, grad_project, (((0,), (0,)), ((), ())), preferred_element_type=jnp.float32
    )
    grad_bias = jnp.sum(grad_project, axis=0, dtype=jnp.float32)
    return (
        grad_tokens.reshape(width, width, model),
        grad_weight,
        grad_bias,
        grad_table_rows,
        grad_table_cols,
    )


def spread_normed(values):
    tile_h = values.shape[0]
    margin = WIN - 1
    right = passed_along(values[:, :margin], "cols", -1)
    wide = jnp.concatenate([values, right], axis=1)
    parts = [wide]
    for step in range(1, (margin + tile_h - 1) // tile_h + 1):
        count = min(tile_h, margin - (step - 1) * tile_h)
        parts.append(passed_along(wide[:count], "rows", -step))
    return jnp.concatenate(parts, axis=0)


def spread_grads(values):
    tile_h = values.shape[0]
    margin = WIN - 1
    right = passed_along(values[:, :margin], "cols", -1)
    wide = jnp.concatenate([values, right], axis=1)
    parts = [wide]
    for step in range(1, (margin + tile_h - 1) // tile_h + 1):
        count = min(tile_h, margin - (step - 1) * tile_h)
        parts.append(passed_along(wide[:count], "rows", -step))
    return jnp.concatenate(parts, axis=0)


def collect_attended(buffer, tile_h, tile_w):
    margin = WIN - 1
    wide = buffer[:tile_h]
    for step in range(1, (margin + tile_h - 1) // tile_h + 1):
        count = min(tile_h, margin - (step - 1) * tile_h)
        start = step * tile_h
        arrived = passed_along(buffer[start : start + count], "rows", step)
        wide = wide.at[:count].add(arrived)
    arrived = passed_along(wide[:, tile_w:], "cols", 1)
    return wide[:, :tile_w].at[:, :margin].add(arrived)


def collect_grads(buffer, tile_h, tile_w):
    margin = WIN - 1
    wide = buffer[:tile_h]
    for step in range(1, (margin + tile_h - 1) // tile_h + 1):
        count = min(tile_h, margin - (step - 1) * tile_h)
        start = step * tile_h
        arrived = passed_along(
            buffer[start : start + count].astype(jnp.bfloat16), "rows", step
        ).astype(jnp.float32)
        wide = wide.at[:count].add(arrived)
    arrived = passed_along(wide[:, tile_w:].astype(jnp.bfloat16), "cols", 1).astype(jnp.float32)
    return wide[:, :tile_w].at[:, :margin].add(arrived)


def shards(
    image_in,
    ln1_gain,
    ln1_bias,
    w_qkv,
    qv_bias,
    rel_rows,
    rel_cols,
    w_proj,
    proj_bias,
    ln2_gain,
    ln2_bias,
    w_fc1,
    fc1_bias,
    w_fc2,
    fc2_bias,
    cotangent,
):
    devices = lax.axis_size(("dp", "rows", "cols"))
    tile_h = image_in.shape[1]
    tile_w = image_in.shape[2]
    model = image_in.shape[3]
    head_size = model // HEADS
    onehot = position_onehot(jnp.bfloat16)
    table_rows = jnp.einsum(
        "ijr,rc->ijc", onehot, rel_rows, preferred_element_type=jnp.float32
    ).astype(jnp.bfloat16)
    table_cols = jnp.einsum(
        "ijr,rc->ijc", onehot, rel_cols, preferred_element_type=jnp.float32
    ).astype(jnp.bfloat16)
    row_index = lax.axis_index("rows")
    col_index = lax.axis_index("cols")
    first_row = (row_index * tile_h + WIN - 1) // WIN
    first_col = (col_index * tile_w + WIN - 1) // WIN
    slots = []
    for slot_row in range(-(-tile_h // WIN)):
        for slot_col in range(-(-tile_w // WIN)):
            window_row = first_row + slot_row
            window_col = first_col + slot_col
            valid = (
                (window_row * WIN < (row_index + 1) * tile_h)
                & (window_row < NWIN)
                & (window_col * WIN < (col_index + 1) * tile_w)
                & (window_col < NWIN)
            )
            slots.append(
                (
                    valid,
                    window_row * WIN - row_index * tile_h,
                    window_col * WIN - col_index * tile_w,
                )
            )

    def widened(shard):
        shape = list(shard.shape)
        shape[0] = shape[0] * devices
        return jnp.zeros(shape, jnp.float32)

    initial = (
        widened(ln1_gain),
        widened(ln1_bias),
        widened(w_qkv),
        widened(qv_bias),
        widened(w_proj),
        widened(proj_bias),
        widened(ln2_gain),
        widened(ln2_bias),
        widened(w_fc1),
        widened(fc1_bias),
        widened(w_fc2),
        widened(fc2_bias),
        jnp.zeros((WIN, WIN, head_size), jnp.float32),
        jnp.zeros((WIN, WIN, head_size), jnp.float32),
    )

    def step_image(totals, pair):
        image, grad_image = pair
        gathered = (
            lax.all_gather(ln1_gain, ("dp", "rows", "cols"), axis=0, tiled=True),
            lax.all_gather(ln1_bias, ("dp", "rows", "cols"), axis=0, tiled=True),
            lax.all_gather(w_qkv, ("dp", "rows", "cols"), axis=0, tiled=True),
            lax.all_gather(qv_bias, ("dp", "rows", "cols"), axis=0, tiled=True),
            lax.all_gather(w_proj, ("dp", "rows", "cols"), axis=0, tiled=True),
            lax.all_gather(proj_bias, ("dp", "rows", "cols"), axis=0, tiled=True),
            lax.all_gather(ln2_gain, ("dp", "rows", "cols"), axis=0, tiled=True),
            lax.all_gather(ln2_bias, ("dp", "rows", "cols"), axis=0, tiled=True),
            lax.all_gather(w_fc1, ("dp", "rows", "cols"), axis=0, tiled=True),
            lax.all_gather(fc1_bias, ("dp", "rows", "cols"), axis=0, tiled=True),
            lax.all_gather(w_fc2, ("dp", "rows", "cols"), axis=0, tiled=True),
            lax.all_gather(fc2_bias, ("dp", "rows", "cols"), axis=0, tiled=True),
        )
        (
            first_gain,
            first_shift,
            qkv_full,
            qv_full,
            proj_full,
            proj_shift,
            second_gain,
            second_shift,
            up_full,
            up_shift,
            down_full,
            down_shift,
        ) = gathered
        bias_row = jnp.concatenate(
            [
                qv_full[:, 0].astype(jnp.float32),
                jnp.zeros((model,), jnp.float32),
                qv_full[:, 1].astype(jnp.float32),
            ]
        )
        image_float = image.astype(jnp.float32)
        normed_float, first_pull = jax.vjp(
            layer_norm, image_float, first_gain.astype(jnp.float32), first_shift.astype(jnp.float32)
        )
        normed = normed_float.astype(jnp.bfloat16)
        extended = spread_normed(normed)

        def attend_window(window):
            return window_forward(window, qkv_full, bias_row, table_rows, table_cols)

        def skip_window(window):
            return (
                jnp.zeros((WIN, WIN, model), jnp.bfloat16),
                jnp.zeros((WIN * WIN, 3 * model), jnp.bfloat16),
                jnp.zeros((HEADS, WIN * WIN, 1), jnp.float32),
            )

        attended_buffer = jnp.zeros(extended.shape, jnp.bfloat16)
        kept = []
        for valid, local_row, local_col in slots:
            window = lax.dynamic_slice(extended, (local_row, local_col, 0), (WIN, WIN, model))
            attended, project, log_total = lax.cond(valid, attend_window, skip_window, window)
            region = lax.dynamic_slice(
                attended_buffer, (local_row, local_col, 0), (WIN, WIN, model)
            )
            attended_buffer = lax.dynamic_update_slice(
                attended_buffer, region + attended, (local_row, local_col, 0)
            )
            kept.append((window, project, log_total))
        attended_tile = collect_attended(attended_buffer, tile_h, tile_w).reshape(
            tile_h * tile_w, model
        )
        branch = jnp.dot(
            attended_tile, proj_full, preferred_element_type=jnp.float32
        ) + proj_shift.astype(jnp.float32)
        middle = image_float.reshape(tile_h * tile_w, model) + branch
        normed2_float, second_pull = jax.vjp(
            layer_norm, middle, second_gain.astype(jnp.float32), second_shift.astype(jnp.float32)
        )
        normed2 = normed2_float.astype(jnp.bfloat16)
        hidden = jnp.dot(normed2, up_full, preferred_element_type=jnp.float32) + up_shift.astype(
            jnp.float32
        )
        active_float, gelu_pull = jax.vjp(exact_gelu, hidden)
        active = active_float.astype(jnp.bfloat16)
        mixed = jnp.dot(active, down_full, preferred_element_type=jnp.float32) + down_shift.astype(
            jnp.float32
        )
        output = (middle + mixed).astype(jnp.bfloat16).reshape(tile_h, tile_w, model)
        grad_mixed = grad_image.reshape(tile_h * tile_w, model)
        grad_down = lax.dot_general(
            active, grad_mixed, (((0,), (0,)), ((), ())), preferred_element_type=jnp.float32
        )
        grad_down_shift = jnp.sum(grad_mixed, axis=0, dtype=jnp.float32)
        grad_active = lax.dot_general(
            grad_mixed, down_full, (((1,), (1,)), ((), ())), preferred_element_type=jnp.float32
        )
        grad_hidden = gelu_pull(grad_active)[0].astype(jnp.bfloat16)
        grad_up = lax.dot_general(
            normed2, grad_hidden, (((0,), (0,)), ((), ())), preferred_element_type=jnp.float32
        )
        grad_up_shift = jnp.sum(grad_hidden, axis=0, dtype=jnp.float32)
        grad_normed2 = lax.dot_general(
            grad_hidden, up_full, (((1,), (1,)), ((), ())), preferred_element_type=jnp.float32
        )
        grad_middle_norm, grad_second_gain, grad_second_shift = second_pull(grad_normed2)
        grad_middle = grad_mixed.astype(jnp.float32) + grad_middle_norm
        grad_branch = grad_middle.astype(jnp.bfloat16)
        grad_proj = lax.dot_general(
            attended_tile, grad_branch, (((0,), (0,)), ((), ())), preferred_element_type=jnp.float32
        )
        grad_proj_shift = jnp.sum(grad_branch, axis=0, dtype=jnp.float32)
        grad_attended = lax.dot_general(
            grad_branch, proj_full, (((1,), (1,)), ((), ())), preferred_element_type=jnp.float32
        ).astype(jnp.bfloat16)
        grad_extended = spread_grads(grad_attended.reshape(tile_h, tile_w, model))

        def grad_window_fn(operands):
            window, project, log_total, grad_part = operands
            return window_backward(
                window, project, log_total, grad_part, qkv_full, table_rows, table_cols
            )

        def skip_grad(operands):
            return (
                jnp.zeros((WIN, WIN, model), jnp.float32),
                jnp.zeros((model, 3 * model), jnp.float32),
                jnp.zeros((3 * model,), jnp.float32),
                jnp.zeros((WIN, WIN, head_size), jnp.float32),
                jnp.zeros((WIN, WIN, head_size), jnp.float32),
            )

        grad_buffer = jnp.zeros(extended.shape, jnp.float32)
        grad_qkv = totals[2]
        grad_qv = totals[3]
        grad_table_rows = totals[12]
        grad_table_cols = totals[13]
        for (valid, local_row, local_col), (window, project, log_total) in zip(slots, kept):
            grad_part = lax.dynamic_slice(
                grad_extended, (local_row, local_col, 0), (WIN, WIN, model)
            )
            grad_tokens, grad_weight, grad_bias, table_rows_part, table_cols_part = lax.cond(
                valid, grad_window_fn, skip_grad, (window, project, log_total, grad_part)
            )
            region = lax.dynamic_slice(grad_buffer, (local_row, local_col, 0), (WIN, WIN, model))
            grad_buffer = lax.dynamic_update_slice(
                grad_buffer, region + grad_tokens, (local_row, local_col, 0)
            )
            grad_qkv = grad_qkv + grad_weight
            grad_qv = grad_qv + jnp.stack([grad_bias[:model], grad_bias[2 * model :]], axis=1)
            grad_table_rows = grad_table_rows + table_rows_part
            grad_table_cols = grad_table_cols + table_cols_part
        grad_normed = collect_grads(grad_buffer, tile_h, tile_w)
        grad_image_norm, grad_first_gain, grad_first_shift = first_pull(grad_normed)
        grad_input = grad_middle.reshape(tile_h, tile_w, model) + grad_image_norm
        updated = (
            totals[0] + grad_first_gain,
            totals[1] + grad_first_shift,
            grad_qkv,
            grad_qv,
            totals[4] + grad_proj,
            totals[5] + grad_proj_shift,
            totals[6] + grad_second_gain,
            totals[7] + grad_second_shift,
            totals[8] + grad_up,
            totals[9] + grad_up_shift,
            totals[10] + grad_down,
            totals[11] + grad_down_shift,
            grad_table_rows,
            grad_table_cols,
        )
        return (updated, (output, grad_input))

    totals, (outputs, grad_inputs) = lax.scan(step_image, initial, (image_in, cotangent))
    (
        total_first_gain,
        total_first_shift,
        total_qkv,
        total_qv,
        total_proj,
        total_proj_shift,
        total_second_gain,
        total_second_shift,
        total_up,
        total_up_shift,
        total_down,
        total_down_shift,
        total_table_rows,
        total_table_cols,
    ) = totals
    summed = (
        lax.psum_scatter(total_first_gain, ("dp", "rows", "cols"), scatter_dimension=0, tiled=True),
        lax.psum_scatter(
            total_first_shift, ("dp", "rows", "cols"), scatter_dimension=0, tiled=True
        ),
        lax.psum_scatter(total_qkv, ("dp", "rows", "cols"), scatter_dimension=0, tiled=True),
        lax.psum_scatter(total_qv, ("dp", "rows", "cols"), scatter_dimension=0, tiled=True),
        lax.psum_scatter(total_proj, ("dp", "rows", "cols"), scatter_dimension=0, tiled=True),
        lax.psum_scatter(total_proj_shift, ("dp", "rows", "cols"), scatter_dimension=0, tiled=True),
        lax.psum_scatter(
            total_second_gain, ("dp", "rows", "cols"), scatter_dimension=0, tiled=True
        ),
        lax.psum_scatter(
            total_second_shift, ("dp", "rows", "cols"), scatter_dimension=0, tiled=True
        ),
        lax.psum_scatter(total_up, ("dp", "rows", "cols"), scatter_dimension=0, tiled=True),
        lax.psum_scatter(total_up_shift, ("dp", "rows", "cols"), scatter_dimension=0, tiled=True),
        lax.psum_scatter(total_down, ("dp", "rows", "cols"), scatter_dimension=0, tiled=True),
        lax.psum_scatter(total_down_shift, ("dp", "rows", "cols"), scatter_dimension=0, tiled=True),
    )
    onehot_float = position_onehot(jnp.float32)
    local_rows = jnp.einsum("ijr,ijc->rc", onehot_float, total_table_rows, precision=highest)
    local_cols = jnp.einsum("ijr,ijc->rc", onehot_float, total_table_cols, precision=highest)
    grad_rows_table, grad_cols_table = lax.psum((local_rows, local_cols), ("dp", "rows", "cols"))
    return (
        outputs,
        grad_inputs,
        summed[0],
        summed[1],
        summed[2],
        summed[3],
        grad_rows_table,
        grad_cols_table,
        summed[4],
        summed[5],
        summed[6],
        summed[7],
        summed[8],
        summed[9],
        summed[10],
        summed[11],
    )


def solution(mesh):
    in_specs = (
        P("dp", "rows", "cols", None),
        P(("dp", "rows", "cols")),
        P(("dp", "rows", "cols")),
        P(("dp", "rows", "cols"), None),
        P(("dp", "rows", "cols"), None),
        P(),
        P(),
        P(("dp", "rows", "cols"), None),
        P(("dp", "rows", "cols")),
        P(("dp", "rows", "cols")),
        P(("dp", "rows", "cols")),
        P(("dp", "rows", "cols"), None),
        P(("dp", "rows", "cols")),
        P(("dp", "rows", "cols"), None),
        P(("dp", "rows", "cols")),
        P("dp", "rows", "cols", None),
    )
    out_specs = (
        P("dp", "rows", "cols", None),
        P("dp", "rows", "cols", None),
        P(("dp", "rows", "cols")),
        P(("dp", "rows", "cols")),
        P(("dp", "rows", "cols"), None),
        P(("dp", "rows", "cols"), None),
        P(),
        P(),
        P(("dp", "rows", "cols"), None),
        P(("dp", "rows", "cols")),
        P(("dp", "rows", "cols")),
        P(("dp", "rows", "cols")),
        P(("dp", "rows", "cols"), None),
        P(("dp", "rows", "cols")),
        P(("dp", "rows", "cols"), None),
        P(("dp", "rows", "cols")),
    )
    return jax.shard_map(shards, mesh=mesh, in_specs=in_specs, out_specs=out_specs, check_vma=False)
```

profile of v0, /device:TPU:1, one launch (start us, length us, event | category | flops | bytes accessed | tf_op | source)
XLA Modules:
  0.0 6524.2 jit_solution(6031764412333732571)
XLA Ops:
  9.7 4876.4 %while.49 = (s32[]{:T(128)}, f32[1280]{0:T(1024)}, f32[1280]{0:T(1024)}, f32[1280,3840]{0,1:T(8,128)}, f32[1280,2]{0,1:T(2,128)}, /*index=5*/f32[1280,1280]{1,0:...) while((s32[]{:T(128)}, f32[1280]{0:T(1024)}, ...), condition=%wide.region_76.77_spmd.clone, body=%wide.region_0.76_spmd.clone.sunk | while | flops 86446391296 | bytes 2038261760 | solution.py:433
  18.8 43.0 all-reduce.25
  97.0 100.9 %all-gather.3 = bf16[32,40,2]{1,2,0:T(2,128)(2,1)S(1)} all-gather(bf16[1,40,2]{1,2,0:T(2,128)(2,1)S(1)} %bitcast.805), channel_id=1, replica_groups=mesh['dp'=4,'rows'=4,'cols'=2] {'dp','rows','cols'}, dimensions={0}, use_global_device_ids=true | all-gather | bytes 5280 | tf_op jit(solution)/shard_map/while/body/eval_jaxpr/all_gather | solution.py:269
  203.4 113.6 %conditional.37 = (bf16[14,14,1280]{2,1,0:T(8,128)(2,1)}, bf16[196,3840]{1,0:T(8,128)(2,1)S(1)}, f32[16,196,1]{1,0,2:T(8,128)S(1)}) conditional(s32[]{:T(128)} %convert_element_type.715, () %tuple.376, (bf16[14,14,1280]{2,0,1:T(8,128)(2,1)}, bf16[1280,3840]{1,0:T(8,128)(2,1)}, f32[3840]{0:T(1024)S(1)}, bf16[14,14,80]{2,1,0:T(8,128)(2,1)S(1)}, ...), branch_computations={%region_7.7_spmd, %region_8.10_spmd} | conditional | flops 2144782592 | bytes 60310380 | solution.py:321
  253.5 36.4 copy.628
  318.2 113.8 %conditional.36 = (bf16[14,14,1280]{2,1,0:T(8,128)(2,1)}, bf16[196,3840]{1,0:T(8,128)(2,1)S(1)}, f32[16,196,1]{1,0,2:T(8,128)S(1)}) conditional(s32[]{:T(128)} %convert_element_type.711, () %tuple.374, (bf16[14,14,1280]{2,0,1:T(8,128)(2,1)}, bf16[1280,3840]{1,0:T(8,128)(2,1)}, f32[3840]{0:T(1024)S(1)}, bf16[14,14,80]{2,1,0:T(8,128)(2,1)S(1)}, ...), branch_computations={%region_3.3_spmd, %region_4.6_spmd} | conditional | flops 2144782592 | bytes 60310380 | solution.py:321
  369.1 36.3 copy.617
  447.9 111.6 %conditional.38 = (bf16[14,14,1280]{2,1,0:T(8,128)(2,1)}, bf16[196,3840]{1,0:T(8,128)(2,1)S(1)}, f32[16,196,1]{1,0,2:T(8,128)S(1)}) conditional(s32[]{:T(128)} %convert_element_type.716, () %tuple.378, (bf16[14,14,1280]{2,0,1:T(8,128)(2,1)}, bf16[1280,3840]{1,0:T(8,128)(2,1)}, f32[3840]{0:T(1024)S(1)}, bf16[14,14,80]{2,1,0:T(8,128)(2,1)S(1)}, ...), branch_computations={%region_11.11_spmd, %region_12.14_spmd} | conditional | flops 2144782592 | bytes 60310380 | solution.py:321
  496.4 36.2 copy.639
  567.4 111.2 %conditional.39 = (bf16[14,14,1280]{2,1,0:T(8,128)(2,1)}, bf16[196,3840]{1,0:T(8,128)(2,1)S(1)}, f32[16,196,1]{1,0,2:T(8,128)S(1)}) conditional(s32[]{:T(128)} %convert_element_type.717, () %tuple.380, (bf16[14,14,1280]{2,0,1:T(8,128)(2,1)}, bf16[1280,3840]{1,0:T(8,128)(2,1)}, f32[3840]{0:T(1024)S(1)}, bf16[14,14,80]{2,1,0:T(8,128)(2,1)S(1)}, ...), branch_computations={%region_15.15_spmd, %region_16.18_spmd} | conditional | flops 2144782592 | bytes 60310380 | solution.py:321
  615.8 36.2 copy.650
  686.6 112.6 %conditional.40 = (bf16[14,14,1280]{2,1,0:T(8,128)(2,1)}, bf16[196,3840]{1,0:T(8,128)(2,1)S(1)}, f32[16,196,1]{1,0,2:T(8,128)S(1)}) conditional(s32[]{:T(128)} %convert_element_type.718, () %tuple.382, (bf16[14,14,1280]{2,0,1:T(8,128)(2,1)}, bf16[1280,3840]{1,0:T(8,128)(2,1)}, f32[3840]{0:T(1024)S(1)}, bf16[14,14,80]{2,1,0:T(8,128)(2,1)S(1)}, ...), branch_computations={%region_19.19_spmd, %region_20.22_spmd} | conditional | flops 2144782592 | bytes 60310380 | solution.py:321
  736.1 36.2 copy.661
  807.2 108.8 %conditional.41 = (bf16[14,14,1280]{2,1,0:T(8,128)(2,1)}, bf16[196,3840]{1,0:T(8,128)(2,1)S(1)}, f32[16,196,1]{1,0,2:T(8,128)S(1)}) conditional(s32[]{:T(128)} %convert_element_type.719, () %tuple.384, (bf16[14,14,1280]{2,0,1:T(8,128)(2,1)}, bf16[1280,3840]{1,0:T(8,128)(2,1)}, f32[3840]{0:T(1024)S(1)}, bf16[14,14,80]{2,1,0:T(8,128)(2,1)S(1)}, ...), branch_computations={%region_23.23_spmd, %region_24.26_spmd} | conditional | flops 2144782592 | bytes 60310380 | solution.py:321
  855.0 36.2 copy.672
  1133.0 191.3 %conditional.42 = (f32[1280,3840]{0,1:T(8,128)}, f32[3840]{0:T(1024)S(1)}, f32[14,14,80]{2,1,0:T(8,128)S(1)}, f32[14,14,80]{2,1,0:T(8,128)S(1)}, f32[14,14,1280]{2,0,1:T(8,128)S(1)}) conditional(s32[]{:T(128)} %convert_element_type.711, () %tuple.373, (bf16[196,3840]{1,0:T(8,128)(2,1)S(1)}, bf16[14,14,80]{2,1,0:T(8,128)(2,1)}, ...), branch_computations={%region_31.31_spmd, %region_32.36_spmd} | conditional | flops 4650800128 | bytes 103000816 | solution.py:401
  1336.2 192.7 %conditional.43 = (f32[1280,3840]{0,1:T(8,128)}, f32[3840]{0:T(1024)}, f32[14,14,80]{2,1,0:T(8,128)}, f32[14,14,80]{2,1,0:T(8,128)S(1)}, f32[14,14,1280]{2,0,1:T(8,128)S(1)}) conditional(s32[]{:T(128)} %convert_element_type.715, () %tuple.387, (bf16[196,3840]{1,0:T(8,128)(2,1)S(1)}, bf16[14,14,80]{2,1,0:T(8,128)(2,1)}, ...), branch_computations={%region_37.37_spmd, %region_38.42_spmd} | conditional | flops 4650800128 | bytes 102688440 | solution.py:401
  1538.3 192.1 %conditional.44 = (f32[1280,3840]{0,1:T(8,128)}, f32[3840]{0:T(1024)}, f32[14,14,80]{2,1,0:T(8,128)}, f32[14,14,80]{2,1,0:T(8,128)}, f32[14,14,1280]{2,0,1:T(8,128)S(1)}) conditional(s32[]{:T(128)} %convert_element_type.716, () %tuple.389, (bf16[196,3840]{1,0:T(8,128)(2,1)S(1)}, bf16[14,14,80]{2,1,0:T(8,128)(2,1)}, bf16[14,14,80]{2,1,0:T(8,128)(2,1)}, ...), branch_computations={%region_43.43_spmd, %region_44.48_spmd} | conditional | flops 4650800128 | bytes 102688440 | solution.py:401
  1739.6 191.2 %conditional.45 = (f32[1280,3840]{0,1:T(8,128)}, f32[3840]{0:T(1024)}, f32[14,14,80]{2,1,0:T(8,128)}, f32[14,14,80]{2,1,0:T(8,128)S(1)}, f32[14,14,1280]{2,0,1:T(8,128)S(1)}) conditional(s32[]{:T(128)} %convert_element_type.717, () %tuple.391, (bf16[196,3840]{1,0:T(8,128)(2,1)S(1)}, bf16[14,14,80]{2,1,0:T(8,128)(2,1)}, ...), branch_computations={%region_49.49_spmd, %region_50.54_spmd} | conditional | flops 4650800128 | bytes 102688440 | solution.py:401
  1940.1 192.2 %conditional.46 = (f32[1280,3840]{0,1:T(8,128)}, f32[3840]{0:T(1024)}, f32[14,14,80]{2,1,0:T(8,128)}, f32[14,14,80]{2,1,0:T(8,128)}, f32[14,14,1280]{2,0,1:T(8,128)S(1)}) conditional(s32[]{:T(128)} %convert_element_type.718, () %tuple.393, (bf16[196,3840]{1,0:T(8,128)(2,1)S(1)}, bf16[14,14,80]{2,1,0:T(8,128)(2,1)}, bf16[14,14,80]{2,1,0:T(8,128)(2,1)}, ...), branch_computations={%region_55.55_spmd, %region_56.60_spmd} | conditional | flops 4650800128 | bytes 102688440 | solution.py:401
  2141.5 191.5 %conditional.47 = (f32[1280,3840]{0,1:T(8,128)}, f32[3840]{0:T(1024)S(1)}, f32[14,14,80]{2,1,0:T(8,128)S(1)}, f32[14,14,80]{2,1,0:T(8,128)S(1)}, f32[14,14,1280]{2,0,1:T(8,128)S(1)}) conditional(s32[]{:T(128)} %convert_element_type.719, () %tuple.395, (bf16[196,3840]{1,0:T(8,128)(2,1)S(1)}, bf16[14,14,80]{2,1,0:T(8,128)(2,1)}, ...), branch_computations={%region_61.61_spmd, %region_62.66_spmd} | conditional | flops 4650800128 | bytes 103000816 | solution.py:401
  2346.0 44.0 fusion.574
  2450.6 47.1 all-reduce.25
  2532.9 98.6 %all-gather.3 = bf16[32,40,2]{1,2,0:T(2,128)(2,1)S(1)} all-gather(bf16[1,40,2]{1,2,0:T(2,128)(2,1)S(1)} %bitcast.805), channel_id=1, replica_groups=mesh['dp'=4,'rows'=4,'cols'=2] {'dp','rows','cols'}, dimensions={0}, use_global_device_ids=true | all-gather | bytes 5280 | tf_op jit(solution)/shard_map/while/body/eval_jaxpr/all_gather | solution.py:269
  2637.0 113.6 %conditional.37 = (bf16[14,14,1280]{2,1,0:T(8,128)(2,1)}, bf16[196,3840]{1,0:T(8,128)(2,1)S(1)}, f32[16,196,1]{1,0,2:T(8,128)S(1)}) conditional(s32[]{:T(128)} %convert_element_type.715, () %tuple.376, (bf16[14,14,1280]{2,0,1:T(8,128)(2,1)}, bf16[1280,3840]{1,0:T(8,128)(2,1)}, f32[3840]{0:T(1024)S(1)}, bf16[14,14,80]{2,1,0:T(8,128)(2,1)S(1)}, ...), branch_computations={%region_7.7_spmd, %region_8.10_spmd} | conditional | flops 2144782592 | bytes 60310380 | solution.py:321
  2687.2 36.4 copy.628
  2751.8 113.5 %conditional.36 = (bf16[14,14,1280]{2,1,0:T(8,128)(2,1)}, bf16[196,3840]{1,0:T(8,128)(2,1)S(1)}, f32[16,196,1]{1,0,2:T(8,128)S(1)}) conditional(s32[]{:T(128)} %convert_element_type.711, () %tuple.374, (bf16[14,14,1280]{2,0,1:T(8,128)(2,1)}, bf16[1280,3840]{1,0:T(8,128)(2,1)}, f32[3840]{0:T(1024)S(1)}, bf16[14,14,80]{2,1,0:T(8,128)(2,1)S(1)}, ...), branch_computations={%region_3.3_spmd, %region_4.6_spmd} | conditional | flops 2144782592 | bytes 60310380 | solution.py:321
  2802.1 36.6 copy.617
  2881.2 111.6 %conditional.38 = (bf16[14,14,1280]{2,1,0:T(8,128)(2,1)}, bf16[196,3840]{1,0:T(8,128)(2,1)S(1)}, f32[16,196,1]{1,0,2:T(8,128)S(1)}) conditional(s32[]{:T(128)} %convert_element_type.716, () %tuple.378, (bf16[14,14,1280]{2,0,1:T(8,128)(2,1)}, bf16[1280,3840]{1,0:T(8,128)(2,1)}, f32[3840]{0:T(1024)S(1)}, bf16[14,14,80]{2,1,0:T(8,128)(2,1)S(1)}, ...), branch_computations={%region_11.11_spmd, %region_12.14_spmd} | conditional | flops 2144782592 | bytes 60310380 | solution.py:321
  2929.7 36.2 copy.639
  3000.7 111.2 %conditional.39 = (bf16[14,14,1280]{2,1,0:T(8,128)(2,1)}, bf16[196,3840]{1,0:T(8,128)(2,1)S(1)}, f32[16,196,1]{1,0,2:T(8,128)S(1)}) conditional(s32[]{:T(128)} %convert_element_type.717, () %tuple.380, (bf16[14,14,1280]{2,0,1:T(8,128)(2,1)}, bf16[1280,3840]{1,0:T(8,128)(2,1)}, f32[3840]{0:T(1024)S(1)}, bf16[14,14,80]{2,1,0:T(8,128)(2,1)S(1)}, ...), branch_computations={%region_15.15_spmd, %region_16.18_spmd} | conditional | flops 2144782592 | bytes 60310380 | solution.py:321
  3049.1 36.2 copy.650
  3119.9 112.6 %conditional.40 = (bf16[14,14,1280]{2,1,0:T(8,128)(2,1)}, bf16[196,3840]{1,0:T(8,128)(2,1)S(1)}, f32[16,196,1]{1,0,2:T(8,128)S(1)}) conditional(s32[]{:T(128)} %convert_element_type.718, () %tuple.382, (bf16[14,14,1280]{2,0,1:T(8,128)(2,1)}, bf16[1280,3840]{1,0:T(8,128)(2,1)}, f32[3840]{0:T(1024)S(1)}, bf16[14,14,80]{2,1,0:T(8,128)(2,1)S(1)}, ...), branch_computations={%region_19.19_spmd, %region_20.22_spmd} | conditional | flops 2144782592 | bytes 60310380 | solution.py:321
  3169.4 36.2 copy.661
  3240.5 108.8 %conditional.41 = (bf16[14,14,1280]{2,1,0:T(8,128)(2,1)}, bf16[196,3840]{1,0:T(8,128)(2,1)S(1)}, f32[16,196,1]{1,0,2:T(8,128)S(1)}) conditional(s32[]{:T(128)} %convert_element_type.719, () %tuple.384, (bf16[14,14,1280]{2,0,1:T(8,128)(2,1)}, bf16[1280,3840]{1,0:T(8,128)(2,1)}, f32[3840]{0:T(1024)S(1)}, bf16[14,14,80]{2,1,0:T(8,128)(2,1)S(1)}, ...), branch_computations={%region_23.23_spmd, %region_24.26_spmd} | conditional | flops 2144782592 | bytes 60310380 | solution.py:321
  3288.3 36.2 copy.672
  3570.1 191.3 %conditional.42 = (f32[1280,3840]{0,1:T(8,128)}, f32[3840]{0:T(1024)S(1)}, f32[14,14,80]{2,1,0:T(8,128)S(1)}, f32[14,14,80]{2,1,0:T(8,128)S(1)}, f32[14,14,1280]{2,0,1:T(8,128)S(1)}) conditional(s32[]{:T(128)} %convert_element_type.711, () %tuple.373, (bf16[196,3840]{1,0:T(8,128)(2,1)S(1)}, bf16[14,14,80]{2,1,0:T(8,128)(2,1)}, ...), branch_computations={%region_31.31_spmd, %region_32.36_spmd} | conditional | flops 4650800128 | bytes 103000816 | solution.py:401
  3773.3 192.7 %conditional.43 = (f32[1280,3840]{0,1:T(8,128)}, f32[3840]{0:T(1024)}, f32[14,14,80]{2,1,0:T(8,128)}, f32[14,14,80]{2,1,0:T(8,128)S(1)}, f32[14,14,1280]{2,0,1:T(8,128)S(1)}) conditional(s32[]{:T(128)} %convert_element_type.715, () %tuple.387, (bf16[196,3840]{1,0:T(8,128)(2,1)S(1)}, bf16[14,14,80]{2,1,0:T(8,128)(2,1)}, ...), branch_computations={%region_37.37_spmd, %region_38.42_spmd} | conditional | flops 4650800128 | bytes 102688440 | solution.py:401
  3975.3 192.1 %conditional.44 = (f32[1280,3840]{0,1:T(8,128)}, f32[3840]{0:T(1024)}, f32[14,14,80]{2,1,0:T(8,128)}, f32[14,14,80]{2,1,0:T(8,128)}, f32[14,14,1280]{2,0,1:T(8,128)S(1)}) conditional(s32[]{:T(128)} %convert_element_type.716, () %tuple.389, (bf16[196,3840]{1,0:T(8,128)(2,1)S(1)}, bf16[14,14,80]{2,1,0:T(8,128)(2,1)}, bf16[14,14,80]{2,1,0:T(8,128)(2,1)}, ...), branch_computations={%region_43.43_spmd, %region_44.48_spmd} | conditional | flops 4650800128 | bytes 102688440 | solution.py:401
  4176.7 191.2 %conditional.45 = (f32[1280,3840]{0,1:T(8,128)}, f32[3840]{0:T(1024)}, f32[14,14,80]{2,1,0:T(8,128)}, f32[14,14,80]{2,1,0:T(8,128)S(1)}, f32[14,14,1280]{2,0,1:T(8,128)S(1)}) conditional(s32[]{:T(128)} %convert_element_type.717, () %tuple.391, (bf16[196,3840]{1,0:T(8,128)(2,1)S(1)}, bf16[14,14,80]{2,1,0:T(8,128)(2,1)}, ...), branch_computations={%region_49.49_spmd, %region_50.54_spmd} | conditional | flops 4650800128 | bytes 102688440 | solution.py:401
  4377.2 192.2 %conditional.46 = (f32[1280,3840]{0,1:T(8,128)}, f32[3840]{0:T(1024)}, f32[14,14,80]{2,1,0:T(8,128)}, f32[14,14,80]{2,1,0:T(8,128)}, f32[14,14,1280]{2,0,1:T(8,128)S(1)}) conditional(s32[]{:T(128)} %convert_element_type.718, () %tuple.393, (bf16[196,3840]{1,0:T(8,128)(2,1)S(1)}, bf16[14,14,80]{2,1,0:T(8,128)(2,1)}, bf16[14,14,80]{2,1,0:T(8,128)(2,1)}, ...), branch_computations={%region_55.55_spmd, %region_56.60_spmd} | conditional | flops 4650800128 | bytes 102688440 | solution.py:401
  4578.5 191.5 %conditional.47 = (f32[1280,3840]{0,1:T(8,128)}, f32[3840]{0:T(1024)S(1)}, f32[14,14,80]{2,1,0:T(8,128)S(1)}, f32[14,14,80]{2,1,0:T(8,128)S(1)}, f32[14,14,1280]{2,0,1:T(8,128)S(1)}) conditional(s32[]{:T(128)} %convert_element_type.719, () %tuple.395, (bf16[196,3840]{1,0:T(8,128)(2,1)S(1)}, bf16[14,14,80]{2,1,0:T(8,128)(2,1)}, ...), branch_computations={%region_61.61_spmd, %region_62.66_spmd} | conditional | flops 4650800128 | bytes 103000816 | solution.py:401
  4783.1 49.6 fusion.574
  4913.6 116.7 %all-reduce.28.cloned.1.call-done = (f32[1280]{0:T(1024)}, f32[1280]{0:T(1024)}, f32[1280,2]{0,1:T(2,128)}, f32[27,80]{1,0:T(8,128)}, f32[27,80]{1,0:T(8,128)}, ...) async-done(((f32[1280]{0:T(1024)}, f32[1280]{0:T(1024)}, f32[1280,2]{0,1:T(2,128)}, f32[27,80]{1,0:T(8,128)}, ...) | async-done | bytes 78736
  5040.6 140.5 %reduce-scatter.8.cloned.1.call-done = f32[40,1280]{1,0:T(8,128)} async-done(((f32[1280,1280]{1,0:T(8,128)}), f32[40,1280]{1,0:T(8,128)}) %reduce-scatter.8.cloned.1.call-update) | async-done | bytes 204816 | tf_op jit(solution)/shard_map/reduce_scatter | solution.py:457
  5181.1 219.7 %reduce-scatter.6.cloned.1.call-done = f32[40,3840]{1,0:T(8,128)} async-done(((f32[1280,3840]{1,0:T(8,128)}), f32[40,3840]{1,0:T(8,128)}) %reduce-scatter.6.cloned.1.call-update) | async-done | bytes 614416 | tf_op jit(solution)/shard_map/reduce_scatter | solution.py:455
  5400.8 556.7 %reduce-scatter.10.cloned.1.call-done = f32[40,5120]{1,0:T(8,128)} async-done(((f32[1280,5120]{1,0:T(8,128)}), f32[40,5120]{1,0:T(8,128)}) %reduce-scatter.10.cloned.1.call-update) | async-done | bytes 819216 | tf_op jit(solution)/shard_map/reduce_scatter | solution.py:465
  5957.4 556.3 %reduce-scatter.12.cloned.1.call-done = f32[160,1280]{1,0:T(8,128)} async-done(((f32[5120,1280]{1,0:T(8,128)}), f32[160,1280]{1,0:T(8,128)}) %reduce-scatter.12.cloned.1.call-update) | async-done | bytes 819216 | tf_op jit(solution)/shard_map/reduce_scatter | solution.py:467
  (1723 shorter events, 4083.3 us)
Async XLA Ops:
  10.0 797.2 %copy-start.8 = (bf16[14,14,80]{2,1,0:T(8,128)(2,1)}, bf16[14,14,80]{2,1,0:T(8,128)(2,1)S(1)}, u32[]{:S(2)}) copy-start(bf16[14,14,80]{2,1,0:T(8,128)(2,1)S(1)} %get-tuple-element.2776) | copy-start | bytes 94084 | tf_op jit(solution)/shard_map/while
  10.0 797.2 %copy-start.16 = (bf16[14,14,80]{2,1,0:T(8,128)(2,1)}, bf16[14,14,80]{2,1,0:T(8,128)(2,1)S(1)}, u32[]{:S(2)}) copy-start(bf16[14,14,80]{2,1,0:T(8,128)(2,1)S(1)} %get-tuple-element.2777) | copy-start | bytes 94084 | tf_op jit(solution)/shard_map/while
  10.0 193.4 %all-gather.9.cloned.1.call-start = ((), (), s32[]{:S(2)}) async-start(), calls=%async_computation.9 | async-start | bytes 10137600 | tf_op jit(solution)/shard_map/while/body/eval_jaxpr/all_gather | solution.py:268
  10.7 959.4 %all-gather.11.cloned.1.call-start = ((), (), s32[]{:S(2)}) async-start(), calls=%async_computation.10 | async-start | bytes 3379200 | tf_op jit(solution)/shard_map/while/body/eval_jaxpr/all_gather | solution.py:270
  11.5 965.3 %all-gather.13.cloned.1.call-start = ((), (), s32[]{:S(2)}) async-start(), calls=%async_computation.11 | async-start | bytes 13516800 | tf_op jit(solution)/shard_map/while/body/eval_jaxpr/all_gather | solution.py:274
  12.2 998.5 %all-gather.15.cloned.1.call-start = ((), (), s32[]{:S(2)}) async-start(), calls=%async_computation.12 | async-start | bytes 13516800 | tf_op jit(solution)/shard_map/while/body/eval_jaxpr/all_gather | solution.py:276
  66.6 30.3 copy-start.150
  66.7 27.2 collective-permute-start
  95.6 102.5 %collective-permute-start.1 = (bf16[13,45,1280]{2,1,0:T(8,128)(2,1)}, bf16[13,45,1280]{2,1,0:T(8,128)(2,1)}, u32[]{:S(2)}, u32[]{:S(2)}) collective-permute-start(bf16[13,45,1280]{2,1,0:T(8,128)(2,1)} %copy.1341), channel_id=1, source_target_pairs={{2,0},{4,2},{6,4},{3,1},{5,3},{7,5},{10,8},{12,10},{14,12},{11,9},... | collective-permute-start | bytes 4492808 | tf_op jit(solution)/shard_map/while/body/eval_jaxpr/ppermute | solution.py:18
  925.4 29.7 collective-permute-start.2
  928.5 32.0 copy-start.3
  959.2 7.8 collective-permute-start.3
  1053.5 43.8 collective-permute-start.4
  1098.8 32.2 collective-permute-start.5
  1107.2 25.8 copy-start.31
  1107.2 25.8 copy-start.59
  1107.2 25.8 copy-start.113
  2344.6 55.2 collective-permute-start.6
  2404.4 18.5 copy-start.127
  2404.4 18.7 copy-start.130
  2421.6 7.5 collective-permute-start.7
  2441.9 798.5 %copy-start.8 = (bf16[14,14,80]{2,1,0:T(8,128)(2,1)}, bf16[14,14,80]{2,1,0:T(8,128)(2,1)S(1)}, u32[]{:S(2)}) copy-start(bf16[14,14,80]{2,1,0:T(8,128)(2,1)S(1)} %get-tuple-element.2776) | copy-start | bytes 94084 | tf_op jit(solution)/shard_map/while
  2441.9 798.5 %copy-start.16 = (bf16[14,14,80]{2,1,0:T(8,128)(2,1)}, bf16[14,14,80]{2,1,0:T(8,128)(2,1)S(1)}, u32[]{:S(2)}) copy-start(bf16[14,14,80]{2,1,0:T(8,128)(2,1)S(1)} %get-tuple-element.2777) | copy-start | bytes 94084 | tf_op jit(solution)/shard_map/while
  2441.9 195.1 %all-gather.9.cloned.1.call-start = ((), (), s32[]{:S(2)}) async-start(), calls=%async_computation.9 | async-start | bytes 10137600 | tf_op jit(solution)/shard_map/while/body/eval_jaxpr/all_gather | solution.py:268
  2442.5 958.7 %all-gather.11.cloned.1.call-start = ((), (), s32[]{:S(2)}) async-start(), calls=%async_computation.10 | async-start | bytes 3379200 | tf_op jit(solution)/shard_map/while/body/eval_jaxpr/all_gather | solution.py:270
  2443.1 964.8 %all-gather.13.cloned.1.call-start = ((), (), s32[]{:S(2)}) async-start(), calls=%async_computation.11 | async-start | bytes 13516800 | tf_op jit(solution)/shard_map/while/body/eval_jaxpr/all_gather | solution.py:274
  2443.9 997.9 %all-gather.15.cloned.1.call-start = ((), (), s32[]{:S(2)}) async-start(), calls=%async_computation.12 | async-start | bytes 13516800 | tf_op jit(solution)/shard_map/while/body/eval_jaxpr/all_gather | solution.py:276
  2502.6 30.3 copy-start.150
  2502.6 27.2 collective-permute-start
  2531.6 100.1 %collective-permute-start.1 = (bf16[13,45,1280]{2,1,0:T(8,128)(2,1)}, bf16[13,45,1280]{2,1,0:T(8,128)(2,1)}, u32[]{:S(2)}, u32[]{:S(2)}) collective-permute-start(bf16[13,45,1280]{2,1,0:T(8,128)(2,1)} %copy.1341), channel_id=1, source_target_pairs={{2,0},{4,2},{6,4},{3,1},{5,3},{7,5},{10,8},{12,10},{14,12},{11,9},... | collective-permute-start | bytes 4492808 | tf_op jit(solution)/shard_map/while/body/eval_jaxpr/ppermute | solution.py:18
  3358.7 27.4 collective-permute-start.2
  3361.8 29.8 copy-start.3
  3390.3 7.8 collective-permute-start.3
  3484.5 51.9 collective-permute-start.4
  3504.8 18.8 copy-start.145
  3537.9 30.2 collective-permute-start.5
  3549.2 20.9 copy-start.31
  3549.2 20.9 copy-start.59
  3549.2 20.9 copy-start.113
  4781.7 60.8 collective-permute-start.6
  4847.1 18.7 copy-start.130
  4864.3 7.5 collective-permute-start.7
  4886.2 144.1 %all-reduce.28.cloned.1.call-start = ((), (), s32[]{:S(2)}) async-start(), calls=%async_computation.8 | async-start | bytes 225280
  4889.8 291.3 %reduce-scatter.8.cloned.1.call-start = ((), (), s32[]{:S(2)}) async-start(), calls=%async_computation.5 | async-start | bytes 6758400 | tf_op jit(solution)/shard_map/reduce_scatter | solution.py:457
  4890.4 510.4 %reduce-scatter.6.cloned.1.call-start = ((), (), s32[]{:S(2)}) async-start(), calls=%async_computation.4 | async-start | bytes 20275200 | tf_op jit(solution)/shard_map/reduce_scatter | solution.py:455
  4912.1 1045.3 %reduce-scatter.10.cloned.1.call-start = ((), (), s32[]{:S(2)}) async-start(), calls=%async_computation.6 | async-start | bytes 27033600 | tf_op jit(solution)/shard_map/reduce_scatter | solution.py:465
  4912.8 1601.0 %reduce-scatter.12.cloned.1.call-start = ((), (), s32[]{:S(2)}) async-start(), calls=%async_computation.7 | async-start | bytes 27033600 | tf_op jit(solution)/shard_map/reduce_scatter | solution.py:467
  4913.6 1602.8 %copy-start.1 = (bf16[27,80]{1,0:T(8,128)(2,1)S(1)}, bf16[27,80]{1,0:T(8,128)(2,1)}, u32[]{:S(2)}) copy-start(bf16[27,80]{1,0:T(8,128)(2,1)} %param.55) | copy-start | bytes 12964
  (293 other events, 1563.7 us)
Sparse Core Ops, SparseCore 0:
  14.3 102.0 all-gather.8
  119.6 62.8 all-gather.10
  185.7 97.4 all-gather.12
  286.3 96.7 all-gather.14
  2445.9 106.2 all-gather.8
  2555.3 63.2 all-gather.10
  2621.8 97.4 all-gather.12
  2722.5 96.7 all-gather.14
Sparse Core Ops, SparseCore 1:
  4893.7 136.6 all-reduce.27
  5033.1 147.9 reduce-scatter.7
  5189.1 211.6 reduce-scatter.5
  5403.8 553.6 reduce-scatter.9
  5960.5 553.3 reduce-scatter.11
where the time goes:
time: 6570 us; the launch traced here: 6520 us
  local copies, waits for them, and re-layouts  2390 us (36%)
  waiting for transfers between devices  1750 us (27%)
  matrix products  1540 us (23%)
  other arithmetic  503 us (8%)
  blocking collectives  290 us (4%)
    reshape x36, local copies, waits for them, and re-layouts, scores_of(): return scores.reshape(heads, width * width, width * width)  811 us
    reduce_scatter x1, waiting for transfers between devices, shards(): lax.psum_scatter(total_up, ('dp', 'rows', 'cols'), scatter_dimension=0, t...  557 us
    reduce_scatter x1, waiting for transfers between devices, shards(): lax.psum_scatter(total_down, ('dp', 'rows', 'cols'), scatter_dimension=0,...  556 us
    add x12, local copies, waits for them, and re-layouts, scores_of(): scores + along_rows[:, :, :, :, None] + along_cols[:, :, :, None, :]  435 us
    dot_general x24, matrix products, scores_of(): jnp.einsum('abhc,ijhc->habij', query, key, preferred_element_type=jnp.flo...  313 us
    reduce_scatter x1, waiting for transfers between devices, shards(): lax.psum_scatter(total_qkv, ('dp', 'rows', 'cols'), scatter_dimension=0,...  220 us
    dot_general x12, matrix products, window_backward(): jnp.einsum('habij,ijhc->abhc', grid, key, preferred_element_type=jnp.floa...  213 us
    all_gather x2, blocking collectives, step_image(): lax.all_gather(qv_bias, ('dp', 'rows', 'cols'), axis=0, tiled=True)  200 us
  transfers between devices with their start and end apart: 29, of which 15 were waited for; matrix products, arithmetic and copies ran while one was open for 28% of the time, Pallas kernels for 0%

commit v1 on v0

v1 whole, which is shorter than its diff:
```python
import functools

import jax
import jax.numpy as jnp
import numpy as np
from jax import lax
from jax.experimental import pallas as pl
from jax.experimental.pallas import tpu as pltpu
from jax.sharding import PartitionSpec as P

HEADS = 16
WIN = 14
NWIN = 5
SIDE = 16
HD = 80
KEYS = WIN * SIDE
TOK = SIDE * SIDE
LANES = 128
DEPTH = 128
REL = 2 * WIN - 1
NEG = -1e30
ALL = ("dp", "rows", "cols")
MIB = 1024 * 1024

eps = 1e-06


def dot(a, b):
    return jnp.dot(a, b, preferred_element_type=jnp.float32)


def dot_nt(a, b):
    return lax.dot_general(a, b, (((1,), (1,)), ((), ())), preferred_element_type=jnp.float32)


def dot_tn(a, b):
    return lax.dot_general(a, b, (((0,), (0,)), ((), ())), preferred_element_type=jnp.float32)


def offset_onehot(dtype):
    a = jnp.arange(WIN)[:, None]
    i = jnp.arange(SIDE)[None, :]
    offset = jnp.where(i < WIN, a - i + WIN - 1, -1)
    return (offset[:, :, None] == jnp.arange(REL)).astype(dtype).reshape(KEYS, REL)


def wide_tables(rel_rows, rel_cols):
    onehot = offset_onehot(jnp.bfloat16)
    return jnp.concatenate(
        [dot(onehot, table).astype(jnp.bfloat16) for table in (rel_rows, rel_cols)], axis=0
    )


def narrow_tables(grad):
    onehot = offset_onehot(jnp.float32)
    return [
        lax.dot_general(
            onehot,
            grad[n * KEYS : (n + 1) * KEYS],
            (((0,), (0,)), ((), ())),
            precision=lax.Precision.HIGHEST,
        )
        for n in (0, 1)
    ]


def key_indicator():
    row = lax.broadcasted_iota(jnp.int32, (DEPTH - HD, TOK), 0)
    key = lax.broadcasted_iota(jnp.int32, (DEPTH - HD, TOK), 1)
    return ((row == key // SIDE) | (row - SIDE == key % SIDE)).astype(jnp.bfloat16)


def query_offsets(query, tab_ref, lane):
    halves = []
    for half in range(2):
        low = half * 8
        count = min(8, WIN - low)
        part = dot(
            tab_ref[low * SIDE : (low + count) * SIDE], query[:, half * LANES : (half + 1) * LANES]
        )
        rows = part[:SIDE]
        for a in range(1, count):
            rows = jnp.where(
                lane[:, :LANES] // SIDE == a, part[a * SIDE : (a + 1) * SIDE], rows
            )
        halves.append(rows)
    part = dot(tab_ref[KEYS:], query)
    cols = part[:SIDE]
    for b in range(1, WIN):
        cols = jnp.where(lane % SIDE == b, part[b * SIDE : (b + 1) * SIDE], cols)
    return jnp.concatenate(halves, axis=1), cols


def attention_forward_kernel(
    project_ref, tab_ref, ind_ref, attended_ref, weights_ref, inverse_ref, turned_ref
):
    model = turned_ref.shape[0]
    lane = lax.broadcasted_iota(jnp.int32, (SIDE, TOK), 1)
    sub = lax.broadcasted_iota(jnp.int32, (SIDE, TOK), 0)
    ind = ind_ref[...]
    scale = HD**-0.5
    zeros = jnp.zeros((DEPTH - HD - 2 * SIDE, TOK), jnp.bfloat16)
    for head in range(HEADS):
        low = head * HD
        query = project_ref[low : low + HD]
        key = project_ref[model + low : model + low + HD]
        value = project_ref[2 * model + low : 2 * model + low + HD]
        rows, cols = query_offsets(query, tab_ref, lane)
        rows = (rows * HD**0.5).astype(jnp.bfloat16)
        cols = jnp.where(sub < WIN, cols * HD**0.5, NEG).astype(jnp.bfloat16)
        query_wide = jnp.concatenate([query, rows, cols, zeros], axis=0)
        key_wide = jnp.concatenate([key, ind], axis=0)
        scores = dot_tn(key_wide, query_wide)[:KEYS]
        maxima = jnp.max(scores, axis=0, keepdims=True)
        weights = jnp.exp((scores - maxima) * scale)
        inverse = 1.0 / jnp.sum(weights, axis=0, keepdims=True)
        weights = weights.astype(jnp.bfloat16)
        weights_ref[0, head] = weights
        inverse_ref[0, head : head + 1] = inverse
        attended = dot(value[:, :KEYS], weights)
        turned_ref[low : low + HD] = (attended * inverse).astype(jnp.bfloat16)
    attended_ref[...] = turned_ref[...].T


def attention_forward(project, tab, ind):
    model = project.shape[0] // 3
    slots = project.shape[1] // TOK
    return pl.pallas_call(
        attention_forward_kernel,
        grid=(slots,),
        in_specs=[
            pl.BlockSpec((3 * model, TOK), lambda i: (0, i)),
            pl.BlockSpec((2 * KEYS, HD), lambda i: (0, 0)),
            pl.BlockSpec((DEPTH - HD, TOK), lambda i: (0, 0)),
        ],
        out_specs=[
            pl.BlockSpec((TOK, model), lambda i: (i, 0)),
            pl.BlockSpec((1, HEADS, KEYS, TOK), lambda i: (i, 0, 0, 0)),
            pl.BlockSpec((1, HEADS, TOK), lambda i: (i, 0, 0)),
        ],
        out_shape=[
            jax.ShapeDtypeStruct((slots * TOK, model), jnp.bfloat16),
            jax.ShapeDtypeStruct((slots, HEADS, KEYS, TOK), jnp.bfloat16),
            jax.ShapeDtypeStruct((slots, HEADS, TOK), jnp.float32),
        ],
        scratch_shapes=[pltpu.VMEM((model, TOK), jnp.bfloat16)],
        compiler_params=pltpu.CompilerParams(vmem_limit_bytes=48 * MIB),
        cost_estimate=pl.CostEstimate(
            flops=slots * HEADS * 800 * 2 * TOK * LANES,
            bytes_accessed=slots * 6 * MIB,
            transcendentals=slots * HEADS * KEYS * TOK,
        ),
    )(project, tab, ind)


def attention_backward_kernel(
    project_ref, weights_ref, inverse_ref, grad_ref, tab_ref, ind_ref, out_ref, dtab_ref, turned_ref
):
    model = turned_ref.shape[0]
    lane = lax.broadcasted_iota(jnp.int32, (SIDE, TOK), 1)
    ind = ind_ref[...]
    tab = tab_ref[...]
    scale = HD**-0.5

    @pl.when(pl.program_id(0) == 0)
    def _():
        dtab_ref[...] = jnp.zeros_like(dtab_ref)

    turned_ref[...] = grad_ref[...].T
    total = jnp.zeros(dtab_ref.shape, jnp.float32)
    for head in range(HEADS):
        low = head * HD
        query = project_ref[low : low + HD]
        key = project_ref[model + low : model + low + HD]
        value = project_ref[2 * model + low : 2 * model + low + HD]
        inverse = inverse_ref[0, head : head + 1]
        grad = (turned_ref[low : low + HD] * inverse).astype(jnp.bfloat16)
        weights = weights_ref[0, head]
        weights_float = weights.astype(jnp.float32)
        terms = weights_float * dot_tn(value, grad)[:KEYS]
        inner = jnp.sum(terms, axis=0, keepdims=True) * inverse
        grad_scores = (terms - weights_float * inner).astype(jnp.bfloat16)
        grad_value = dot_nt(grad, weights)
        grad_key = dot_nt(query, grad_scores) * scale
        key_wide = jnp.concatenate([key, ind], axis=0)
        grad_wide = dot(key_wide[:, :KEYS], grad_scores)
        rows = grad_wide[HD : HD + SIDE]
        cols = grad_wide[HD + SIDE : HD + 2 * SIDE]
        spread = jnp.concatenate(
            [jnp.where(lane // SIDE == a, rows, 0.0) for a in range(WIN)]
            + [jnp.where(lane % SIDE == b, cols, 0.0) for b in range(WIN)],
            axis=0,
        ).astype(jnp.bfloat16)
        grad_query = grad_wide[:HD] * scale + dot_tn(tab, spread)
        total = total + dot_nt(spread, query)
        out_ref[low : low + HD] = grad_query.astype(jnp.bfloat16)
        out_ref[model + low : model + low + HD, :KEYS] = grad_key.astype(jnp.bfloat16)
        out_ref[2 * model + low : 2 * model + low + HD, :KEYS] = grad_value.astype(jnp.bfloat16)
    out_ref[model:, KEYS:] = jnp.zeros((2 * model, TOK - KEYS), jnp.bfloat16)
    dtab_ref[...] += total


def attention_backward(project, weights, inverse, grad, tab, ind):
    model = project.shape[0] // 3
    slots = project.shape[1] // TOK
    return pl.pallas_call(
        attention_backward_kernel,
        grid=(slots,),
        in_specs=[
            pl.BlockSpec((3 * model, TOK), lambda i: (0, i)),
            pl.BlockSpec((1, HEADS, KEYS, TOK), lambda i: (i, 0, 0, 0)),
            pl.BlockSpec((1, HEADS, TOK), lambda i: (i, 0, 0)),
            pl.BlockSpec((TOK, model), lambda i: (i, 0)),
            pl.BlockSpec((2 * KEYS, HD), lambda i: (0, 0)),
            pl.BlockSpec((DEPTH - HD, TOK), lambda i: (0, 0)),
        ],
        out_specs=[
            pl.BlockSpec((3 * model, TOK), lambda i: (0, i)),
            pl.BlockSpec((2 * KEYS, HD), lambda i: (0, 0)),
        ],
        out_shape=[
            jax.ShapeDtypeStruct((3 * model, slots * TOK), jnp.bfloat16),
            jax.ShapeDtypeStruct((2 * KEYS, HD), jnp.float32),
        ],
        scratch_shapes=[pltpu.VMEM((model, TOK), jnp.bfloat16)],
        compiler_params=pltpu.CompilerParams(vmem_limit_bytes=48 * MIB),
        cost_estimate=pl.CostEstimate(
            flops=slots * HEADS * 1600 * 2 * TOK * LANES,
            bytes_accessed=slots * 7 * MIB,
            transcendentals=0,
        ),
    )(project, weights, inverse, grad, tab, ind)


def mlp_kernel(
    rows,
    normed_ref,
    turned_ref,
    cot_ref,
    up_ref,
    down_ref,
    shift_ref,
    mixed0_ref,
    grad0_ref,
    mixed_ref,
    grad_ref,
    dup_ref,
    ddown_ref,
    dshift_ref,
    active_ref,
    hidden_ref,
):
    tokens = normed_ref.shape[0]

    @pl.when(pl.program_id(0) == 0)
    def _():
        mixed_ref[...] = mixed0_ref[...]
        grad_ref[...] = grad0_ref[...]

    up = up_ref[...]
    down = down_ref[...]
    shift = shift_ref[...]
    total = jnp.zeros(shift.shape, jnp.float32)
    for step in range(tokens // rows):
        part = slice(step * rows, (step + 1) * rows)
        hidden = dot(normed_ref[part], up) + shift
        grad_active = dot_nt(cot_ref[part], down)
        half = 0.5 + 0.5 * lax.erf(hidden * 0.5**0.5)
        active = (hidden * half).astype(jnp.bfloat16)
        slope = half + hidden * jnp.exp(hidden * hidden * -0.5) * (2 * np.pi) ** -0.5
        grad_hidden = (grad_active * slope).astype(jnp.bfloat16)
        active_ref[part] = active
        hidden_ref[part] = grad_hidden
        total = total + jnp.sum(grad_hidden.astype(jnp.float32), axis=0, keepdims=True)
        mixed_ref[part] += dot(active, down)
        grad_ref[part] += dot_nt(grad_hidden, up)
    dshift_ref[...] = total
    ddown_ref[...] = dot_tn(active_ref[...], cot_ref[...]).astype(jnp.bfloat16)
    dup_ref[...] = dot(turned_ref[...], hidden_ref[...]).astype(jnp.bfloat16)


def mlp(normed, turned, cot, up, down, shift, mixed0, grad0):
    tokens, model = normed.shape
    hidden = up.shape[1]
    block = 512 if hidden % 512 == 0 else 256
    rows = min(512, tokens)
    once = pl.Buffered(1)
    whole = pl.BlockSpec((tokens, model), lambda i: (0, 0), pipeline_mode=once)
    return pl.pallas_call(
        functools.partial(mlp_kernel, rows),
        grid=(hidden // block,),
        in_specs=[
            whole,
            pl.BlockSpec((model, tokens), lambda i: (0, 0), pipeline_mode=once),
            whole,
            pl.BlockSpec((model, block), lambda i: (0, i)),
            pl.BlockSpec((block, model), lambda i: (i, 0)),
            pl.BlockSpec((1, block), lambda i: (0, i)),
            whole,
            whole,
        ],
        out_specs=[
            pl.BlockSpec((tokens, model), lambda i: (0, 0)),
            pl.BlockSpec((tokens, model), lambda i: (0, 0)),
            pl.BlockSpec((model, block), lambda i: (0, i)),
            pl.BlockSpec((block, model), lambda i: (i, 0)),
            pl.BlockSpec((1, block), lambda i: (0, i)),
        ],
        out_shape=[
            jax.ShapeDtypeStruct((tokens, model), jnp.float32),
            jax.ShapeDtypeStruct((tokens, model), jnp.float32),
            jax.ShapeDtypeStruct((model, hidden), jnp.bfloat16),
            jax.ShapeDtypeStruct((hidden, model), jnp.bfloat16),
            jax.ShapeDtypeStruct((1, hidden), jnp.float32),
        ],
        scratch_shapes=[pltpu.VMEM((tokens, block), jnp.bfloat16)] * 2,
        compiler_params=pltpu.CompilerParams(vmem_limit_bytes=56 * MIB),
        cost_estimate=pl.CostEstimate(
            flops=12 * tokens * model * hidden,
            bytes_accessed=8 * model * hidden + 24 * tokens * model,
            transcendentals=2 * tokens * hidden,
        ),
    )(normed, turned, cot, up, down, shift, mixed0, grad0)


def normalised(values):
    average = jnp.mean(values, axis=-1, keepdims=True)
    centered = values - average
    variance = jnp.mean(centered * centered, axis=-1, keepdims=True)
    inverse = lax.rsqrt(variance + eps)
    return centered * inverse, inverse


def norm_backward(unit, inverse, gain, grad):
    scaled = grad * gain
    grad_values = inverse * (
        scaled
        - jnp.mean(scaled, axis=-1, keepdims=True)
        - unit * jnp.mean(scaled * unit, axis=-1, keepdims=True)
    )
    return grad_values, jnp.sum(grad * unit, axis=0), jnp.sum(grad, axis=0)


def axis_bits(axis):
    count = lax.axis_size(axis)
    return [(axis, 1 << bit) for bit in range(count.bit_length() - 1)]


def flipped(value, bit):
    axis, mask = bit
    return lax.ppermute(value, axis, [(i, i ^ mask) for i in range(lax.axis_size(axis))])


def bit_of(bit):
    axis, mask = bit
    return (lax.axis_index(axis) // mask) % 2


def device_bits():
    return [bit for axis in ALL for bit in reversed(axis_bits(axis))]


def scatter_sum(value, order):
    left = device_bits()
    block = value.shape[0] >> len(left)
    value = value.reshape((2,) * len(left) + (block,) + value.shape[1:])
    for bit in order:
        place = left.index(bit)
        mine = bit_of(bit)
        sent = lax.dynamic_index_in_dim(value, 1 - mine, place, keepdims=False)
        kept = lax.dynamic_index_in_dim(value, mine, place, keepdims=False)
        value = kept.astype(jnp.float32) + flipped(sent, bit).astype(jnp.float32)
        left.remove(bit)
        if left:
            value = value.astype(jnp.bfloat16)
    return value


def all_sum(value):
    for bit in reversed(device_bits()):
        value = value + flipped(value, bit)
    return value


def small_gather(value):
    for bit in reversed(device_bits()):
        arrived = flipped(value, bit)
        value = jnp.where(
            bit_of(bit) == 0,
            jnp.concatenate([value, arrived], axis=0),
            jnp.concatenate([arrived, value], axis=0),
        )
    return value


def halves_to_image(tiles):
    col = lax.axis_index("cols")
    kept = lax.dynamic_index_in_dim(tiles, col, 0, keepdims=False)
    sent = lax.dynamic_index_in_dim(tiles, 1 - col, 0, keepdims=False)
    arrived = lax.ppermute(sent, "cols", [(0, 1), (1, 0)])
    return jnp.where(
        col == 0,
        jnp.concatenate([kept, arrived], axis=1),
        jnp.concatenate([arrived, kept], axis=1),
    )


def image_to_halves(image):
    col = lax.axis_index("cols")
    width = image.shape[1] // 2
    kept = lax.dynamic_slice_in_dim(image, col * width, width, 1)
    sent = lax.dynamic_slice_in_dim(image, (1 - col) * width, width, 1)
    arrived = lax.ppermute(sent, "cols", [(0, 1), (1, 0)])
    return jnp.where(col == 0, jnp.stack([kept, arrived]), jnp.stack([arrived, kept]))


def column_windows(tile):
    height, width, model = tile.shape
    wide = jnp.pad(tile, ((0, 0), (0, NWIN * WIN - width), (0, 0)))
    wide = wide.reshape(height, NWIN, WIN, model).transpose(1, 0, 2, 3)
    return jnp.pad(wide, ((0, 0), (0, 0), (0, SIDE - WIN), (0, 0)))


def column_rows(windows, width):
    _, height, _, model = windows.shape
    wide = windows[:, :, :WIN].transpose(1, 0, 2, 3).reshape(height, NWIN * WIN, model)
    return wide[:, :width]


def pad_rows(value, top, bottom):
    widths = [(0, 0)] * value.ndim
    widths[-3] = (top, bottom)
    return jnp.pad(value, widths)


def near_plan():
    return lax.axis_size("rows") == NWIN - 1


def spread(tile):
    height = tile.shape[0]
    count = lax.axis_size("rows")
    row = lax.axis_index("rows")
    windows = column_windows(tile)
    if not near_plan():
        windows = lax.all_gather(windows, "rows", axis=1, tiled=True)
        extra = NWIN * WIN - windows.shape[1]
        windows = jnp.pad(windows, ((0, 0), (0, extra), (0, 0), (0, 0)))
        windows = windows.reshape(NWIN, NWIN, WIN, SIDE, -1).transpose(1, 0, 2, 3, 4)
        windows = windows.reshape((NWIN * NWIN,) + windows.shape[2:])
        slots = -(-NWIN * NWIN // count)
        windows = jnp.pad(
            windows, ((0, slots * count - NWIN * NWIN), (0, SIDE - WIN), (0, 0), (0, 0))
        )
        return lax.dynamic_slice_in_dim(windows, row * slots, slots, 0)
    step = height - WIN
    last = count - 1
    halo = step * last
    rest = height * count - WIN * count
    down = lax.ppermute(windows[:, height - halo :], "rows", [(i, i + 1) for i in range(last)])
    main = lax.dynamic_slice_in_dim(
        jnp.concatenate([down, windows], axis=1), halo - step * row, WIN, 1
    )
    tail = windows[:, height - rest :]
    extra = tail[last]
    for target in range(last):
        arrived = lax.ppermute(tail[target], "rows", [(last, target)])
        extra = jnp.where(row == target, arrived, extra)
    more = jnp.where(row == last, tail[last + 1 :], jnp.zeros_like(tail[last + 1 :]))
    ends = jnp.concatenate([extra[None], more], axis=0)
    return jnp.concatenate([pad_rows(main, 0, SIDE - WIN), pad_rows(ends, 0, SIDE - rest)], axis=0)


def collect(windows, height, width):
    count = lax.axis_size("rows")
    row = lax.axis_index("rows")
    if not near_plan():
        windows = lax.all_gather(windows[:, :WIN], "rows", axis=0, tiled=True)
        windows = windows[: NWIN * NWIN].reshape((NWIN, NWIN) + windows.shape[1:])
        windows = windows.transpose(1, 0, 2, 3, 4).reshape(NWIN, NWIN * WIN, SIDE, -1)
        return column_rows(lax.dynamic_slice_in_dim(windows, row * height, height, 1), width)
    step = height - WIN
    last = count - 1
    halo = step * last
    rest = height * count - WIN * count
    main = windows[:NWIN, :WIN]
    ends = windows[NWIN:, :rest]
    up = lax.ppermute(main[:, :halo], "rows", [(i + 1, i) for i in range(last)])
    tail = jnp.concatenate(
        [lax.ppermute(ends[0], "rows", [(source, last)])[None] for source in range(last)] + [ends],
        axis=0,
    )
    below = jnp.where(row == last, tail, pad_rows(up, 0, rest - halo))
    whole = jnp.concatenate([main, below], axis=1)
    return column_rows(lax.dynamic_slice_in_dim(whole, step * row, height, 1), width)


def token_mask(slots, height, width):
    count = lax.axis_size("rows")
    row = lax.axis_index("rows")
    slot = lax.broadcasted_iota(jnp.int32, (slots, SIDE, SIDE, 1), 0)
    i = lax.broadcasted_iota(jnp.int32, (slots, SIDE, SIDE, 1), 1)
    j = lax.broadcasted_iota(jnp.int32, (slots, SIDE, SIDE, 1), 2)
    if near_plan():
        window_row = jnp.where(slot < NWIN, row, NWIN - 1)
        extra = jnp.where(row == count - 1, row + slot - NWIN, row)
        window_col = jnp.where(slot < NWIN, slot, extra)
        held = (slot <= NWIN) | (row == count - 1)
    else:
        window = row * slots + slot
        window_row = window // NWIN
        window_col = window % NWIN
        held = window < NWIN * NWIN
    inside = (window_row * WIN + i < height) & (window_col * WIN + j < width)
    return (held & inside & (i < WIN) & (j < WIN)).astype(jnp.float32)


def shards(
    image_in,
    ln1_gain,
    ln1_bias,
    w_qkv,
    qv_bias,
    rel_rows,
    rel_cols,
    w_proj,
    proj_bias,
    ln2_gain,
    ln2_bias,
    w_fc1,
    fc1_bias,
    w_fc2,
    fc2_bias,
    cotangent,
):
    devices = lax.axis_size(ALL)
    me = lax.axis_index(ALL)
    images, tile_h, tile_w, model = image_in.shape
    tokens = images * tile_h * tile_w
    width = tile_w * lax.axis_size("cols")
    share = model // devices
    unit = fc1_bias.shape[0]
    part = unit // 2

    def gathered(shard):
        return lax.all_gather(shard, ALL, axis=0, tiled=True)

    vectors = [ln1_gain, ln1_bias, qv_bias[:, 0], qv_bias[:, 1], proj_bias, ln2_gain, ln2_bias]
    vectors = small_gather(jnp.concatenate(vectors + [fc2_bias, fc1_bias])[None])
    vectors = vectors.astype(jnp.float32)
    gain1, shift1, query_shift, value_shift, proj_shift, gain2, shift2, down_shift = (
        vectors[:, n * share : (n + 1) * share].reshape(model) for n in range(8)
    )
    up_shift = vectors[:, 8 * share :]
    qkv_full = gathered(w_qkv)
    proj_full = gathered(w_proj)
    up_parts = w_fc1.reshape(share, devices, 2, part)
    ups = [gathered(up_parts[:, :, n].reshape(share, devices * part)) for n in (0, 1)]
    downs = [gathered(w_fc2[n * part : (n + 1) * part]) for n in (0, 1)]

    raw = spread(halves_to_image(image_in))
    slots = raw.shape[0]
    there = token_mask(slots, tile_h * lax.axis_size("rows"), width)
    window_unit, _ = normalised(raw.astype(jnp.float32))
    window_tokens = ((window_unit * gain1 + shift1) * there).astype(jnp.bfloat16)
    window_tokens = window_tokens.reshape(slots * TOK, model)
    shift_qkv = jnp.concatenate([query_shift, jnp.zeros((model,), jnp.float32), value_shift])
    project = lax.dot_general(
        qkv_full, window_tokens, (((0,), (1,)), ((), ())), preferred_element_type=jnp.float32
    )
    project = (project + shift_qkv[:, None]).astype(jnp.bfloat16)
    tab = wide_tables(rel_rows, rel_cols)
    ind = key_indicator()
    attended_windows, weights, inverse = attention_forward(project, tab, ind)
    attended = image_to_halves(
        collect(attended_windows.reshape(slots, SIDE, SIDE, model), tile_h, width)
    ).reshape(tokens, model)

    image = image_in.astype(jnp.float32).reshape(tokens, model)
    cot = cotangent.reshape(tokens, model)
    middle = image + dot(attended, proj_full) + proj_shift
    unit2, inverse2 = normalised(middle)
    normed2 = (unit2 * gain2 + shift2).astype(jnp.bfloat16)
    turned2 = normed2.T
    mixed = jnp.zeros((tokens, model), jnp.float32)
    grad_normed2 = jnp.zeros((tokens, model), jnp.float32)
    grad_ups, grad_downs, grad_up_shifts = [], [], []
    for n in (0, 1):
        shift = up_shift[:, n * part : (n + 1) * part].reshape(1, devices * part)
        mixed, grad_normed2, grad_up, grad_down, grad_shift = mlp(
            normed2, turned2, cot, ups[n], downs[n], shift, mixed, grad_normed2
        )
        grad_ups.append(grad_up)
        grad_downs.append(grad_down)
        grad_up_shifts.append(grad_shift.reshape(devices, part))
    output = (middle + mixed + down_shift).astype(jnp.bfloat16).reshape(image_in.shape)

    dp_bits = axis_bits("dp")
    core, chips = dp_bits[:1], dp_bits[1:]
    x_first = core + axis_bits("cols") + chips + axis_bits("rows")
    y_first = core + chips + axis_bits("cols") + axis_bits("rows")
    sum_ups = [scatter_sum(grad, x_first) for grad in grad_ups]
    sum_downs = [scatter_sum(grad, y_first) for grad in grad_downs]

    grad_middle, grad_gain2, grad_shift2 = norm_backward(unit2, inverse2, gain2, grad_normed2)
    grad_middle = grad_middle + cot.astype(jnp.float32)
    grad_branch = grad_middle.astype(jnp.bfloat16)
    grad_attended = dot_nt(grad_branch, proj_full).astype(jnp.bfloat16)
    grad_proj = dot_tn(attended, grad_branch).astype(jnp.bfloat16)
    sum_proj = scatter_sum(grad_proj, x_first)

    def rows_of(vector):
        return vector.reshape(devices, -1)

    early = jnp.concatenate(
        [
            rows_of(jnp.sum(grad_branch, axis=0, dtype=jnp.float32)),
            rows_of(grad_gain2),
            rows_of(grad_shift2),
            rows_of(jnp.sum(cot, axis=0, dtype=jnp.float32)),
        ]
        + grad_up_shifts,
        axis=1,
    )
    early = lax.dynamic_index_in_dim(all_sum(early), me, 0, keepdims=False)

    grad_windows = spread(halves_to_image(grad_attended.reshape(image_in.shape)))
    grad_project, grad_tab = attention_backward(
        project, weights, inverse, grad_windows.reshape(slots * TOK, model), tab, ind
    )
    grad_qkv = lax.dot_general(
        window_tokens, grad_project, (((0,), (1,)), ((), ())), preferred_element_type=jnp.float32
    ).astype(jnp.bfloat16)
    cut = 3 * model // 2
    sum_qkv = [scatter_sum(grad_qkv[:, :cut], x_first), scatter_sum(grad_qkv[:, cut:], y_first)]
    grad_tokens = lax.dot_general(
        grad_project, qkv_full, (((0,), (1,)), ((), ())), preferred_element_type=jnp.float32
    ).astype(jnp.bfloat16)
    grad_normed = image_to_halves(
        collect(grad_tokens.reshape(slots, SIDE, SIDE, model), tile_h, width)
    )
    unit1, inverse1 = normalised(image)
    grad_image, grad_gain1, grad_shift1 = norm_backward(
        unit1, inverse1, gain1, grad_normed.reshape(tokens, model).astype(jnp.float32)
    )
    grad_in = (grad_middle + grad_image).reshape(image_in.shape)
    grad_sums = jnp.sum(grad_project, axis=1, dtype=jnp.float32)
    late = jnp.concatenate(
        [
            rows_of(grad_gain1),
            rows_of(grad_shift1),
            rows_of(grad_sums[:model]),
            rows_of(grad_sums[2 * model :]),
        ],
        axis=1,
    )
    grad_tables = jnp.stack(narrow_tables(grad_tab))
    late, grad_tables = all_sum_pair(late, grad_tables)
    late = lax.dynamic_index_in_dim(late, me, 0, keepdims=False)

    grad_fc1 = jnp.stack([grad.reshape(share, devices, part) for grad in sum_ups], axis=2)
    return (
        output,
        grad_in,
        late[:share],
        late[share : 2 * share],
        jnp.concatenate(sum_qkv, axis=1),
        jnp.stack([late[2 * share : 3 * share], late[3 * share :]], axis=1),
        grad_tables[0],
        grad_tables[1],
        sum_proj,
        early[:share],
        early[share : 2 * share],
        early[2 * share : 3 * share],
        grad_fc1.reshape(share, devices * unit),
        early[4 * share :],
        jnp.concatenate(sum_downs, axis=0),
        early[3 * share : 4 * share],
    )


def all_sum_pair(first, second):
    sizes = first.size
    joined = all_sum(jnp.concatenate([first.reshape(-1), second.reshape(-1)]))
    return joined[:sizes].reshape(first.shape), joined[sizes:].reshape(second.shape)


def solution(mesh):
    tile = P("dp", "rows", "cols", None)
    vector = P(ALL)
    matrix = P(ALL, None)
    in_specs = (
        tile, vector, vector, matrix, matrix, P(), P(), matrix, vector, vector, vector,
        matrix, vector, matrix, vector, tile,
    )
    out_specs = (
        tile, tile, vector, vector, matrix, matrix, P(), P(), matrix, vector, vector, vector,
        matrix, vector, matrix, vector,
    )
    return jax.shard_map(shards, mesh=mesh, in_specs=in_specs, out_specs=out_specs, check_vma=False)
```

time: 6570 us -> 1140 us (0.17)
  local copies, waits for them, and re-layouts: 2390 us -> 147 us
  matrix products: 1540 us -> 93.6 us
  waiting for transfers between devices: 1750 us -> 443 us
  other arithmetic: 503 us -> 121 us
  blocking collectives: 290 us -> 0 us
  Pallas kernels: 0 us -> 212 us
  starting transfers between devices: 23.3 us -> 96.7 us
    reduce_scatter x4 -> x0, waiting for transfers between devices: 1470 us -> none  [the longest x1 557 us: shards(): lax.psum_scatter(total_up, ('dp', 'rows', 'cols'), scatter_dimension=0, t...]
    dot_general x226 -> x10, matrix products: 1470 us -> 93.6 us  [the longest x1 25.7 us: shards(): lax.dot_general(grad_project, qkv_full, (((0,), (1,)), ((), ())), preferr...]
    reshape x192 -> x18, local copies, waits for them, and re-layouts: 1210 us -> 6.99 us  [the longest x1 2.74 us: shards(): grad_fc1.reshape(share, devices * unit)]
    add x24 -> x4, local copies, waits for them, and re-layouts: 447 us -> 0.92 us  [the longest x1 0.68 us: shards(): window_unit * gain1 + shift1]
    reduce_sum x52 -> x10, other arithmetic: 279 us -> 32.5 us  [the longest x2 12.3 us: norm_backward(): return (grad_values, jnp.sum(grad * unit, axis=0), jnp.sum(grad, axis=0))]
    pallas_call x0 -> x4, Pallas kernels: none -> 212 us  [the longest x2 108 us: mlp(): pl.pallas_call(functools.partial(mlp_kernel, rows), grid=(hidden // block...]
    ppermute x16 -> x70, waiting for transfers between devices: 154 us -> 353 us  [the longest x50 196 us: flipped(): lax.ppermute(value, axis, [(i, i ^ mask) for i in range(lax.axis_size(axi...]
    all_gather x2 -> x0, blocking collectives: 200 us -> none  [step_image(): lax.all_gather(qv_bias, ('dp', 'rows', 'cols'), axis=0, tiled=True)]
  transfers between devices with their start and end apart: 29 -> 76, of which waited for: 15 -> 30; matrix products, arithmetic and copies ran while one was open for 28% -> 31% of each run, Pallas kernels for 0% -> 19%
where the time goes in v1:
time: 1140 us; the launch traced here: 1130 us
  waiting for transfers between devices  443 us (39%)
  Pallas kernels  212 us (19%)
  local copies, waits for them, and re-layouts  147 us (13%)
  other arithmetic  121 us (11%)
  starting transfers between devices  96.7 us (8%)
  matrix products  93.6 us (8%)
  between operations  16.7 us (1%)
    ppermute x50, waiting for transfers between devices, flipped(): lax.ppermute(value, axis, [(i, i ^ mask) for i in range(lax.axis_size(axi...  196 us
    pallas_call x2, Pallas kernels, mlp(): pl.pallas_call(functools.partial(mlp_kernel, rows), grid=(hidden // block...  108 us
    all_gather x6, waiting for transfers between devices, gathered(): return lax.all_gather(shard, ALL, axis=0, tiled=True)  87.9 us
    ppermute x50, starting transfers between devices, flipped(): lax.ppermute(value, axis, [(i, i ^ mask) for i in range(lax.axis_size(axi...  60 us
    pallas_call x1, Pallas kernels, attention_backward(): pl.pallas_call(attention_backward_kernel, grid=(slots,), in_specs=[pl.Blo...  54.7 us
    pallas_call x1, Pallas kernels, attention_forward(): pl.pallas_call(attention_forward_kernel, grid=(slots,), in_specs=[pl.Bloc...  49.4 us
    ppermute x6, waiting for transfers between devices, spread(): arrived = lax.ppermute(tail[target], 'rows', [(last, target)])  46.9 us
    ppermute x2, waiting for transfers between devices, image_to_halves(): arrived = lax.ppermute(sent, 'cols', [(0, 1), (1, 0)])  40.2 us
  transfers between devices with their start and end apart: 76, of which 30 were waited for; matrix products, arithmetic and copies ran while one was open for 31% of the time, Pallas kernels for 19%

profile of v1, /device:TPU:1, one launch (start us, length us, event | category | flops | bytes accessed | tf_op | source)
XLA Modules:
  0.0 1129.5 jit_solution(254759797342363278)
XLA Ops:
  10.5 4.5 slice_reduce_fusion
  27.7 36.4 %collective-permute-done.5 = bf16[1,480]{1,0:T(2,128)(2,1)S(1)} collective-permute-done((bf16[1,480]{1,0:T(2,128)(2,1)S(1)}, bf16[1,480]{1,0:T(2,128)(2,1)S(1)}, u32[]{:S(2)}, u32[]{:S(2)}) %collective-permute-start.5) | collective-permute-done | bytes 992 | tf_op jit(solution)/shard_map/ppermute | solution.py:351
  81.6 4.5 collective-permute-start.1
  93.9 29.9 %collective-permute-done.4 = bf16[8,16,1280]{2,0,1:T(8,128)(2,1)} collective-permute-done((bf16[8,16,1280]{2,0,1:T(8,128)(2,1)}, bf16[8,16,1280]{2,0,1:T(8,128)(2,1)}, u32[]{:S(2)}, u32[]{:S(2)}) %collective-permute-start.4) | collective-permute-done | bytes 327712 | tf_op jit(solution)/shard_map/ppermute | solution.py:467
  132.4 6.1 fusion.22
  139.7 8.9 copy.181
  152.0 24.7 %fusion.project_ref = bf16[3840,1792]{1,0:T(8,128)(2,1)} fusion(f32[3840]{0:T(1024)S(1)} %copy-done.54, bf16[1792,1280]{1,0:T(8,128)(2,1)} %fusion.7, bf16[1280,3840]{1,0:T(8,128)(2,1)} %all-gather.7.cloned.1.call-done), kind=kOutput, calls=%fused_computation.3 | convolution fusion | flops 17629839360 | bytes 28195840 | tf_op jit(solution)/shard_map/dot_general | solution.py:568
  176.7 49.4 %shard_map.279 = (bf16[1792,1280]{1,0:T(8,128)(2,1)S(1)}, bf16[7,16,224,256]{3,2,1,0:T(8,128)(2,1)}, f32[7,16,256]{2,1,0:T(8,128)S(1)}) custom-call(bf16[3840,1792]{1,0:T(8,128)(2,1)} %fusion.project_ref, bf16[448,80]{1,0:T(8,128)(2,1)S(1)} %pad_maximum_fusion.3.tab_ref, bf16[48,256]{1,0:T(8,128)(2,1)S(1)} %fusion.74.ind_ref), custom_call_target="tpu_custom_call" | custom-call | flops 5872025600 | bytes 44040192 | tf_op jit(solution)/shard_map/pallas_call | solution.py:128
  229.8 7.7 collective-permute-start.10
  248.0 22.1 %collective-permute-done.13 = bf16[5,6,16,1280]{3,2,1,0:T(8,128)(2,1)} collective-permute-done((bf16[5,6,16,1280]{3,2,1,0:T(8,128)(2,1)}, bf16[5,6,16,1280]{3,2,1,0:T(8,128)(2,1)}, u32[]{:S(2)}, u32[]{:S(2)}) %collective-permute-start.13) | collective-permute-done | bytes 1228832 | tf_op jit(solution)/shard_map/ppermute | solution.py:488
  279.0 7.8 copy.176
  293.5 19.6 %collective-permute-done.14 = bf16[16,32,1280]{2,0,1:T(8,128)(2,1)} collective-permute-done((bf16[16,32,1280]{2,0,1:T(8,128)(2,1)}, bf16[16,32,1280]{2,0,1:T(8,128)(2,1)}, u32[]{:S(2)}, u32[]{:S(2)}) %collective-permute-start.14) | collective-permute-done | bytes 1310752 | tf_op jit(solution)/shard_map/ppermute | solution.py:413
  316.9 8.6 fusion.90
  331.6 4.9 add_convert_fusion.2.normed_ref
  336.5 7.5 all-gather.17.cloned.1.call-done.down_ref
  346.7 54.1 %shard_map.280 = (f32[1024,1280]{1,0:T(8,128)}, f32[1024,1280]{1,0:T(8,128)}, bf16[1280,2560]{1,0:T(8,128)(2,1)}, bf16[2560,1280]{1,0:T(8,128)(2,1)}, f32[1,2560]{1,0:T(1,128)}) custom-call(bf16[1024,1280]{1,0:T(8,128)(2,1)} %add_convert_fusion.2.normed_ref, bf16[1280,1024]{1,0:T(8,128)(2,1)} %copy.195.turned_ref, bf16[1024,1280]{1,0:T(8,128)(2,1)} %bitcast.382, ...), custom_call_target="tpu_custom_call" | custom-call | flops 40265318400 | bytes 57671680 | tf_op jit(solution)/shard_map/pallas_call | solution.py:289
  400.8 5.2 constant_dynamic-slice_fusion.4
  408.2 8.3 all-gather.11.cloned.1.call-done.up_ref
  416.5 72.0 %all-gather.13.cloned.1.call-done.down_ref = bf16[2560,1280]{1,0:T(8,128)(2,1)} async-done(((bf16[80,1280]{1,0:T(8,128)(2,1)}), bf16[2560,1280]{1,0:T(8,128)(2,1)}) %all-gather.13.cloned.1.call-update) | async-done | bytes 6553616 | tf_op jit(solution)/shard_map/all_gather | solution.py:546
  488.6 53.7 %shard_map.281 = (f32[1024,1280]{1,0:T(8,128)}, f32[1024,1280]{1,0:T(8,128)}, bf16[1280,2560]{1,0:T(8,128)(2,1)}, bf16[2560,1280]{1,0:T(8,128)(2,1)}, f32[1,2560]{1,0:T(1,128)}) custom-call(bf16[1024,1280]{1,0:T(8,128)(2,1)} %add_convert_fusion.2.normed_ref, bf16[1280,1024]{1,0:T(8,128)(2,1)} %copy.195.turned_ref, bf16[1024,1280]{1,0:T(8,128)(2,1)} %bitcast.383, ...), custom_call_target="tpu_custom_call" | custom-call | flops 40265318400 | bytes 57671680 | tf_op jit(solution)/shard_map/pallas_call | solution.py:289
  542.4 6.1 multiply_reduce_fusion.1
  549.5 6.6 convert_reduce_fusion.2
  557.7 6.7 convolution_convert_fusion.1
  588.8 13.4 %collective-permute-done.15 = bf16[16,32,1280]{2,0,1:T(8,128)(2,1)S(1)} collective-permute-done((bf16[16,32,1280]{2,0,1:T(8,128)(2,1)S(1)}, bf16[16,32,1280]{2,0,1:T(8,128)(2,1)S(1)}, u32[]{:S(2)}, u32[]{:S(2)}) %collective-permute-start.15) | collective-permute-done | bytes 1310752 | tf_op jit(solution)/shard_map/ppermute | solution.py:400
  609.7 17.0 %collective-permute-done.19 = bf16[8,16,1280]{2,0,1:T(8,128)(2,1)S(1)} collective-permute-done((bf16[8,16,1280]{2,0,1:T(8,128)(2,1)S(1)}, bf16[8,16,1280]{2,0,1:T(8,128)(2,1)S(1)}, u32[]{:S(2)}, u32[]{:S(2)}) %collective-permute-start.19) | collective-permute-done | bytes 327712 | tf_op jit(solution)/shard_map/ppermute | solution.py:467
  631.7 20.3 %collective-permute-done.16 = bf16[5,6,16,1280]{3,2,1,0:T(8,128)(2,1)S(1)} collective-permute-done((bf16[5,6,16,1280]{3,2,1,0:T(8,128)(2,1)S(1)}, bf16[5,6,16,1280]{3,2,1,0:T(8,128)(2,1)S(1)}, u32[]{:S(2)}, u32[]{:S(2)}) %collective-permute-start.16) | collective-permute-done | bytes 1228832 | tf_op jit(solution)/shard_map/ppermute | solution.py:460
  657.2 54.7 %shard_map.282 = (bf16[3840,1792]{1,0:T(8,128)(2,1)}, f32[448,80]{1,0:T(8,128)S(1)}) custom-call(bf16[3840,1792]{1,0:T(8,128)(2,1)} %fusion.project_ref, bf16[7,16,224,256]{3,2,1,0:T(8,128)(2,1)} %get-tuple-element.36.weights_ref, f32[7,16,256]{2,1,0:T(8,128)S(1)} %get-tuple-element.37.inverse_ref, bf16[1792,1280]{1,0:T(8,128)(2,1)S(1)} %bitcast.363, ...), custom_call_target="tpu_custom_call" | custom-call | flops 11744051200 | bytes 51380224 | tf_op jit(solution)/shard_map/pallas_call | solution.py:206
  712.0 22.9 %convolution_convert_fusion = bf16[1280,3840]{1,0:T(8,128)(2,1)} fusion(bf16[1792,1280]{1,0:T(8,128)(2,1)S(1)} %bitcast.410, bf16[3840,1792]{1,0:T(8,128)(2,1)} %get-tuple-element.38), kind=kOutput, calls=%fused_computation.2 | convolution fusion | flops 17620992000 | bytes 28180480 | tf_op jit(solution)/shard_map/dot_general | solution.py:631
  734.8 8.4 fusion.84
  743.2 25.7 %convolution_convert_fusion.2 = bf16[1792,1280]{1,0:T(8,128)(2,1)} fusion(bf16[3840,1792]{1,0:T(8,128)(2,1)} %get-tuple-element.38, bf16[1280,3840]{1,0:T(8,128)(2,1)} %all-gather.7.cloned.1.call-done), kind=kOutput, calls=%fused_computation.15 | convolution fusion | flops 17618370560 | bytes 28180480 | tf_op jit(solution)/shard_map/dot_general | solution.py:636
  768.9 6.8 convert_reduce_fusion
  775.7 5.4 constant_dynamic-slice_fusion.11
  828.5 14.1 %collective-permute-done.23 = bf16[5,6,16,1280]{3,2,1,0:T(8,128)(2,1)} collective-permute-done((bf16[5,6,16,1280]{3,2,1,0:T(8,128)(2,1)S(1)}, bf16[5,6,16,1280]{3,2,1,0:T(8,128)(2,1)}, u32[]{:S(2)}, u32[]{:S(2)}) %collective-permute-start.23) | collective-permute-done | bytes 1228832 | tf_op jit(solution)/shard_map/ppermute | solution.py:488
  846.6 6.5 collective-permute-start.30
  860.5 29.0 %collective-permute-done.66 = bf16[2,2,2,80,1280]{4,3,0,1,2:T(8,128)(2,1)} collective-permute-done((bf16[2,2,2,80,1280]{4,3,0,1,2:T(8,128)(2,1)}, bf16[2,2,2,80,1280]{4,3,0,1,2:T(8,128)(2,1)}, u32[]{:S(2)}, u32[]{:S(2)}) %collective-permute-start.66) | collective-permute-done | bytes 1638432 | tf_op jit(solution)/shard_map/ppermute | solution.py:351
  897.6 27.9 %collective-permute-done.56 = bf16[2,2,2,40,2560]{4,3,2,1,0:T(8,128)(2,1)S(1)} collective-permute-done((bf16[2,2,2,40,2560]{4,3,2,1,0:T(8,128)(2,1)S(1)}, bf16[2,2,2,40,2560]{4,3,2,1,0:T(8,128)(2,1)S(1)}, u32[]{:S(2)}, u32[]{:S(2)}) %collective-permute-start.56) | collective-permute-done | bytes 1638432 | tf_op jit(solution)/shard_map/ppermute | solution.py:351
  933.1 20.6 %collective-permute-done.24 = bf16[16,32,1280]{2,0,1:T(8,128)(2,1)S(1)} collective-permute-done((bf16[16,32,1280]{2,0,1:T(8,128)(2,1)S(1)}, bf16[16,32,1280]{2,0,1:T(8,128)(2,1)S(1)}, u32[]{:S(2)}, u32[]{:S(2)}) %collective-permute-start.24) | collective-permute-done | bytes 1310752 | tf_op jit(solution)/shard_map/ppermute | solution.py:413
  953.7 6.2 multiply_reduce_fusion.2
  963.4 26.3 %collective-permute-done.25 = f32[9440]{0:T(1024)S(1)} collective-permute-done((f32[9440]{0:T(1024)S(1)}, f32[9440]{0:T(1024)S(1)}, u32[]{:S(2)}, u32[]{:S(2)}) %collective-permute-start.25) | collective-permute-done | bytes 37792 | tf_op jit(solution)/shard_map/ppermute | solution.py:351
  993.6 4.2 collective-permute-done.27
  1000.3 5.7 copy.206
  1006.6 5.1 fusion.15
  1029.0 7.9 collective-permute-done.68
  1037.6 12.4 %collective-permute-done.53 = bf16[2,40,2560]{2,1,0:T(8,128)(2,1)S(1)} collective-permute-done((bf16[2,40,2560]{2,1,0:T(8,128)(2,1)S(1)}, bf16[2,40,2560]{2,1,0:T(8,128)(2,1)S(1)}, u32[]{:S(2)}, u32[]{:S(2)}) %collective-permute-start.53) | collective-permute-done | bytes 409632 | tf_op jit(solution)/shard_map/ppermute | solution.py:351
  1050.2 11.1 collective-permute-done.58
  1068.2 9.8 collective-permute-done.54
  1103.7 5.9 collective-permute-done.38
  1111.0 10.5 collective-permute-done.39
  (577 shorter events, 279.3 us)
Async XLA Ops:
  7.2 144.8 %all-gather.7.cloned.1.call-start = ((), (), s32[]{:S(2)}) async-start(), calls=%async_computation | async-start | bytes 10137600 | tf_op jit(solution)/shard_map/all_gather | solution.py:546
  7.9 309.0 %all-gather.9.cloned.1.call-start = ((), (), s32[]{:S(2)}) async-start(), calls=%async_computation.1 | async-start | bytes 3379200 | tf_op jit(solution)/shard_map/all_gather | solution.py:546
  8.7 327.8 %all-gather.15.cloned.1.call-start = ((), (), s32[]{:S(2)}) async-start(), calls=%async_computation.4 | async-start | bytes 6758400 | tf_op jit(solution)/shard_map/all_gather | solution.py:546
  17.2 326.8 %all-gather.17.cloned.1.call-start = ((), (), s32[]{:S(2)}) async-start(), calls=%async_computation.5 | async-start | bytes 6758400 | tf_op jit(solution)/shard_map/all_gather | solution.py:546
  19.0 397.5 %all-gather.11.cloned.1.call-start = ((), (), s32[]{:S(2)}) async-start(), calls=%async_computation.2 | async-start | bytes 6758400 | tf_op jit(solution)/shard_map/all_gather | solution.py:546
  21.2 467.4 %all-gather.13.cloned.1.call-start = ((), (), s32[]{:S(2)}) async-start(), calls=%async_computation.3 | async-start | bytes 6758400 | tf_op jit(solution)/shard_map/all_gather | solution.py:546
  24.4 53.5 %collective-permute-start = (bf16[16,32,1280]{2,0,1:T(8,128)(2,1)}, bf16[16,32,1280]{2,0,1:T(8,128)(2,1)}, u32[]{:S(2)}, u32[]{:S(2)}) collective-permute-start(bf16[16,32,1280]{2,0,1:T(8,128)(2,1)} %bitcast.355), channel_id=1, source_target_pairs={{0,1},{1,0},{2,3},{3,2},{4,5},{5,4},{6,7},{7,6},{8,9},{9,8},{10,11... | collective-permute-start | bytes 3932168 | tf_op jit(solution)/shard_map/ppermute | solution.py:400
  26.6 37.5 %collective-permute-start.5 = (bf16[1,480]{1,0:T(2,128)(2,1)S(1)}, bf16[1,480]{1,0:T(2,128)(2,1)S(1)}, u32[]{:S(2)}, u32[]{:S(2)}) collective-permute-start(bf16[1,480]{1,0:T(2,128)(2,1)S(1)} %broadcast_in_dim.88), channel_id=1, source_target_pairs={{0,1},{1,0},{2,3},{3,2},{4,5},{5,4},{6,7},{7,6},{8,9},{9,8},{10,11... | collective-permute-start | bytes 2888 | tf_op jit(solution)/shard_map/ppermute | solution.py:351
  81.6 43.3 %collective-permute-start.1 = (bf16[5,6,16,1280]{3,2,1,0:T(8,128)(2,1)}, bf16[5,6,16,1280]{3,2,1,0:T(8,128)(2,1)}, u32[]{:S(2)}, u32[]{:S(2)}) collective-permute-start(bf16[5,6,16,1280]{3,2,1,0:T(8,128)(2,1)} %copy.179), channel_id=1, source_target_pairs={{0,2},{2,4},{4,6},{1,3},{3,5},{5,7},{8,10},{10,12},{12,14},{9,11},... | collective-permute-start | bytes 3686408 | tf_op jit(solution)/shard_map/ppermute | solution.py:460
  89.8 33.9 %collective-permute-start.4 = (bf16[8,16,1280]{2,0,1:T(8,128)(2,1)}, bf16[8,16,1280]{2,0,1:T(8,128)(2,1)}, u32[]{:S(2)}, u32[]{:S(2)}) collective-permute-start(bf16[8,16,1280]{2,0,1:T(8,128)(2,1)} %get-tuple-element.74), channel_id=1, source_target_pairs={{6,0},{7,1},{14,8},{15,9},{22,16},{23,17},{30,24},{31,25}} | collective-permute-start | bytes 983048 | tf_op jit(solution)/shard_map/ppermute | solution.py:467
  227.3 42.9 %collective-permute-start.13 = (bf16[5,6,16,1280]{3,2,1,0:T(8,128)(2,1)}, bf16[5,6,16,1280]{3,2,1,0:T(8,128)(2,1)}, u32[]{:S(2)}, u32[]{:S(2)}) collective-permute-start(bf16[5,6,16,1280]{3,2,1,0:T(8,128)(2,1)} %slice.350), channel_id=1, source_target_pairs={{2,0},{4,2},{6,4},{3,1},{5,3},{7,5},{10,8},{12,10},{14,12},{11,9},... | collective-permute-start | bytes 3686408 | tf_op jit(solution)/shard_map/ppermute | solution.py:488
  229.8 42.0 %collective-permute-start.10 = (bf16[8,16,1280]{2,0,1:T(8,128)(2,1)}, bf16[8,16,1280]{2,0,1:T(8,128)(2,1)S(1)}, u32[]{:S(2)}, u32[]{:S(2)}) collective-permute-start(bf16[8,16,1280]{2,0,1:T(8,128)(2,1)} %bitcast.358), channel_id=1, source_target_pairs={{0,6},{1,7},{8,14},{9,15},{16,22},{17,23},{24,30},{25,31}} | collective-permute-start | bytes 983048 | tf_op jit(solution)/shard_map/ppermute | solution.py:490
  237.6 34.3 %collective-permute-start.11 = (bf16[8,16,1280]{2,0,1:T(8,128)(2,1)}, bf16[8,16,1280]{2,0,1:T(8,128)(2,1)S(1)}, u32[]{:S(2)}, u32[]{:S(2)}) collective-permute-start(bf16[8,16,1280]{2,0,1:T(8,128)(2,1)} %bitcast.358), channel_id=1, source_target_pairs={{2,6},{3,7},{10,14},{11,15},{18,22},{19,23},{26,30},{27,31}} | collective-permute-start | bytes 983048 | tf_op jit(solution)/shard_map/ppermute | solution.py:490
  238.2 33.6 %collective-permute-start.12 = (bf16[8,16,1280]{2,0,1:T(8,128)(2,1)}, bf16[8,16,1280]{2,0,1:T(8,128)(2,1)}, u32[]{:S(2)}, u32[]{:S(2)}) collective-permute-start(bf16[8,16,1280]{2,0,1:T(8,128)(2,1)} %bitcast.358), channel_id=1, source_target_pairs={{4,6},{5,7},{12,14},{13,15},{20,22},{21,23},{28,30},{29,31}} | collective-permute-start | bytes 983048 | tf_op jit(solution)/shard_map/ppermute | solution.py:490
  277.3 35.8 %collective-permute-start.14 = (bf16[16,32,1280]{2,0,1:T(8,128)(2,1)}, bf16[16,32,1280]{2,0,1:T(8,128)(2,1)}, u32[]{:S(2)}, u32[]{:S(2)}) collective-permute-start(bf16[16,32,1280]{2,0,1:T(8,128)(2,1)} %get-tuple-element.84), channel_id=1, source_target_pairs={{0,1},{1,0},{2,3},{3,2},{4,5},{5,4},{6,7},{7,6},{8,9},{9,8},{10,11... | collective-permute-start | bytes 3932168 | tf_op jit(solution)/shard_map/ppermute | solution.py:413
  408.0 398.1 %collective-permute-start.60 = (bf16[2,2,2,2,80,1280]{5,4,1,2,3,0:T(8,128)(2,1)}, bf16[2,2,2,2,80,1280]{5,4,1,2,3,0:T(8,128)(2,1)}, u32[]{:S(2)}, u32[]{:S(2)}) collective-permute-start(bf16[2,2,2,2,80,1280]{5,4,1,2,3,0:T(8,128)(2,1)} %bitcast.349), channel_id=1, source_target_pairs={{0,8},{8,0},{16,24},{24,16},{1,9},{9,1},{17,25},{25,17},{2,10},{10... | collective-permute-start | bytes 9830408 | tf_op jit(solution)/shard_map/ppermute | solution.py:351
  572.7 29.6 %collective-permute-start.15 = (bf16[16,32,1280]{2,0,1:T(8,128)(2,1)S(1)}, bf16[16,32,1280]{2,0,1:T(8,128)(2,1)S(1)}, u32[]{:S(2)}, u32[]{:S(2)}) collective-permute-start(bf16[16,32,1280]{2,0,1:T(8,128)(2,1)S(1)} %bitcast.421), channel_id=1, source_target_pairs={{0,1},{1,0},{2,3},{3,2},{4,5},{5,4},{6,7},{7,6},{8,9},{9,8},{10,11... | collective-permute-start | bytes 3932168 | tf_op jit(solution)/shard_map/ppermute | solution.py:400
  575.5 30.2 %collective-permute-start.40 = (bf16[2,2,2,2,40,1280]{5,4,1,2,0,3:T(8,128)(2,1)S(1)}, bf16[2,2,2,2,40,1280]{5,4,1,2,0,3:T(8,128)(2,1)S(1)}, u32[]{:S(2)}, u32[]{:S(2)}) collective-permute-start(bf16[2,2,2,2,40,1280]{5,4,1,2,0,3:T(8,128)(2,1)S(1)} %bitcast.420), channel_id=1, source_target_pairs={{0,8},{8,0},{16,24},{24,16},{1,9},{9,1},{17,25},{25,17},{2,10},{10... | collective-permute-start | bytes 4915208 | tf_op jit(solution)/shard_map/ppermute | solution.py:351
  604.4 22.4 %collective-permute-start.19 = (bf16[8,16,1280]{2,0,1:T(8,128)(2,1)S(1)}, bf16[8,16,1280]{2,0,1:T(8,128)(2,1)S(1)}, u32[]{:S(2)}, u32[]{:S(2)}) collective-permute-start(bf16[8,16,1280]{2,0,1:T(8,128)(2,1)S(1)} %get-tuple-element.70), channel_id=1, source_target_pairs={{6,0},{7,1},{14,8},{15,9},{22,16},{23,17},{30,24},{31,25}} | collective-permute-start | bytes 983048 | tf_op jit(solution)/shard_map/ppermute | solution.py:467
  606.2 22.6 %collective-permute-start.41 = (bf16[2,2,2,40,1280]{4,3,1,2,0:T(8,128)(2,1)S(1)}, bf16[2,2,2,40,1280]{4,3,1,2,0:T(8,128)(2,1)S(1)}, u32[]{:S(2)}, u32[]{:S(2)}) collective-permute-start(bf16[2,2,2,40,1280]{4,3,1,2,0:T(8,128)(2,1)S(1)} %dynamic-slice_bitcast_fusion.14), channel_id=1, source_target_pairs={{0,1},{1,0},{2,3},{3,2},{4,5},{5,4},{6,7},{7,6},{8,9},{9,8},{10,11... | collective-permute-start | bytes 2457608 | tf_op jit(solution)/shard_map/ppermute | solution.py:351
  607.6 214.4 %collective-permute-start.65 = (bf16[2,2,2,2,80,1280]{5,4,1,2,3,0:T(8,128)(2,1)}, bf16[2,2,2,2,80,1280]{5,4,1,2,3,0:T(8,128)(2,1)}, u32[]{:S(2)}, u32[]{:S(2)}) collective-permute-start(bf16[2,2,2,2,80,1280]{5,4,1,2,3,0:T(8,128)(2,1)} %bitcast.348), channel_id=1, source_target_pairs={{0,8},{8,0},{16,24},{24,16},{1,9},{9,1},{17,25},{25,17},{2,10},{10... | collective-permute-start | bytes 9830408 | tf_op jit(solution)/shard_map/ppermute | solution.py:351
  609.6 201.9 %collective-permute-start.50 = (bf16[2,2,2,2,40,2560]{5,4,3,2,1,0:T(8,128)(2,1)}, bf16[2,2,2,2,40,2560]{5,4,3,2,1,0:T(8,128)(2,1)}, u32[]{:S(2)}, u32[]{:S(2)}) collective-permute-start(bf16[2,2,2,2,40,2560]{5,4,3,2,1,0:T(8,128)(2,1)} %dynamic-slice_bitcast_fusion.1), channel_id=1, source_target_pairs={{0,8},{8,0},{16,24},{24,16},{1,9},{9,1},{17,25},{25,17},{2,10},{10... | collective-permute-start | bytes 9830408 | tf_op jit(solution)/shard_map/ppermute | solution.py:351
  626.8 25.2 %collective-permute-start.16 = (bf16[5,6,16,1280]{3,2,1,0:T(8,128)(2,1)S(1)}, bf16[5,6,16,1280]{3,2,1,0:T(8,128)(2,1)S(1)}, u32[]{:S(2)}, u32[]{:S(2)}) collective-permute-start(bf16[5,6,16,1280]{3,2,1,0:T(8,128)(2,1)S(1)} %copy.199), channel_id=1, source_target_pairs={{0,2},{2,4},{4,6},{1,3},{3,5},{5,7},{8,10},{10,12},{12,14},{9,11},... | collective-permute-start | bytes 3686408 | tf_op jit(solution)/shard_map/ppermute | solution.py:460
  628.7 188.3 %collective-permute-start.55 = (bf16[2,2,2,2,40,2560]{5,4,3,2,1,0:T(8,128)(2,1)}, bf16[2,2,2,2,40,2560]{5,4,3,2,1,0:T(8,128)(2,1)}, u32[]{:S(2)}, u32[]{:S(2)}) collective-permute-start(bf16[2,2,2,2,40,2560]{5,4,3,2,1,0:T(8,128)(2,1)} %dynamic-slice_bitcast_fusion), channel_id=1, source_target_pairs={{0,8},{8,0},{16,24},{24,16},{1,9},{9,1},{17,25},{25,17},{2,10},{10... | collective-permute-start | bytes 9830408 | tf_op jit(solution)/shard_map/ppermute | solution.py:351
  652.0 131.8 %collective-permute-start.42 = (bf16[2,2,40,1280]{3,2,0,1:T(8,128)(2,1)S(1)}, bf16[2,2,40,1280]{3,2,0,1:T(8,128)(2,1)S(1)}, u32[]{:S(2)}, u32[]{:S(2)}) collective-permute-start(bf16[2,2,40,1280]{3,2,0,1:T(8,128)(2,1)S(1)} %dynamic-slice_bitcast_fusion.21), channel_id=1, source_target_pairs={{0,16},{8,24},{16,0},{24,8},{1,17},{9,25},{17,1},{25,9},{2,18},{10... | collective-permute-start | bytes 1228808 | tf_op jit(solution)/shard_map/ppermute | solution.py:351
  802.4 44.2 %collective-permute-start.20 = (bf16[8,16,1280]{2,0,1:T(8,128)(2,1)}, bf16[8,16,1280]{2,0,1:T(8,128)(2,1)S(1)}, u32[]{:S(2)}, u32[]{:S(2)}) collective-permute-start(bf16[8,16,1280]{2,0,1:T(8,128)(2,1)} %bitcast.357), channel_id=1, source_target_pairs={{0,6},{1,7},{8,14},{9,15},{16,22},{17,23},{24,30},{25,31}} | collective-permute-start | bytes 983048 | tf_op jit(solution)/shard_map/ppermute | solution.py:490
  806.0 47.1 %collective-permute-start.21 = (bf16[8,16,1280]{2,0,1:T(8,128)(2,1)}, bf16[8,16,1280]{2,0,1:T(8,128)(2,1)}, u32[]{:S(2)}, u32[]{:S(2)}) collective-permute-start(bf16[8,16,1280]{2,0,1:T(8,128)(2,1)} %bitcast.357), channel_id=1, source_target_pairs={{2,6},{3,7},{10,14},{11,15},{18,22},{19,23},{26,30},{27,31}} | collective-permute-start | bytes 983048 | tf_op jit(solution)/shard_map/ppermute | solution.py:490
  811.6 41.7 %collective-permute-start.22 = (bf16[8,16,1280]{2,0,1:T(8,128)(2,1)}, bf16[8,16,1280]{2,0,1:T(8,128)(2,1)}, u32[]{:S(2)}, u32[]{:S(2)}) collective-permute-start(bf16[8,16,1280]{2,0,1:T(8,128)(2,1)} %bitcast.357), channel_id=1, source_target_pairs={{4,6},{5,7},{12,14},{13,15},{20,22},{21,23},{28,30},{29,31}} | collective-permute-start | bytes 983048 | tf_op jit(solution)/shard_map/ppermute | solution.py:490
  817.1 25.5 %collective-permute-start.23 = (bf16[5,6,16,1280]{3,2,1,0:T(8,128)(2,1)S(1)}, bf16[5,6,16,1280]{3,2,1,0:T(8,128)(2,1)}, u32[]{:S(2)}, u32[]{:S(2)}) collective-permute-start(bf16[5,6,16,1280]{3,2,1,0:T(8,128)(2,1)S(1)} %copy-done.40), channel_id=1, source_target_pairs={{2,0},{4,2},{6,4},{3,1},{5,3},{7,5},{10,8},{12,10},{14,12},{11,9},... | collective-permute-start | bytes 3686408 | tf_op jit(solution)/shard_map/ppermute | solution.py:488
  822.0 35.9 %collective-permute-start.61 = (bf16[2,2,2,80,1280]{4,3,0,1,2:T(8,128)(2,1)}, bf16[2,2,2,80,1280]{4,3,0,1,2:T(8,128)(2,1)S(1)}, u32[]{:S(2)}, u32[]{:S(2)}) collective-permute-start(bf16[2,2,2,80,1280]{4,3,0,1,2:T(8,128)(2,1)} %dynamic-slice_bitcast_fusion.3), channel_id=1, source_target_pairs={{0,16},{8,24},{16,0},{24,8},{1,17},{9,25},{17,1},{25,9},{2,18},{10... | collective-permute-start | bytes 4915208 | tf_op jit(solution)/shard_map/ppermute | solution.py:351
  842.6 46.9 %collective-permute-start.66 = (bf16[2,2,2,80,1280]{4,3,0,1,2:T(8,128)(2,1)}, bf16[2,2,2,80,1280]{4,3,0,1,2:T(8,128)(2,1)}, u32[]{:S(2)}, u32[]{:S(2)}) collective-permute-start(bf16[2,2,2,80,1280]{4,3,0,1,2:T(8,128)(2,1)} %dynamic-slice_bitcast_fusion.2), channel_id=1, source_target_pairs={{0,16},{8,24},{16,0},{24,8},{1,17},{9,25},{17,1},{25,9},{2,18},{10... | collective-permute-start | bytes 4915208 | tf_op jit(solution)/shard_map/ppermute | solution.py:351
  846.6 81.0 %collective-permute-start.30 = (bf16[2,2,2,2,40,1920]{5,4,1,2,0,3:T(8,128)(2,1)S(1)}, bf16[2,2,2,2,40,1920]{5,4,1,2,0,3:T(8,128)(2,1)S(1)}, u32[]{:S(2)}, u32[]{:S(2)}) collective-permute-start(bf16[2,2,2,2,40,1920]{5,4,1,2,0,3:T(8,128)(2,1)S(1)} %bitcast.419), channel_id=1, source_target_pairs={{0,8},{8,0},{16,24},{24,16},{1,9},{9,1},{17,25},{25,17},{2,10},{10... | collective-permute-start | bytes 7372808 | tf_op jit(solution)/shard_map/ppermute | solution.py:351
  853.2 77.4 %collective-permute-start.35 = (bf16[2,2,2,2,40,1920]{5,4,1,2,3,0:T(8,128)(2,1)S(1)}, bf16[2,2,2,2,40,1920]{5,4,1,2,3,0:T(8,128)(2,1)S(1)}, u32[]{:S(2)}, u32[]{:S(2)}) collective-permute-start(bf16[2,2,2,2,40,1920]{5,4,1,2,3,0:T(8,128)(2,1)S(1)} %bitcast.418), channel_id=1, source_target_pairs={{0,8},{8,0},{16,24},{24,16},{1,9},{9,1},{17,25},{25,17},{2,10},{10... | collective-permute-start | bytes 7372808 | tf_op jit(solution)/shard_map/ppermute | solution.py:351
  853.2 40.2 %collective-permute-start.51 = (bf16[2,2,2,40,2560]{4,3,2,1,0:T(8,128)(2,1)}, bf16[2,2,2,40,2560]{4,3,2,1,0:T(8,128)(2,1)}, u32[]{:S(2)}, u32[]{:S(2)}) collective-permute-start(bf16[2,2,2,40,2560]{4,3,2,1,0:T(8,128)(2,1)} %dynamic-slice_bitcast_fusion.5), channel_id=1, source_target_pairs={{0,1},{1,0},{2,3},{3,2},{4,5},{5,4},{6,7},{7,6},{8,9},{9,8},{10,11... | collective-permute-start | bytes 4915208 | tf_op jit(solution)/shard_map/ppermute | solution.py:351
  859.1 66.4 %collective-permute-start.56 = (bf16[2,2,2,40,2560]{4,3,2,1,0:T(8,128)(2,1)S(1)}, bf16[2,2,2,40,2560]{4,3,2,1,0:T(8,128)(2,1)S(1)}, u32[]{:S(2)}, u32[]{:S(2)}) collective-permute-start(bf16[2,2,2,40,2560]{4,3,2,1,0:T(8,128)(2,1)S(1)} %copy-done.39), channel_id=1, source_target_pairs={{0,1},{1,0},{2,3},{3,2},{4,5},{5,4},{6,7},{7,6},{8,9},{9,8},{10,11... | collective-permute-start | bytes 4915208 | tf_op jit(solution)/shard_map/ppermute | solution.py:351
  889.5 64.2 %collective-permute-start.24 = (bf16[16,32,1280]{2,0,1:T(8,128)(2,1)S(1)}, bf16[16,32,1280]{2,0,1:T(8,128)(2,1)S(1)}, u32[]{:S(2)}, u32[]{:S(2)}) collective-permute-start(bf16[16,32,1280]{2,0,1:T(8,128)(2,1)S(1)} %get-tuple-element.79), channel_id=1, source_target_pairs={{0,1},{1,0},{2,3},{3,2},{4,5},{5,4},{6,7},{7,6},{8,9},{9,8},{10,11... | collective-permute-start | bytes 3932168 | tf_op jit(solution)/shard_map/ppermute | solution.py:413
  893.5 122.2 %collective-permute-start.62 = (bf16[2,2,80,1280]{3,2,0,1:T(8,128)(2,1)}, bf16[2,2,80,1280]{3,2,0,1:T(8,128)(2,1)}, u32[]{:S(2)}, u32[]{:S(2)}) collective-permute-start(bf16[2,2,80,1280]{3,2,0,1:T(8,128)(2,1)} %dynamic-slice_bitcast_fusion.11), channel_id=1, source_target_pairs={{0,1},{1,0},{2,3},{3,2},{4,5},{5,4},{6,7},{7,6},{8,9},{9,8},{10,11... | collective-permute-start | bytes 2457608 | tf_op jit(solution)/shard_map/ppermute | solution.py:351
  925.5 92.2 %collective-permute-start.67 = (bf16[2,2,80,1280]{3,2,0,1:T(8,128)(2,1)}, bf16[2,2,80,1280]{3,2,0,1:T(8,128)(2,1)}, u32[]{:S(2)}, u32[]{:S(2)}) collective-permute-start(bf16[2,2,80,1280]{3,2,0,1:T(8,128)(2,1)} %dynamic-slice_bitcast_fusion.10), channel_id=1, source_target_pairs={{0,1},{1,0},{2,3},{3,2},{4,5},{5,4},{6,7},{7,6},{8,9},{9,8},{10,11... | collective-permute-start | bytes 2457608 | tf_op jit(solution)/shard_map/ppermute | solution.py:351
  927.6 92.4 %collective-permute-start.52 = (bf16[2,2,40,2560]{3,2,1,0:T(8,128)(2,1)}, bf16[2,2,40,2560]{3,2,1,0:T(8,128)(2,1)}, u32[]{:S(2)}, u32[]{:S(2)}) collective-permute-start(bf16[2,2,40,2560]{3,2,1,0:T(8,128)(2,1)} %dynamic-slice_bitcast_fusion.13), channel_id=1, source_target_pairs={{0,16},{8,24},{16,0},{24,8},{1,17},{9,25},{17,1},{25,9},{2,18},{10... | collective-permute-start | bytes 2457608 | tf_op jit(solution)/shard_map/ppermute | solution.py:351
  930.5 91.6 %collective-permute-start.57 = (bf16[2,2,40,2560]{3,2,1,0:T(8,128)(2,1)}, bf16[2,2,40,2560]{3,2,1,0:T(8,128)(2,1)}, u32[]{:S(2)}, u32[]{:S(2)}) collective-permute-start(bf16[2,2,40,2560]{3,2,1,0:T(8,128)(2,1)} %dynamic-slice_bitcast_fusion.12), channel_id=1, source_target_pairs={{0,16},{8,24},{16,0},{24,8},{1,17},{9,25},{17,1},{25,9},{2,18},{10... | collective-permute-start | bytes 2457608 | tf_op jit(solution)/shard_map/ppermute | solution.py:351
  960.3 29.4 %collective-permute-start.25 = (f32[9440]{0:T(1024)S(1)}, f32[9440]{0:T(1024)S(1)}, u32[]{:S(2)}, u32[]{:S(2)}) collective-permute-start(f32[9440]{0:T(1024)S(1)} %constant_dynamic-update-slice_fusion), channel_id=1, source_target_pairs={{0,1},{1,0},{2,3},{3,2},{4,5},{5,4},{6,7},{7,6},{8,9},{9,8},{10,11... | collective-permute-start | bytes 113288 | tf_op jit(solution)/shard_map/ppermute | solution.py:351
  1011.7 49.7 %collective-permute-start.31 = (bf16[2,2,2,40,1920]{4,3,1,2,0:T(8,128)(2,1)}, bf16[2,2,2,40,1920]{4,3,1,2,0:T(8,128)(2,1)S(1)}, u32[]{:S(2)}, u32[]{:S(2)}) collective-permute-start(bf16[2,2,2,40,1920]{4,3,1,2,0:T(8,128)(2,1)} %dynamic-slice_bitcast_fusion.9), channel_id=1, source_target_pairs={{0,1},{1,0},{2,3},{3,2},{4,5},{5,4},{6,7},{7,6},{8,9},{9,8},{10,11... | collective-permute-start | bytes 3686408 | tf_op jit(solution)/shard_map/ppermute | solution.py:351
  1015.6 49.5 %collective-permute-start.36 = (bf16[2,2,2,40,1920]{4,3,0,1,2:T(8,128)(2,1)}, bf16[2,2,2,40,1920]{4,3,0,1,2:T(8,128)(2,1)S(1)}, u32[]{:S(2)}, u32[]{:S(2)}) collective-permute-start(bf16[2,2,2,40,1920]{4,3,0,1,2:T(8,128)(2,1)} %dynamic-slice_bitcast_fusion.8), channel_id=1, source_target_pairs={{0,16},{8,24},{16,0},{24,8},{1,17},{9,25},{17,1},{25,9},{2,18},{10... | collective-permute-start | bytes 3686408 | tf_op jit(solution)/shard_map/ppermute | solution.py:351
  1022.2 27.9 %collective-permute-start.53 = (bf16[2,40,2560]{2,1,0:T(8,128)(2,1)S(1)}, bf16[2,40,2560]{2,1,0:T(8,128)(2,1)S(1)}, u32[]{:S(2)}, u32[]{:S(2)}) collective-permute-start(bf16[2,40,2560]{2,1,0:T(8,128)(2,1)S(1)} %dynamic-slice_bitcast_fusion.20), channel_id=1, source_target_pairs={{0,2},{2,0},{4,6},{6,4},{1,3},{3,1},{5,7},{7,5},{8,10},{10,8},{12,... | collective-permute-start | bytes 1228808 | tf_op jit(solution)/shard_map/ppermute | solution.py:351
  1028.1 33.2 %collective-permute-start.58 = (bf16[2,40,2560]{2,1,0:T(8,128)(2,1)S(1)}, bf16[2,40,2560]{2,1,0:T(8,128)(2,1)S(1)}, u32[]{:S(2)}, u32[]{:S(2)}) collective-permute-start(bf16[2,40,2560]{2,1,0:T(8,128)(2,1)S(1)} %dynamic-slice_bitcast_fusion.19), channel_id=1, source_target_pairs={{0,2},{2,0},{4,6},{6,4},{1,3},{3,1},{5,7},{7,5},{8,10},{10,8},{12,... | collective-permute-start | bytes 1228808 | tf_op jit(solution)/shard_map/ppermute | solution.py:351
  1036.9 45.5 %collective-permute-start.64 = (bf16[80,1280]{1,0:T(8,128)(2,1)S(1)}, bf16[80,1280]{1,0:T(8,128)(2,1)S(1)}, u32[]{:S(2)}, u32[]{:S(2)}) collective-permute-start(bf16[80,1280]{1,0:T(8,128)(2,1)S(1)} %dynamic-slice_bitcast_fusion.25), channel_id=1, source_target_pairs={{0,4},{2,6},{4,0},{6,2},{1,5},{3,7},{5,1},{7,3},{8,12},{10,14},{12... | collective-permute-start | bytes 614408 | tf_op jit(solution)/shard_map/ppermute | solution.py:351
  1050.1 40.6 %collective-permute-start.69 = (bf16[80,1280]{1,0:T(8,128)(2,1)S(1)}, bf16[80,1280]{1,0:T(8,128)(2,1)}, u32[]{:S(2)}, u32[]{:S(2)}) collective-permute-start(bf16[80,1280]{1,0:T(8,128)(2,1)S(1)} %dynamic-slice_bitcast_fusion.24), channel_id=1, source_target_pairs={{0,4},{2,6},{4,0},{6,2},{1,5},{3,7},{5,1},{7,3},{8,12},{10,14},{12... | collective-permute-start | bytes 614408 | tf_op jit(solution)/shard_map/ppermute | solution.py:351
  1065.1 28.6 %collective-permute-start.32 = (bf16[2,2,40,1920]{3,2,0,1:T(8,128)(2,1)}, bf16[2,2,40,1920]{3,2,0,1:T(8,128)(2,1)}, u32[]{:S(2)}, u32[]{:S(2)}) collective-permute-start(bf16[2,2,40,1920]{3,2,0,1:T(8,128)(2,1)} %dynamic-slice_bitcast_fusion.16), channel_id=1, source_target_pairs={{0,16},{8,24},{16,0},{24,8},{1,17},{9,25},{17,1},{25,9},{2,18},{10... | collective-permute-start | bytes 1843208 | tf_op jit(solution)/shard_map/ppermute | solution.py:351
  (117 other events, 1557.9 us)
Sparse Core Ops, SparseCore 0:
  11.0 100.7 all-gather.6
  114.7 61.9 all-gather.8
  179.6 72.4 all-gather.14
  254.9 89.0 all-gather.16
  347.3 69.1 all-gather.10
  419.3 69.2 all-gather.12

commit v2 on v1

v2 whole, which is shorter than its diff:
```python
import functools

import jax
import jax.numpy as jnp
import numpy as np
from jax import lax
from jax.experimental import pallas as pl
from jax.experimental.pallas import tpu as pltpu
from jax.sharding import PartitionSpec as P

HEADS = 16
HALF = HEADS // 2
WIN = 14
NWIN = 5
SIDE = 16
HD = 80
KEYS = WIN * SIDE
TOK = SIDE * SIDE
LANES = 128
DEPTH = 128
REL = 2 * WIN - 1
NEG = -1e30
END = 24
ALL = ("dp", "rows", "cols")
MIB = 1024 * 1024
PARTS = 4

eps = 1e-06


def dot(a, b):
    return jnp.dot(a, b, preferred_element_type=jnp.float32)


def dot_nt(a, b):
    return lax.dot_general(a, b, (((1,), (1,)), ((), ())), preferred_element_type=jnp.float32)


def dot_tn(a, b):
    return lax.dot_general(a, b, (((0,), (0,)), ((), ())), preferred_element_type=jnp.float32)


def offset_onehot(dtype):
    a = jnp.arange(WIN)[:, None]
    i = jnp.arange(SIDE)[None, :]
    offset = jnp.where(i < WIN, a - i + WIN - 1, -1)
    return (offset[:, :, None] == jnp.arange(REL)).astype(dtype).reshape(KEYS, REL)


def wide_tables(rel_rows, rel_cols):
    onehot = offset_onehot(jnp.bfloat16)
    return jnp.concatenate(
        [dot(onehot, table).astype(jnp.bfloat16) for table in (rel_rows, rel_cols)], axis=0
    )


def narrow_tables(grad):
    onehot = offset_onehot(jnp.float32)
    return [
        lax.dot_general(
            onehot,
            grad[n * KEYS : (n + 1) * KEYS],
            (((0,), (0,)), ((), ())),
            precision=lax.Precision.HIGHEST,
        )
        for n in (0, 1)
    ]


def key_indicator():
    row = lax.broadcasted_iota(jnp.int32, (DEPTH - HD, TOK), 0)
    key = lax.broadcasted_iota(jnp.int32, (DEPTH - HD, TOK), 1)
    return ((row == key // SIDE) | (row - SIDE == key % SIDE)).astype(jnp.bfloat16)


def query_offsets(query, tab_ref, lane):
    halves = []
    for half in range(2):
        low = half * 8
        count = min(8, WIN - low)
        part = dot(
            tab_ref[low * SIDE : (low + count) * SIDE], query[:, half * LANES : (half + 1) * LANES]
        )
        rows = part[:SIDE]
        for a in range(1, count):
            rows = jnp.where(
                lane[:, :LANES] // SIDE == a, part[a * SIDE : (a + 1) * SIDE], rows
            )
        halves.append(rows)
    part = dot(tab_ref[KEYS:], query)
    cols = part[:SIDE]
    for b in range(1, WIN):
        cols = jnp.where(lane % SIDE == b, part[b * SIDE : (b + 1) * SIDE], cols)
    return jnp.concatenate(halves, axis=1), cols


def attention_forward_kernel(
    project_ref, tab_ref, ind_ref, attended_ref, weights_ref, inverse_ref, turned_ref
):
    model = turned_ref.shape[0]
    lane = lax.broadcasted_iota(jnp.int32, (SIDE, TOK), 1)
    sub = lax.broadcasted_iota(jnp.int32, (SIDE, TOK), 0)
    ind = ind_ref[...]
    scale = HD**-0.5
    zeros = jnp.zeros((DEPTH - HD - 2 * SIDE, TOK), jnp.bfloat16)
    for head in range(HEADS):
        low = head * HD
        place = head // HALF * 3 * model // 2 + head % HALF * HD
        query = project_ref[place : place + HD]
        key = project_ref[model // 2 + place : model // 2 + place + HD]
        value = project_ref[model + place : model + place + HD]
        rows, cols = query_offsets(query, tab_ref, lane)
        rows = (rows * HD**0.5).astype(jnp.bfloat16)
        cols = jnp.where(sub < WIN, cols * HD**0.5, NEG).astype(jnp.bfloat16)
        query_wide = jnp.concatenate([query, rows, cols, zeros], axis=0)
        key_wide = jnp.concatenate([key, ind], axis=0)
        scores = dot_tn(key_wide, query_wide)[:KEYS]
        maxima = jnp.max(scores, axis=0, keepdims=True)
        weights = jnp.exp((scores - maxima) * scale)
        inverse = 1.0 / jnp.sum(weights, axis=0, keepdims=True)
        weights = weights.astype(jnp.bfloat16)
        weights_ref[0, head] = weights
        inverse_ref[0, head : head + 1] = inverse
        attended = dot(value[:, :KEYS], weights)
        turned_ref[low : low + HD] = (attended * inverse).astype(jnp.bfloat16)
    attended_ref[...] = turned_ref[...].T


def attention_forward(project, tab, ind):
    model = project.shape[0] // 3
    slots = project.shape[1] // TOK
    return pl.pallas_call(
        attention_forward_kernel,
        grid=(slots,),
        in_specs=[
            pl.BlockSpec((3 * model, TOK), lambda i: (0, i)),
            pl.BlockSpec((2 * KEYS, HD), lambda i: (0, 0)),
            pl.BlockSpec((DEPTH - HD, TOK), lambda i: (0, 0)),
        ],
        out_specs=[
            pl.BlockSpec((TOK, model), lambda i: (i, 0)),
            pl.BlockSpec((1, HEADS, KEYS, TOK), lambda i: (i, 0, 0, 0)),
            pl.BlockSpec((1, HEADS, TOK), lambda i: (i, 0, 0)),
        ],
        out_shape=[
            jax.ShapeDtypeStruct((slots * TOK, model), jnp.bfloat16),
            jax.ShapeDtypeStruct((slots, HEADS, KEYS, TOK), jnp.bfloat16),
            jax.ShapeDtypeStruct((slots, HEADS, TOK), jnp.float32),
        ],
        scratch_shapes=[pltpu.VMEM((model, TOK), jnp.bfloat16)],
        compiler_params=pltpu.CompilerParams(vmem_limit_bytes=48 * MIB),
        cost_estimate=pl.CostEstimate(
            flops=slots * 7_000_000_000,
            bytes_accessed=slots * 6 * MIB,
            transcendentals=slots * HEADS * KEYS * TOK,
        ),
    )(project, tab, ind)


def attention_backward_kernel(
    project_ref, weights_ref, inverse_ref, grad_ref, tab_ref, ind_ref, out_ref, dtab_ref, turned_ref
):
    model = turned_ref.shape[0]
    lane = lax.broadcasted_iota(jnp.int32, (SIDE, TOK), 1)
    ind = ind_ref[...]
    tab = tab_ref[...]
    scale = HD**-0.5

    @pl.when(pl.program_id(0) == 0)
    def _():
        dtab_ref[...] = jnp.zeros_like(dtab_ref)

    turned_ref[...] = grad_ref[...].T
    total = jnp.zeros(dtab_ref.shape, jnp.float32)
    for head in range(HALF):
        low = head * HD
        query = project_ref[low : low + HD]
        key = project_ref[model + low : model + low + HD]
        value = project_ref[2 * model + low : 2 * model + low + HD]
        inverse = inverse_ref[0, head : head + 1]
        grad = (turned_ref[low : low + HD] * inverse).astype(jnp.bfloat16)
        weights = weights_ref[0, head]
        weights_float = weights.astype(jnp.float32)
        terms = weights_float * dot_tn(value, grad)[:KEYS]
        inner = jnp.sum(terms, axis=0, keepdims=True) * inverse
        grad_scores = (terms - weights_float * inner).astype(jnp.bfloat16)
        grad_value = dot_nt(grad, weights)
        grad_key = dot_nt(query, grad_scores) * scale
        key_wide = jnp.concatenate([key, ind], axis=0)
        grad_wide = dot(key_wide[:, :KEYS], grad_scores)
        rows = grad_wide[HD : HD + SIDE]
        cols = grad_wide[HD + SIDE : HD + 2 * SIDE]
        spread = jnp.concatenate(
            [jnp.where(lane // SIDE == a, rows, 0.0) for a in range(WIN)]
            + [jnp.where(lane % SIDE == b, cols, 0.0) for b in range(WIN)],
            axis=0,
        ).astype(jnp.bfloat16)
        grad_query = grad_wide[:HD] * scale + dot_tn(tab, spread)
        total = total + dot_nt(spread, query)
        out_ref[low : low + HD] = grad_query.astype(jnp.bfloat16)
        out_ref[model + low : model + low + HD, :KEYS] = grad_key.astype(jnp.bfloat16)
        out_ref[2 * model + low : 2 * model + low + HD, :KEYS] = grad_value.astype(jnp.bfloat16)
    out_ref[model:, KEYS:] = jnp.zeros((2 * model, TOK - KEYS), jnp.bfloat16)
    dtab_ref[...] += total


def attention_backward(project, weights, inverse, grad, tab, ind, half):
    model = project.shape[0] // 6
    slots = project.shape[1] // TOK
    return pl.pallas_call(
        attention_backward_kernel,
        grid=(slots,),
        in_specs=[
            pl.BlockSpec((3 * model, TOK), lambda i: (half, i)),
            pl.BlockSpec((1, HALF, KEYS, TOK), lambda i: (i, half, 0, 0)),
            pl.BlockSpec((1, HALF, TOK), lambda i: (i, half, 0)),
            pl.BlockSpec((TOK, model), lambda i: (i, half)),
            pl.BlockSpec((2 * KEYS, HD), lambda i: (0, 0)),
            pl.BlockSpec((DEPTH - HD, TOK), lambda i: (0, 0)),
        ],
        out_specs=[
            pl.BlockSpec((3 * model, TOK), lambda i: (0, i)),
            pl.BlockSpec((2 * KEYS, HD), lambda i: (0, 0)),
        ],
        out_shape=[
            jax.ShapeDtypeStruct((3 * model, slots * TOK), jnp.bfloat16),
            jax.ShapeDtypeStruct((2 * KEYS, HD), jnp.float32),
        ],
        scratch_shapes=[pltpu.VMEM((model, TOK), jnp.bfloat16)],
        compiler_params=pltpu.CompilerParams(vmem_limit_bytes=48 * MIB),
        cost_estimate=pl.CostEstimate(
            flops=slots * 4_000_000_000, bytes_accessed=slots * 4 * MIB, transcendentals=0
        ),
    )(project, weights, inverse, grad, tab, ind)


def write_placed(table_ref, kept_ref, sent_ref, core_stride, write):
    devices = table_ref.shape[0] - 1
    for core in (0, 1):

        @pl.when(table_ref[devices] == core)
        def _():
            def write_block(block, rows, value):
                place = table_ref[block]
                if block // core_stride % 2 == core:
                    kept_ref[place, rows] = value
                else:
                    sent_ref[place - devices // 2, rows] = value

            write(write_block)


def mlp_kernel(rows, begins, ends, placed, core_stride, *refs):
    if placed:
        table_ref, *refs = refs
    normed_ref, cot_ref, up_ref, down_ref, shift_ref, mixed0_ref, grad0_ref = refs[:7]
    last_ref, mixed_ref, grad_ref, dup_ref, ddown_ref, dshift_ref = refs[7:13]
    active_ref, hidden_ref = refs[13:15]
    sum_ref = refs[15] if ends else mixed_ref
    tokens = normed_ref.shape[0]
    step = pl.program_id(0) * pl.num_programs(1) + pl.program_id(1)

    @pl.when(step == 0)
    def _():
        sum_ref[...] = jnp.zeros_like(sum_ref)
        grad_ref[...] = jnp.zeros_like(grad_ref)

    piece = mixed0_ref.shape[0]

    @pl.when(step < tokens // piece)
    def _():
        place = pl.ds(pl.multiple_of(step * piece, piece), piece)
        sum_ref[place] += mixed0_ref[...]
        if not begins:
            grad_ref[place] += grad0_ref[...]

    up = up_ref[...]
    down = down_ref[...]
    shift = shift_ref[...]
    total = jnp.zeros(shift.shape, jnp.float32)
    for step_rows in range(tokens // rows):
        part = slice(step_rows * rows, (step_rows + 1) * rows)
        hidden = dot(normed_ref[part], up) + shift
        grad_active = dot_nt(cot_ref[part], down)
        half = 0.5 + 0.5 * lax.erf(hidden * 0.5**0.5)
        active = (hidden * half).astype(jnp.bfloat16)
        slope = half + hidden * jnp.exp(hidden * hidden * -0.5) * (2 * np.pi) ** -0.5
        grad_hidden = (grad_active * slope).astype(jnp.bfloat16)
        active_ref[part] = active
        hidden_ref[part] = grad_hidden
        total = total + jnp.sum(grad_hidden.astype(jnp.float32), axis=0, keepdims=True)
        sum_ref[part] += dot(active, down)
        grad_ref[part] += dot_nt(grad_hidden, up)
    dshift_ref[...] = total
    grad_down = dot_tn(active_ref[...], cot_ref[...]).astype(jnp.bfloat16)
    grad_up = dot_tn(normed_ref[...], hidden_ref[...]).astype(jnp.bfloat16)
    if not placed:
        ddown_ref[...] = grad_down
        dup_ref[...] = grad_up
    else:
        devices = table_ref.shape[0] - 1
        share, wide = grad_up.shape[0] // devices, grad_up.shape[1]
        steps = grad_up.shape[0] // wide
        for index in range(steps):

            @pl.when(pl.program_id(1) == index)
            def _():
                def write(write_block):
                    for block in range(devices):
                        part = grad_up[block * share : (block + 1) * share]
                        write_block(block, slice(index * share, (index + 1) * share), part)
                    for block in range(devices // steps):
                        part = grad_down[block * share : (block + 1) * share]
                        for n in range(steps):
                            low = (steps + n) * share
                            piece = part[:, n * wide : (n + 1) * wide]
                            place = index * devices // steps + block
                            write_block(place, slice(low, low + share), piece)

                write_placed(table_ref, ddown_ref, dup_ref, core_stride, write)
    if ends:

        @pl.when(step == pl.num_programs(0) * pl.num_programs(1) - 1)
        def _():
            mixed_ref[...] = (sum_ref[...] + last_ref[...]).astype(jnp.bfloat16)


def mlp(normed, cot, joint, shift, mixed0, grad0, last, first, count, table):
    tokens, model = normed.shape
    devices = table.shape[0] - 1
    share = model // devices
    steps = 2
    block = model // steps
    begins, ends = first == 0, first + count == PARTS
    placed = share % 8 == 0
    if placed:
        shape = (devices // 2, count * 2 * steps * share, block)
        shapes = [jax.ShapeDtypeStruct(shape, jnp.bfloat16)] * 2
        spec = pl.BlockSpec((devices // 2, 2 * steps * share, block), lambda p, i, *_: (0, p, 0))
        specs = [spec, spec]
    else:
        shapes = [
            jax.ShapeDtypeStruct((model, count * model), jnp.bfloat16),
            jax.ShapeDtypeStruct((count * model, model), jnp.bfloat16),
        ]
        specs = [
            pl.BlockSpec((model, block), lambda p, i, *_: (0, p * steps + i)),
            pl.BlockSpec((block, model), lambda p, i, *_: (p * steps + i, 0)),
        ]
    pieces = count * steps
    piece = pl.BlockSpec((tokens // pieces, model), lambda p, i, *_: (p * steps + i, 0))
    once = pl.Buffered(1)
    whole = pl.BlockSpec((tokens, model), lambda p, i, *_: (0, 0), pipeline_mode=once)
    core_stride = lax.axis_size("rows") * lax.axis_size("cols")
    mixed, grad, sent, kept, grad_shift = pl.pallas_call(
        functools.partial(mlp_kernel, tokens // 2, begins, ends, placed, core_stride),
        grid_spec=pltpu.PrefetchScalarGridSpec(
            num_scalar_prefetch=1 if placed else 0,
            grid=(count, steps),
            in_specs=[
                whole,
                whole,
                pl.BlockSpec((model, block), lambda p, i, *_: (0, (first + p) * steps + i)),
                pl.BlockSpec((block, model), lambda p, i, *_: (i, PARTS + first + p)),
                pl.BlockSpec((1, block), lambda p, i, *_: (0, (first + p) * steps + i)),
                piece,
                pl.BlockSpec((8, LANES), lambda p, i, *_: (0, 0)) if begins else piece,
                pl.BlockSpec((1, model), lambda p, i, *_: (0, 0)),
            ],
            out_specs=[
                whole,
                whole,
                specs[0],
                specs[1],
                pl.BlockSpec((1, block), lambda p, i, *_: (0, p * steps + i)),
            ],
            scratch_shapes=[pltpu.VMEM((tokens, block), jnp.bfloat16)] * 2
            + ([pltpu.VMEM((tokens, model), jnp.float32)] if ends else []),
        ),
        out_shape=[
            jax.ShapeDtypeStruct((tokens, model), jnp.bfloat16 if ends else jnp.float32),
            jax.ShapeDtypeStruct((tokens, model), jnp.float32),
            shapes[0],
            shapes[1],
            jax.ShapeDtypeStruct((1, count * model), jnp.float32),
        ],
        compiler_params=pltpu.CompilerParams(vmem_limit_bytes=62 * MIB),
        cost_estimate=pl.CostEstimate(
            flops=16 * tokens * model * model * count,
            bytes_accessed=8 * model * model * count + 24 * tokens * model,
            transcendentals=2 * tokens * model * count,
        ),
    )(*([table] if placed else []), normed, cot, joint, joint, shift, mixed0, grad0, last)
    if placed:
        return mixed, grad, (sent, kept), grad_shift
    down = kept.reshape(count, devices, share, model).transpose(1, 0, 2, 3)
    parts = [sent.reshape(devices, share, -1), down.reshape(devices, -1, model)]
    return mixed, grad, parts, grad_shift


def window_gradient_kernel(own, core_stride, table_ref, *refs):
    tokens_ref, grad_ref, *ready, sent_ref, kept_ref, sums_ref = refs
    devices = table_ref.shape[0] - 1
    share = tokens_ref.shape[0] // devices
    step = pl.program_id(0)

    def place(value):
        def write(write_block):
            for block in range(devices):
                part = value[block * share : (block + 1) * share]
                write_block(block, slice(0, share), part)

        write_placed(table_ref, kept_ref, sent_ref, core_stride, write)

    @pl.when(step < own)
    def _():
        grad = grad_ref[...]
        place(dot_nt(tokens_ref[...], grad).astype(jnp.bfloat16))
        sums_ref[...] = dot_nt(jnp.ones((8, grad.shape[1]), jnp.bfloat16), grad)

    for ready_ref in ready:

        @pl.when(step >= own)
        def _():
            place(ready_ref[...])


def window_gradient(turned, grad, ready, table):
    model, tokens = turned.shape
    devices = table.shape[0] - 1
    wide = model // 2
    own = grad.shape[0] // wide
    steps = own + sum(one.shape[1] // wide for one in ready)
    shape = jax.ShapeDtypeStruct((devices // 2, model // devices, steps * wide), jnp.bfloat16)
    spec = pl.BlockSpec((devices // 2, model // devices, wide), lambda n, *_: (0, 0, n))
    core_stride = lax.axis_size("rows") * lax.axis_size("cols")
    return pl.pallas_call(
        functools.partial(window_gradient_kernel, own, core_stride),
        grid_spec=pltpu.PrefetchScalarGridSpec(
            num_scalar_prefetch=1,
            grid=(steps,),
            in_specs=[
                pl.BlockSpec((model, tokens), lambda n, *_: (0, 0), pipeline_mode=pl.Buffered(1)),
                pl.BlockSpec((wide, tokens), lambda n, *_: (jnp.minimum(n, own - 1), 0)),
            ]
            + [pl.BlockSpec((model, wide), lambda n, *_: (0, jnp.maximum(n - own, 0)))] * len(ready),
            out_specs=[
                spec,
                spec,
                pl.BlockSpec((8, wide), lambda n, *_: (0, jnp.minimum(n, own - 1))),
            ],
        ),
        out_shape=[shape, shape, jax.ShapeDtypeStruct((8, own * wide), jnp.float32)],
        compiler_params=pltpu.CompilerParams(vmem_limit_bytes=56 * MIB),
        cost_estimate=pl.CostEstimate(
            flops=2 * tokens * model * own * wide,
            bytes_accessed=2 * (tokens * model + tokens * own * wide + model * steps * wide),
            transcendentals=0,
        ),
    )(table, turned, grad, *ready)


def hidden_parts(unit):
    return 5 if unit % 160 == 0 else 1


def normalised(values):
    average = jnp.mean(values, axis=-1, keepdims=True)
    centered = values - average
    variance = jnp.mean(centered * centered, axis=-1, keepdims=True)
    inverse = lax.rsqrt(variance + eps)
    return centered * inverse, inverse


def norm_backward(unit, inverse, gain, grad):
    scaled = grad * gain
    return inverse * (
        scaled
        - jnp.mean(scaled, axis=-1, keepdims=True)
        - unit * jnp.mean(scaled * unit, axis=-1, keepdims=True)
    )


def column_sum(value):
    return jnp.sum(value, axis=0, keepdims=True)


def row_block(tokens):
    return tokens // 4


def row_norm_kernel(rows_ref, vectors_ref, out_ref):
    unit, _ = normalised(rows_ref[...].astype(jnp.float32))
    out_ref[...] = (unit * vectors_ref[0:1] + vectors_ref[1:2]).astype(jnp.bfloat16)


def row_norm(rows, vectors):
    tokens, model = rows.shape
    block = pl.BlockSpec((row_block(tokens), model), lambda i: (i, 0))
    return pl.pallas_call(
        row_norm_kernel,
        grid=(4,),
        in_specs=[block, pl.BlockSpec((8, model), lambda i: (0, 0))],
        out_specs=block,
        out_shape=jax.ShapeDtypeStruct((tokens, model), jnp.bfloat16),
        cost_estimate=pl.CostEstimate(
            flops=8 * tokens * model, bytes_accessed=4 * tokens * model, transcendentals=0
        ),
    )(rows, vectors)


def middle_kernel(attended_ref, proj_ref, image_ref, vectors_ref, middle_ref, normed_ref):
    branch = dot(attended_ref[...], proj_ref[...]) + vectors_ref[0:1]
    middle = image_ref[...].astype(jnp.float32) + branch
    unit, _ = normalised(middle)
    normed = (unit * vectors_ref[1:2] + vectors_ref[2:3]).astype(jnp.bfloat16)
    middle_ref[...] = middle
    normed_ref[...] = normed


def middle_forward(attended, proj, image, vectors):
    tokens, model = attended.shape
    rows = row_block(tokens)
    block = pl.BlockSpec((rows, model), lambda i: (i, 0))
    return pl.pallas_call(
        middle_kernel,
        grid=(tokens // rows,),
        in_specs=[
            block,
            pl.BlockSpec((model, model), lambda i: (0, 2 * PARTS)),
            block,
            pl.BlockSpec((8, model), lambda i: (0, 0)),
        ],
        out_specs=[block, block],
        out_shape=[
            jax.ShapeDtypeStruct((tokens, model), jnp.float32),
            jax.ShapeDtypeStruct((tokens, model), jnp.bfloat16),
        ],
        compiler_params=pltpu.CompilerParams(vmem_limit_bytes=40 * MIB),
        cost_estimate=pl.CostEstimate(
            flops=2 * tokens * model * model, bytes_accessed=12 * tokens * model, transcendentals=0
        ),
    )(attended, proj, image, vectors)


def middle_backward_kernel(
    grad_ref, middle_ref, cot_ref, attended_ref, proj_ref, vectors_ref,
    grad_middle_ref, grad_attended_ref, dproj_ref, sums_ref, total_ref,
):
    step = pl.program_id(0)

    @pl.when(step == 0)
    def _():
        sums_ref[...] = jnp.zeros_like(sums_ref)
        total_ref[...] = jnp.zeros_like(total_ref)

    middle = middle_ref[...]
    unit, inverse = normalised(middle)
    grad = grad_ref[...]
    cot = cot_ref[...].astype(jnp.float32)
    grad_middle = cot + norm_backward(unit, inverse, vectors_ref[1:2], grad)
    branch = grad_middle.astype(jnp.bfloat16)
    grad_middle_ref[...] = grad_middle
    grad_attended_ref[...] = dot_nt(branch, proj_ref[...]).astype(jnp.bfloat16)
    total_ref[...] += dot_tn(attended_ref[...], branch)
    sums_ref[0:1] += column_sum(branch.astype(jnp.float32))
    sums_ref[1:2] += column_sum(grad * unit)
    sums_ref[2:3] += column_sum(grad)
    sums_ref[3:4] += column_sum(cot)

    @pl.when(step == pl.num_programs(0) - 1)
    def _():
        dproj_ref[...] = total_ref[...].astype(jnp.bfloat16)


def middle_backward(grad, middle, cot, attended, proj, vectors):
    tokens, model = attended.shape
    rows = row_block(tokens)
    block = pl.BlockSpec((rows, model), lambda i: (i, 0))
    few = pl.BlockSpec((8, model), lambda i: (0, 0))
    return pl.pallas_call(
        middle_backward_kernel,
        grid=(tokens // rows,),
        in_specs=[
            block, block, block, block,
            pl.BlockSpec((model, model), lambda i: (0, 2 * PARTS)),
            few,
        ],
        out_specs=[block, block, pl.BlockSpec((model, model), lambda i: (0, 0)), few],
        out_shape=[
            jax.ShapeDtypeStruct((tokens, model), jnp.float32),
            jax.ShapeDtypeStruct((tokens, model), jnp.bfloat16),
            jax.ShapeDtypeStruct((model, model), jnp.bfloat16),
            jax.ShapeDtypeStruct((8, model), jnp.float32),
        ],
        scratch_shapes=[pltpu.VMEM((model, model), jnp.float32)],
        compiler_params=pltpu.CompilerParams(vmem_limit_bytes=56 * MIB),
        cost_estimate=pl.CostEstimate(
            flops=4 * tokens * model * model, bytes_accessed=24 * tokens * model, transcendentals=0
        ),
    )(grad, middle, cot, attended, proj, vectors)


def image_backward_kernel(
    rows_ref, first_ref, second_ref, grad_middle_ref, vectors_ref, out_ref, sums_ref
):
    @pl.when(pl.program_id(0) == 0)
    def _():
        sums_ref[...] = jnp.zeros_like(sums_ref)

    unit, inverse = normalised(rows_ref[...].astype(jnp.float32))
    grad = first_ref[...].astype(jnp.float32) + second_ref[...].astype(jnp.float32)
    total = grad_middle_ref[...] + norm_backward(unit, inverse, vectors_ref[0:1], grad)
    out_ref[...] = total.astype(jnp.bfloat16)
    sums_ref[0:1] += column_sum(grad * unit)
    sums_ref[1:2] += column_sum(grad)


def image_backward(rows, first, second, grad_middle, vectors):
    tokens, model = rows.shape
    block = pl.BlockSpec((row_block(tokens), model), lambda i: (i, 0))
    few = pl.BlockSpec((8, model), lambda i: (0, 0))
    return pl.pallas_call(
        image_backward_kernel,
        grid=(4,),
        in_specs=[block, block, block, block, few],
        out_specs=[block, few],
        out_shape=[
            jax.ShapeDtypeStruct((tokens, model), jnp.bfloat16),
            jax.ShapeDtypeStruct((8, model), jnp.float32),
        ],
        cost_estimate=pl.CostEstimate(
            flops=12 * tokens * model, bytes_accessed=10 * tokens * model, transcendentals=0
        ),
    )(rows, first, second, grad_middle, vectors)


def main_place(width):
    col = lax.broadcasted_iota(jnp.int32, (width, NWIN * SIDE), 0)
    slot = lax.broadcasted_iota(jnp.int32, (width, NWIN * SIDE), 1)
    inside = slot % SIDE < WIN
    return (inside & (col == slot // SIDE * WIN + slot % SIDE)).astype(jnp.bfloat16)


def end_starts(width, count):
    starts = [b * WIN // 8 * 8 for b in range(count - 1)]
    return starts + [width - END]


def end_place(width):
    count = lax.axis_size("rows")
    row = lax.axis_index("rows")
    start = jnp.array(end_starts(width, count))[row]
    col = start + lax.broadcasted_iota(jnp.int32, (END, 2 * SIDE), 0)
    slot = lax.broadcasted_iota(jnp.int32, (END, 2 * SIDE), 1)
    held = (slot % SIDE < WIN) & ((slot < SIDE) | (row == count - 1))
    window = row + slot // SIDE
    return (held & (col == window * WIN + slot % SIDE)).astype(jnp.bfloat16)


def to_windows_kernel(width, rest, rows_ref, main_ref, end_ref, out_ref):
    out_ref[...] = jnp.zeros_like(out_ref)
    for i in range(WIN):
        part = dot_tn(main_ref[...], rows_ref[i * width : (i + 1) * width]).astype(jnp.bfloat16)
        for b in range(NWIN):
            out_ref[b * TOK + i * SIDE : b * TOK + (i + 1) * SIDE] = part[b * SIDE : (b + 1) * SIDE]
    first = WIN * width
    for i in range(rest):
        part = rows_ref[first + i * END : first + (i + 1) * END]
        part = dot_tn(end_ref[...], part).astype(jnp.bfloat16)
        for b in range(2):
            place = (NWIN + b) * TOK + i * SIDE
            out_ref[place : place + SIDE] = part[b * SIDE : (b + 1) * SIDE]


def to_rows_kernel(width, rest, windows_ref, main_ref, end_ref, out_ref):
    for i in range(WIN):
        part = jnp.concatenate(
            [windows_ref[b * TOK + i * SIDE : b * TOK + (i + 1) * SIDE] for b in range(NWIN)],
            axis=0,
        )
        out_ref[i * width : (i + 1) * width] = dot(main_ref[...], part).astype(jnp.bfloat16)
    first = WIN * width
    for i in range(rest):
        part = jnp.concatenate(
            [
                windows_ref[b * TOK + i * SIDE : b * TOK + (i + 1) * SIDE]
                for b in range(NWIN, NWIN + 2)
            ],
            axis=0,
        )
        part = dot(end_ref[...], part).astype(jnp.bfloat16)
        out_ref[first + i * END : first + (i + 1) * END] = part


def rearranged(kernel, value, width, rest, tokens):
    model = value.shape[1]
    lanes = model // 5
    main, end = main_place(width), end_place(width)
    return pl.pallas_call(
        functools.partial(kernel, width, rest),
        grid=(5,),
        in_specs=[
            pl.BlockSpec((value.shape[0], lanes), lambda i: (0, i)),
            pl.BlockSpec(main.shape, lambda i: (0, 0)),
            pl.BlockSpec(end.shape, lambda i: (0, 0)),
        ],
        out_specs=pl.BlockSpec((tokens, lanes), lambda i: (0, i)),
        out_shape=jax.ShapeDtypeStruct((tokens, model), jnp.bfloat16),
        compiler_params=pltpu.CompilerParams(vmem_limit_bytes=32 * MIB),
        cost_estimate=pl.CostEstimate(
            flops=200 * tokens * model, bytes_accessed=6 * tokens * model, transcendentals=0
        ),
    )(value, main, end)


def axis_bits(axis):
    count = lax.axis_size(axis)
    return [(axis, 1 << bit) for bit in range(count.bit_length() - 1)]


def flipped(value, bit):
    axis, mask = bit
    return lax.ppermute(value, axis, [(i, i ^ mask) for i in range(lax.axis_size(axis))])


def bit_of(bit):
    axis, mask = bit
    return (lax.axis_index(axis) // mask) % 2


def device_bits():
    return [bit for axis in ALL for bit in reversed(axis_bits(axis))]


def after(value, others):
    return lax.optimization_barrier((value, others))[0]


def beside(flights, value, kernel):
    return sync(kernel(launch(value, flights)), flights)


class Flight:

    def __init__(self, steps):
        self.steps = steps
        self.sent = self.arrived = self.value = None
        self.flying = True

    def advance(self):
        try:
            self.sent, self.arrived = self.steps.send(self.arrived)
        except StopIteration as end:
            self.sent, self.arrived, self.flying = [], [], False
            self.value = end.value

    def finish(self):
        while self.flying:
            self.advance()
        return self.value


def launch(value, flights):
    for one in flights:
        if one.flying:
            one.advance()
    return after(value, [one.sent for one in flights])


def sync(value, flights):
    flights = [one for one in flights if one.flying]
    value, arrived = lax.optimization_barrier((value, [one.arrived for one in flights]))
    for one, pieces in zip(flights, arrived):
        one.arrived = pieces
    return value


def index_masks(bits):
    weights = {"cols": 1, "rows": lax.axis_size("cols")}
    weights["dp"] = weights["rows"] * lax.axis_size("rows")
    return [weights[axis] * mask for axis, mask in bits]


def halving_orders():
    dp, rows, cols = axis_bits("dp"), axis_bits("rows"), axis_bits("cols")
    core, chips = dp[:1], dp[1:]
    (core,) = index_masks(core)
    orders = [cols + chips + rows, chips + rows[:1] + cols + rows[1:]]
    return core, [index_masks(order) for order in orders]


def block_tables():
    core, orders = halving_orders()
    me = lax.axis_index(ALL)
    steps = len(orders[0])
    flips = []
    for order in orders:
        place = np.arange(1 << steps)
        flips.append(sum((place >> (steps - 1 - n) & 1) * mask for n, mask in enumerate(order)))
    flips = [jnp.asarray(flip, jnp.int32) for flip in flips]
    first = (me & core) == 0
    there = (me ^ core) ^ jnp.where(first, flips[1], flips[0])
    here = me ^ jnp.where(first, flips[0], flips[1])
    return there, here


def place_table():
    there, here = block_tables()
    blocks = jnp.concatenate([here, there])
    count = blocks.shape[0]
    hit = blocks[:, None] == jnp.arange(count)[None, :]
    places = jnp.sum(jnp.where(hit, jnp.arange(count)[:, None], 0), axis=0)
    core, _ = halving_orders()
    return jnp.concatenate([places, (lax.axis_index(ALL) // core % 2)[None]]).astype(jnp.int32)


def partner_permute(value, step):
    core, orders = halving_orders()
    pairs = []
    for index in range(lax.axis_size(ALL)):
        order = orders[(index & core) // core]
        pairs.append((index, index ^ (core if step == 0 else order[step - 1])))
    return lax.ppermute(value, ALL, pairs)


def packed_shape(parts):
    if len({part.shape[1] for part in parts}) == 1:
        return parts[0].shape[1], sum(part.shape[2] for part in parts)
    wide = 2 * LANES
    return sum(part.shape[1] * part.shape[2] // wide for part in parts), wide


def pack_into(refs, write):
    rows, wide = packed_shape(refs)
    side = rows == refs[0].shape[1]
    place = 0
    for ref in refs:
        height, width = ref.shape[1:]
        if side:
            write(slice(0, rows), slice(place, place + width), ref[0])
            place += width
            continue
        for low in range(0, width, wide):
            write(slice(place, place + height), slice(0, wide), ref[0, :, low : low + wide])
            place += height


def pack_kernel(table_ref, *refs):
    def write(rows, cols, value):
        refs[-1][0, rows, cols] = value

    pack_into(refs[:-1], write)


def pack(parts, table):
    count = table.shape[0]
    rows, wide = packed_shape(parts)
    return pl.pallas_call(
        pack_kernel,
        grid_spec=pltpu.PrefetchScalarGridSpec(
            num_scalar_prefetch=1,
            grid=(count,),
            in_specs=[
                pl.BlockSpec((1,) + part.shape[1:], lambda i, table: (table[i], 0, 0))
                for part in parts
            ],
            out_specs=pl.BlockSpec((1, rows, wide), lambda i, table: (i, 0, 0)),
        ),
        out_shape=jax.ShapeDtypeStruct((count, rows, wide), jnp.bfloat16),
        cost_estimate=pl.CostEstimate(
            flops=0, bytes_accessed=4 * count * rows * wide, transcendentals=0
        ),
    )(table, *parts)


def summed(sent, kept):
    held = [kept]
    size = 2 * kept.shape[0]
    step = 0
    while size > 1:
        if step:
            sent = sum(piece[size // 2 : size].astype(jnp.float32) for piece in held)
            sent = sent.astype(jnp.bfloat16)
        held = yield [sent], [partner_permute(sent, step)] + held
        size //= 2
        step += 1
    return sum(piece[0].astype(jnp.float32) for piece in held)


def summed_packed(parts):
    there, here = block_tables()
    total = yield from summed(pack(parts, there), pack(parts, here))
    shapes = [part.shape[1:] for part in parts]
    rows, wide = packed_shape(parts)
    out = []
    place = 0
    for height, width in shapes:
        if rows == height:
            out.append(total[:, place : place + width])
            place += width
        else:
            pieces = width // wide
            piece = total[place : place + pieces * height].reshape(pieces, height, wide)
            out.append(piece.transpose(1, 0, 2).reshape(height, width))
            place += pieces * height
    return out


def summed_mlp(parts, share):
    total = yield from summed(*parts)
    wide = total.shape[1]
    total = total.reshape(-1, 2, 2, share, wide)
    up = total[:, 0].transpose(2, 0, 1, 3).reshape(share, -1)
    down = total[:, 1].transpose(0, 2, 1, 3).reshape(-1, 2 * wide)
    return [up, down]


def summed_columns(sent, kept, widths):
    total = yield from summed(sent, kept)
    places = np.cumsum([0] + list(widths))
    return [total[:, low : low + width] for low, width in zip(places, widths)]


def all_sum(value):
    for bit in reversed(device_bits()):
        value = value + flipped(value, bit)
    return value


def small_gather(value):
    for bit in reversed(device_bits()):
        arrived = flipped(value, bit)
        value = jnp.where(
            bit_of(bit) == 0,
            jnp.concatenate([value, arrived], axis=0),
            jnp.concatenate([arrived, value], axis=0),
        )
    return value


SWAP = [(0, 1), (1, 0)]


def split_tiles(tiles):
    col = lax.axis_index("cols")
    kept = lax.dynamic_index_in_dim(tiles, col, 0, keepdims=False)
    sent = lax.dynamic_index_in_dim(tiles, 1 - col, 0, keepdims=False)
    return kept, sent, lax.ppermute(sent, "cols", SWAP)


def join_tiles(kept, arrived):
    return jnp.where(
        lax.axis_index("cols") == 0,
        jnp.concatenate([kept, arrived], axis=1),
        jnp.concatenate([arrived, kept], axis=1),
    )


def split_image(image):
    col = lax.axis_index("cols")
    width = image.shape[1] // 2
    kept = lax.dynamic_slice_in_dim(image, col * width, width, 1)
    sent = lax.dynamic_slice_in_dim(image, (1 - col) * width, width, 1)
    return kept, sent, lax.ppermute(sent, "cols", SWAP)


def join_image(kept, arrived):
    return jnp.where(
        lax.axis_index("cols") == 0, jnp.stack([kept, arrived]), jnp.stack([arrived, kept])
    )


def halves_to_image(tiles):
    kept, _, arrived = split_tiles(tiles)
    return join_tiles(kept, arrived)


def image_to_halves(image):
    kept, _, arrived = split_image(image)
    return join_image(kept, arrived)


def column_windows(rows):
    width = rows.shape[1]
    parts = []
    for b in range(NWIN):
        piece = rows[:, b * WIN : min((b + 1) * WIN, width)]
        parts.append(jnp.pad(piece, ((0, 0), (0, SIDE - piece.shape[1]), (0, 0))))
    return jnp.stack(parts)


def column_rows(windows, width):
    parts = [windows[b, :, : min(WIN, width - b * WIN)] for b in range(len(windows))]
    return jnp.concatenate(parts, axis=1)


def pad_rows(value, top, bottom):
    widths = [(0, 0)] * value.ndim
    widths[-3] = (top, bottom)
    return jnp.pad(value, widths)


class Layout:

    def __init__(self, tiles):
        self.tiles = tiles
        _, self.height, tile_w, self.model = tiles
        self.width = 2 * tile_w
        self.count = lax.axis_size("rows")
        self.row = lax.axis_index("rows")
        self.near = self.count == NWIN - 1
        self.step = self.height - WIN
        self.halo = self.step * (self.count - 1)
        self.rest = self.height * self.count - WIN * self.count
        if self.near:
            self.slots = NWIN + 2
            self.tokens = WIN * self.width + self.rest * END
        else:
            self.slots = -(-NWIN * NWIN // self.count)
            self.tokens = 2 * self.height * tile_w

    def enter(self, tiles):
        if not self.near:
            return tiles.reshape(self.tokens, self.model)
        last, rest, halo = self.count - 1, self.rest, self.halo
        top = self.height - rest
        kept_low, sent_low, low = split_tiles(tiles[:, top:])
        kept_up, sent_up, up = split_tiles(tiles[:, :top])
        low, up = yield [sent_low, sent_up], [low, up]
        lower = join_tiles(kept_low, low)
        upper = join_tiles(kept_up, up)
        starts = end_starts(self.width, self.count)
        sent = [lower[rest - halo :]]
        arrived = [lax.ppermute(sent[0], "rows", [(i, i + 1) for i in range(last)])]
        for target in range(last):
            sent.append(lower[:, starts[target] : starts[target] + END])
            arrived.append(lax.ppermute(sent[-1], "rows", [(last, target)]))
        down, *arrived = yield sent, arrived
        end = lower[:, starts[last] :]
        for target in range(last):
            end = jnp.where(self.row == target, arrived[target], end)
        held = jnp.sum(end_place(self.width), axis=1).astype(jnp.bfloat16)
        end = end * held[None, :, None]
        whole = jnp.concatenate([down, upper, lower], axis=0)
        main = lax.dynamic_slice_in_dim(whole, halo - self.step * self.row, WIN, 0)
        return jnp.concatenate(
            [main.reshape(-1, self.model), end.reshape(-1, self.model)], axis=0
        )

    def leave(self, tokens):
        if not self.near:
            return tokens.reshape(self.tiles)
        last, rest, halo = self.count - 1, self.rest, self.halo
        top = self.height - rest
        main = tokens[: WIN * self.width].reshape(WIN, self.width, self.model)
        end = tokens[WIN * self.width :].reshape(rest, END, self.model)
        held = jnp.sum(end_place(self.width), axis=1).astype(jnp.bfloat16)
        end = end * held[None, :, None]
        up = lax.ppermute(main[:halo], "rows", [(i + 1, i) for i in range(last)])
        pieces = [lax.ppermute(end, "rows", [(source, last)]) for source in range(last)]
        upper = lax.dynamic_slice_in_dim(main, self.step * self.row, top, 0)
        kept_up, sent_up, arrived_up = split_image(upper)
        up, arrived_up, *pieces = yield [end, sent_up], [up, arrived_up] + pieces
        tail = 0
        for start, piece in zip(end_starts(self.width, self.count), pieces + [end]):
            tail = tail + jnp.pad(piece, ((0, 0), (start, self.width - END - start), (0, 0)))
        below = jnp.where(self.row == last, tail, pad_rows(up, 0, rest - halo))
        whole = jnp.concatenate([main, below], axis=0)
        place = self.step * self.row + top
        kept_low, sent_low, arrived_low = split_image(
            lax.dynamic_slice_in_dim(whole, place, rest, 0)
        )
        (arrived_low,) = yield [sent_low], [arrived_low]
        upper = join_image(kept_up, arrived_up)
        lower = join_image(kept_low, arrived_low)
        return jnp.concatenate([upper, lower], axis=1)

    def to_windows(self, tokens):
        if self.near:
            total = self.slots * TOK
            return rearranged(to_windows_kernel, tokens, self.width, self.rest, total)
        windows = column_windows(halves_to_image(tokens.reshape(self.tiles)))
        windows = lax.all_gather(windows, "rows", axis=1, tiled=True)
        extra = NWIN * WIN - windows.shape[1]
        windows = jnp.pad(windows, ((0, 0), (0, extra), (0, 0), (0, 0)))
        windows = windows.reshape(NWIN, NWIN, WIN, SIDE, self.model).transpose(1, 0, 2, 3, 4)
        windows = windows.reshape(NWIN * NWIN, WIN, SIDE, self.model)
        extra = self.slots * self.count - NWIN * NWIN
        windows = jnp.pad(windows, ((0, extra), (0, SIDE - WIN), (0, 0), (0, 0)))
        windows = lax.dynamic_slice_in_dim(windows, self.row * self.slots, self.slots, 0)
        return windows.reshape(self.slots * TOK, self.model)

    def to_rows(self, windows):
        if self.near:
            return rearranged(to_rows_kernel, windows, self.width, self.rest, self.tokens)
        windows = windows.reshape(self.slots, SIDE, SIDE, self.model)
        windows = lax.all_gather(windows[:, :WIN], "rows", axis=0, tiled=True)
        windows = windows[: NWIN * NWIN].reshape(NWIN, NWIN, WIN, SIDE, self.model)
        windows = windows.transpose(1, 0, 2, 3, 4).reshape(NWIN, NWIN * WIN, SIDE, self.model)
        windows = lax.dynamic_slice_in_dim(windows, self.row * self.height, self.height, 1)
        return image_to_halves(column_rows(windows, self.width)).reshape(self.tokens, self.model)


def shards(
    image_in,
    ln1_gain,
    ln1_bias,
    w_qkv,
    qv_bias,
    rel_rows,
    rel_cols,
    w_proj,
    proj_bias,
    ln2_gain,
    ln2_bias,
    w_fc1,
    fc1_bias,
    w_fc2,
    fc2_bias,
    cotangent,
):
    devices = lax.axis_size(ALL)
    me = lax.axis_index(ALL)
    model = image_in.shape[3]
    layout = Layout(image_in.shape)
    tokens = layout.tokens
    share = model // devices
    unit = fc1_bias.shape[0]

    rows = Flight(layout.enter(image_in))
    cot = Flight(layout.enter(cotangent))
    rows.advance()

    def gathered(shard):
        return lax.all_gather(shard, ALL, axis=0, tiled=True)

    vectors = [ln1_gain, ln1_bias, qv_bias[:, 0], qv_bias[:, 1], proj_bias, ln2_gain, ln2_bias]
    vectors = small_gather(jnp.concatenate(vectors + [fc2_bias, fc1_bias])[None])
    vectors = vectors.astype(jnp.float32)
    gain1, shift1, query_shift, value_shift, proj_shift, gain2, shift2, down_shift = (
        vectors[:, n * share : (n + 1) * share].reshape(1, model) for n in range(8)
    )
    norm_vectors = jnp.pad(jnp.concatenate([gain1, shift1], axis=0), ((0, 6), (0, 0)))
    middle_vectors = jnp.concatenate([proj_shift, gain2, shift2, down_shift], axis=0)
    middle_vectors = jnp.pad(middle_vectors, ((0, 4), (0, 0)))
    up_shift = vectors[:, 8 * share :].reshape(devices, PARTS, share)
    up_shift = up_shift.transpose(1, 0, 2).reshape(1, devices * unit)
    half = model // 2
    thirds = [w_qkv[:, n * half : (n + 1) * half] for n in (0, 2, 4, 1, 3, 5)]
    qkv_full = gathered(jnp.concatenate(thirds, axis=1))
    up_shard = w_fc1.reshape(share, devices, PARTS, share).transpose(0, 2, 1, 3)
    down_shard = [w_fc2[n * share : (n + 1) * share] for n in range(PARTS)]
    joint = gathered(
        jnp.concatenate([up_shard.reshape(share, devices * unit)] + down_shard + [w_proj], axis=1)
    )

    norm_vectors = sync(norm_vectors, [rows])
    norm_vectors = launch(norm_vectors, [rows, cot])
    norm_vectors = sync(norm_vectors, [rows])
    rows = rows.finish()
    window_tokens = layout.to_windows(row_norm(rows, norm_vectors))
    turned_tokens = window_tokens.T
    nothing = jnp.zeros((1, half), jnp.float32)
    shift_qkv = jnp.concatenate(
        [query_shift[:, :half], nothing, value_shift[:, :half]]
        + [query_shift[:, half:], nothing, value_shift[:, half:]],
        axis=1,
    )
    project = lax.dot_general(
        qkv_full, window_tokens, (((0,), (1,)), ((), ())), preferred_element_type=jnp.float32
    )
    project = (project + shift_qkv.reshape(3 * model, 1)).astype(jnp.bfloat16)
    project = sync(project, [cot])
    project = launch(project, [cot])
    tab = wide_tables(rel_rows, rel_cols)
    ind = key_indicator()
    attended_windows, weights, inverse = attention_forward(project, tab, ind)
    attended = layout.to_rows(attended_windows)
    attended, cot, turned_tokens, joint = sync(
        (attended, cot.finish(), turned_tokens, joint), []
    )
    middle, normed2 = middle_forward(attended, joint, rows, middle_vectors)

    mixed = middle
    grad_normed2 = jnp.zeros((8, LANES), jnp.float32)
    table = place_table()
    sums = []
    shifts = []
    for first, count in ((0, 2), (2, 2)):

        def step(normed2):
            return mlp(
                normed2,
                cot,
                joint,
                up_shift,
                mixed,
                grad_normed2,
                down_shift,
                first,
                count,
                table,
            )

        mixed, grad_normed2, blocks, grad_shift = beside(sums, normed2, step)
        shifts.append(grad_shift.reshape(count, devices, share))
        if isinstance(blocks, list):
            sums.append(Flight(summed_packed(blocks)))
        else:
            sums.append(Flight(summed_mlp(blocks, share)))

    output = Flight(layout.leave(mixed))
    grad_normed2 = launch(grad_normed2, sums)
    grad_middle, grad_attended, grad_proj, middle_sums = sync(
        middle_backward(grad_normed2, middle, cot, attended, joint, middle_vectors), sums[1:]
    )

    def rows_of(vector):
        return vector.reshape(devices, -1)

    def attention_step(half):
        return attention_backward(project, weights, inverse, grad_windows, tab, ind, half)

    def project_step(grad_project, half):
        return lax.dot_general(
            grad_project,
            qkv_full[:, half * 3 * model // 2 : (half + 1) * 3 * model // 2],
            (((0,), (1,)), ((), ())),
            preferred_element_type=jnp.float32,
        ).astype(jnp.bfloat16)

    grad_windows = layout.to_windows(launch(grad_attended, sums[1:] + [output]))
    grad_project, grad_tab = sync(attention_step(0), sums[:1])
    grad_project = launch(grad_project, sums[:1])
    sent, kept, sums0 = sync(
        window_gradient(turned_tokens, grad_project, [grad_proj], table), sums[1:] + [output]
    )
    sums.append(Flight(summed_columns(sent, kept, [3 * half, model])))
    grad_project = launch(grad_project, sums[1:] + [output])
    first_rows = layout.to_rows(project_step(grad_project, 0))
    first_rows, grad_windows = sync((first_rows, grad_windows), sums[:1] + sums[-1:])
    grad_windows = launch(grad_windows, sums[:1] + sums[-1:])
    grad_project, grad_part = sync(attention_step(1), sums + [output])
    grad_project = launch(grad_project, sums + [output])
    sent, kept, sums1 = window_gradient(turned_tokens, grad_project, [], table)
    sums.append(Flight(summed_columns(sent, kept, [3 * half])))
    grad_project = launch(grad_project, sums[-1:])
    second_rows = sync(project_step(grad_project, 1), sums)
    second_rows = layout.to_rows(launch(second_rows, sums))
    grad_tab = grad_tab + grad_part
    grad_sums = [sums0[0], sums1[0]]
    grad_rows, norm_sums = image_backward(
        rows, first_rows, second_rows, grad_middle, norm_vectors
    )
    grad_rows, norm_sums = sync((grad_rows, norm_sums), sums)
    grad_in = Flight(layout.leave(grad_rows))
    norm_sums = launch(norm_sums, sums + [grad_in])

    up_shift_sums = jnp.concatenate(shifts, axis=0).transpose(1, 0, 2).reshape(devices, unit)
    small = jnp.concatenate(
        [
            rows_of(norm_sums[0]),
            rows_of(norm_sums[1]),
            rows_of(jnp.concatenate([piece[:half] for piece in grad_sums])),
            rows_of(jnp.concatenate([piece[2 * half :] for piece in grad_sums])),
        ]
        + [rows_of(middle_sums[n]) for n in range(4)]
        + [up_shift_sums],
        axis=1,
    )
    small, grad_tables = all_sum_pair(small, jnp.stack(narrow_tables(grad_tab)))
    small = lax.dynamic_index_in_dim(small, me, 0, keepdims=False)

    ups, downs = zip(*[one.finish() for one in sums[:-2]])
    (first_qkv, sum_proj), (last_qkv,) = (one.finish() for one in sums[-2:])
    grad_fc1 = jnp.concatenate([grad.reshape(share, -1, devices, share) for grad in ups], axis=1)
    thirds = [
        piece[:, n * half : (n + 1) * half] for n in range(3) for piece in (first_qkv, last_qkv)
    ]
    return (
        output.finish(),
        grad_in.finish().astype(jnp.float32),
        small[:share],
        small[share : 2 * share],
        jnp.concatenate(thirds, axis=1),
        jnp.stack([small[2 * share : 3 * share], small[3 * share : 4 * share]], axis=1),
        grad_tables[0],
        grad_tables[1],
        sum_proj,
        small[4 * share : 5 * share],
        small[5 * share : 6 * share],
        small[6 * share : 7 * share],
        grad_fc1.transpose(0, 2, 1, 3).reshape(share, devices * unit),
        small[8 * share :],
        jnp.concatenate(downs, axis=0),
        small[7 * share : 8 * share],
    )


def all_sum_pair(first, second):
    sizes = first.size
    joined = all_sum(jnp.concatenate([first.reshape(-1), second.reshape(-1)]))
    return joined[:sizes].reshape(first.shape), joined[sizes:].reshape(second.shape)


def solution(mesh):
    tile = P("dp", "rows", "cols", None)
    vector = P(ALL)
    matrix = P(ALL, None)
    in_specs = (
        tile, vector, vector, matrix, matrix, P(), P(), matrix, vector, vector, vector,
        matrix, vector, matrix, vector, tile,
    )
    out_specs = (
        tile, tile, vector, vector, matrix, matrix, P(), P(), matrix, vector, vector, vector,
        matrix, vector, matrix, vector,
    )
    return jax.shard_map(shards, mesh=mesh, in_specs=in_specs, out_specs=out_specs, check_vma=False)
```

time: 1140 us -> 888 us (0.78)
  waiting for transfers between devices: 443 us -> 192 us
  Pallas kernels: 212 us -> 353 us
  local copies, waits for them, and re-layouts: 147 us -> 93.7 us
  matrix products: 93.6 us -> 55.4 us
  other arithmetic: 121 us -> 92 us
  starting transfers between devices: 96.7 us -> 74.9 us
    ppermute x50 -> x10, waiting for transfers between devices: 196 us -> 13.5 us  [flipped(): lax.ppermute(value, axis, [(i, i ^ mask) for i in range(lax.axis_size(axi...]
    pallas_call x2 -> x13, Pallas kernels: 108 us -> 244 us  [the longest x2 142 us: mlp(): pl.pallas_call(functools.partial(mlp_kernel, tokens // 2, begins, ends, p...]
    ppermute x20 -> x44, waiting for transfers between devices: 157 us -> 90.1 us  [the longest x6 42.5 us: enter(): arrived.append(lax.ppermute(sent[-1], 'rows', [(last, target)]))]
    ppermute x50 -> x10, starting transfers between devices: 60 us -> 19.4 us  [flipped(): lax.ppermute(value, axis, [(i, i ^ mask) for i in range(lax.axis_size(axi...]
    reduce_sum x10 -> x2, other arithmetic: 32.5 us -> 0.28 us  [the longest x1 0.19 us: enter(): held = jnp.sum(end_place(self.width), axis=1).astype(jnp.bfloat16)]
    dot_general x4 -> x2, matrix products: 59.2 us -> 28.7 us  [project_step(): lax.dot_general(grad_project, qkv_full[:, half * 3 * model // 2:(half + 1...]
    dynamic_slice x17 -> x2, local copies, waits for them, and re-layouts: 28.8 us -> 1.6 us  [the longest x1 1.01 us: split_image(): sent = lax.dynamic_slice_in_dim(image, (1 - col) * width, width, 1)]
    convert_element_type x4 -> x0, local copies, waits for them, and re-layouts: 23 us -> none  [the longest x1 8.86 us: shards(): window_unit, _ = normalised(raw.astype(jnp.float32))]
  transfers between devices with their start and end apart: 76 -> 56, of which waited for: 30 -> 18; matrix products, arithmetic and copies ran while one was open for 31% -> 24% of each run, Pallas kernels for 19% -> 31%
where the time goes in v2:
time: 888 us; the launch traced here: 877 us
  Pallas kernels  353 us (40%)
  waiting for transfers between devices  192 us (22%)
  local copies, waits for them, and re-layouts  93.7 us (11%)
  other arithmetic  92 us (10%)
  starting transfers between devices  74.9 us (8%)
  matrix products  55.4 us (6%)
  between operations  16.1 us (2%)
    pallas_call x2, Pallas kernels, mlp(): pl.pallas_call(functools.partial(mlp_kernel, tokens // 2, begins, ends, p...  142 us
    all_gather x2, waiting for transfers between devices, gathered(): return lax.all_gather(shard, ALL, axis=0, tiled=True)  88.3 us
    pallas_call x2, Pallas kernels, attention_backward(): pl.pallas_call(attention_backward_kernel, grid=(slots,), in_specs=[pl.Blo...  59 us
    pallas_call x1, Pallas kernels, attention_forward(): pl.pallas_call(attention_forward_kernel, grid=(slots,), in_specs=[pl.Bloc...  49.3 us
    pallas_call x2, Pallas kernels, window_gradient(): pl.pallas_call(functools.partial(window_gradient_kernel, own, core_stride...  48.4 us
    convert_element_type x16, other arithmetic, summed(): sent = sent.astype(jnp.bfloat16)  45.5 us
    ppermute x6, waiting for transfers between devices, enter(): arrived.append(lax.ppermute(sent[-1], 'rows', [(last, target)]))  42.5 us
    dot_general x2, matrix products, project_step(): lax.dot_general(grad_project, qkv_full[:, half * 3 * model // 2:(half + 1...  28.7 us
  transfers between devices with their start and end apart: 56, of which 18 were waited for; matrix products, arithmetic and copies ran while one was open for 24% of the time, Pallas kernels for 31%

profile of v2, /device:TPU:1, one launch (start us, length us, event | category | flops | bytes accessed | tf_op | source)
XLA Modules:
  0.0 876.6 jit_solution(9098988948763289152)
XLA Ops:
  12.9 5.0 reshape.287
  18.2 3.3 reshape.288
  28.2 4.8 concatenate.142
  50.9 3.1 collective-permute-start.3
  60.7 13.9 %collective-permute-done.6 = bf16[8,32,1280]{2,1,0:T(8,128)(2,1)} collective-permute-done((bf16[8,32,1280]{2,1,0:T(8,128)(2,1)}, bf16[8,32,1280]{2,1,0:T(8,128)(2,1)}, u32[]{:S(2)}, u32[]{:S(2)}) %collective-permute-start.6) | collective-permute-done | bytes 655392 | tf_op jit(solution)/shard_map/ppermute | solution.py:949
  76.7 3.4 collective-permute-start.7
  85.0 17.2 %collective-permute-done.8 = bf16[8,24,1280]{2,1,0:T(8,128)(2,1)S(1)} collective-permute-done((bf16[8,24,1280]{2,1,0:T(8,128)(2,1)S(1)}, bf16[8,24,1280]{2,1,0:T(8,128)(2,1)S(1)}, u32[]{:S(2)}, u32[]{:S(2)}) %collective-permute-start.8) | collective-permute-done | bytes 491552 | tf_op jit(solution)/shard_map/ppermute | solution.py:1038
  104.0 9.6 %collective-permute-done.7 = bf16[6,64,1280]{2,1,0:T(8,128)(2,1)S(1)} collective-permute-done((bf16[6,64,1280]{2,1,0:T(8,128)(2,1)S(1)}, bf16[6,64,1280]{2,1,0:T(8,128)(2,1)S(1)}, u32[]{:S(2)}, u32[]{:S(2)}) %collective-permute-start.7) | collective-permute-done | bytes 983072 | tf_op jit(solution)/shard_map/ppermute | solution.py:1035
  116.5 4.9 shard_map.378.rows_ref
  127.8 7.2 copy.87
  135.0 25.5 %add_convert_fusion.project_ref = bf16[3840,1792]{1,0:T(8,128)(2,1)} fusion(bf16[1280,3840]{1,0:T(8,128)(2,1)} %all-gather.3.cloned.1.call-done, bf16[1792,1280]{1,0:T(8,128)(2,1)} %copy-done.5, f32[3840]{0:T(1024)S(1)} %reduce.4), kind=kOutput, calls=%fused_computation | convolution fusion | flops 17629839360 | bytes 28195840 | tf_op jit(solution)/shard_map/dot_general | solution.py:1170
  165.0 4.8 collective-permute-start.13
  169.9 49.3 %shard_map.380 = (bf16[1792,1280]{1,0:T(8,128)(2,1)S(1)}, bf16[7,16,224,256]{3,2,1,0:T(8,128)(2,1)}, f32[7,16,256]{2,1,0:T(8,128)S(1)}) custom-call(bf16[3840,1792]{1,0:T(8,128)(2,1)} %add_convert_fusion.project_ref, bf16[448,80]{1,0:T(8,128)(2,1)S(1)} %pad_maximum_fusion.4.tab_ref, bf16[48,256]{1,0:T(8,128)(2,1)S(1)} %fusion.25.ind_ref), custom_call_target="tpu_custom_call" | custom-call | flops 49000001536 | bytes 44040192 | tf_op jit(solution)/shard_map/pallas_call | solution.py:132
  221.3 2.6 maximum_select_fusion.3
  223.9 25.3 %collective-permute-done.16 = bf16[8,24,1280]{2,1,0:T(8,128)(2,1)S(1)} collective-permute-done((bf16[8,24,1280]{2,1,0:T(8,128)(2,1)S(1)}, bf16[8,24,1280]{2,1,0:T(8,128)(2,1)S(1)}, u32[]{:S(2)}, u32[]{:S(2)}) %collective-permute-start.16) | collective-permute-done | bytes 491552 | tf_op jit(solution)/shard_map/ppermute | solution.py:1038
  252.2 88.3 %all-gather.5.cloned.1.call-done.proj_ref.refs_3_.refs_4_ = bf16[1280,11520]{1,0:T(8,128)(2,1)} async-done(((bf16[40,11520]{1,0:T(8,128)(2,1)}), bf16[1280,11520]{1,0:T(8,128)(2,1)}) %all-gather.5.cloned.1.call-update) | async-done | bytes 29491216 | tf_op jit(solution)/shard_map/all_gather | solution.py:1136
  342.3 7.8 shard_map.382
  354.7 70.2 %shard_map.383 = (f32[1088,1280]{1,0:T(8,128)}, f32[1088,1280]{1,0:T(8,128)}, bf16[16,320,640]{2,1,0:T(8,128)(2,1)}, bf16[16,320,640]{2,1,0:T(8,128)(2,1)}, f32[1,2560]{1,0:T(1,128)}) custom-call(s32[33]{0:T(128)} %pad_add_fusion.1.refs_0_.table_ref, bf16[1088,1280]{1,0:T(8,128)(2,1)} %copy-done.22, bf16[1088,1280]{1,0:T(8,128)(2,1)} %pad_maximum_fusion.1.refs_2_.cot_ref, ...), custom_call_target="tpu_custom_call" | custom-call | flops 57042534400 | bytes 59637760 | tf_op jit(solution)/shard_map/pallas_call | solution.py:355
  425.3 71.6 %shard_map.384 = (bf16[1088,1280]{1,0:T(8,128)(2,1)}, f32[1088,1280]{1,0:T(8,128)}, bf16[16,320,640]{2,1,0:T(8,128)(2,1)}, bf16[16,320,640]{2,1,0:T(8,128)(2,1)}, f32[1,2560]{1,0:T(1,128)}) custom-call(s32[33]{0:T(128)} %pad_add_fusion.1.refs_0_.table_ref, bf16[1088,1280]{1,0:T(8,128)(2,1)} %copy-done.22, ...), custom_call_target="tpu_custom_call" | custom-call | flops 57042534400 | bytes 59637760 | tf_op jit(solution)/shard_map/pallas_call | solution.py:355
  502.8 3.0 collective-permute-start.23
  506.5 4.4 add_convert_fusion.2
  512.1 21.5 %shard_map.385 = (f32[1088,1280]{1,0:T(8,128)}, bf16[1088,1280]{1,0:T(8,128)(2,1)}, bf16[1280,1280]{1,0:T(8,128)(2,1)}, f32[8,1280]{1,0:T(8,128)}) custom-call(f32[1088,1280]{1,0:T(8,128)} %get-tuple-element.197.grad_ref, f32[1088,1280]{1,0:T(8,128)} %copy-done.9, bf16[1088,1280]{1,0:T(8,128)(2,1)} %pad_maximum_fusion.1.refs_2_.cot_ref, ...), custom_call_target="tpu_custom_call" | custom-call | flops 7130316800 | bytes 33423360 | tf_op jit(solution)/shard_map/pallas_call | solution.py:581
  534.9 3.9 add_convert_fusion.1
  542.4 30.2 %shard_map.387 = (bf16[1920,1792]{1,0:T(8,128)(2,1)}, f32[448,80]{1,0:T(8,128)S(1)}) custom-call(bf16[3840,1792]{1,0:T(8,128)(2,1)} %add_convert_fusion.project_ref, bf16[7,16,224,256]{3,2,1,0:T(8,128)(2,1)} %get-tuple-element.191.weights_ref, f32[7,16,256]{2,1,0:T(8,128)S(1)} %get-tuple-element.192.inverse_ref, bf16[1792,1280]{1,0:T(8,128)(2,1)S(1)} %shard_map.386.grad_ref, ...), custom_call_target="tpu_custom_call" | custom-call | flops 28000000000 | bytes 29360128 | tf_op jit(solution)/shard_map/pallas_call | solution.py:210
  574.0 4.3 add_convert_fusion.5
  579.9 25.9 %shard_map.388 = (bf16[16,40,3200]{2,1,0:T(8,128)(2,1)}, bf16[16,40,3200]{2,1,0:T(8,128)(2,1)}, f32[8,1920]{1,0:T(8,128)}) custom-call(s32[33]{0:T(128)} %pad_add_fusion.1.refs_0_.table_ref, bf16[1280,1792]{1,0:T(8,128)(2,1)} %bitcast.124, bf16[1920,1792]{1,0:T(8,128)(2,1)} %get-tuple-element.227.refs_1_, bf16[1280,1280]{1,0:T(8,128)(2,1)} %get-tuple-element.214.refs_2_), custom_call_target="tpu_custom_call" | custom-call | flops 8808038400 | bytes 19660800 | tf_op jit(solution)/shard_map/pallas_call | solution.py:437
  612.4 4.3 add_convert_fusion.4
  623.2 13.8 %convolution_convert_fusion.1.windows_ref = bf16[1792,1280]{1,0:T(8,128)(2,1)S(1)} fusion(bf16[1920,1792]{1,0:T(8,128)(2,1)} %get-tuple-element.227.refs_1_, bf16[1280,3840]{1,0:T(8,128)(2,1)} %all-gather.3.cloned.1.call-done), kind=kOutput, calls=%fused_computation.2 | convolution fusion | flops 8810332160 | bytes 16384000 | tf_op jit(solution)/shard_map/dot_general | solution.py:1226
  641.6 4.0 add_convert_fusion.9
  649.3 28.8 %shard_map.390 = (bf16[1920,1792]{1,0:T(8,128)(2,1)}, f32[448,80]{1,0:T(8,128)S(1)}) custom-call(bf16[3840,1792]{1,0:T(8,128)(2,1)} %add_convert_fusion.project_ref, bf16[7,16,224,256]{3,2,1,0:T(8,128)(2,1)} %get-tuple-element.191.weights_ref, f32[7,16,256]{2,1,0:T(8,128)S(1)} %get-tuple-element.192.inverse_ref, bf16[1792,1280]{1,0:T(8,128)(2,1)S(1)} %bitcast.117, ...), custom_call_target="tpu_custom_call" | custom-call | flops 28000000000 | bytes 29360128 | tf_op jit(solution)/shard_map/pallas_call | solution.py:210
  678.1 3.2 add_convert_fusion.13
  683.7 3.2 add_convert_fusion.8
  691.0 22.5 %shard_map.391 = (bf16[16,40,1920]{2,1,0:T(8,128)(2,1)}, bf16[16,40,1920]{2,1,0:T(8,128)(2,1)}, f32[8,1920]{1,0:T(8,128)}) custom-call(s32[33]{0:T(128)} %pad_add_fusion.1.refs_0_.table_ref, bf16[1280,1792]{1,0:T(8,128)(2,1)} %bitcast.125, bf16[1920,1792]{1,0:T(8,128)(2,1)} %get-tuple-element.256.refs_1_), custom_call_target="tpu_custom_call" | custom-call | flops 8808038400 | bytes 16384000 | tf_op jit(solution)/shard_map/pallas_call | solution.py:437
  717.2 14.9 %convolution_convert_fusion.windows_ref = bf16[1792,1280]{1,0:T(8,128)(2,1)} fusion(bf16[1920,1792]{1,0:T(8,128)(2,1)} %get-tuple-element.256.refs_1_, bf16[1280,3840]{1,0:T(8,128)(2,1)} %all-gather.3.cloned.1.call-done), kind=kOutput, calls=%fused_computation.1 | convolution fusion | flops 8810332160 | bytes 16384000 | tf_op jit(solution)/shard_map/dot_general | solution.py:1226
  737.1 2.7 add_convert_fusion.12
  756.0 9.2 %shard_map.393 = (bf16[1088,1280]{1,0:T(8,128)(2,1)}, f32[8,1280]{1,0:T(8,128)}) custom-call(bf16[1088,1280]{1,0:T(8,128)(2,1)} %pad_maximum_fusion.rows_ref.image_ref, bf16[1088,1280]{1,0:T(8,128)(2,1)} %copy-done.6, bf16[1088,1280]{1,0:T(8,128)(2,1)} %copy-done.7, f32[1088,1280]{1,0:T(8,128)} %get-tuple-element.271.grad_middle_ref, ...), custom_call_target="tpu_custom_call" | custom-call | flops 16711680 | bytes 13926400 | tf_op jit(solution)/shard_map/pallas_call | solution.py:623
  771.8 4.9 collective-permute-start.40
  786.1 3.1 reshape_reshape.7
  791.3 3.8 copy.94
  795.1 5.4 reshape.304
  804.3 7.0 collective-permute-done.51
  813.8 6.4 collective-permute-done.50
  822.0 3.9 collective-permute-done.52
  829.9 2.8 fusion.8
  847.5 3.9 collective-permute-start.48
  852.7 3.3 collective-permute-done.49
  859.4 6.8 collective-permute-done.44
  866.6 2.7 maximum_convert_fusion
  (412 shorter events, 188.8 us)
Async XLA Ops:
  7.2 127.8 %all-gather.3.cloned.1.call-start = ((), (), s32[]{:S(2)}) async-start(), calls=%async_computation | async-start | bytes 10137600 | tf_op jit(solution)/shard_map/all_gather | solution.py:1136
  12.9 327.7 %all-gather.5.cloned.1.call-start = ((), (), s32[]{:S(2)}) async-start(), calls=%async_computation.1 | async-start | bytes 30412800 | tf_op jit(solution)/shard_map/all_gather | solution.py:1136
  33.0 11.0 %collective-permute-start = (bf16[1,480]{1,0:T(2,128)(2,1)S(1)}, bf16[1,480]{1,0:T(2,128)(2,1)S(1)}, u32[]{:S(2)}, u32[]{:S(2)}) collective-permute-start(bf16[1,480]{1,0:T(2,128)(2,1)S(1)} %broadcast_in_dim.70), channel_id=1, source_target_pairs={{0,1},{1,0},{2,3},{3,2},{4,5},{5,4},{6,7},{7,6},{8,9},{9,8},{10,11... | collective-permute-start | bytes 2888 | tf_op jit(solution)/shard_map/ppermute | solution.py:724
  36.2 24.5 %collective-permute-start.5 = (bf16[8,32,1280]{2,1,0:T(8,128)(2,1)}, bf16[8,32,1280]{2,1,0:T(8,128)(2,1)}, u32[]{:S(2)}, u32[]{:S(2)}) collective-permute-start(bf16[8,32,1280]{2,1,0:T(8,128)(2,1)} %get-tuple-element.340), channel_id=1, source_target_pairs={{0,1},{1,0},{2,3},{3,2},{4,5},{5,4},{6,7},{7,6},{8,9},{9,8},{10,11... | collective-permute-start | bytes 1966088 | tf_op jit(solution)/shard_map/ppermute | solution.py:949
  37.4 37.2 %collective-permute-start.6 = (bf16[8,32,1280]{2,1,0:T(8,128)(2,1)}, bf16[8,32,1280]{2,1,0:T(8,128)(2,1)}, u32[]{:S(2)}, u32[]{:S(2)}) collective-permute-start(bf16[8,32,1280]{2,1,0:T(8,128)(2,1)} %get-tuple-element.335), channel_id=1, source_target_pairs={{0,1},{1,0},{2,3},{3,2},{4,5},{5,4},{6,7},{7,6},{8,9},{9,8},{10,11... | collective-permute-start | bytes 1966088 | tf_op jit(solution)/shard_map/ppermute | solution.py:949
  40.0 120.5 %collective-permute-start.11 = (bf16[8,32,1280]{2,1,0:T(8,128)(2,1)}, bf16[8,32,1280]{2,1,0:T(8,128)(2,1)}, u32[]{:S(2)}, u32[]{:S(2)}) collective-permute-start(bf16[8,32,1280]{2,1,0:T(8,128)(2,1)} %get-tuple-element.333), channel_id=1, source_target_pairs={{0,1},{1,0},{2,3},{3,2},{4,5},{5,4},{6,7},{7,6},{8,9},{9,8},{10,11... | collective-permute-start | bytes 1966088 | tf_op jit(solution)/shard_map/ppermute | solution.py:949
  76.7 36.8 %collective-permute-start.7 = (bf16[6,64,1280]{2,1,0:T(8,128)(2,1)S(1)}, bf16[6,64,1280]{2,1,0:T(8,128)(2,1)S(1)}, u32[]{:S(2)}, u32[]{:S(2)}) collective-permute-start(bf16[6,64,1280]{2,1,0:T(8,128)(2,1)S(1)} %slice.730), channel_id=1, source_target_pairs={{0,2},{2,4},{4,6},{1,3},{3,5},{5,7},{8,10},{10,12},{12,14},{9,11},... | collective-permute-start | bytes 2949128 | tf_op jit(solution)/shard_map/ppermute | solution.py:1035
  80.3 21.9 %collective-permute-start.8 = (bf16[8,24,1280]{2,1,0:T(8,128)(2,1)S(1)}, bf16[8,24,1280]{2,1,0:T(8,128)(2,1)S(1)}, u32[]{:S(2)}, u32[]{:S(2)}) collective-permute-start(bf16[8,24,1280]{2,1,0:T(8,128)(2,1)S(1)} %get-tuple-element.338), channel_id=1, source_target_pairs={{6,0},{7,1},{14,8},{15,9},{22,16},{23,17},{30,24},{31,25}} | collective-permute-start | bytes 1474568 | tf_op jit(solution)/shard_map/ppermute | solution.py:1038
  81.6 22.4 %collective-permute-start.9 = (bf16[8,24,1280]{2,1,0:T(8,128)(2,1)S(1)}, bf16[8,24,1280]{2,1,0:T(8,128)(2,1)S(1)}, u32[]{:S(2)}, u32[]{:S(2)}) collective-permute-start(bf16[8,24,1280]{2,1,0:T(8,128)(2,1)S(1)} %get-tuple-element.337), channel_id=1, source_target_pairs={{6,2},{7,3},{14,10},{15,11},{22,18},{23,19},{30,26},{31,27}} | collective-permute-start | bytes 1474568 | tf_op jit(solution)/shard_map/ppermute | solution.py:1038
  82.3 21.7 %collective-permute-start.10 = (bf16[8,24,1280]{2,1,0:T(8,128)(2,1)S(1)}, bf16[8,24,1280]{2,1,0:T(8,128)(2,1)S(1)}, u32[]{:S(2)}, u32[]{:S(2)}) collective-permute-start(bf16[8,24,1280]{2,1,0:T(8,128)(2,1)S(1)} %get-tuple-element.336), channel_id=1, source_target_pairs={{6,4},{7,5},{14,12},{15,13},{22,20},{23,21},{30,28},{31,29}} | collective-permute-start | bytes 1474568 | tf_op jit(solution)/shard_map/ppermute | solution.py:1038
  102.1 58.4 %collective-permute-start.12 = (bf16[8,32,1280]{2,1,0:T(8,128)(2,1)}, bf16[8,32,1280]{2,1,0:T(8,128)(2,1)}, u32[]{:S(2)}, u32[]{:S(2)}) collective-permute-start(bf16[8,32,1280]{2,1,0:T(8,128)(2,1)} %get-tuple-element.328), channel_id=1, source_target_pairs={{0,1},{1,0},{2,3},{3,2},{4,5},{5,4},{6,7},{7,6},{8,9},{9,8},{10,11... | collective-permute-start | bytes 1966088 | tf_op jit(solution)/shard_map/ppermute | solution.py:949
  162.3 61.6 %collective-permute-start.14 = (bf16[8,24,1280]{2,1,0:T(8,128)(2,1)S(1)}, bf16[8,24,1280]{2,1,0:T(8,128)(2,1)S(1)}, u32[]{:S(2)}, u32[]{:S(2)}) collective-permute-start(bf16[8,24,1280]{2,1,0:T(8,128)(2,1)S(1)} %get-tuple-element.329), channel_id=1, source_target_pairs={{6,4},{7,5},{14,12},{15,13},{22,20},{23,21},{30,28},{31,29}} | collective-permute-start | bytes 1474568 | tf_op jit(solution)/shard_map/ppermute | solution.py:1038
  163.0 60.9 %collective-permute-start.15 = (bf16[8,24,1280]{2,1,0:T(8,128)(2,1)S(1)}, bf16[8,24,1280]{2,1,0:T(8,128)(2,1)S(1)}, u32[]{:S(2)}, u32[]{:S(2)}) collective-permute-start(bf16[8,24,1280]{2,1,0:T(8,128)(2,1)S(1)} %get-tuple-element.330), channel_id=1, source_target_pairs={{6,2},{7,3},{14,10},{15,11},{22,18},{23,19},{30,26},{31,27}} | collective-permute-start | bytes 1474568 | tf_op jit(solution)/shard_map/ppermute | solution.py:1038
  163.7 85.5 %collective-permute-start.16 = (bf16[8,24,1280]{2,1,0:T(8,128)(2,1)S(1)}, bf16[8,24,1280]{2,1,0:T(8,128)(2,1)S(1)}, u32[]{:S(2)}, u32[]{:S(2)}) collective-permute-start(bf16[8,24,1280]{2,1,0:T(8,128)(2,1)S(1)} %get-tuple-element.331), channel_id=1, source_target_pairs={{6,0},{7,1},{14,8},{15,9},{22,16},{23,17},{30,24},{31,25}} | collective-permute-start | bytes 1474568 | tf_op jit(solution)/shard_map/ppermute | solution.py:1038
  165.0 84.4 %collective-permute-start.13 = (bf16[6,64,1280]{2,1,0:T(8,128)(2,1)S(1)}, bf16[6,64,1280]{2,1,0:T(8,128)(2,1)S(1)}, u32[]{:S(2)}, u32[]{:S(2)}) collective-permute-start(bf16[6,64,1280]{2,1,0:T(8,128)(2,1)S(1)} %slice.741), channel_id=1, source_target_pairs={{0,2},{2,4},{4,6},{1,3},{3,5},{5,7},{8,10},{10,12},{12,14},{9,11},... | collective-permute-start | bytes 2949128 | tf_op jit(solution)/shard_map/ppermute | solution.py:1035
  424.9 71.9 %collective-permute-start.17 = (bf16[16,320,640]{2,1,0:T(8,128)(2,1)}, bf16[16,320,640]{2,1,0:T(8,128)(2,1)}, u32[]{:S(2)}, u32[]{:S(2)}) collective-permute-start(bf16[16,320,640]{2,1,0:T(8,128)(2,1)} %get-tuple-element.179), channel_id=1, source_target_pairs={{0,8},{1,9},{2,10},{3,11},{4,12},{5,13},{6,14},{7,15},{8,0},{9,1},... | collective-permute-start | bytes 19660808 | tf_op jit(solution)/shard_map/ppermute | solution.py:824
  496.9 38.1 %collective-permute-start.18 = (bf16[16,320,640]{2,1,0:T(8,128)(2,1)}, bf16[16,320,640]{2,1,0:T(8,128)(2,1)}, u32[]{:S(2)}, u32[]{:S(2)}) collective-permute-start(bf16[16,320,640]{2,1,0:T(8,128)(2,1)} %get-tuple-element.196), channel_id=1, source_target_pairs={{0,8},{1,9},{2,10},{3,11},{4,12},{5,13},{6,14},{7,15},{8,0},{9,1},... | collective-permute-start | bytes 19660808 | tf_op jit(solution)/shard_map/ppermute | solution.py:824
  502.8 75.5 %collective-permute-start.23 = (bf16[8,24,1280]{2,1,0:T(8,128)(2,1)S(1)}, bf16[8,24,1280]{2,1,0:T(8,128)(2,1)S(1)}, u32[]{:S(2)}, u32[]{:S(2)}) collective-permute-start(bf16[8,24,1280]{2,1,0:T(8,128)(2,1)S(1)} %broadcast_multiply_fusion.1), channel_id=1, source_target_pairs={{0,6},{1,7},{8,14},{9,15},{16,22},{17,23},{24,30},{25,31}} | collective-permute-start | bytes 1474568 | tf_op jit(solution)/shard_map/ppermute | solution.py:1061
  505.8 100.0 %collective-permute-start.24 = (bf16[8,24,1280]{2,1,0:T(8,128)(2,1)S(1)}, bf16[8,24,1280]{2,1,0:T(8,128)(2,1)S(1)}, u32[]{:S(2)}, u32[]{:S(2)}) collective-permute-start(bf16[8,24,1280]{2,1,0:T(8,128)(2,1)S(1)} %broadcast_multiply_fusion.1), channel_id=1, source_target_pairs={{2,6},{3,7},{10,14},{11,15},{18,22},{19,23},{26,30},{27,31}} | collective-permute-start | bytes 1474568 | tf_op jit(solution)/shard_map/ppermute | solution.py:1061
  510.9 61.7 %collective-permute-start.19 = (bf16[8,320,640]{2,1,0:T(8,128)(2,1)}, bf16[8,320,640]{2,1,0:T(8,128)(2,1)}, u32[]{:S(2)}, u32[]{:S(2)}) collective-permute-start(bf16[8,320,640]{2,1,0:T(8,128)(2,1)} %add_convert_fusion.2), channel_id=1, source_target_pairs={{0,1},{1,0},{2,3},{3,2},{4,5},{5,4},{6,7},{7,6},{8,24},{9,25},{10,... | collective-permute-start | bytes 9830408 | tf_op jit(solution)/shard_map/ppermute | solution.py:824
  534.6 71.2 %collective-permute-start.22 = (bf16[8,32,1280]{2,1,0:T(8,128)(2,1)}, bf16[8,32,1280]{2,1,0:T(8,128)(2,1)}, u32[]{:S(2)}, u32[]{:S(2)}) collective-permute-start(bf16[8,32,1280]{2,1,0:T(8,128)(2,1)} %constant_dynamic-slice_fusion.2), channel_id=1, source_target_pairs={{0,1},{1,0},{2,3},{3,2},{4,5},{5,4},{6,7},{7,6},{8,9},{9,8},{10,11... | collective-permute-start | bytes 1966088 | tf_op jit(solution)/shard_map/ppermute | solution.py:965
  538.8 67.0 %collective-permute-start.20 = (bf16[8,320,640]{2,1,0:T(8,128)(2,1)S(1)}, bf16[8,320,640]{2,1,0:T(8,128)(2,1)}, u32[]{:S(2)}, u32[]{:S(2)}) collective-permute-start(bf16[8,320,640]{2,1,0:T(8,128)(2,1)S(1)} %add_convert_fusion.1), channel_id=1, source_target_pairs={{0,1},{1,0},{2,3},{3,2},{4,5},{5,4},{6,7},{7,6},{8,24},{9,25},{10,... | collective-permute-start | bytes 9830408 | tf_op jit(solution)/shard_map/ppermute | solution.py:824
  572.7 33.2 %collective-permute-start.21 = (bf16[6,64,1280]{2,1,0:T(8,128)(2,1)S(1)}, bf16[6,64,1280]{2,1,0:T(8,128)(2,1)S(1)}, u32[]{:S(2)}, u32[]{:S(2)}) collective-permute-start(bf16[6,64,1280]{2,1,0:T(8,128)(2,1)S(1)} %bitcast.138), channel_id=1, source_target_pairs={{2,0},{4,2},{6,4},{3,1},{5,3},{7,5},{10,8},{12,10},{14,12},{11,9},... | collective-permute-start | bytes 2949128 | tf_op jit(solution)/shard_map/ppermute | solution.py:1060
  578.3 27.5 %collective-permute-start.25 = (bf16[8,24,1280]{2,1,0:T(8,128)(2,1)S(1)}, bf16[8,24,1280]{2,1,0:T(8,128)(2,1)}, u32[]{:S(2)}, u32[]{:S(2)}) collective-permute-start(bf16[8,24,1280]{2,1,0:T(8,128)(2,1)S(1)} %broadcast_multiply_fusion.1), channel_id=1, source_target_pairs={{4,6},{5,7},{12,14},{13,15},{20,22},{21,23},{28,30},{29,31}} | collective-permute-start | bytes 1474568 | tf_op jit(solution)/shard_map/ppermute | solution.py:1061
  606.6 35.1 %collective-permute-start.27 = (bf16[16,40,3200]{2,1,0:T(8,128)(2,1)}, bf16[16,40,3200]{2,1,0:T(8,128)(2,1)}, u32[]{:S(2)}, u32[]{:S(2)}) collective-permute-start(bf16[16,40,3200]{2,1,0:T(8,128)(2,1)} %get-tuple-element.226), channel_id=1, source_target_pairs={{0,8},{1,9},{2,10},{3,11},{4,12},{5,13},{6,14},{7,15},{8,0},{9,1},... | collective-permute-start | bytes 12288008 | tf_op jit(solution)/shard_map/ppermute | solution.py:824
  608.4 33.2 %collective-permute-start.26 = (bf16[4,320,640]{2,1,0:T(8,128)(2,1)}, bf16[4,320,640]{2,1,0:T(8,128)(2,1)}, u32[]{:S(2)}, u32[]{:S(2)}) collective-permute-start(bf16[4,320,640]{2,1,0:T(8,128)(2,1)} %add_convert_fusion.5), channel_id=1, source_target_pairs={{0,16},{1,17},{2,18},{3,19},{4,20},{5,21},{6,22},{7,23},{8,10},{9,... | collective-permute-start | bytes 4915208 | tf_op jit(solution)/shard_map/ppermute | solution.py:824
  616.7 61.4 %collective-permute-start.29 = (bf16[4,320,640]{2,1,0:T(8,128)(2,1)}, bf16[4,320,640]{2,1,0:T(8,128)(2,1)}, u32[]{:S(2)}, u32[]{:S(2)}) collective-permute-start(bf16[4,320,640]{2,1,0:T(8,128)(2,1)} %add_convert_fusion.4), channel_id=1, source_target_pairs={{0,16},{1,17},{2,18},{3,19},{4,20},{5,21},{6,22},{7,23},{8,10},{9,... | collective-permute-start | bytes 4915208 | tf_op jit(solution)/shard_map/ppermute | solution.py:824
  621.4 56.7 %collective-permute-start.31 = (bf16[8,32,1280]{2,1,0:T(8,128)(2,1)}, bf16[8,32,1280]{2,1,0:T(8,128)(2,1)}, u32[]{:S(2)}, u32[]{:S(2)}) collective-permute-start(bf16[8,32,1280]{2,1,0:T(8,128)(2,1)} %get-tuple-element.319), channel_id=1, source_target_pairs={{0,1},{1,0},{2,3},{3,2},{4,5},{5,4},{6,7},{7,6},{8,9},{9,8},{10,11... | collective-permute-start | bytes 1966088 | tf_op jit(solution)/shard_map/ppermute | solution.py:965
  645.6 32.5 %collective-permute-start.28 = (bf16[2,320,640]{2,1,0:T(8,128)(2,1)}, bf16[2,320,640]{2,1,0:T(8,128)(2,1)}, u32[]{:S(2)}, u32[]{:S(2)}) collective-permute-start(bf16[2,320,640]{2,1,0:T(8,128)(2,1)} %add_convert_fusion.9), channel_id=1, source_target_pairs={{0,2},{1,3},{2,0},{3,1},{4,6},{5,7},{6,4},{7,5},{8,9},{9,8},{10,11... | collective-permute-start | bytes 2457608 | tf_op jit(solution)/shard_map/ppermute | solution.py:824
  648.9 29.2 %collective-permute-start.30 = (bf16[8,40,3200]{2,1,0:T(8,128)(2,1)S(1)}, bf16[8,40,3200]{2,1,0:T(8,128)(2,1)S(1)}, u32[]{:S(2)}, u32[]{:S(2)}) collective-permute-start(bf16[8,40,3200]{2,1,0:T(8,128)(2,1)S(1)} %add_convert_fusion.3), channel_id=1, source_target_pairs={{0,1},{1,0},{2,3},{3,2},{4,5},{5,4},{6,7},{7,6},{8,24},{9,25},{10,... | collective-permute-start | bytes 6144008 | tf_op jit(solution)/shard_map/ppermute | solution.py:824
  681.4 55.7 %collective-permute-start.32 = (bf16[1,320,640]{2,1,0:T(8,128)(2,1)}, bf16[1,320,640]{2,1,0:T(8,128)(2,1)}, u32[]{:S(2)}, u32[]{:S(2)}) collective-permute-start(bf16[1,320,640]{2,1,0:T(8,128)(2,1)} %add_convert_fusion.13), channel_id=1, source_target_pairs={{0,4},{1,5},{2,6},{3,7},{4,0},{5,1},{6,2},{7,3},{8,12},{9,13},{10,... | collective-permute-start | bytes 1228808 | tf_op jit(solution)/shard_map/ppermute | solution.py:824
  686.9 50.2 %collective-permute-start.33 = (bf16[2,320,640]{2,1,0:T(8,128)(2,1)}, bf16[2,320,640]{2,1,0:T(8,128)(2,1)S(1)}, u32[]{:S(2)}, u32[]{:S(2)}) collective-permute-start(bf16[2,320,640]{2,1,0:T(8,128)(2,1)} %add_convert_fusion.8), channel_id=1, source_target_pairs={{0,2},{1,3},{2,0},{3,1},{4,6},{5,7},{6,4},{7,5},{8,9},{9,8},{10,11... | collective-permute-start | bytes 2457608 | tf_op jit(solution)/shard_map/ppermute | solution.py:824
  690.7 46.4 %collective-permute-start.34 = (bf16[4,40,3200]{2,1,0:T(8,128)(2,1)}, bf16[4,40,3200]{2,1,0:T(8,128)(2,1)}, u32[]{:S(2)}, u32[]{:S(2)}) collective-permute-start(bf16[4,40,3200]{2,1,0:T(8,128)(2,1)} %add_convert_fusion.7), channel_id=1, source_target_pairs={{0,16},{1,17},{2,18},{3,19},{4,20},{5,21},{6,22},{7,23},{8,10},{9,... | collective-permute-start | bytes 3072008 | tf_op jit(solution)/shard_map/ppermute | solution.py:824
  713.5 23.6 %collective-permute-start.35 = (bf16[16,40,1920]{2,1,0:T(8,128)(2,1)}, bf16[16,40,1920]{2,1,0:T(8,128)(2,1)}, u32[]{:S(2)}, u32[]{:S(2)}) collective-permute-start(bf16[16,40,1920]{2,1,0:T(8,128)(2,1)} %get-tuple-element.255), channel_id=1, source_target_pairs={{0,8},{1,9},{2,10},{3,11},{4,12},{5,13},{6,14},{7,15},{8,0},{9,1},... | collective-permute-start | bytes 7372808 | tf_op jit(solution)/shard_map/ppermute | solution.py:824
  739.8 25.3 %collective-permute-start.36 = (bf16[1,320,640]{2,1,0:T(8,128)(2,1)}, bf16[1,320,640]{2,1,0:T(8,128)(2,1)}, u32[]{:S(2)}, u32[]{:S(2)}) collective-permute-start(bf16[1,320,640]{2,1,0:T(8,128)(2,1)} %add_convert_fusion.12), channel_id=1, source_target_pairs={{0,4},{1,5},{2,6},{3,7},{4,0},{5,1},{6,2},{7,3},{8,12},{9,13},{10,... | collective-permute-start | bytes 1228808 | tf_op jit(solution)/shard_map/ppermute | solution.py:824
  742.2 22.9 %collective-permute-start.38 = (bf16[8,40,1920]{2,1,0:T(8,128)(2,1)S(1)}, bf16[8,40,1920]{2,1,0:T(8,128)(2,1)}, u32[]{:S(2)}, u32[]{:S(2)}) collective-permute-start(bf16[8,40,1920]{2,1,0:T(8,128)(2,1)S(1)} %add_convert_fusion.6), channel_id=1, source_target_pairs={{0,1},{1,0},{2,3},{3,2},{4,5},{5,4},{6,7},{7,6},{8,24},{9,25},{10,... | collective-permute-start | bytes 3686408 | tf_op jit(solution)/shard_map/ppermute | solution.py:824
  744.3 20.8 %collective-permute-start.37 = (bf16[2,40,3200]{2,1,0:T(8,128)(2,1)S(1)}, bf16[2,40,3200]{2,1,0:T(8,128)(2,1)}, u32[]{:S(2)}, u32[]{:S(2)}) collective-permute-start(bf16[2,40,3200]{2,1,0:T(8,128)(2,1)S(1)} %add_convert_fusion.11), channel_id=1, source_target_pairs={{0,2},{1,3},{2,0},{3,1},{4,6},{5,7},{6,4},{7,5},{8,9},{9,8},{10,11... | collective-permute-start | bytes 1536008 | tf_op jit(solution)/shard_map/ppermute | solution.py:824
  768.8 59.1 %collective-permute-start.42 = (bf16[8,24,1280]{2,1,0:T(8,128)(2,1)S(1)}, bf16[8,24,1280]{2,1,0:T(8,128)(2,1)}, u32[]{:S(2)}, u32[]{:S(2)}) collective-permute-start(bf16[8,24,1280]{2,1,0:T(8,128)(2,1)S(1)} %broadcast_multiply_fusion), channel_id=1, source_target_pairs={{4,6},{5,7},{12,14},{13,15},{20,22},{21,23},{28,30},{29,31}} | collective-permute-start | bytes 1474568 | tf_op jit(solution)/shard_map/ppermute | solution.py:1061
  770.4 57.5 %collective-permute-start.41 = (bf16[8,24,1280]{2,1,0:T(8,128)(2,1)S(1)}, bf16[8,24,1280]{2,1,0:T(8,128)(2,1)}, u32[]{:S(2)}, u32[]{:S(2)}) collective-permute-start(bf16[8,24,1280]{2,1,0:T(8,128)(2,1)S(1)} %broadcast_multiply_fusion), channel_id=1, source_target_pairs={{2,6},{3,7},{10,14},{11,15},{18,22},{19,23},{26,30},{27,31}} | collective-permute-start | bytes 1474568 | tf_op jit(solution)/shard_map/ppermute | solution.py:1061
  771.8 56.1 %collective-permute-start.40 = (bf16[8,24,1280]{2,1,0:T(8,128)(2,1)S(1)}, bf16[8,24,1280]{2,1,0:T(8,128)(2,1)}, u32[]{:S(2)}, u32[]{:S(2)}) collective-permute-start(bf16[8,24,1280]{2,1,0:T(8,128)(2,1)S(1)} %broadcast_multiply_fusion), channel_id=1, source_target_pairs={{0,6},{1,7},{8,14},{9,15},{16,22},{17,23},{24,30},{25,31}} | collective-permute-start | bytes 1474568 | tf_op jit(solution)/shard_map/ppermute | solution.py:1061
  776.7 51.3 %collective-permute-start.43 = (bf16[6,64,1280]{2,1,0:T(8,128)(2,1)}, bf16[6,64,1280]{2,1,0:T(8,128)(2,1)}, u32[]{:S(2)}, u32[]{:S(2)}) collective-permute-start(bf16[6,64,1280]{2,1,0:T(8,128)(2,1)} %bitcast.30), channel_id=1, source_target_pairs={{2,0},{4,2},{6,4},{3,1},{5,3},{7,5},{10,8},{12,10},{14,12},{11,9},... | collective-permute-start | bytes 2949128 | tf_op jit(solution)/shard_map/ppermute | solution.py:1060
  780.4 30.8 %collective-permute-start.51 = (bf16[4,40,1920]{2,1,0:T(8,128)(2,1)}, bf16[4,40,1920]{2,1,0:T(8,128)(2,1)}, u32[]{:S(2)}, u32[]{:S(2)}) collective-permute-start(bf16[4,40,1920]{2,1,0:T(8,128)(2,1)} %add_convert_fusion.10), channel_id=1, source_target_pairs={{0,16},{1,17},{2,18},{3,19},{4,20},{5,21},{6,22},{7,23},{8,10},{9,... | collective-permute-start | bytes 1843208 | tf_op jit(solution)/shard_map/ppermute | solution.py:824
  811.2 8.9 %collective-permute-start.50 = (bf16[1,40,3200]{2,1,0:T(8,128)(2,1)S(1)}, bf16[1,40,3200]{2,1,0:T(8,128)(2,1)S(1)}, u32[]{:S(2)}, u32[]{:S(2)}) collective-permute-start(bf16[1,40,3200]{2,1,0:T(8,128)(2,1)S(1)} %add_convert_fusion.15), channel_id=1, source_target_pairs={{0,4},{1,5},{2,6},{3,7},{4,0},{5,1},{6,2},{7,3},{8,12},{9,13},{10,... | collective-permute-start | bytes 768008 | tf_op jit(solution)/shard_map/ppermute | solution.py:824
  820.2 5.7 collective-permute-start.52
  827.9 13.1 %collective-permute-start.53 = (bf16[1,40,1920]{2,1,0:T(8,128)(2,1)}, bf16[1,40,1920]{2,1,0:T(8,128)(2,1)}, u32[]{:S(2)}, u32[]{:S(2)}) collective-permute-start(bf16[1,40,1920]{2,1,0:T(8,128)(2,1)} %add_convert_fusion.16), channel_id=1, source_target_pairs={{0,4},{1,5},{2,6},{3,7},{4,0},{5,1},{6,2},{7,3},{8,12},{9,13},{10,... | collective-permute-start | bytes 460808 | tf_op jit(solution)/shard_map/ppermute | solution.py:824
  835.9 30.5 %collective-permute-start.39 = (bf16[8,32,1280]{2,1,0:T(8,128)(2,1)}, bf16[8,32,1280]{2,1,0:T(8,128)(2,1)S(1)}, u32[]{:S(2)}, u32[]{:S(2)}) collective-permute-start(bf16[8,32,1280]{2,1,0:T(8,128)(2,1)} %get-tuple-element.325), channel_id=1, source_target_pairs={{0,1},{1,0},{2,3},{3,2},{4,5},{5,4},{6,7},{7,6},{8,9},{9,8},{10,11... | collective-permute-start | bytes 1966088 | tf_op jit(solution)/shard_map/ppermute | solution.py:965
  837.1 29.1 %collective-permute-start.44 = (bf16[8,32,1280]{2,1,0:T(8,128)(2,1)}, bf16[8,32,1280]{2,1,0:T(8,128)(2,1)S(1)}, u32[]{:S(2)}, u32[]{:S(2)}) collective-permute-start(bf16[8,32,1280]{2,1,0:T(8,128)(2,1)} %get-tuple-element.317), channel_id=1, source_target_pairs={{0,1},{1,0},{2,3},{3,2},{4,5},{5,4},{6,7},{7,6},{8,9},{9,8},{10,11... | collective-permute-start | bytes 1966088 | tf_op jit(solution)/shard_map/ppermute | solution.py:965
  847.5 4.8 collective-permute-start.48
  (69 other events, 1972.0 us)
Sparse Core Ops, SparseCore 0:
  13.0 113.0 all-gather.2
  129.6 210.8 all-gather.4

commit v3 on v2

--- a/solution.py
+++ b/solution.py
@@ -360,8 +360,8 @@
             in_specs=[
                 whole,
                 whole,
-                pl.BlockSpec((model, block), lambda p, i, *_: (0, (first + p) * steps + i)),
-                pl.BlockSpec((block, model), lambda p, i, *_: (i, PARTS + first + p)),
+                pl.BlockSpec((model, block), lambda p, i, *_: (0, p * steps + i)),
+                pl.BlockSpec((block, model), lambda p, i, *_: (i, count + p)),
                 pl.BlockSpec((1, block), lambda p, i, *_: (0, (first + p) * steps + i)),
                 piece,
                 pl.BlockSpec((8, LANES), lambda p, i, *_: (0, 0)) if begins else piece,
@@ -401,7 +401,7 @@
 def window_gradient_kernel(own, core_stride, table_ref, *refs):
     tokens_ref, grad_ref, *ready, sent_ref, kept_ref, sums_ref = refs
     devices = table_ref.shape[0] - 1
-    share = tokens_ref.shape[0] // devices
+    share = tokens_ref.shape[1] // devices
     step = pl.program_id(0)
 
     def place(value):
@@ -414,9 +414,11 @@
 
     @pl.when(step < own)
     def _():
-        grad = grad_ref[...]
-        place(dot_nt(tokens_ref[...], grad).astype(jnp.bfloat16))
-        sums_ref[...] = dot_nt(jnp.ones((8, grad.shape[1]), jnp.bfloat16), grad)
+        place(dot(grad_ref[...], tokens_ref[...]).astype(jnp.bfloat16).T)
+        total = 0
+        for low in range(0, grad_ref.shape[1], LANES):
+            total = total + grad_ref[:, low : low + LANES].astype(jnp.float32)
+        sums_ref[...] = total
 
     for ready_ref in ready:
 
@@ -425,8 +427,8 @@
             place(ready_ref[...])
 
 
-def window_gradient(turned, grad, ready, table):
-    model, tokens = turned.shape
+def window_gradient(rows, grad, ready, table):
+    tokens, model = rows.shape
     devices = table.shape[0] - 1
     wide = model // 2
     own = grad.shape[0] // wide
@@ -440,24 +442,24 @@
             num_scalar_prefetch=1,
             grid=(steps,),
             in_specs=[
-                pl.BlockSpec((model, tokens), lambda n, *_: (0, 0), pipeline_mode=pl.Buffered(1)),
+                pl.BlockSpec((tokens, model), lambda n, *_: (0, 0), pipeline_mode=pl.Buffered(1)),
                 pl.BlockSpec((wide, tokens), lambda n, *_: (jnp.minimum(n, own - 1), 0)),
             ]
             + [pl.BlockSpec((model, wide), lambda n, *_: (0, jnp.maximum(n - own, 0)))] * len(ready),
             out_specs=[
                 spec,
                 spec,
-                pl.BlockSpec((8, wide), lambda n, *_: (0, jnp.minimum(n, own - 1))),
+                pl.BlockSpec((wide, LANES), lambda n, *_: (jnp.minimum(n, own - 1), 0)),
             ],
         ),
-        out_shape=[shape, shape, jax.ShapeDtypeStruct((8, own * wide), jnp.float32)],
+        out_shape=[shape, shape, jax.ShapeDtypeStruct((own * wide, LANES), jnp.float32)],
         compiler_params=pltpu.CompilerParams(vmem_limit_bytes=56 * MIB),
         cost_estimate=pl.CostEstimate(
             flops=2 * tokens * model * own * wide,
             bytes_accessed=2 * (tokens * model + tokens * own * wide + model * steps * wide),
             transcendentals=0,
         ),
-    )(table, turned, grad, *ready)
+    )(table, rows, grad, *ready)
 
 
 def hidden_parts(unit):
@@ -527,7 +529,7 @@
         grid=(tokens // rows,),
         in_specs=[
             block,
-            pl.BlockSpec((model, model), lambda i: (0, 2 * PARTS)),
+            pl.BlockSpec((model, model), lambda i: (0, PARTS)),
             block,
             pl.BlockSpec((8, model), lambda i: (0, 0)),
         ],
@@ -545,24 +547,23 @@
 
 def middle_backward_kernel(
     grad_ref, middle_ref, cot_ref, attended_ref, proj_ref, vectors_ref,
-    grad_middle_ref, grad_attended_ref, dproj_ref, sums_ref, total_ref,
+    grad_middle_ref, grad_attended_ref, dproj_ref, sums_ref, branch_ref,
 ):
     step = pl.program_id(0)
 
     @pl.when(step == 0)
     def _():
         sums_ref[...] = jnp.zeros_like(sums_ref)
-        total_ref[...] = jnp.zeros_like(total_ref)
-
-    middle = middle_ref[...]
-    unit, inverse = normalised(middle)
+
+    rows = middle_ref.shape[0]
+    unit, inverse = normalised(middle_ref[...])
     grad = grad_ref[...]
     cot = cot_ref[...].astype(jnp.float32)
     grad_middle = cot + norm_backward(unit, inverse, vectors_ref[1:2], grad)
     branch = grad_middle.astype(jnp.bfloat16)
     grad_middle_ref[...] = grad_middle
+    branch_ref[pl.ds(pl.multiple_of(step * rows, rows), rows)] = branch
     grad_attended_ref[...] = dot_nt(branch, proj_ref[...]).astype(jnp.bfloat16)
-    total_ref[...] += dot_tn(attended_ref[...], branch)
     sums_ref[0:1] += column_sum(branch.astype(jnp.float32))
     sums_ref[1:2] += column_sum(grad * unit)
     sums_ref[2:3] += column_sum(grad)
@@ -570,7 +571,7 @@
 
     @pl.when(step == pl.num_programs(0) - 1)
     def _():
-        dproj_ref[...] = total_ref[...].astype(jnp.bfloat16)
+        dproj_ref[...] = dot_tn(attended_ref[...], branch_ref[...]).astype(jnp.bfloat16)
 
 
 def middle_backward(grad, middle, cot, attended, proj, vectors):
@@ -582,8 +583,9 @@
         middle_backward_kernel,
         grid=(tokens // rows,),
         in_specs=[
-            block, block, block, block,
-            pl.BlockSpec((model, model), lambda i: (0, 2 * PARTS)),
+            block, block, block,
+            pl.BlockSpec((tokens, model), lambda i: (0, 0), pipeline_mode=pl.Buffered(1)),
+            pl.BlockSpec((model, model), lambda i: (0, PARTS), pipeline_mode=pl.Buffered(1)),
             few,
         ],
         out_specs=[block, block, pl.BlockSpec((model, model), lambda i: (0, 0)), few],
@@ -593,7 +595,7 @@
             jax.ShapeDtypeStruct((model, model), jnp.bfloat16),
             jax.ShapeDtypeStruct((8, model), jnp.float32),
         ],
-        scratch_shapes=[pltpu.VMEM((model, model), jnp.float32)],
+        scratch_shapes=[pltpu.VMEM((tokens, model), jnp.bfloat16)],
         compiler_params=pltpu.CompilerParams(vmem_limit_bytes=56 * MIB),
         cost_estimate=pl.CostEstimate(
             flops=4 * tokens * model * model, bytes_accessed=24 * tokens * model, transcendentals=0
@@ -643,8 +645,7 @@
 
 
 def end_starts(width, count):
-    starts = [b * WIN // 8 * 8 for b in range(count - 1)]
-    return starts + [width - END]
+    return [b * WIN for b in range(count - 1)] + [width - END]
 
 
 def end_place(width):
@@ -924,7 +925,8 @@
 
 def all_sum(value):
     for bit in reversed(device_bits()):
-        value = value + flipped(value, bit)
+        (arrived,) = yield [value], [flipped(value, bit)]
+        value = value + arrived
     return value
 
 
@@ -1026,20 +1028,21 @@
         last, rest, halo = self.count - 1, self.rest, self.halo
         top = self.height - rest
         kept_low, sent_low, low = split_tiles(tiles[:, top:])
-        kept_up, sent_up, up = split_tiles(tiles[:, :top])
-        low, up = yield [sent_low, sent_up], [low, up]
+        (low,) = yield [sent_low], [low]
         lower = join_tiles(kept_low, low)
-        upper = join_tiles(kept_up, up)
+        kept_up, sent_up, up = split_tiles(after(tiles[:, :top], low))
         starts = end_starts(self.width, self.count)
         sent = [lower[rest - halo :]]
         arrived = [lax.ppermute(sent[0], "rows", [(i, i + 1) for i in range(last)])]
         for target in range(last):
-            sent.append(lower[:, starts[target] : starts[target] + END])
+            sent.append(lower[:, starts[target] : starts[target] + SIDE])
             arrived.append(lax.ppermute(sent[-1], "rows", [(last, target)]))
-        down, *arrived = yield sent, arrived
+        up, down, *arrived = yield sent + [sent_up], [up] + arrived
+        upper = join_tiles(kept_up, up)
         end = lower[:, starts[last] :]
         for target in range(last):
-            end = jnp.where(self.row == target, arrived[target], end)
+            piece = jnp.pad(arrived[target], ((0, 0), (0, END - SIDE), (0, 0)))
+            end = jnp.where(self.row == target, piece, end)
         held = jnp.sum(end_place(self.width), axis=1).astype(jnp.bfloat16)
         end = end * held[None, :, None]
         whole = jnp.concatenate([down, upper, lower], axis=0)
@@ -1058,13 +1061,15 @@
         held = jnp.sum(end_place(self.width), axis=1).astype(jnp.bfloat16)
         end = end * held[None, :, None]
         up = lax.ppermute(main[:halo], "rows", [(i + 1, i) for i in range(last)])
-        pieces = [lax.ppermute(end, "rows", [(source, last)]) for source in range(last)]
+        piece = end[:, :SIDE]
+        pieces = [lax.ppermute(piece, "rows", [(source, last)]) for source in range(last)]
         upper = lax.dynamic_slice_in_dim(main, self.step * self.row, top, 0)
         kept_up, sent_up, arrived_up = split_image(upper)
-        up, arrived_up, *pieces = yield [end, sent_up], [up, arrived_up] + pieces
+        up, arrived_up, *pieces = yield [piece, sent_up], [up, arrived_up] + pieces
         tail = 0
         for start, piece in zip(end_starts(self.width, self.count), pieces + [end]):
-            tail = tail + jnp.pad(piece, ((0, 0), (start, self.width - END - start), (0, 0)))
+            rest_wide = self.width - piece.shape[1] - start
+            tail = tail + jnp.pad(piece, ((0, 0), (start, rest_wide), (0, 0)))
         below = jnp.where(self.row == last, tail, pad_rows(up, 0, rest - halo))
         whole = jnp.concatenate([main, below], axis=0)
         place = self.step * self.row + top
@@ -1137,6 +1142,8 @@
 
     vectors = [ln1_gain, ln1_bias, qv_bias[:, 0], qv_bias[:, 1], proj_bias, ln2_gain, ln2_bias]
     vectors = small_gather(jnp.concatenate(vectors + [fc2_bias, fc1_bias])[None])
+    vectors = launch(sync(vectors, [rows]), [rows])
+    w_fc1 = after(w_fc1, rows.sent)
     vectors = vectors.astype(jnp.float32)
     gain1, shift1, query_shift, value_shift, proj_shift, gain2, shift2, down_shift = (
         vectors[:, n * share : (n + 1) * share].reshape(1, model) for n in range(8)
@@ -1151,22 +1158,23 @@
     qkv_full = gathered(jnp.concatenate(thirds, axis=1))
     up_shard = w_fc1.reshape(share, devices, PARTS, share).transpose(0, 2, 1, 3)
     down_shard = [w_fc2[n * share : (n + 1) * share] for n in range(PARTS)]
+    up_shard = up_shard.reshape(share, devices * unit)
+    cut = PARTS // 2
     joint = gathered(
-        jnp.concatenate([up_shard.reshape(share, devices * unit)] + down_shard + [w_proj], axis=1)
-    )
-
-    norm_vectors = sync(norm_vectors, [rows])
-    norm_vectors = launch(norm_vectors, [rows, cot])
+        jnp.concatenate([up_shard[:, : cut * model]] + down_shard[:cut] + [w_proj], axis=1)
+    )
+    joint2 = gathered(jnp.concatenate([up_shard[:, cut * model :]] + down_shard[cut:], axis=1))
+
     norm_vectors = sync(norm_vectors, [rows])
     rows = rows.finish()
     window_tokens = layout.to_windows(row_norm(rows, norm_vectors))
-    turned_tokens = window_tokens.T
     nothing = jnp.zeros((1, half), jnp.float32)
     shift_qkv = jnp.concatenate(
         [query_shift[:, :half], nothing, value_shift[:, :half]]
         + [query_shift[:, half:], nothing, value_shift[:, half:]],
         axis=1,
     )
+    window_tokens = launch(window_tokens, [cot])
     project = lax.dot_general(
         qkv_full, window_tokens, (((0,), (1,)), ((), ())), preferred_element_type=jnp.float32
     )
@@ -1177,9 +1185,7 @@
     ind = key_indicator()
     attended_windows, weights, inverse = attention_forward(project, tab, ind)
     attended = layout.to_rows(attended_windows)
-    attended, cot, turned_tokens, joint = sync(
-        (attended, cot.finish(), turned_tokens, joint), []
-    )
+    attended, cot, joint = sync((attended, cot.finish(), joint), [])
     middle, normed2 = middle_forward(attended, joint, rows, middle_vectors)
 
     mixed = middle
@@ -1193,7 +1199,7 @@
             return mlp(
                 normed2,
                 cot,
-                joint,
+                joint if first == 0 else joint2,
                 up_shift,
                 mixed,
                 grad_normed2,
@@ -1203,6 +1209,8 @@
                 table,
             )
 
+        if first:
+            mixed, joint2 = sync((mixed, joint2), [])
         mixed, grad_normed2, blocks, grad_shift = beside(sums, normed2, step)
         shifts.append(grad_shift.reshape(count, devices, share))
         if isinstance(blocks, list):
@@ -1234,7 +1242,7 @@
     grad_project, grad_tab = sync(attention_step(0), sums[:1])
     grad_project = launch(grad_project, sums[:1])
     sent, kept, sums0 = sync(
-        window_gradient(turned_tokens, grad_project, [grad_proj], table), sums[1:] + [output]
+        window_gradient(window_tokens, grad_project, [grad_proj], table), sums[1:] + [output]
     )
     sums.append(Flight(summed_columns(sent, kept, [3 * half, model])))
     grad_project = launch(grad_project, sums[1:] + [output])
@@ -1243,20 +1251,19 @@
     grad_windows = launch(grad_windows, sums[:1] + sums[-1:])
     grad_project, grad_part = sync(attention_step(1), sums + [output])
     grad_project = launch(grad_project, sums + [output])
-    sent, kept, sums1 = window_gradient(turned_tokens, grad_project, [], table)
+    sent, kept, sums1 = sync(
+        window_gradient(window_tokens, grad_project, [], table), sums + [output]
+    )
     sums.append(Flight(summed_columns(sent, kept, [3 * half])))
-    grad_project = launch(grad_project, sums[-1:])
-    second_rows = sync(project_step(grad_project, 1), sums)
-    second_rows = layout.to_rows(launch(second_rows, sums))
-    grad_tab = grad_tab + grad_part
-    grad_sums = [sums0[0], sums1[0]]
-    grad_rows, norm_sums = image_backward(
-        rows, first_rows, second_rows, grad_middle, norm_vectors
-    )
-    grad_rows, norm_sums = sync((grad_rows, norm_sums), sums)
+    grad_project = launch(grad_project, sums)
+    grad_tokens = sync(project_step(grad_project, 1), sums)
+    second_rows = layout.to_rows(launch(grad_tokens, sums))
+    grad_rows, norm_sums = sync(
+        image_backward(rows, first_rows, second_rows, grad_middle, norm_vectors), sums
+    )
     grad_in = Flight(layout.leave(grad_rows))
-    norm_sums = launch(norm_sums, sums + [grad_in])
-
+
+    grad_sums = [jnp.sum(piece, axis=1) for piece in (sums0, sums1)]
     up_shift_sums = jnp.concatenate(shifts, axis=0).transpose(1, 0, 2).reshape(devices, unit)
     small = jnp.concatenate(
         [
@@ -1269,39 +1276,54 @@
         + [up_shift_sums],
         axis=1,
     )
-    small, grad_tables = all_sum_pair(small, jnp.stack(narrow_tables(grad_tab)))
+    shape = small.shape
+    small = [small.reshape(-1)] + [
+        table.reshape(-1) for table in narrow_tables(grad_tab + grad_part)
+    ]
+    small = Flight(all_sum(jnp.concatenate(small)))
+    sums.append(small)
+
+    def formatted(ups, downs):
+        ups = [grad.reshape(share, -1, devices, share) for grad in ups]
+        ups = jnp.concatenate(ups, axis=1).transpose(0, 2, 1, 3)
+        return ups.reshape(share, devices * unit), jnp.concatenate(downs, axis=0)
+
+    launch(norm_sums, [grad_in] + sums)
+    done = output.finish()
+    done = sync(done, sums)
+    launch(done, sums)
+    grad_fc1, grad_fc2 = formatted(*zip(*[one.finish() for one in sums[:-3]]))
+    grad_fc1, grad_fc2 = sync((grad_fc1, grad_fc2), sums + [grad_in])
+    launch(grad_fc1, [grad_in] + sums)
+    first_qkv, sum_proj = sums[-3].finish()
+    first_qkv, sum_proj = sync((first_qkv, sum_proj), sums + [grad_in])
+    launch(first_qkv, [grad_in] + sums)
+    (last_qkv,) = sums[-2].finish()
+    small = small.finish()
+    tables = small[shape[0] * shape[1] :].reshape(2, REL, HD)
+    small = small[: shape[0] * shape[1]].reshape(shape)
     small = lax.dynamic_index_in_dim(small, me, 0, keepdims=False)
-
-    ups, downs = zip(*[one.finish() for one in sums[:-2]])
-    (first_qkv, sum_proj), (last_qkv,) = (one.finish() for one in sums[-2:])
-    grad_fc1 = jnp.concatenate([grad.reshape(share, -1, devices, share) for grad in ups], axis=1)
     thirds = [
         piece[:, n * half : (n + 1) * half] for n in range(3) for piece in (first_qkv, last_qkv)
     ]
     return (
-        output.finish(),
+        done,
         grad_in.finish().astype(jnp.float32),
         small[:share],
         small[share : 2 * share],
         jnp.concatenate(thirds, axis=1),
         jnp.stack([small[2 * share : 3 * share], small[3 * share : 4 * share]], axis=1),
-        grad_tables[0],
-        grad_tables[1],
+        tables[0],
+        tables[1],
         sum_proj,
         small[4 * share : 5 * share],
         small[5 * share : 6 * share],
         small[6 * share : 7 * share],
-        grad_fc1.transpose(0, 2, 1, 3).reshape(share, devices * unit),
+        grad_fc1,
         small[8 * share :],
-        jnp.concatenate(downs, axis=0),
+        grad_fc2,
         small[7 * share : 8 * share],
     )
-
-
-def all_sum_pair(first, second):
-    sizes = first.size
-    joined = all_sum(jnp.concatenate([first.reshape(-1), second.reshape(-1)]))
-    return joined[:sizes].reshape(first.shape), joined[sizes:].reshape(second.shape)
 
 
 def solution(mesh):

time: 888 us -> 793 us (0.89)
  waiting for transfers between devices: 192 us -> 94.8 us
  Pallas kernels: 353 us -> 340 us
    all_gather x2 -> x3, waiting for transfers between devices: 88.3 us -> 33.1 us  [gathered(): return lax.all_gather(shard, ALL, axis=0, tiled=True)]
    ppermute x6, waiting for transfers between devices: 42.5 us -> 0.02 us  [enter(): arrived.append(lax.ppermute(sent[-1], 'rows', [(last, target)]))]
    ppermute x20, waiting for transfers between devices: 17.3 us -> 4.64 us  [partner_permute(): return lax.ppermute(value, ALL, pairs)]
    pallas_call x2, Pallas kernels: 48.4 us -> 35.9 us  [window_gradient(): pl.pallas_call(functools.partial(window_gradient_kernel, own, core_stride...]
    unnamed x147 -> x127, local copies, waits for them, and re-layouts: 27 us -> 26 us
  transfers between devices with their start and end apart: 56 -> 57, of which waited for: 18 -> 12; matrix products, arithmetic and copies ran while one was open for 24% -> 27% of each run, Pallas kernels for 31% -> 43%
where the time goes in v3:
time: 793 us; the launch traced here: 783 us
  Pallas kernels  340 us (43%)
  local copies, waits for them, and re-layouts  100 us (13%)
  other arithmetic  95.8 us (12%)
  waiting for transfers between devices  94.8 us (12%)
  starting transfers between devices  81.2 us (10%)
  matrix products  55.1 us (7%)
  between operations  15.8 us (2%)
    pallas_call x2, Pallas kernels, mlp(): pl.pallas_call(functools.partial(mlp_kernel, tokens // 2, begins, ends, p...  142 us
    pallas_call x2, Pallas kernels, attention_backward(): pl.pallas_call(attention_backward_kernel, grid=(slots,), in_specs=[pl.Blo...  59.1 us
    pallas_call x1, Pallas kernels, attention_forward(): pl.pallas_call(attention_forward_kernel, grid=(slots,), in_specs=[pl.Bloc...  49.4 us
    convert_element_type x16, other arithmetic, summed(): sent = sent.astype(jnp.bfloat16)  46.6 us
    pallas_call x2, Pallas kernels, window_gradient(): pl.pallas_call(functools.partial(window_gradient_kernel, own, core_stride...  35.9 us
    all_gather x3, waiting for transfers between devices, gathered(): return lax.all_gather(shard, ALL, axis=0, tiled=True)  33.1 us
    dot_general x2, matrix products, project_step(): lax.dot_general(grad_project, qkv_full[:, half * 3 * model // 2:(half + 1...  28.3 us
    unnamed x127, local copies, waits for them, and re-layouts  26 us
  transfers between devices with their start and end apart: 57, of which 12 were waited for; matrix products, arithmetic and copies ran while one was open for 27% of the time, Pallas kernels for 43%

profile of v3, /device:TPU:1, one launch (start us, length us, event | category | flops | bytes accessed | tf_op | source)
XLA Modules:
  0.0 782.8 jit_solution(7023538537995483377)
XLA Ops:
  13.7 4.8 concatenate.145
  28.6 3.3 collective-permute-start.3
  37.2 17.2 %collective-permute-done.5 = bf16[8,32,1280]{2,1,0:T(8,128)(2,1)S(1)} collective-permute-done((bf16[8,32,1280]{2,1,0:T(8,128)(2,1)}, bf16[8,32,1280]{2,1,0:T(8,128)(2,1)S(1)}, u32[]{:S(2)}, u32[]{:S(2)}) %collective-permute-start.5) | collective-permute-done | bytes 655392 | tf_op jit(solution)/shard_map/ppermute | solution.py:951
  60.0 5.7 reshape.310
  67.3 3.3 reshape.311
  84.3 4.2 collective-permute-start.7
  106.7 12.1 %collective-permute-done.7 = bf16[6,64,1280]{2,1,0:T(8,128)(2,1)} collective-permute-done((bf16[6,64,1280]{2,1,0:T(8,128)(2,1)}, bf16[6,64,1280]{2,1,0:T(8,128)(2,1)}, u32[]{:S(2)}, u32[]{:S(2)}) %collective-permute-start.7) | collective-permute-done | bytes 983072 | tf_op jit(solution)/shard_map/ppermute | solution.py:1036
  124.8 4.9 shard_map.378.rows_ref
  136.3 25.7 %add_convert_fusion.project_ref = bf16[3840,1792]{1,0:T(8,128)(2,1)} fusion(bf16[1280,3840]{1,0:T(8,128)(2,1)} %all-gather.4.cloned.1.call-done, bf16[1792,1280]{1,0:T(8,128)(2,1)} %copy-done.9, f32[3840]{0:T(1024)S(1)} %reduce.4), kind=kOutput, calls=%fused_computation | convolution fusion | flops 17629839360 | bytes 28195840 | tf_op jit(solution)/shard_map/dot_general | solution.py:1178
  166.6 5.5 collective-permute-start.12
  173.8 49.4 %shard_map.380 = (bf16[1792,1280]{1,0:T(8,128)(2,1)S(1)}, bf16[7,16,224,256]{3,2,1,0:T(8,128)(2,1)}, f32[7,16,256]{2,1,0:T(8,128)S(1)}) custom-call(bf16[3840,1792]{1,0:T(8,128)(2,1)} %add_convert_fusion.project_ref, bf16[448,80]{1,0:T(8,128)(2,1)S(1)} %pad_maximum_fusion.6.tab_ref, bf16[48,256]{1,0:T(8,128)(2,1)S(1)} %fusion.27.ind_ref), custom_call_target="tpu_custom_call" | custom-call | flops 49000001536 | bytes 44040192 | tf_op jit(solution)/shard_map/pallas_call | solution.py:132
  228.9 14.3 %all-gather.6.cloned.1.call-done.proj_ref.refs_3_.refs_4_ = bf16[1280,6400]{1,0:T(8,128)(2,1)} async-done(((bf16[40,6400]{1,0:T(8,128)(2,1)}), bf16[1280,6400]{1,0:T(8,128)(2,1)}) %all-gather.6.cloned.1.call-update) | async-done | bytes 16384016 | tf_op jit(solution)/shard_map/all_gather | solution.py:1141
  245.0 7.8 shard_map.382
  257.3 70.4 %shard_map.383 = (f32[1088,1280]{1,0:T(8,128)}, f32[1088,1280]{1,0:T(8,128)}, bf16[16,320,640]{2,1,0:T(8,128)(2,1)}, bf16[16,320,640]{2,1,0:T(8,128)(2,1)}, f32[1,2560]{1,0:T(1,128)}) custom-call(s32[33]{0:T(128)} %pad_add_fusion.1.refs_0_.table_ref, bf16[1088,1280]{1,0:T(8,128)(2,1)} %copy-done.18, bf16[1088,1280]{1,0:T(8,128)(2,1)} %pad_maximum_fusion.1.refs_2_.cot_ref, ...), custom_call_target="tpu_custom_call" | custom-call | flops 57042534400 | bytes 59637760 | tf_op jit(solution)/shard_map/pallas_call | solution.py:355
  328.0 18.8 %all-gather.8.cloned.1.call-done.refs_3_.refs_4_ = bf16[1280,5120]{1,0:T(8,128)(2,1)} async-done(((bf16[40,5120]{1,0:T(8,128)(2,1)}), bf16[1280,5120]{1,0:T(8,128)(2,1)}) %all-gather.8.cloned.1.call-update) | async-done | bytes 13107216 | tf_op jit(solution)/shard_map/all_gather | solution.py:1141
  346.8 72.0 %shard_map.384 = (bf16[1088,1280]{1,0:T(8,128)(2,1)}, f32[1088,1280]{1,0:T(8,128)}, bf16[16,320,640]{2,1,0:T(8,128)(2,1)}, bf16[16,320,640]{2,1,0:T(8,128)(2,1)}, f32[1,2560]{1,0:T(1,128)}) custom-call(s32[33]{0:T(128)} %pad_add_fusion.1.refs_0_.table_ref, bf16[1088,1280]{1,0:T(8,128)(2,1)} %copy-done.18, ...), custom_call_target="tpu_custom_call" | custom-call | flops 57042534400 | bytes 59637760 | tf_op jit(solution)/shard_map/pallas_call | solution.py:355
  424.7 3.1 collective-permute-start.23
  428.6 4.4 add_convert_fusion.2
  434.2 20.3 %shard_map.385 = (f32[1088,1280]{1,0:T(8,128)}, bf16[1088,1280]{1,0:T(8,128)(2,1)}, bf16[1280,1280]{1,0:T(8,128)(2,1)}, f32[8,1280]{1,0:T(8,128)}) custom-call(f32[1088,1280]{1,0:T(8,128)} %get-tuple-element.242.grad_ref, f32[1088,1280]{1,0:T(8,128)} %copy-done.8, bf16[1088,1280]{1,0:T(8,128)(2,1)} %pad_maximum_fusion.1.refs_2_.cot_ref, ...), custom_call_target="tpu_custom_call" | custom-call | flops 7130316800 | bytes 33423360 | tf_op jit(solution)/shard_map/pallas_call | solution.py:582
  455.7 3.9 add_convert_fusion.1
  463.2 30.3 %shard_map.387 = (bf16[1920,1792]{1,0:T(8,128)(2,1)}, f32[448,80]{1,0:T(8,128)S(1)}) custom-call(bf16[3840,1792]{1,0:T(8,128)(2,1)} %add_convert_fusion.project_ref, bf16[7,16,224,256]{3,2,1,0:T(8,128)(2,1)} %get-tuple-element.236.weights_ref, f32[7,16,256]{2,1,0:T(8,128)S(1)} %get-tuple-element.237.inverse_ref, bf16[1792,1280]{1,0:T(8,128)(2,1)S(1)} %shard_map.386.grad_ref, ...), custom_call_target="tpu_custom_call" | custom-call | flops 28000000000 | bytes 29360128 | tf_op jit(solution)/shard_map/pallas_call | solution.py:210
  494.9 4.2 add_convert_fusion.5
  499.9 19.8 %shard_map.388 = (bf16[16,40,3200]{2,1,0:T(8,128)(2,1)}, bf16[16,40,3200]{2,1,0:T(8,128)(2,1)}, f32[1920,128]{1,0:T(8,128)}) custom-call(s32[33]{0:T(128)} %pad_add_fusion.1.refs_0_.table_ref, bf16[1792,1280]{1,0:T(8,128)(2,1)} %copy-done.9, bf16[1920,1792]{1,0:T(8,128)(2,1)} %get-tuple-element.272.refs_1_, bf16[1280,1280]{1,0:T(8,128)(2,1)} %get-tuple-element.259.refs_2_), custom_call_target="tpu_custom_call" | custom-call | flops 8808038400 | bytes 19660800 | tf_op jit(solution)/shard_map/pallas_call | solution.py:439
  527.8 4.3 add_convert_fusion.4
  533.7 2.6 fusion.11
  538.3 13.4 %convolution_convert_fusion.1.windows_ref = bf16[1792,1280]{1,0:T(8,128)(2,1)S(1)} fusion(bf16[1920,1792]{1,0:T(8,128)(2,1)} %get-tuple-element.272.refs_1_, bf16[1280,3840]{1,0:T(8,128)(2,1)} %all-gather.4.cloned.1.call-done), kind=kOutput, calls=%fused_computation.2 | convolution fusion | flops 8810332160 | bytes 16384000 | tf_op jit(solution)/shard_map/dot_general | solution.py:1234
  553.9 2.6 maximum_select_fusion.4
  556.5 4.0 add_convert_fusion.9
  564.2 28.8 %shard_map.390 = (bf16[1920,1792]{1,0:T(8,128)(2,1)}, f32[448,80]{1,0:T(8,128)S(1)}) custom-call(bf16[3840,1792]{1,0:T(8,128)(2,1)} %add_convert_fusion.project_ref, bf16[7,16,224,256]{3,2,1,0:T(8,128)(2,1)} %get-tuple-element.236.weights_ref, f32[7,16,256]{2,1,0:T(8,128)S(1)} %get-tuple-element.237.inverse_ref, bf16[1792,1280]{1,0:T(8,128)(2,1)S(1)} %bitcast.112, ...), custom_call_target="tpu_custom_call" | custom-call | flops 28000000000 | bytes 29360128 | tf_op jit(solution)/shard_map/pallas_call | solution.py:210
  593.1 3.2 add_convert_fusion.13
  597.9 3.2 add_convert_fusion.8
  602.3 2.6 add_convert_fusion.7
  606.0 16.0 %shard_map.391 = (bf16[16,40,1920]{2,1,0:T(8,128)(2,1)}, bf16[16,40,1920]{2,1,0:T(8,128)(2,1)}, f32[1920,128]{1,0:T(8,128)}) custom-call(s32[33]{0:T(128)} %pad_add_fusion.1.refs_0_.table_ref, bf16[1792,1280]{1,0:T(8,128)(2,1)} %copy-done.9, bf16[1920,1792]{1,0:T(8,128)(2,1)} %get-tuple-element.313.refs_1_), custom_call_target="tpu_custom_call" | custom-call | flops 8808038400 | bytes 16384000 | tf_op jit(solution)/shard_map/pallas_call | solution.py:439
  622.4 2.7 maximum_select_fusion.5
  626.8 3.0 pad_maximum_fusion.2
  629.8 4.6 collective-permute-done.34
  634.4 2.6 add_convert_fusion.12
  642.1 14.9 %convolution_convert_fusion.windows_ref = bf16[1792,1280]{1,0:T(8,128)(2,1)} fusion(bf16[1920,1792]{1,0:T(8,128)(2,1)} %get-tuple-element.313.refs_1_, bf16[1280,3840]{1,0:T(8,128)(2,1)} %all-gather.4.cloned.1.call-done), kind=kOutput, calls=%fused_computation.1 | convolution fusion | flops 8810332160 | bytes 16384000 | tf_op jit(solution)/shard_map/dot_general | solution.py:1234
  660.1 3.0 add_convert_fusion.6
  676.5 4.2 reshape.327
  687.8 9.4 %shard_map.393 = (bf16[1088,1280]{1,0:T(8,128)(2,1)}, f32[8,1280]{1,0:T(8,128)}) custom-call(bf16[1088,1280]{1,0:T(8,128)(2,1)} %pad_maximum_fusion.rows_ref.image_ref, bf16[1088,1280]{1,0:T(8,128)(2,1)} %copy-done.5, bf16[1088,1280]{1,0:T(8,128)(2,1)} %copy-done.6, f32[1088,1280]{1,0:T(8,128)} %get-tuple-element.324.grad_middle_ref, ...), custom_call_target="tpu_custom_call" | custom-call | flops 16711680 | bytes 13926400 | tf_op jit(solution)/shard_map/pallas_call | solution.py:625
  704.2 3.8 collective-permute-start.46
  726.9 5.3 collective-permute-done.45
  732.3 9.5 %collective-permute-done.43 = f32[19680]{0:T(1024)S(1)} collective-permute-done((f32[19680]{0:T(1024)S(1)}, f32[19680]{0:T(1024)S(1)}, u32[]{:S(2)}, u32[]{:S(2)}) %collective-permute-start.43) | collective-permute-done | bytes 78752 | tf_op jit(solution)/shard_map/ppermute | solution.py:725
  751.1 5.4 collective-permute-done.50
  756.5 7.6 collective-permute-start.52
  765.6 2.7 maximum_convert_fusion
  769.0 3.5 collective-permute-done.53
  (403 shorter events, 198.6 us)
Async XLA Ops:
  7.2 129.1 %all-gather.4.cloned.1.call-start = ((), (), s32[]{:S(2)}) async-start(), calls=%async_computation | async-start | bytes 10137600 | tf_op jit(solution)/shard_map/all_gather | solution.py:1141
  12.9 230.3 %all-gather.6.cloned.1.call-start = ((), (), s32[]{:S(2)}) async-start(), calls=%async_computation.1 | async-start | bytes 16896000 | tf_op jit(solution)/shard_map/all_gather | solution.py:1141
  32.9 21.6 %collective-permute-start.5 = (bf16[8,32,1280]{2,1,0:T(8,128)(2,1)}, bf16[8,32,1280]{2,1,0:T(8,128)(2,1)S(1)}, u32[]{:S(2)}, u32[]{:S(2)}) collective-permute-start(bf16[8,32,1280]{2,1,0:T(8,128)(2,1)} %get-tuple-element.417), channel_id=1, source_target_pairs={{0,1},{1,0},{2,3},{3,2},{4,5},{5,4},{6,7},{7,6},{8,9},{9,8},{10,11... | collective-permute-start | bytes 1966088 | tf_op jit(solution)/shard_map/ppermute | solution.py:951
  73.4 273.3 %all-gather.8.cloned.1.call-start = ((), (), s32[]{:S(2)}) async-start(), calls=%async_computation.2 | async-start | bytes 13516800 | tf_op jit(solution)/shard_map/all_gather | solution.py:1141
  82.0 24.7 %collective-permute-start.6 = (bf16[8,32,1280]{2,1,0:T(8,128)(2,1)}, bf16[8,32,1280]{2,1,0:T(8,128)(2,1)}, u32[]{:S(2)}, u32[]{:S(2)}) collective-permute-start(bf16[8,32,1280]{2,1,0:T(8,128)(2,1)} %get-tuple-element.412), channel_id=1, source_target_pairs={{0,1},{1,0},{2,3},{3,2},{4,5},{5,4},{6,7},{7,6},{8,9},{9,8},{10,11... | collective-permute-start | bytes 1966088 | tf_op jit(solution)/shard_map/ppermute | solution.py:951
  84.3 34.5 %collective-permute-start.7 = (bf16[6,64,1280]{2,1,0:T(8,128)(2,1)}, bf16[6,64,1280]{2,1,0:T(8,128)(2,1)}, u32[]{:S(2)}, u32[]{:S(2)}) collective-permute-start(bf16[6,64,1280]{2,1,0:T(8,128)(2,1)} %slice.762), channel_id=1, source_target_pairs={{0,2},{2,4},{4,6},{1,3},{3,5},{5,7},{8,10},{10,12},{12,14},{9,11},... | collective-permute-start | bytes 2949128 | tf_op jit(solution)/shard_map/ppermute | solution.py:1036
  88.5 18.0 %collective-permute-start.8 = (bf16[8,16,1280]{2,1,0:T(8,128)(2,1)}, bf16[8,16,1280]{2,1,0:T(8,128)(2,1)}, u32[]{:S(2)}, u32[]{:S(2)}) collective-permute-start(bf16[8,16,1280]{2,1,0:T(8,128)(2,1)} %get-tuple-element.415), channel_id=1, source_target_pairs={{6,0},{7,1},{14,8},{15,9},{22,16},{23,17},{30,24},{31,25}} | collective-permute-start | bytes 983048 | tf_op jit(solution)/shard_map/ppermute | solution.py:1039
  89.8 16.8 %collective-permute-start.9 = (bf16[8,16,1280]{2,1,0:T(8,128)(2,1)}, bf16[8,16,1280]{2,1,0:T(8,128)(2,1)}, u32[]{:S(2)}, u32[]{:S(2)}) collective-permute-start(bf16[8,16,1280]{2,1,0:T(8,128)(2,1)} %get-tuple-element.414), channel_id=1, source_target_pairs={{6,2},{7,3},{14,10},{15,11},{22,18},{23,19},{30,26},{31,27}} | collective-permute-start | bytes 983048 | tf_op jit(solution)/shard_map/ppermute | solution.py:1039
  91.2 15.5 %collective-permute-start.10 = (bf16[8,16,1280]{2,1,0:T(8,128)(2,1)}, bf16[8,16,1280]{2,1,0:T(8,128)(2,1)}, u32[]{:S(2)}, u32[]{:S(2)}) collective-permute-start(bf16[8,16,1280]{2,1,0:T(8,128)(2,1)} %get-tuple-element.413), channel_id=1, source_target_pairs={{6,4},{7,5},{14,12},{15,13},{22,20},{23,21},{30,28},{31,29}} | collective-permute-start | bytes 983048 | tf_op jit(solution)/shard_map/ppermute | solution.py:1039
  106.6 55.4 %collective-permute-start.11 = (bf16[8,32,1280]{2,1,0:T(8,128)(2,1)}, bf16[8,32,1280]{2,1,0:T(8,128)(2,1)}, u32[]{:S(2)}, u32[]{:S(2)}) collective-permute-start(bf16[8,32,1280]{2,1,0:T(8,128)(2,1)} %get-tuple-element.410), channel_id=1, source_target_pairs={{0,1},{1,0},{2,3},{3,2},{4,5},{5,4},{6,7},{7,6},{8,9},{9,8},{10,11... | collective-permute-start | bytes 1966088 | tf_op jit(solution)/shard_map/ppermute | solution.py:951
  163.9 61.2 %collective-permute-start.16 = (bf16[8,16,1280]{2,1,0:T(8,128)(2,1)S(1)}, bf16[8,16,1280]{2,1,0:T(8,128)(2,1)S(1)}, u32[]{:S(2)}, u32[]{:S(2)}) collective-permute-start(bf16[8,16,1280]{2,1,0:T(8,128)(2,1)S(1)} %get-tuple-element.408), channel_id=1, source_target_pairs={{6,0},{7,1},{14,8},{15,9},{22,16},{23,17},{30,24},{31,25}} | collective-permute-start | bytes 983048 | tf_op jit(solution)/shard_map/ppermute | solution.py:1039
  165.2 59.9 %collective-permute-start.15 = (bf16[8,16,1280]{2,1,0:T(8,128)(2,1)S(1)}, bf16[8,16,1280]{2,1,0:T(8,128)(2,1)S(1)}, u32[]{:S(2)}, u32[]{:S(2)}) collective-permute-start(bf16[8,16,1280]{2,1,0:T(8,128)(2,1)S(1)} %get-tuple-element.407), channel_id=1, source_target_pairs={{6,2},{7,3},{14,10},{15,11},{22,18},{23,19},{30,26},{31,27}} | collective-permute-start | bytes 983048 | tf_op jit(solution)/shard_map/ppermute | solution.py:1039
  165.9 59.3 %collective-permute-start.14 = (bf16[8,16,1280]{2,1,0:T(8,128)(2,1)S(1)}, bf16[8,16,1280]{2,1,0:T(8,128)(2,1)S(1)}, u32[]{:S(2)}, u32[]{:S(2)}) collective-permute-start(bf16[8,16,1280]{2,1,0:T(8,128)(2,1)S(1)} %get-tuple-element.406), channel_id=1, source_target_pairs={{6,4},{7,5},{14,12},{15,13},{22,20},{23,21},{30,28},{31,29}} | collective-permute-start | bytes 983048 | tf_op jit(solution)/shard_map/ppermute | solution.py:1039
  166.6 59.4 %collective-permute-start.12 = (bf16[6,64,1280]{2,1,0:T(8,128)(2,1)S(1)}, bf16[6,64,1280]{2,1,0:T(8,128)(2,1)S(1)}, u32[]{:S(2)}, u32[]{:S(2)}) collective-permute-start(bf16[6,64,1280]{2,1,0:T(8,128)(2,1)S(1)} %slice.775), channel_id=1, source_target_pairs={{0,2},{2,4},{4,6},{1,3},{3,5},{5,7},{8,10},{10,12},{12,14},{9,11},... | collective-permute-start | bytes 2949128 | tf_op jit(solution)/shard_map/ppermute | solution.py:1036
  172.2 53.3 %collective-permute-start.13 = (bf16[8,32,1280]{2,1,0:T(8,128)(2,1)S(1)}, bf16[8,32,1280]{2,1,0:T(8,128)(2,1)S(1)}, u32[]{:S(2)}, u32[]{:S(2)}) collective-permute-start(bf16[8,32,1280]{2,1,0:T(8,128)(2,1)S(1)} %get-tuple-element.405), channel_id=1, source_target_pairs={{0,1},{1,0},{2,3},{3,2},{4,5},{5,4},{6,7},{7,6},{8,9},{9,8},{10,11... | collective-permute-start | bytes 1966088 | tf_op jit(solution)/shard_map/ppermute | solution.py:951
  327.7 91.1 %collective-permute-start.17 = (bf16[16,320,640]{2,1,0:T(8,128)(2,1)}, bf16[16,320,640]{2,1,0:T(8,128)(2,1)}, u32[]{:S(2)}, u32[]{:S(2)}) collective-permute-start(bf16[16,320,640]{2,1,0:T(8,128)(2,1)} %get-tuple-element.223), channel_id=1, source_target_pairs={{0,8},{1,9},{2,10},{3,11},{4,12},{5,13},{6,14},{7,15},{8,0},{9,1},... | collective-permute-start | bytes 19660808 | tf_op jit(solution)/shard_map/ppermute | solution.py:825
  418.8 36.9 %collective-permute-start.18 = (bf16[16,320,640]{2,1,0:T(8,128)(2,1)}, bf16[16,320,640]{2,1,0:T(8,128)(2,1)}, u32[]{:S(2)}, u32[]{:S(2)}) collective-permute-start(bf16[16,320,640]{2,1,0:T(8,128)(2,1)} %get-tuple-element.241), channel_id=1, source_target_pairs={{0,8},{1,9},{2,10},{3,11},{4,12},{5,13},{6,14},{7,15},{8,0},{9,1},... | collective-permute-start | bytes 19660808 | tf_op jit(solution)/shard_map/ppermute | solution.py:825
  424.7 74.4 %collective-permute-start.23 = (bf16[8,16,1280]{2,1,0:T(8,128)(2,1)S(1)}, bf16[8,16,1280]{2,1,0:T(8,128)(2,1)S(1)}, u32[]{:S(2)}, u32[]{:S(2)}) collective-permute-start(bf16[8,16,1280]{2,1,0:T(8,128)(2,1)S(1)} %slice.787), channel_id=1, source_target_pairs={{0,6},{1,7},{8,14},{9,15},{16,22},{17,23},{24,30},{25,31}} | collective-permute-start | bytes 983048 | tf_op jit(solution)/shard_map/ppermute | solution.py:1065
  427.9 91.9 %collective-permute-start.24 = (bf16[8,16,1280]{2,1,0:T(8,128)(2,1)S(1)}, bf16[8,16,1280]{2,1,0:T(8,128)(2,1)S(1)}, u32[]{:S(2)}, u32[]{:S(2)}) collective-permute-start(bf16[8,16,1280]{2,1,0:T(8,128)(2,1)S(1)} %slice.787), channel_id=1, source_target_pairs={{2,6},{3,7},{10,14},{11,15},{18,22},{19,23},{26,30},{27,31}} | collective-permute-start | bytes 983048 | tf_op jit(solution)/shard_map/ppermute | solution.py:1065
  433.0 60.6 %collective-permute-start.19 = (bf16[8,320,640]{2,1,0:T(8,128)(2,1)}, bf16[8,320,640]{2,1,0:T(8,128)(2,1)}, u32[]{:S(2)}, u32[]{:S(2)}) collective-permute-start(bf16[8,320,640]{2,1,0:T(8,128)(2,1)} %add_convert_fusion.2), channel_id=1, source_target_pairs={{0,1},{1,0},{2,3},{3,2},{4,5},{5,4},{6,7},{7,6},{8,24},{9,25},{10,... | collective-permute-start | bytes 9830408 | tf_op jit(solution)/shard_map/ppermute | solution.py:825
  455.5 64.3 %collective-permute-start.22 = (bf16[8,32,1280]{2,1,0:T(8,128)(2,1)}, bf16[8,32,1280]{2,1,0:T(8,128)(2,1)}, u32[]{:S(2)}, u32[]{:S(2)}) collective-permute-start(bf16[8,32,1280]{2,1,0:T(8,128)(2,1)} %constant_dynamic-slice_fusion.2), channel_id=1, source_target_pairs={{0,1},{1,0},{2,3},{3,2},{4,5},{5,4},{6,7},{7,6},{8,9},{9,8},{10,11... | collective-permute-start | bytes 1966088 | tf_op jit(solution)/shard_map/ppermute | solution.py:967
  459.6 60.2 %collective-permute-start.20 = (bf16[8,320,640]{2,1,0:T(8,128)(2,1)S(1)}, bf16[8,320,640]{2,1,0:T(8,128)(2,1)}, u32[]{:S(2)}, u32[]{:S(2)}) collective-permute-start(bf16[8,320,640]{2,1,0:T(8,128)(2,1)S(1)} %add_convert_fusion.1), channel_id=1, source_target_pairs={{0,1},{1,0},{2,3},{3,2},{4,5},{5,4},{6,7},{7,6},{8,24},{9,25},{10,... | collective-permute-start | bytes 9830408 | tf_op jit(solution)/shard_map/ppermute | solution.py:825
  493.6 26.2 %collective-permute-start.21 = (bf16[6,64,1280]{2,1,0:T(8,128)(2,1)S(1)}, bf16[6,64,1280]{2,1,0:T(8,128)(2,1)S(1)}, u32[]{:S(2)}, u32[]{:S(2)}) collective-permute-start(bf16[6,64,1280]{2,1,0:T(8,128)(2,1)S(1)} %bitcast.133), channel_id=1, source_target_pairs={{2,0},{4,2},{6,4},{3,1},{5,3},{7,5},{10,8},{12,10},{14,12},{11,9},... | collective-permute-start | bytes 2949128 | tf_op jit(solution)/shard_map/ppermute | solution.py:1063
  499.1 20.7 %collective-permute-start.25 = (bf16[8,16,1280]{2,1,0:T(8,128)(2,1)S(1)}, bf16[8,16,1280]{2,1,0:T(8,128)(2,1)S(1)}, u32[]{:S(2)}, u32[]{:S(2)}) collective-permute-start(bf16[8,16,1280]{2,1,0:T(8,128)(2,1)S(1)} %slice.787), channel_id=1, source_target_pairs={{4,6},{5,7},{12,14},{13,15},{20,22},{21,23},{28,30},{29,31}} | collective-permute-start | bytes 983048 | tf_op jit(solution)/shard_map/ppermute | solution.py:1065
  520.8 35.7 %collective-permute-start.27 = (bf16[16,40,3200]{2,1,0:T(8,128)(2,1)}, bf16[16,40,3200]{2,1,0:T(8,128)(2,1)}, u32[]{:S(2)}, u32[]{:S(2)}) collective-permute-start(bf16[16,40,3200]{2,1,0:T(8,128)(2,1)} %get-tuple-element.271), channel_id=1, source_target_pairs={{0,8},{1,9},{2,10},{3,11},{4,12},{5,13},{6,14},{7,15},{8,0},{9,1},... | collective-permute-start | bytes 12288008 | tf_op jit(solution)/shard_map/ppermute | solution.py:825
  523.2 33.3 %collective-permute-start.26 = (bf16[4,320,640]{2,1,0:T(8,128)(2,1)}, bf16[4,320,640]{2,1,0:T(8,128)(2,1)}, u32[]{:S(2)}, u32[]{:S(2)}) collective-permute-start(bf16[4,320,640]{2,1,0:T(8,128)(2,1)} %add_convert_fusion.5), channel_id=1, source_target_pairs={{0,16},{1,17},{2,18},{3,19},{4,20},{5,21},{6,22},{7,23},{8,10},{9,... | collective-permute-start | bytes 4915208 | tf_op jit(solution)/shard_map/ppermute | solution.py:825
  532.1 61.0 %collective-permute-start.29 = (bf16[4,320,640]{2,1,0:T(8,128)(2,1)}, bf16[4,320,640]{2,1,0:T(8,128)(2,1)}, u32[]{:S(2)}, u32[]{:S(2)}) collective-permute-start(bf16[4,320,640]{2,1,0:T(8,128)(2,1)} %add_convert_fusion.4), channel_id=1, source_target_pairs={{0,16},{1,17},{2,18},{3,19},{4,20},{5,21},{6,22},{7,23},{8,10},{9,... | collective-permute-start | bytes 4915208 | tf_op jit(solution)/shard_map/ppermute | solution.py:825
  536.3 56.7 %collective-permute-start.31 = (bf16[8,32,1280]{2,1,0:T(8,128)(2,1)}, bf16[8,32,1280]{2,1,0:T(8,128)(2,1)}, u32[]{:S(2)}, u32[]{:S(2)}) collective-permute-start(bf16[8,32,1280]{2,1,0:T(8,128)(2,1)} %get-tuple-element.397), channel_id=1, source_target_pairs={{0,1},{1,0},{2,3},{3,2},{4,5},{5,4},{6,7},{7,6},{8,9},{9,8},{10,11... | collective-permute-start | bytes 1966088 | tf_op jit(solution)/shard_map/ppermute | solution.py:967
  560.5 32.6 %collective-permute-start.28 = (bf16[2,320,640]{2,1,0:T(8,128)(2,1)}, bf16[2,320,640]{2,1,0:T(8,128)(2,1)}, u32[]{:S(2)}, u32[]{:S(2)}) collective-permute-start(bf16[2,320,640]{2,1,0:T(8,128)(2,1)} %add_convert_fusion.9), channel_id=1, source_target_pairs={{0,2},{1,3},{2,0},{3,1},{4,6},{5,7},{6,4},{7,5},{8,9},{9,8},{10,11... | collective-permute-start | bytes 2457608 | tf_op jit(solution)/shard_map/ppermute | solution.py:825
  563.8 29.3 %collective-permute-start.30 = (bf16[8,40,3200]{2,1,0:T(8,128)(2,1)S(1)}, bf16[8,40,3200]{2,1,0:T(8,128)(2,1)S(1)}, u32[]{:S(2)}, u32[]{:S(2)}) collective-permute-start(bf16[8,40,3200]{2,1,0:T(8,128)(2,1)S(1)} %add_convert_fusion.3), channel_id=1, source_target_pairs={{0,1},{1,0},{2,3},{3,2},{4,5},{5,4},{6,7},{7,6},{8,24},{9,25},{10,... | collective-permute-start | bytes 6144008 | tf_op jit(solution)/shard_map/ppermute | solution.py:825
  596.3 33.5 %collective-permute-start.32 = (bf16[1,320,640]{2,1,0:T(8,128)(2,1)}, bf16[1,320,640]{2,1,0:T(8,128)(2,1)S(1)}, u32[]{:S(2)}, u32[]{:S(2)}) collective-permute-start(bf16[1,320,640]{2,1,0:T(8,128)(2,1)} %add_convert_fusion.13), channel_id=1, source_target_pairs={{0,4},{1,5},{2,6},{3,7},{4,0},{5,1},{6,2},{7,3},{8,12},{9,13},{10,... | collective-permute-start | bytes 1228808 | tf_op jit(solution)/shard_map/ppermute | solution.py:825
  601.1 28.7 %collective-permute-start.33 = (bf16[2,320,640]{2,1,0:T(8,128)(2,1)}, bf16[2,320,640]{2,1,0:T(8,128)(2,1)}, u32[]{:S(2)}, u32[]{:S(2)}) collective-permute-start(bf16[2,320,640]{2,1,0:T(8,128)(2,1)} %add_convert_fusion.8), channel_id=1, source_target_pairs={{0,2},{1,3},{2,0},{3,1},{4,6},{5,7},{6,4},{7,5},{8,9},{9,8},{10,11... | collective-permute-start | bytes 2457608 | tf_op jit(solution)/shard_map/ppermute | solution.py:825
  604.9 29.5 %collective-permute-start.34 = (bf16[4,40,3200]{2,1,0:T(8,128)(2,1)}, bf16[4,40,3200]{2,1,0:T(8,128)(2,1)}, u32[]{:S(2)}, u32[]{:S(2)}) collective-permute-start(bf16[4,40,3200]{2,1,0:T(8,128)(2,1)} %add_convert_fusion.7), channel_id=1, source_target_pairs={{0,16},{1,17},{2,18},{3,19},{4,20},{5,21},{6,22},{7,23},{8,10},{9,... | collective-permute-start | bytes 3072008 | tf_op jit(solution)/shard_map/ppermute | solution.py:825
  637.0 23.1 %collective-permute-start.35 = (bf16[1,320,640]{2,1,0:T(8,128)(2,1)}, bf16[1,320,640]{2,1,0:T(8,128)(2,1)}, u32[]{:S(2)}, u32[]{:S(2)}) collective-permute-start(bf16[1,320,640]{2,1,0:T(8,128)(2,1)} %add_convert_fusion.12), channel_id=1, source_target_pairs={{0,4},{1,5},{2,6},{3,7},{4,0},{5,1},{6,2},{7,3},{8,12},{9,13},{10,... | collective-permute-start | bytes 1228808 | tf_op jit(solution)/shard_map/ppermute | solution.py:825
  638.7 21.3 %collective-permute-start.36 = (bf16[2,40,3200]{2,1,0:T(8,128)(2,1)S(1)}, bf16[2,40,3200]{2,1,0:T(8,128)(2,1)}, u32[]{:S(2)}, u32[]{:S(2)}) collective-permute-start(bf16[2,40,3200]{2,1,0:T(8,128)(2,1)S(1)} %add_convert_fusion.11), channel_id=1, source_target_pairs={{0,2},{1,3},{2,0},{3,1},{4,6},{5,7},{6,4},{7,5},{8,9},{9,8},{10,11... | collective-permute-start | bytes 1536008 | tf_op jit(solution)/shard_map/ppermute | solution.py:825
  639.9 20.1 %collective-permute-start.37 = (bf16[16,40,1920]{2,1,0:T(8,128)(2,1)}, bf16[16,40,1920]{2,1,0:T(8,128)(2,1)}, u32[]{:S(2)}, u32[]{:S(2)}) collective-permute-start(bf16[16,40,1920]{2,1,0:T(8,128)(2,1)} %get-tuple-element.312), channel_id=1, source_target_pairs={{0,8},{1,9},{2,10},{3,11},{4,12},{5,13},{6,14},{7,15},{8,0},{9,1},... | collective-permute-start | bytes 7372808 | tf_op jit(solution)/shard_map/ppermute | solution.py:825
  663.1 35.0 %collective-permute-start.39 = (bf16[8,40,1920]{2,1,0:T(8,128)(2,1)}, bf16[8,40,1920]{2,1,0:T(8,128)(2,1)}, u32[]{:S(2)}, u32[]{:S(2)}) collective-permute-start(bf16[8,40,1920]{2,1,0:T(8,128)(2,1)} %add_convert_fusion.6), channel_id=1, source_target_pairs={{0,1},{1,0},{2,3},{3,2},{4,5},{5,4},{6,7},{7,6},{8,24},{9,25},{10,... | collective-permute-start | bytes 3686408 | tf_op jit(solution)/shard_map/ppermute | solution.py:825
  665.7 32.4 %collective-permute-start.38 = (bf16[1,40,3200]{2,1,0:T(8,128)(2,1)}, bf16[1,40,3200]{2,1,0:T(8,128)(2,1)S(1)}, u32[]{:S(2)}, u32[]{:S(2)}) collective-permute-start(bf16[1,40,3200]{2,1,0:T(8,128)(2,1)} %add_convert_fusion.15), channel_id=1, source_target_pairs={{0,4},{1,5},{2,6},{3,7},{4,0},{5,1},{6,2},{7,3},{8,12},{9,13},{10,... | collective-permute-start | bytes 768008 | tf_op jit(solution)/shard_map/ppermute | solution.py:825
  703.3 16.2 %collective-permute-start.40 = (bf16[4,40,1920]{2,1,0:T(8,128)(2,1)}, bf16[4,40,1920]{2,1,0:T(8,128)(2,1)S(1)}, u32[]{:S(2)}, u32[]{:S(2)}) collective-permute-start(bf16[4,40,1920]{2,1,0:T(8,128)(2,1)} %add_convert_fusion.10), channel_id=1, source_target_pairs={{0,16},{1,17},{2,18},{3,19},{4,20},{5,21},{6,22},{7,23},{8,10},{9,... | collective-permute-start | bytes 1843208 | tf_op jit(solution)/shard_map/ppermute | solution.py:825
  704.2 18.0 %collective-permute-start.46 = (bf16[8,16,1280]{2,1,0:T(8,128)(2,1)}, bf16[8,16,1280]{2,1,0:T(8,128)(2,1)}, u32[]{:S(2)}, u32[]{:S(2)}) collective-permute-start(bf16[8,16,1280]{2,1,0:T(8,128)(2,1)} %slice.800), channel_id=1, source_target_pairs={{0,6},{1,7},{8,14},{9,15},{16,22},{17,23},{24,30},{25,31}} | collective-permute-start | bytes 983048 | tf_op jit(solution)/shard_map/ppermute | solution.py:1065
  708.0 14.5 %collective-permute-start.47 = (bf16[8,16,1280]{2,1,0:T(8,128)(2,1)}, bf16[8,16,1280]{2,1,0:T(8,128)(2,1)}, u32[]{:S(2)}, u32[]{:S(2)}) collective-permute-start(bf16[8,16,1280]{2,1,0:T(8,128)(2,1)} %slice.800), channel_id=1, source_target_pairs={{2,6},{3,7},{10,14},{11,15},{18,22},{19,23},{26,30},{27,31}} | collective-permute-start | bytes 983048 | tf_op jit(solution)/shard_map/ppermute | solution.py:1065
  709.4 17.5 %collective-permute-start.48 = (bf16[8,16,1280]{2,1,0:T(8,128)(2,1)}, bf16[8,16,1280]{2,1,0:T(8,128)(2,1)}, u32[]{:S(2)}, u32[]{:S(2)}) collective-permute-start(bf16[8,16,1280]{2,1,0:T(8,128)(2,1)} %slice.800), channel_id=1, source_target_pairs={{4,6},{5,7},{12,14},{13,15},{20,22},{21,23},{28,30},{29,31}} | collective-permute-start | bytes 983048 | tf_op jit(solution)/shard_map/ppermute | solution.py:1065
  718.2 23.5 %collective-permute-start.44 = (bf16[6,64,1280]{2,1,0:T(8,128)(2,1)}, bf16[6,64,1280]{2,1,0:T(8,128)(2,1)S(1)}, u32[]{:S(2)}, u32[]{:S(2)}) collective-permute-start(bf16[6,64,1280]{2,1,0:T(8,128)(2,1)} %bitcast.132), channel_id=1, source_target_pairs={{2,0},{4,2},{6,4},{3,1},{5,3},{7,5},{10,8},{12,10},{14,12},{11,9},... | collective-permute-start | bytes 2949128 | tf_op jit(solution)/shard_map/ppermute | solution.py:1063
  719.5 12.7 %collective-permute-start.45 = (bf16[8,32,1280]{2,1,0:T(8,128)(2,1)S(1)}, bf16[8,32,1280]{2,1,0:T(8,128)(2,1)S(1)}, u32[]{:S(2)}, u32[]{:S(2)}) collective-permute-start(bf16[8,32,1280]{2,1,0:T(8,128)(2,1)S(1)} %constant_dynamic-slice_fusion), channel_id=1, source_target_pairs={{0,1},{1,0},{2,3},{3,2},{4,5},{5,4},{6,7},{7,6},{8,9},{9,8},{10,11... | collective-permute-start | bytes 1966088 | tf_op jit(solution)/shard_map/ppermute | solution.py:967
  722.2 19.6 %collective-permute-start.42 = (bf16[2,40,1920]{2,1,0:T(8,128)(2,1)S(1)}, bf16[2,40,1920]{2,1,0:T(8,128)(2,1)S(1)}, u32[]{:S(2)}, u32[]{:S(2)}) collective-permute-start(bf16[2,40,1920]{2,1,0:T(8,128)(2,1)S(1)} %add_convert_fusion.14), channel_id=1, source_target_pairs={{0,2},{1,3},{2,0},{3,1},{4,6},{5,7},{6,4},{7,5},{8,9},{9,8},{10,11... | collective-permute-start | bytes 921608 | tf_op jit(solution)/shard_map/ppermute | solution.py:825
  722.5 19.3 %collective-permute-start.43 = (f32[19680]{0:T(1024)S(1)}, f32[19680]{0:T(1024)S(1)}, u32[]{:S(2)}, u32[]{:S(2)}) collective-permute-start(f32[19680]{0:T(1024)S(1)} %add.722), channel_id=1, source_target_pairs={{0,2},{2,0},{4,6},{6,4},{1,3},{3,1},{5,7},{7,5},{8,10},{10,8},{12,... | collective-permute-start | bytes 236168 | tf_op jit(solution)/shard_map/ppermute | solution.py:725
  745.0 11.5 %collective-permute-start.51 = (bf16[8,32,1280]{2,1,0:T(8,128)(2,1)S(1)}, bf16[8,32,1280]{2,1,0:T(8,128)(2,1)S(1)}, u32[]{:S(2)}, u32[]{:S(2)}) collective-permute-start(bf16[8,32,1280]{2,1,0:T(8,128)(2,1)S(1)} %get-tuple-element.395), channel_id=1, source_target_pairs={{0,1},{1,0},{2,3},{3,2},{4,5},{5,4},{6,7},{7,6},{8,9},{9,8},{10,11... | collective-permute-start | bytes 1966088 | tf_op jit(solution)/shard_map/ppermute | solution.py:967
  756.5 11.8 %collective-permute-start.52 = (f32[19680]{0:T(1024)S(1)}, f32[19680]{0:T(1024)S(1)}, u32[]{:S(2)}, u32[]{:S(2)}) collective-permute-start(f32[19680]{0:T(1024)S(1)} %add.739), channel_id=1, source_target_pairs={{0,8},{8,0},{16,24},{24,16},{1,9},{9,1},{17,25},{25,17},{2,10},{10... | collective-permute-start | bytes 236168 | tf_op jit(solution)/shard_map/ppermute | solution.py:725
  (63 other events, 1195.7 us)
Sparse Core Ops, SparseCore 0:
  13.0 104.9 all-gather.3
  121.4 121.6 all-gather.5
  246.0 100.7 all-gather.7

commit v4 on v3

--- a/solution.py
+++ b/solution.py
@@ -10,6 +10,7 @@
 
 HEADS = 16
 HALF = HEADS // 2
+GROUP = 8
 WIN = 14
 NWIN = 5
 SIDE = 16
@@ -103,26 +104,38 @@
     ind = ind_ref[...]
     scale = HD**-0.5
     zeros = jnp.zeros((DEPTH - HD - 2 * SIDE, TOK), jnp.bfloat16)
-    for head in range(HEADS):
-        low = head * HD
-        place = head // HALF * 3 * model // 2 + head % HALF * HD
+
+    def place_of(head):
+        return head // HALF * 3 * model // 2 + head % HALF * HD
+
+    def wide(head):
+        place = place_of(head)
         query = project_ref[place : place + HD]
         key = project_ref[model // 2 + place : model // 2 + place + HD]
-        value = project_ref[model + place : model + place + HD]
         rows, cols = query_offsets(query, tab_ref, lane)
         rows = (rows * HD**0.5).astype(jnp.bfloat16)
         cols = jnp.where(sub < WIN, cols * HD**0.5, NEG).astype(jnp.bfloat16)
-        query_wide = jnp.concatenate([query, rows, cols, zeros], axis=0)
-        key_wide = jnp.concatenate([key, ind], axis=0)
-        scores = dot_tn(key_wide, query_wide)[:KEYS]
+        query = jnp.concatenate([query, rows, cols, zeros], axis=0)
+        return jnp.concatenate([key, ind], axis=0), query
+
+    def softmax(scores):
         maxima = jnp.max(scores, axis=0, keepdims=True)
         weights = jnp.exp((scores - maxima) * scale)
         inverse = 1.0 / jnp.sum(weights, axis=0, keepdims=True)
-        weights = weights.astype(jnp.bfloat16)
-        weights_ref[0, head] = weights
-        inverse_ref[0, head : head + 1] = inverse
-        attended = dot(value[:, :KEYS], weights)
-        turned_ref[low : low + HD] = (attended * inverse).astype(jnp.bfloat16)
+        return weights.astype(jnp.bfloat16), inverse
+
+    for first in range(0, HEADS, GROUP):
+        heads = range(first, first + GROUP)
+        scores = [wide(head) for head in heads]
+        scores = [dot_tn(key, query)[:KEYS] for key, query in scores]
+        results = [softmax(one) for one in scores]
+        for head, (weights, inverse) in zip(heads, results):
+            low = head * HD
+            place = model + place_of(head)
+            weights_ref[0, head] = weights
+            inverse_ref[0, head : head + 1] = inverse
+            attended = dot(project_ref[place : place + HD, :KEYS], weights)
+            turned_ref[low : low + HD] = (attended * inverse).astype(jnp.bfloat16)
     attended_ref[...] = turned_ref[...].T
 
 
@@ -148,9 +161,9 @@
             jax.ShapeDtypeStruct((slots, HEADS, TOK), jnp.float32),
         ],
         scratch_shapes=[pltpu.VMEM((model, TOK), jnp.bfloat16)],
-        compiler_params=pltpu.CompilerParams(vmem_limit_bytes=48 * MIB),
+        compiler_params=pltpu.CompilerParams(vmem_limit_bytes=60 * MIB),
         cost_estimate=pl.CostEstimate(
-            flops=slots * 7_000_000_000,
+            flops=slots * 3_500_000_000,
             bytes_accessed=slots * 6 * MIB,
             transcendentals=slots * HEADS * KEYS * TOK,
         ),
@@ -172,22 +185,33 @@
 
     turned_ref[...] = grad_ref[...].T
     total = jnp.zeros(dtab_ref.shape, jnp.float32)
-    for head in range(HALF):
+    def products(head):
+        low = head * HD
+        value = project_ref[2 * model + low : 2 * model + low + HD]
+        grad = (turned_ref[low : low + HD] * inverse_ref[0, head : head + 1]).astype(jnp.bfloat16)
+        return grad, dot_tn(value, grad)[:KEYS]
+
+    def score_grads(head, product):
+        weights = weights_ref[0, head].astype(jnp.float32)
+        terms = weights * product
+        inner = jnp.sum(terms, axis=0, keepdims=True) * inverse_ref[0, head : head + 1]
+        return (terms - weights * inner).astype(jnp.bfloat16)
+
+    def wide_grads(head, grad, grad_scores):
         low = head * HD
         query = project_ref[low : low + HD]
         key = project_ref[model + low : model + low + HD]
-        value = project_ref[2 * model + low : 2 * model + low + HD]
-        inverse = inverse_ref[0, head : head + 1]
-        grad = (turned_ref[low : low + HD] * inverse).astype(jnp.bfloat16)
-        weights = weights_ref[0, head]
-        weights_float = weights.astype(jnp.float32)
-        terms = weights_float * dot_tn(value, grad)[:KEYS]
-        inner = jnp.sum(terms, axis=0, keepdims=True) * inverse
-        grad_scores = (terms - weights_float * inner).astype(jnp.bfloat16)
-        grad_value = dot_nt(grad, weights)
+        key = jnp.concatenate([key, ind], axis=0)
+        grad_wide = dot(key[:, :KEYS], grad_scores)
+        grad_value = dot_nt(grad, weights_ref[0, head])
         grad_key = dot_nt(query, grad_scores) * scale
-        key_wide = jnp.concatenate([key, ind], axis=0)
-        grad_wide = dot(key_wide[:, :KEYS], grad_scores)
+        out_ref[model + low : model + low + HD, :KEYS] = grad_key.astype(jnp.bfloat16)
+        out_ref[2 * model + low : 2 * model + low + HD, :KEYS] = grad_value.astype(jnp.bfloat16)
+        return grad_wide
+
+    def offset_grads(head, grad_wide, total):
+        low = head * HD
+        query = project_ref[low : low + HD]
         rows = grad_wide[HD : HD + SIDE]
         cols = grad_wide[HD + SIDE : HD + 2 * SIDE]
         spread = jnp.concatenate(
@@ -196,10 +220,18 @@
             axis=0,
         ).astype(jnp.bfloat16)
         grad_query = grad_wide[:HD] * scale + dot_tn(tab, spread)
-        total = total + dot_nt(spread, query)
         out_ref[low : low + HD] = grad_query.astype(jnp.bfloat16)
-        out_ref[model + low : model + low + HD, :KEYS] = grad_key.astype(jnp.bfloat16)
-        out_ref[2 * model + low : 2 * model + low + HD, :KEYS] = grad_value.astype(jnp.bfloat16)
+        return total + dot_nt(spread, query)
+
+    for first in range(0, HALF, GROUP):
+        heads = range(first, first + GROUP)
+        pairs = [products(head) for head in heads]
+        pairs = [
+            (grad, score_grads(head, product)) for head, (grad, product) in zip(heads, pairs)
+        ]
+        grads = [wide_grads(head, *pair) for head, pair in zip(heads, pairs)]
+        for head, grad_wide in zip(heads, grads):
+            total = offset_grads(head, grad_wide, total)
     out_ref[model:, KEYS:] = jnp.zeros((2 * model, TOK - KEYS), jnp.bfloat16)
     dtab_ref[...] += total
 
@@ -227,9 +259,9 @@
             jax.ShapeDtypeStruct((2 * KEYS, HD), jnp.float32),
         ],
         scratch_shapes=[pltpu.VMEM((model, TOK), jnp.bfloat16)],
-        compiler_params=pltpu.CompilerParams(vmem_limit_bytes=48 * MIB),
+        compiler_params=pltpu.CompilerParams(vmem_limit_bytes=60 * MIB),
         cost_estimate=pl.CostEstimate(
-            flops=slots * 4_000_000_000, bytes_accessed=slots * 4 * MIB, transcendentals=0
+            flops=slots * 2_500_000_000, bytes_accessed=slots * 4 * MIB, transcendentals=0
         ),
     )(project, weights, inverse, grad, tab, ind)
 
@@ -398,6 +430,31 @@
     return mixed, grad, parts, grad_shift
 
 
+def token_gradient_kernel(grad_ref, weight_ref, out_ref):
+    out_ref[...] = dot(weight_ref[...], grad_ref[...]).astype(jnp.bfloat16).T
+
+
+def token_gradient(grad, weight, half):
+    wide, tokens = grad.shape
+    model = weight.shape[0]
+    return pl.pallas_call(
+        token_gradient_kernel,
+        grid=(tokens // TOK,),
+        in_specs=[
+            pl.BlockSpec((wide, TOK), lambda i: (0, i)),
+            pl.BlockSpec((model, wide), lambda i: (0, half), pipeline_mode=pl.Buffered(1)),
+        ],
+        out_specs=pl.BlockSpec((TOK, model), lambda i: (i, 0)),
+        out_shape=jax.ShapeDtypeStruct((tokens, model), jnp.bfloat16),
+        compiler_params=pltpu.CompilerParams(vmem_limit_bytes=40 * MIB),
+        cost_estimate=pl.CostEstimate(
+            flops=2 * tokens * model * wide,
+            bytes_accessed=2 * (wide * tokens + model * wide + tokens * model),
+            transcendentals=0,
+        ),
+    )(grad, weight)
+
+
 def window_gradient_kernel(own, core_stride, table_ref, *refs):
     tokens_ref, grad_ref, *ready, sent_ref, kept_ref, sums_ref = refs
     devices = table_ref.shape[0] - 1
@@ -924,7 +981,7 @@
 
 
 def all_sum(value):
-    for bit in reversed(device_bits()):
+    for bit in axis_bits("dp") + axis_bits("cols") + axis_bits("rows"):
         (arrived,) = yield [value], [flipped(value, bit)]
         value = value + arrived
     return value
@@ -1051,32 +1108,41 @@
             [main.reshape(-1, self.model), end.reshape(-1, self.model)], axis=0
         )
 
-    def leave(self, tokens):
+    def leave(self, tokens, early):
         if not self.near:
             return tokens.reshape(self.tiles)
         last, rest, halo = self.count - 1, self.rest, self.halo
         top = self.height - rest
-        main = tokens[: WIN * self.width].reshape(WIN, self.width, self.model)
-        end = tokens[WIN * self.width :].reshape(rest, END, self.model)
-        held = jnp.sum(end_place(self.width), axis=1).astype(jnp.bfloat16)
+        width, model, step = self.width, self.model, self.step
+        end = tokens[WIN * width :].reshape(rest, END, model)
+        held = jnp.sum(end_place(width), axis=1).astype(jnp.bfloat16)
         end = end * held[None, :, None]
-        up = lax.ppermute(main[:halo], "rows", [(i + 1, i) for i in range(last)])
+        up = tokens[: halo * width].reshape(halo, width, model)
+        up = lax.ppermute(up, "rows", [(i + 1, i) for i in range(last)])
         piece = end[:, :SIDE]
         pieces = [lax.ppermute(piece, "rows", [(source, last)]) for source in range(last)]
-        upper = lax.dynamic_slice_in_dim(main, self.step * self.row, top, 0)
-        kept_up, sent_up, arrived_up = split_image(upper)
-        up, arrived_up, *pieces = yield [piece, sent_up], [up, arrived_up] + pieces
+        upper = lax.dynamic_slice_in_dim(tokens, step * self.row * width, top * width, 0)
+        upper = upper.reshape(top, width, model)
+        if early:
+            kept_up, sent_up, arrived_up = split_image(upper)
+            up, arrived_up, *pieces = yield [piece, sent_up], [up, arrived_up] + pieces
+        else:
+            up, *pieces = yield [piece], [up] + pieces
         tail = 0
-        for start, piece in zip(end_starts(self.width, self.count), pieces + [end]):
-            rest_wide = self.width - piece.shape[1] - start
+        for start, piece in zip(end_starts(width, self.count), pieces + [end]):
+            rest_wide = width - piece.shape[1] - start
             tail = tail + jnp.pad(piece, ((0, 0), (start, rest_wide), (0, 0)))
         below = jnp.where(self.row == last, tail, pad_rows(up, 0, rest - halo))
-        whole = jnp.concatenate([main, below], axis=0)
-        place = self.step * self.row + top
+        whole = tokens[top * width : WIN * width].reshape(WIN - top, width, model)
+        whole = jnp.concatenate([whole, below], axis=0)
         kept_low, sent_low, arrived_low = split_image(
-            lax.dynamic_slice_in_dim(whole, place, rest, 0)
+            lax.dynamic_slice_in_dim(whole, step * self.row, rest, 0)
         )
-        (arrived_low,) = yield [sent_low], [arrived_low]
+        if early:
+            (arrived_low,) = yield [sent_low], [arrived_low]
+        else:
+            kept_up, sent_up, arrived_up = split_image(upper)
+            arrived_up, arrived_low = yield [sent_low, sent_up], [arrived_up, arrived_low]
         upper = join_image(kept_up, arrived_up)
         lower = join_image(kept_low, arrived_low)
         return jnp.concatenate([upper, lower], axis=1)
@@ -1210,7 +1276,8 @@
             )
 
         if first:
-            mixed, joint2 = sync((mixed, joint2), [])
+            mixed = launch(mixed, sums)
+            mixed, joint2 = sync((mixed, joint2), sums)
         mixed, grad_normed2, blocks, grad_shift = beside(sums, normed2, step)
         shifts.append(grad_shift.reshape(count, devices, share))
         if isinstance(blocks, list):
@@ -1218,10 +1285,10 @@
         else:
             sums.append(Flight(summed_mlp(blocks, share)))
 
-    output = Flight(layout.leave(mixed))
+    output = Flight(layout.leave(mixed, False))
     grad_normed2 = launch(grad_normed2, sums)
     grad_middle, grad_attended, grad_proj, middle_sums = sync(
-        middle_backward(grad_normed2, middle, cot, attended, joint, middle_vectors), sums[1:]
+        middle_backward(grad_normed2, middle, cot, attended, joint, middle_vectors), sums
     )
 
     def rows_of(vector):
@@ -1231,14 +1298,9 @@
         return attention_backward(project, weights, inverse, grad_windows, tab, ind, half)
 
     def project_step(grad_project, half):
-        return lax.dot_general(
-            grad_project,
-            qkv_full[:, half * 3 * model // 2 : (half + 1) * 3 * model // 2],
-            (((0,), (1,)), ((), ())),
-            preferred_element_type=jnp.float32,
-        ).astype(jnp.bfloat16)
-
-    grad_windows = layout.to_windows(launch(grad_attended, sums[1:] + [output]))
+        return token_gradient(grad_project, qkv_full, half)
+
+    grad_windows = layout.to_windows(launch(grad_attended, sums + [output]))
     grad_project, grad_tab = sync(attention_step(0), sums[:1])
     grad_project = launch(grad_project, sums[:1])
     sent, kept, sums0 = sync(
@@ -1249,11 +1311,9 @@
     first_rows = layout.to_rows(project_step(grad_project, 0))
     first_rows, grad_windows = sync((first_rows, grad_windows), sums[:1] + sums[-1:])
     grad_windows = launch(grad_windows, sums[:1] + sums[-1:])
-    grad_project, grad_part = sync(attention_step(1), sums + [output])
-    grad_project = launch(grad_project, sums + [output])
-    sent, kept, sums1 = sync(
-        window_gradient(window_tokens, grad_project, [], table), sums + [output]
-    )
+    grad_project, grad_part = sync(attention_step(1), sums[:-1] + [output])
+    grad_project = launch(grad_project, sums[:-1])
+    sent, kept, sums1 = sync(window_gradient(window_tokens, grad_project, [], table), sums)
     sums.append(Flight(summed_columns(sent, kept, [3 * half])))
     grad_project = launch(grad_project, sums)
     grad_tokens = sync(project_step(grad_project, 1), sums)
@@ -1261,7 +1321,9 @@
     grad_rows, norm_sums = sync(
         image_backward(rows, first_rows, second_rows, grad_middle, norm_vectors), sums
     )
-    grad_in = Flight(layout.leave(grad_rows))
+    grad_in = Flight(layout.leave(grad_rows, True))
+    grad_in.advance()
+    norm_sums, *_ = sync([norm_sums] + grad_in.sent, sums)
 
     grad_sums = [jnp.sum(piece, axis=1) for piece in (sums0, sums1)]
     up_shift_sums = jnp.concatenate(shifts, axis=0).transpose(1, 0, 2).reshape(devices, unit)
@@ -1288,12 +1350,13 @@
         ups = jnp.concatenate(ups, axis=1).transpose(0, 2, 1, 3)
         return ups.reshape(share, devices * unit), jnp.concatenate(downs, axis=0)
 
-    launch(norm_sums, [grad_in] + sums)
+    launch(grad_rows, sums)
+    flat = [one.finish() for one in sums[:-3]]
+    flat, output.arrived = sync((flat, output.arrived), sums)
+    launch(flat, sums)
+    grad_fc1, grad_fc2 = formatted(*zip(*flat))
     done = output.finish()
-    done = sync(done, sums)
-    launch(done, sums)
-    grad_fc1, grad_fc2 = formatted(*zip(*[one.finish() for one in sums[:-3]]))
-    grad_fc1, grad_fc2 = sync((grad_fc1, grad_fc2), sums + [grad_in])
+    grad_fc1, grad_fc2, done = sync((grad_fc1, grad_fc2, done), sums + [grad_in])
     launch(grad_fc1, [grad_in] + sums)
     first_qkv, sum_proj = sums[-3].finish()
     first_qkv, sum_proj = sync((first_qkv, sum_proj), sums + [grad_in])

time: 793 us -> 770 us (0.971)
  matrix products: 55.1 us -> 26.8 us
  Pallas kernels: 340 us -> 314 us
  starting transfers between devices: 81.2 us -> 98.8 us
  waiting for transfers between devices: 94.8 us -> 109 us
    pallas_call x1, Pallas kernels: 49.4 us -> 19.9 us  [attention_forward(): pl.pallas_call(attention_forward_kernel, grid=(slots,), in_specs=[pl.Bloc...]
    dot_general x2 -> x0, matrix products: 28.3 us -> none  [project_step(): lax.dot_general(grad_project, qkv_full[:, half * 3 * model // 2:(half + 1...]
    pallas_call x0 -> x2, Pallas kernels: none -> 28 us  [token_gradient(): pl.pallas_call(token_gradient_kernel, grid=(tokens // TOK,), in_specs=[pl...]
    pallas_call x2, Pallas kernels: 59.1 us -> 34.8 us  [attention_backward(): pl.pallas_call(attention_backward_kernel, grid=(slots,), in_specs=[pl.Blo...]
    all_gather x3, waiting for transfers between devices: 33.1 us -> 56.7 us  [gathered(): return lax.all_gather(shard, ALL, axis=0, tiled=True)]
    ppermute x20, starting transfers between devices: 18.9 us -> 36 us  [partner_permute(): return lax.ppermute(value, ALL, pairs)]
    ppermute x10, waiting for transfers between devices: 22.3 us -> 6 us  [flipped(): lax.ppermute(value, axis, [(i, i ^ mask) for i in range(lax.axis_size(axi...]
    unnamed x127 -> x157, local copies, waits for them, and re-layouts: 26 us -> 35.7 us
  transfers between devices with their start and end apart: 57 -> 57, of which waited for: 12 -> 15; matrix products, arithmetic and copies ran while one was open for 27% -> 21% of each run, Pallas kernels for 43% -> 41%
where the time goes in v4:
time: 770 us; the launch traced here: 761 us
  Pallas kernels  314 us (41%)
  waiting for transfers between devices  109 us (14%)
  local copies, waits for them, and re-layouts  101 us (13%)
  starting transfers between devices  98.8 us (13%)
  other arithmetic  96.6 us (13%)
  matrix products  26.8 us (3%)
  between operations  15.6 us (2%)
    pallas_call x2, Pallas kernels, mlp(): pl.pallas_call(functools.partial(mlp_kernel, tokens // 2, begins, ends, p...  142 us
    all_gather x3, waiting for transfers between devices, gathered(): return lax.all_gather(shard, ALL, axis=0, tiled=True)  56.7 us
    convert_element_type x16, other arithmetic, summed(): sent = sent.astype(jnp.bfloat16)  48.1 us
    ppermute x20, starting transfers between devices, partner_permute(): return lax.ppermute(value, ALL, pairs)  36 us
    unnamed x157, local copies, waits for them, and re-layouts  35.7 us
    pallas_call x2, Pallas kernels, window_gradient(): pl.pallas_call(functools.partial(window_gradient_kernel, own, core_stride...  35.7 us
    pallas_call x2, Pallas kernels, attention_backward(): pl.pallas_call(attention_backward_kernel, grid=(slots,), in_specs=[pl.Blo...  34.8 us
    pallas_call x2, Pallas kernels, token_gradient(): pl.pallas_call(token_gradient_kernel, grid=(tokens // TOK,), in_specs=[pl...  28 us
  transfers between devices with their start and end apart: 57, of which 15 were waited for; matrix products, arithmetic and copies ran while one was open for 21% of the time, Pallas kernels for 41%

profile of v4, /device:TPU:1, one launch (start us, length us, event | category | flops | bytes accessed | tf_op | source)
XLA Modules:
  0.0 761.3 jit_solution(5973912015607287522)
XLA Ops:
  13.7 4.8 concatenate.143
  24.1 2.5 collective-permute-start.2
  28.6 3.3 collective-permute-start.3
  37.3 17.3 %collective-permute-done.5 = bf16[8,32,1280]{2,1,0:T(8,128)(2,1)S(1)} collective-permute-done((bf16[8,32,1280]{2,1,0:T(8,128)(2,1)}, bf16[8,32,1280]{2,1,0:T(8,128)(2,1)S(1)}, u32[]{:S(2)}, u32[]{:S(2)}) %collective-permute-start.5) | collective-permute-done | bytes 655392 | tf_op jit(solution)/shard_map/ppermute | solution.py:1008
  60.1 5.6 reshape.332
  67.4 3.3 reshape.333
  85.3 4.3 collective-permute-start.7
  96.7 4.0 collective-permute-done.8
  102.2 3.3 collective-permute-done.6
  105.5 14.3 %collective-permute-done.7 = bf16[6,64,1280]{2,1,0:T(8,128)(2,1)} collective-permute-done((bf16[6,64,1280]{2,1,0:T(8,128)(2,1)}, bf16[6,64,1280]{2,1,0:T(8,128)(2,1)}, u32[]{:S(2)}, u32[]{:S(2)}) %collective-permute-start.7) | collective-permute-done | bytes 983072 | tf_op jit(solution)/shard_map/ppermute | solution.py:1093
  125.7 5.0 shard_map.378.rows_ref
  137.1 25.7 %add_convert_fusion.project_ref = bf16[3840,1792]{1,0:T(8,128)(2,1)} fusion(bf16[1280,3840]{1,0:T(8,128)(2,1)} %all-gather.4.cloned.1.call-done.weight_ref, bf16[1792,1280]{1,0:T(8,128)(2,1)} %copy-done.9, f32[3840]{0:T(1024)S(1)} %reduce.4), kind=kOutput, calls=%fused_computation | convolution fusion | flops 17629839360 | bytes 28195840 | tf_op jit(solution)/shard_map/dot_general | solution.py:1244
  170.6 5.4 collective-permute-start.12
  177.8 19.9 %shard_map.380 = (bf16[1792,1280]{1,0:T(8,128)(2,1)}, bf16[7,16,224,256]{3,2,1,0:T(8,128)(2,1)}, f32[7,16,256]{2,1,0:T(8,128)}) custom-call(bf16[3840,1792]{1,0:T(8,128)(2,1)} %add_convert_fusion.project_ref, bf16[448,80]{1,0:T(8,128)(2,1)} %pad_maximum_fusion.6.tab_ref, bf16[48,256]{1,0:T(8,128)(2,1)} %fusion.25.ind_ref), custom_call_target="tpu_custom_call" | custom-call | flops 24500000768 | bytes 44040192 | tf_op jit(solution)/shard_map/pallas_call | solution.py:145
  207.2 39.1 %all-gather.6.cloned.1.call-done.proj_ref.refs_3_.refs_4_ = bf16[1280,6400]{1,0:T(8,128)(2,1)} async-done(((bf16[40,6400]{1,0:T(8,128)(2,1)}), bf16[1280,6400]{1,0:T(8,128)(2,1)}) %all-gather.6.cloned.1.call-update) | async-done | bytes 16384016 | tf_op jit(solution)/shard_map/all_gather | solution.py:1207
  248.1 7.8 %shard_map.382 = (f32[1088,1280]{1,0:T(8,128)S(1)}, bf16[1088,1280]{1,0:T(8,128)(2,1)S(1)}) custom-call(bf16[1088,1280]{1,0:T(8,128)(2,1)S(1)} %copy-done.4, bf16[1280,6400]{1,0:T(8,128)(2,1)} %all-gather.6.cloned.1.call-done.proj_ref.refs_3_.refs_4_, bf16[1088,1280]{1,0:T(8,128)(2,1)S(1)} %copy-done.2, f32[8,1280]{1,0:T(8,128)S(1)} %select_maximum_fusion.vectors_ref), custom_call_target="tpu_custom_call" | custom-call | flops 3565158400 | bytes 16711680 | tf_op jit(solution)/shard_map/pallas_call | solution.py:584
  260.4 70.2 %shard_map.383 = (f32[1088,1280]{1,0:T(8,128)}, f32[1088,1280]{1,0:T(8,128)}, bf16[16,320,640]{2,1,0:T(8,128)(2,1)}, bf16[16,320,640]{2,1,0:T(8,128)(2,1)}, f32[1,2560]{1,0:T(1,128)}) custom-call(s32[33]{0:T(128)} %pad_add_fusion.1.refs_0_.table_ref, bf16[1088,1280]{1,0:T(8,128)(2,1)} %copy-done.18, bf16[1088,1280]{1,0:T(8,128)(2,1)} %pad_maximum_fusion.1.refs_2_.cot_ref, ...), custom_call_target="tpu_custom_call" | custom-call | flops 57042534400 | bytes 59637760 | tf_op jit(solution)/shard_map/pallas_call | solution.py:387
  330.9 17.6 %all-gather.8.cloned.1.call-done.refs_3_.refs_4_ = bf16[1280,5120]{1,0:T(8,128)(2,1)} async-done(((bf16[40,5120]{1,0:T(8,128)(2,1)}), bf16[1280,5120]{1,0:T(8,128)(2,1)}) %all-gather.8.cloned.1.call-update) | async-done | bytes 13107216 | tf_op jit(solution)/shard_map/all_gather | solution.py:1207
  348.5 5.4 add_convert_fusion.2
  355.1 71.7 %shard_map.384 = (bf16[1088,1280]{1,0:T(8,128)(2,1)}, f32[1088,1280]{1,0:T(8,128)}, bf16[16,320,640]{2,1,0:T(8,128)(2,1)}, bf16[16,320,640]{2,1,0:T(8,128)(2,1)}, f32[1,2560]{1,0:T(1,128)}) custom-call(s32[33]{0:T(128)} %pad_add_fusion.1.refs_0_.table_ref, bf16[1088,1280]{1,0:T(8,128)(2,1)} %copy-done.18, ...), custom_call_target="tpu_custom_call" | custom-call | flops 57042534400 | bytes 59637760 | tf_op jit(solution)/shard_map/pallas_call | solution.py:387
  427.4 4.5 add_convert_fusion.5
  433.9 20.7 %shard_map.385 = (f32[1088,1280]{1,0:T(8,128)}, bf16[1088,1280]{1,0:T(8,128)(2,1)}, bf16[1280,1280]{1,0:T(8,128)(2,1)}, f32[8,1280]{1,0:T(8,128)}) custom-call(f32[1088,1280]{1,0:T(8,128)} %get-tuple-element.261.grad_ref, f32[1088,1280]{1,0:T(8,128)} %copy-done.8, bf16[1088,1280]{1,0:T(8,128)(2,1)} %pad_maximum_fusion.1.refs_2_.cot_ref, ...), custom_call_target="tpu_custom_call" | custom-call | flops 7130316800 | bytes 33423360 | tf_op jit(solution)/shard_map/pallas_call | solution.py:639
  454.7 4.7 add_convert_fusion.1
  459.8 4.1 collective-permute-start.24
  474.7 17.2 %shard_map.387 = (bf16[1920,1792]{1,0:T(8,128)(2,1)}, f32[448,80]{1,0:T(8,128)}) custom-call(bf16[3840,1792]{1,0:T(8,128)(2,1)} %add_convert_fusion.project_ref, bf16[7,16,224,256]{3,2,1,0:T(8,128)(2,1)} %get-tuple-element.232.weights_ref, f32[7,16,256]{2,1,0:T(8,128)} %get-tuple-element.233.inverse_ref, bf16[1792,1280]{1,0:T(8,128)(2,1)} %copy-done.10, ...), custom_call_target="tpu_custom_call" | custom-call | flops 17500000256 | bytes 29360128 | tf_op jit(solution)/shard_map/pallas_call | solution.py:242
  495.7 19.8 %shard_map.388 = (bf16[16,40,3200]{2,1,0:T(8,128)(2,1)}, bf16[16,40,3200]{2,1,0:T(8,128)(2,1)}, f32[1920,128]{1,0:T(8,128)}) custom-call(s32[33]{0:T(128)} %pad_add_fusion.1.refs_0_.table_ref, bf16[1792,1280]{1,0:T(8,128)(2,1)} %copy-done.9, bf16[1920,1792]{1,0:T(8,128)(2,1)} %get-tuple-element.297.refs_1_.grad_ref, ...), custom_call_target="tpu_custom_call" | custom-call | flops 8808038400 | bytes 19660800 | tf_op jit(solution)/shard_map/pallas_call | solution.py:496
  522.1 3.7 collective-permute-start.27
  525.7 4.2 add_convert_fusion.4
  529.9 2.7 collective-permute-start.29
  536.9 13.9 %shard_map.389.windows_ref = bf16[1792,1280]{1,0:T(8,128)(2,1)S(1)} custom-call(bf16[1920,1792]{1,0:T(8,128)(2,1)S(1)} %bitcast.112, bf16[1280,3840]{1,0:T(8,128)(2,1)} %all-gather.4.cloned.1.call-done.weight_ref), custom_call_target="tpu_custom_call" | custom-call | flops 8808038400 | bytes 16384000 | tf_op jit(solution)/shard_map/pallas_call | solution.py:440
  559.1 2.9 add_convert_fusion.3
  563.3 17.6 %shard_map.391 = (bf16[1920,1792]{1,0:T(8,128)(2,1)}, f32[448,80]{1,0:T(8,128)}) custom-call(bf16[3840,1792]{1,0:T(8,128)(2,1)} %add_convert_fusion.project_ref, bf16[7,16,224,256]{3,2,1,0:T(8,128)(2,1)} %get-tuple-element.232.weights_ref, f32[7,16,256]{2,1,0:T(8,128)} %get-tuple-element.233.inverse_ref, bf16[1792,1280]{1,0:T(8,128)(2,1)} %copy-done.10, ...), custom_call_target="tpu_custom_call" | custom-call | flops 17500000256 | bytes 29360128 | tf_op jit(solution)/shard_map/pallas_call | solution.py:242
  585.2 3.2 add_convert_fusion.8
  589.6 15.9 %shard_map.392 = (bf16[16,40,1920]{2,1,0:T(8,128)(2,1)}, bf16[16,40,1920]{2,1,0:T(8,128)(2,1)}, f32[1920,128]{1,0:T(8,128)}) custom-call(s32[33]{0:T(128)} %pad_add_fusion.1.refs_0_.table_ref, bf16[1792,1280]{1,0:T(8,128)(2,1)} %copy-done.9, bf16[1920,1792]{1,0:T(8,128)(2,1)} %get-tuple-element.329.refs_1_.grad_ref), custom_call_target="tpu_custom_call" | custom-call | flops 8808038400 | bytes 16384000 | tf_op jit(solution)/shard_map/pallas_call | solution.py:496
  607.3 2.5 add_convert_fusion.12
  609.8 3.3 add_convert_fusion.7
  613.4 2.9 copy-done.19
  616.4 14.1 %shard_map.393.windows_ref = bf16[1792,1280]{1,0:T(8,128)(2,1)S(1)} custom-call(bf16[1920,1792]{1,0:T(8,128)(2,1)S(1)} %copy-done.19, bf16[1280,3840]{1,0:T(8,128)(2,1)} %all-gather.4.cloned.1.call-done.weight_ref), custom_call_target="tpu_custom_call" | custom-call | flops 8808038400 | bytes 16384000 | tf_op jit(solution)/shard_map/pallas_call | solution.py:440
  632.9 2.6 collective-permute-done.35
  635.5 2.6 add_convert_fusion.6
  651.4 9.2 %shard_map.395 = (bf16[1088,1280]{1,0:T(8,128)(2,1)}, f32[8,1280]{1,0:T(8,128)}) custom-call(bf16[1088,1280]{1,0:T(8,128)(2,1)} %pad_maximum_fusion.rows_ref.image_ref, bf16[1088,1280]{1,0:T(8,128)(2,1)} %copy-done.5, bf16[1088,1280]{1,0:T(8,128)(2,1)} %copy-done.6, f32[1088,1280]{1,0:T(8,128)} %get-tuple-element.348.grad_middle_ref, ...), custom_call_target="tpu_custom_call" | custom-call | flops 16711680 | bytes 13926400 | tf_op jit(solution)/shard_map/pallas_call | solution.py:682
  676.6 3.1 collective-permute-start.46
  690.4 2.5 add_bitcast_fusion
  705.8 4.2 reshape.358
  716.3 17.2 %collective-permute-start.49 = (bf16[1,40,1920]{2,1,0:T(8,128)(2,1)S(1)}, bf16[1,40,1920]{2,1,0:T(8,128)(2,1)S(1)}, u32[]{:S(2)}, u32[]{:S(2)}) collective-permute-start(bf16[1,40,1920]{2,1,0:T(8,128)(2,1)S(1)} %add_convert_fusion.16), channel_id=1, source_target_pairs={{0,4},{1,5},{2,6},{3,7},{4,0},{5,1},{6,2},{7,3},{8,12},{9,13},{10,... | collective-permute-start | bytes 460808 | tf_op jit(solution)/shard_map/ppermute | solution.py:882
  741.1 2.7 maximum_convert_fusion
  743.8 4.9 collective-permute-start.53
  748.8 2.4 collective-permute-done.53
  (436 shorter events, 205.8 us)
Async XLA Ops:
  7.2 129.9 %all-gather.4.cloned.1.call-start = ((), (), s32[]{:S(2)}) async-start(), calls=%async_computation | async-start | bytes 10137600 | tf_op jit(solution)/shard_map/all_gather | solution.py:1207
  12.9 233.4 %all-gather.6.cloned.1.call-start = ((), (), s32[]{:S(2)}) async-start(), calls=%async_computation.1 | async-start | bytes 16896000 | tf_op jit(solution)/shard_map/all_gather | solution.py:1207
  32.9 21.6 %collective-permute-start.5 = (bf16[8,32,1280]{2,1,0:T(8,128)(2,1)}, bf16[8,32,1280]{2,1,0:T(8,128)(2,1)S(1)}, u32[]{:S(2)}, u32[]{:S(2)}) collective-permute-start(bf16[8,32,1280]{2,1,0:T(8,128)(2,1)} %get-tuple-element.455), channel_id=1, source_target_pairs={{0,1},{1,0},{2,3},{3,2},{4,5},{5,4},{6,7},{7,6},{8,9},{9,8},{10,11... | collective-permute-start | bytes 1966088 | tf_op jit(solution)/shard_map/ppermute | solution.py:1008
  74.2 274.2 %all-gather.8.cloned.1.call-start = ((), (), s32[]{:S(2)}) async-start(), calls=%async_computation.2 | async-start | bytes 13516800 | tf_op jit(solution)/shard_map/all_gather | solution.py:1207
  83.2 22.3 %collective-permute-start.6 = (bf16[8,32,1280]{2,1,0:T(8,128)(2,1)}, bf16[8,32,1280]{2,1,0:T(8,128)(2,1)}, u32[]{:S(2)}, u32[]{:S(2)}) collective-permute-start(bf16[8,32,1280]{2,1,0:T(8,128)(2,1)} %get-tuple-element.450), channel_id=1, source_target_pairs={{0,1},{1,0},{2,3},{3,2},{4,5},{5,4},{6,7},{7,6},{8,9},{9,8},{10,11... | collective-permute-start | bytes 1966088 | tf_op jit(solution)/shard_map/ppermute | solution.py:1008
  85.3 34.5 %collective-permute-start.7 = (bf16[6,64,1280]{2,1,0:T(8,128)(2,1)}, bf16[6,64,1280]{2,1,0:T(8,128)(2,1)}, u32[]{:S(2)}, u32[]{:S(2)}) collective-permute-start(bf16[6,64,1280]{2,1,0:T(8,128)(2,1)} %slice.744), channel_id=1, source_target_pairs={{0,2},{2,4},{4,6},{1,3},{3,5},{5,7},{8,10},{10,12},{12,14},{9,11},... | collective-permute-start | bytes 2949128 | tf_op jit(solution)/shard_map/ppermute | solution.py:1093
  89.6 11.1 %collective-permute-start.8 = (bf16[8,16,1280]{2,1,0:T(8,128)(2,1)}, bf16[8,16,1280]{2,1,0:T(8,128)(2,1)}, u32[]{:S(2)}, u32[]{:S(2)}) collective-permute-start(bf16[8,16,1280]{2,1,0:T(8,128)(2,1)} %get-tuple-element.453), channel_id=1, source_target_pairs={{6,0},{7,1},{14,8},{15,9},{22,16},{23,17},{30,24},{31,25}} | collective-permute-start | bytes 983048 | tf_op jit(solution)/shard_map/ppermute | solution.py:1096
  90.9 11.3 %collective-permute-start.9 = (bf16[8,16,1280]{2,1,0:T(8,128)(2,1)}, bf16[8,16,1280]{2,1,0:T(8,128)(2,1)}, u32[]{:S(2)}, u32[]{:S(2)}) collective-permute-start(bf16[8,16,1280]{2,1,0:T(8,128)(2,1)} %get-tuple-element.452), channel_id=1, source_target_pairs={{6,2},{7,3},{14,10},{15,11},{22,18},{23,19},{30,26},{31,27}} | collective-permute-start | bytes 983048 | tf_op jit(solution)/shard_map/ppermute | solution.py:1096
  92.4 9.8 %collective-permute-start.10 = (bf16[8,16,1280]{2,1,0:T(8,128)(2,1)}, bf16[8,16,1280]{2,1,0:T(8,128)(2,1)}, u32[]{:S(2)}, u32[]{:S(2)}) collective-permute-start(bf16[8,16,1280]{2,1,0:T(8,128)(2,1)} %get-tuple-element.451), channel_id=1, source_target_pairs={{6,4},{7,5},{14,12},{15,13},{22,20},{23,21},{30,28},{31,29}} | collective-permute-start | bytes 983048 | tf_op jit(solution)/shard_map/ppermute | solution.py:1096
  100.7 62.1 %collective-permute-start.11 = (bf16[8,32,1280]{2,1,0:T(8,128)(2,1)}, bf16[8,32,1280]{2,1,0:T(8,128)(2,1)}, u32[]{:S(2)}, u32[]{:S(2)}) collective-permute-start(bf16[8,32,1280]{2,1,0:T(8,128)(2,1)} %get-tuple-element.448), channel_id=1, source_target_pairs={{0,1},{1,0},{2,3},{3,2},{4,5},{5,4},{6,7},{7,6},{8,9},{9,8},{10,11... | collective-permute-start | bytes 1966088 | tf_op jit(solution)/shard_map/ppermute | solution.py:1008
  166.5 35.4 %collective-permute-start.16 = (bf16[8,16,1280]{2,1,0:T(8,128)(2,1)}, bf16[8,16,1280]{2,1,0:T(8,128)(2,1)S(1)}, u32[]{:S(2)}, u32[]{:S(2)}) collective-permute-start(bf16[8,16,1280]{2,1,0:T(8,128)(2,1)} %get-tuple-element.446), channel_id=1, source_target_pairs={{6,0},{7,1},{14,8},{15,9},{22,16},{23,17},{30,24},{31,25}} | collective-permute-start | bytes 983048 | tf_op jit(solution)/shard_map/ppermute | solution.py:1096
  167.8 34.1 %collective-permute-start.15 = (bf16[8,16,1280]{2,1,0:T(8,128)(2,1)}, bf16[8,16,1280]{2,1,0:T(8,128)(2,1)}, u32[]{:S(2)}, u32[]{:S(2)}) collective-permute-start(bf16[8,16,1280]{2,1,0:T(8,128)(2,1)} %get-tuple-element.445), channel_id=1, source_target_pairs={{6,2},{7,3},{14,10},{15,11},{22,18},{23,19},{30,26},{31,27}} | collective-permute-start | bytes 983048 | tf_op jit(solution)/shard_map/ppermute | solution.py:1096
  169.2 32.7 %collective-permute-start.14 = (bf16[8,16,1280]{2,1,0:T(8,128)(2,1)}, bf16[8,16,1280]{2,1,0:T(8,128)(2,1)}, u32[]{:S(2)}, u32[]{:S(2)}) collective-permute-start(bf16[8,16,1280]{2,1,0:T(8,128)(2,1)} %get-tuple-element.444), channel_id=1, source_target_pairs={{6,4},{7,5},{14,12},{15,13},{22,20},{23,21},{30,28},{31,29}} | collective-permute-start | bytes 983048 | tf_op jit(solution)/shard_map/ppermute | solution.py:1096
  170.6 33.8 %collective-permute-start.12 = (bf16[6,64,1280]{2,1,0:T(8,128)(2,1)}, bf16[6,64,1280]{2,1,0:T(8,128)(2,1)}, u32[]{:S(2)}, u32[]{:S(2)}) collective-permute-start(bf16[6,64,1280]{2,1,0:T(8,128)(2,1)} %slice.757), channel_id=1, source_target_pairs={{0,2},{2,4},{4,6},{1,3},{3,5},{5,7},{8,10},{10,12},{12,14},{9,11},... | collective-permute-start | bytes 2949128 | tf_op jit(solution)/shard_map/ppermute | solution.py:1093
  176.9 26.9 %collective-permute-start.13 = (bf16[8,32,1280]{2,1,0:T(8,128)(2,1)}, bf16[8,32,1280]{2,1,0:T(8,128)(2,1)S(1)}, u32[]{:S(2)}, u32[]{:S(2)}) collective-permute-start(bf16[8,32,1280]{2,1,0:T(8,128)(2,1)} %get-tuple-element.443), channel_id=1, source_target_pairs={{0,1},{1,0},{2,3},{3,2},{4,5},{5,4},{6,7},{7,6},{8,9},{9,8},{10,11... | collective-permute-start | bytes 1966088 | tf_op jit(solution)/shard_map/ppermute | solution.py:1008
  330.6 17.9 %collective-permute-start.17 = (bf16[16,320,640]{2,1,0:T(8,128)(2,1)}, bf16[16,320,640]{2,1,0:T(8,128)(2,1)}, u32[]{:S(2)}, u32[]{:S(2)}) collective-permute-start(bf16[16,320,640]{2,1,0:T(8,128)(2,1)} %get-tuple-element.242), channel_id=1, source_target_pairs={{0,8},{1,9},{2,10},{3,11},{4,12},{5,13},{6,14},{7,15},{8,0},{9,1},... | collective-permute-start | bytes 19660808 | tf_op jit(solution)/shard_map/ppermute | solution.py:882
  353.9 72.9 %collective-permute-start.18 = (bf16[8,320,640]{2,1,0:T(8,128)(2,1)}, bf16[8,320,640]{2,1,0:T(8,128)(2,1)}, u32[]{:S(2)}, u32[]{:S(2)}) collective-permute-start(bf16[8,320,640]{2,1,0:T(8,128)(2,1)} %add_convert_fusion.2), channel_id=1, source_target_pairs={{0,1},{1,0},{2,3},{3,2},{4,5},{5,4},{6,7},{7,6},{8,24},{9,25},{10,... | collective-permute-start | bytes 9830408 | tf_op jit(solution)/shard_map/ppermute | solution.py:882
  426.8 27.8 %collective-permute-start.20 = (bf16[16,320,640]{2,1,0:T(8,128)(2,1)}, bf16[16,320,640]{2,1,0:T(8,128)(2,1)}, u32[]{:S(2)}, u32[]{:S(2)}) collective-permute-start(bf16[16,320,640]{2,1,0:T(8,128)(2,1)} %get-tuple-element.260), channel_id=1, source_target_pairs={{0,8},{1,9},{2,10},{3,11},{4,12},{5,13},{6,14},{7,15},{8,0},{9,1},... | collective-permute-start | bytes 19660808 | tf_op jit(solution)/shard_map/ppermute | solution.py:882
  431.9 22.7 %collective-permute-start.19 = (bf16[4,320,640]{2,1,0:T(8,128)(2,1)}, bf16[4,320,640]{2,1,0:T(8,128)(2,1)}, u32[]{:S(2)}, u32[]{:S(2)}) collective-permute-start(bf16[4,320,640]{2,1,0:T(8,128)(2,1)} %add_convert_fusion.5), channel_id=1, source_target_pairs={{0,16},{1,17},{2,18},{3,19},{4,20},{5,21},{6,22},{7,23},{8,10},{9,... | collective-permute-start | bytes 4915208 | tf_op jit(solution)/shard_map/ppermute | solution.py:882
  459.4 57.1 %collective-permute-start.22 = (bf16[8,320,640]{2,1,0:T(8,128)(2,1)}, bf16[8,320,640]{2,1,0:T(8,128)(2,1)}, u32[]{:S(2)}, u32[]{:S(2)}) collective-permute-start(bf16[8,320,640]{2,1,0:T(8,128)(2,1)} %add_convert_fusion.1), channel_id=1, source_target_pairs={{0,1},{1,0},{2,3},{3,2},{4,5},{5,4},{6,7},{7,6},{8,24},{9,25},{10,... | collective-permute-start | bytes 9830408 | tf_op jit(solution)/shard_map/ppermute | solution.py:882
  459.8 55.7 %collective-permute-start.24 = (bf16[8,16,1280]{2,1,0:T(8,128)(2,1)S(1)}, bf16[8,16,1280]{2,1,0:T(8,128)(2,1)S(1)}, u32[]{:S(2)}, u32[]{:S(2)}) collective-permute-start(bf16[8,16,1280]{2,1,0:T(8,128)(2,1)S(1)} %slice.769), channel_id=1, source_target_pairs={{0,6},{1,7},{8,14},{9,15},{16,22},{17,23},{24,30},{25,31}} | collective-permute-start | bytes 983048 | tf_op jit(solution)/shard_map/ppermute | solution.py:1123
  463.9 51.6 %collective-permute-start.25 = (bf16[8,16,1280]{2,1,0:T(8,128)(2,1)S(1)}, bf16[8,16,1280]{2,1,0:T(8,128)(2,1)}, u32[]{:S(2)}, u32[]{:S(2)}) collective-permute-start(bf16[8,16,1280]{2,1,0:T(8,128)(2,1)S(1)} %slice.769), channel_id=1, source_target_pairs={{2,6},{3,7},{10,14},{11,15},{18,22},{19,23},{26,30},{27,31}} | collective-permute-start | bytes 983048 | tf_op jit(solution)/shard_map/ppermute | solution.py:1123
  465.3 50.2 %collective-permute-start.26 = (bf16[8,16,1280]{2,1,0:T(8,128)(2,1)S(1)}, bf16[8,16,1280]{2,1,0:T(8,128)(2,1)}, u32[]{:S(2)}, u32[]{:S(2)}) collective-permute-start(bf16[8,16,1280]{2,1,0:T(8,128)(2,1)S(1)} %slice.769), channel_id=1, source_target_pairs={{4,6},{5,7},{12,14},{13,15},{20,22},{21,23},{28,30},{29,31}} | collective-permute-start | bytes 983048 | tf_op jit(solution)/shard_map/ppermute | solution.py:1123
  469.0 22.9 %collective-permute-start.21 = (bf16[2,320,640]{2,1,0:T(8,128)(2,1)S(1)}, bf16[2,320,640]{2,1,0:T(8,128)(2,1)S(1)}, u32[]{:S(2)}, u32[]{:S(2)}) collective-permute-start(bf16[2,320,640]{2,1,0:T(8,128)(2,1)S(1)} %add_convert_fusion.9), channel_id=1, source_target_pairs={{0,2},{1,3},{2,0},{3,1},{4,6},{5,7},{6,4},{7,5},{8,9},{9,8},{10,11... | collective-permute-start | bytes 2457608 | tf_op jit(solution)/shard_map/ppermute | solution.py:882
  492.0 24.5 %collective-permute-start.23 = (bf16[6,64,1280]{2,1,0:T(8,128)(2,1)S(1)}, bf16[6,64,1280]{2,1,0:T(8,128)(2,1)}, u32[]{:S(2)}, u32[]{:S(2)}) collective-permute-start(bf16[6,64,1280]{2,1,0:T(8,128)(2,1)S(1)} %bitcast.134), channel_id=1, source_target_pairs={{2,0},{4,2},{6,4},{3,1},{5,3},{7,5},{10,8},{12,10},{14,12},{11,9},... | collective-permute-start | bytes 2949128 | tf_op jit(solution)/shard_map/ppermute | solution.py:1121
  516.5 42.5 %collective-permute-start.28 = (bf16[16,40,3200]{2,1,0:T(8,128)(2,1)}, bf16[16,40,3200]{2,1,0:T(8,128)(2,1)}, u32[]{:S(2)}, u32[]{:S(2)}) collective-permute-start(bf16[16,40,3200]{2,1,0:T(8,128)(2,1)} %get-tuple-element.292), channel_id=1, source_target_pairs={{0,8},{1,9},{2,10},{3,11},{4,12},{5,13},{6,14},{7,15},{8,0},{9,1},... | collective-permute-start | bytes 12288008 | tf_op jit(solution)/shard_map/ppermute | solution.py:882
  521.0 64.2 %collective-permute-start.30 = (bf16[8,32,1280]{2,1,0:T(8,128)(2,1)}, bf16[8,32,1280]{2,1,0:T(8,128)(2,1)}, u32[]{:S(2)}, u32[]{:S(2)}) collective-permute-start(bf16[8,32,1280]{2,1,0:T(8,128)(2,1)} %get-tuple-element.441), channel_id=1, source_target_pairs={{0,1},{1,0},{2,3},{3,2},{4,5},{5,4},{6,7},{7,6},{8,9},{9,8},{10,11... | collective-permute-start | bytes 1966088 | tf_op jit(solution)/shard_map/ppermute | solution.py:1024
  522.1 36.9 %collective-permute-start.27 = (bf16[1,320,640]{2,1,0:T(8,128)(2,1)}, bf16[1,320,640]{2,1,0:T(8,128)(2,1)}, u32[]{:S(2)}, u32[]{:S(2)}) collective-permute-start(bf16[1,320,640]{2,1,0:T(8,128)(2,1)} %add_convert_fusion.13), channel_id=1, source_target_pairs={{0,4},{1,5},{2,6},{3,7},{4,0},{5,1},{6,2},{7,3},{8,12},{9,13},{10,... | collective-permute-start | bytes 1228808 | tf_op jit(solution)/shard_map/ppermute | solution.py:882
  529.9 55.3 %collective-permute-start.29 = (bf16[4,320,640]{2,1,0:T(8,128)(2,1)}, bf16[4,320,640]{2,1,0:T(8,128)(2,1)}, u32[]{:S(2)}, u32[]{:S(2)}) collective-permute-start(bf16[4,320,640]{2,1,0:T(8,128)(2,1)} %add_convert_fusion.4), channel_id=1, source_target_pairs={{0,16},{1,17},{2,18},{3,19},{4,20},{5,21},{6,22},{7,23},{8,10},{9,... | collective-permute-start | bytes 4915208 | tf_op jit(solution)/shard_map/ppermute | solution.py:882
  536.5 48.7 %collective-permute-start.31 = (bf16[8,32,1280]{2,1,0:T(8,128)(2,1)}, bf16[8,32,1280]{2,1,0:T(8,128)(2,1)}, u32[]{:S(2)}, u32[]{:S(2)}) collective-permute-start(bf16[8,32,1280]{2,1,0:T(8,128)(2,1)} %get-tuple-element.437), channel_id=1, source_target_pairs={{0,1},{1,0},{2,3},{3,2},{4,5},{5,4},{6,7},{7,6},{8,9},{9,8},{10,11... | collective-permute-start | bytes 1966088 | tf_op jit(solution)/shard_map/ppermute | solution.py:1024
  562.1 43.4 %collective-permute-start.33 = (bf16[8,40,3200]{2,1,0:T(8,128)(2,1)S(1)}, bf16[8,40,3200]{2,1,0:T(8,128)(2,1)}, u32[]{:S(2)}, u32[]{:S(2)}) collective-permute-start(bf16[8,40,3200]{2,1,0:T(8,128)(2,1)S(1)} %add_convert_fusion.3), channel_id=1, source_target_pairs={{0,1},{1,0},{2,3},{3,2},{4,5},{5,4},{6,7},{7,6},{8,24},{9,25},{10,... | collective-permute-start | bytes 6144008 | tf_op jit(solution)/shard_map/ppermute | solution.py:882
  588.4 17.1 %collective-permute-start.32 = (bf16[2,320,640]{2,1,0:T(8,128)(2,1)}, bf16[2,320,640]{2,1,0:T(8,128)(2,1)}, u32[]{:S(2)}, u32[]{:S(2)}) collective-permute-start(bf16[2,320,640]{2,1,0:T(8,128)(2,1)} %add_convert_fusion.8), channel_id=1, source_target_pairs={{0,2},{1,3},{2,0},{3,1},{4,6},{5,7},{6,4},{7,5},{8,9},{9,8},{10,11... | collective-permute-start | bytes 2457608 | tf_op jit(solution)/shard_map/ppermute | solution.py:882
  605.5 30.0 %collective-permute-start.36 = (bf16[16,40,1920]{2,1,0:T(8,128)(2,1)}, bf16[16,40,1920]{2,1,0:T(8,128)(2,1)}, u32[]{:S(2)}, u32[]{:S(2)}) collective-permute-start(bf16[16,40,1920]{2,1,0:T(8,128)(2,1)} %get-tuple-element.328), channel_id=1, source_target_pairs={{0,8},{1,9},{2,10},{3,11},{4,12},{5,13},{6,14},{7,15},{8,0},{9,1},... | collective-permute-start | bytes 7372808 | tf_op jit(solution)/shard_map/ppermute | solution.py:882
  609.8 23.1 %collective-permute-start.34 = (bf16[1,320,640]{2,1,0:T(8,128)(2,1)}, bf16[1,320,640]{2,1,0:T(8,128)(2,1)S(1)}, u32[]{:S(2)}, u32[]{:S(2)}) collective-permute-start(bf16[1,320,640]{2,1,0:T(8,128)(2,1)} %add_convert_fusion.12), channel_id=1, source_target_pairs={{0,4},{1,5},{2,6},{3,7},{4,0},{5,1},{6,2},{7,3},{8,12},{9,13},{10,... | collective-permute-start | bytes 1228808 | tf_op jit(solution)/shard_map/ppermute | solution.py:882
  613.1 22.4 %collective-permute-start.35 = (bf16[4,40,3200]{2,1,0:T(8,128)(2,1)}, bf16[4,40,3200]{2,1,0:T(8,128)(2,1)}, u32[]{:S(2)}, u32[]{:S(2)}) collective-permute-start(bf16[4,40,3200]{2,1,0:T(8,128)(2,1)} %add_convert_fusion.7), channel_id=1, source_target_pairs={{0,16},{1,17},{2,18},{3,19},{4,20},{5,21},{6,22},{7,23},{8,10},{9,... | collective-permute-start | bytes 3072008 | tf_op jit(solution)/shard_map/ppermute | solution.py:882
  638.1 22.5 %collective-permute-start.38 = (bf16[8,40,1920]{2,1,0:T(8,128)(2,1)}, bf16[8,40,1920]{2,1,0:T(8,128)(2,1)S(1)}, u32[]{:S(2)}, u32[]{:S(2)}) collective-permute-start(bf16[8,40,1920]{2,1,0:T(8,128)(2,1)} %add_convert_fusion.6), channel_id=1, source_target_pairs={{0,1},{1,0},{2,3},{3,2},{4,5},{5,4},{6,7},{7,6},{8,24},{9,25},{10,... | collective-permute-start | bytes 3686408 | tf_op jit(solution)/shard_map/ppermute | solution.py:882
  641.1 19.5 %collective-permute-start.37 = (bf16[2,40,3200]{2,1,0:T(8,128)(2,1)S(1)}, bf16[2,40,3200]{2,1,0:T(8,128)(2,1)}, u32[]{:S(2)}, u32[]{:S(2)}) collective-permute-start(bf16[2,40,3200]{2,1,0:T(8,128)(2,1)S(1)} %add_convert_fusion.11), channel_id=1, source_target_pairs={{0,2},{1,3},{2,0},{3,1},{4,6},{5,7},{6,4},{7,5},{8,9},{9,8},{10,11... | collective-permute-start | bytes 1536008 | tf_op jit(solution)/shard_map/ppermute | solution.py:882
  667.9 14.2 %collective-permute-start.39 = (bf16[1,40,3200]{2,1,0:T(8,128)(2,1)}, bf16[1,40,3200]{2,1,0:T(8,128)(2,1)}, u32[]{:S(2)}, u32[]{:S(2)}) collective-permute-start(bf16[1,40,3200]{2,1,0:T(8,128)(2,1)} %add_convert_fusion.15), channel_id=1, source_target_pairs={{0,4},{1,5},{2,6},{3,7},{4,0},{5,1},{6,2},{7,3},{8,12},{9,13},{10,... | collective-permute-start | bytes 768008 | tf_op jit(solution)/shard_map/ppermute | solution.py:882
  670.2 15.0 %collective-permute-start.40 = (bf16[4,40,1920]{2,1,0:T(8,128)(2,1)}, bf16[4,40,1920]{2,1,0:T(8,128)(2,1)}, u32[]{:S(2)}, u32[]{:S(2)}) collective-permute-start(bf16[4,40,1920]{2,1,0:T(8,128)(2,1)} %add_convert_fusion.10), channel_id=1, source_target_pairs={{0,16},{1,17},{2,18},{3,19},{4,20},{5,21},{6,22},{7,23},{8,10},{9,... | collective-permute-start | bytes 1843208 | tf_op jit(solution)/shard_map/ppermute | solution.py:882
  675.6 34.4 %collective-permute-start.45 = (bf16[8,32,1280]{2,1,0:T(8,128)(2,1)}, bf16[8,32,1280]{2,1,0:T(8,128)(2,1)}, u32[]{:S(2)}, u32[]{:S(2)}) collective-permute-start(bf16[8,32,1280]{2,1,0:T(8,128)(2,1)} %get-tuple-element.439), channel_id=1, source_target_pairs={{0,1},{1,0},{2,3},{3,2},{4,5},{5,4},{6,7},{7,6},{8,9},{9,8},{10,11... | collective-permute-start | bytes 1966088 | tf_op jit(solution)/shard_map/ppermute | solution.py:1024
  676.6 19.5 %collective-permute-start.46 = (bf16[8,16,1280]{2,1,0:T(8,128)(2,1)}, bf16[8,16,1280]{2,1,0:T(8,128)(2,1)S(1)}, u32[]{:S(2)}, u32[]{:S(2)}) collective-permute-start(bf16[8,16,1280]{2,1,0:T(8,128)(2,1)} %slice.774), channel_id=1, source_target_pairs={{0,6},{1,7},{8,14},{9,15},{16,22},{17,23},{24,30},{25,31}} | collective-permute-start | bytes 983048 | tf_op jit(solution)/shard_map/ppermute | solution.py:1123
  679.7 21.1 %collective-permute-start.47 = (bf16[8,16,1280]{2,1,0:T(8,128)(2,1)}, bf16[8,16,1280]{2,1,0:T(8,128)(2,1)}, u32[]{:S(2)}, u32[]{:S(2)}) collective-permute-start(bf16[8,16,1280]{2,1,0:T(8,128)(2,1)} %slice.774), channel_id=1, source_target_pairs={{2,6},{3,7},{10,14},{11,15},{18,22},{19,23},{26,30},{27,31}} | collective-permute-start | bytes 983048 | tf_op jit(solution)/shard_map/ppermute | solution.py:1123
  682.1 27.9 %collective-permute-start.48 = (bf16[8,16,1280]{2,1,0:T(8,128)(2,1)}, bf16[8,16,1280]{2,1,0:T(8,128)(2,1)}, u32[]{:S(2)}, u32[]{:S(2)}) collective-permute-start(bf16[8,16,1280]{2,1,0:T(8,128)(2,1)} %slice.774), channel_id=1, source_target_pairs={{4,6},{5,7},{12,14},{13,15},{20,22},{21,23},{28,30},{29,31}} | collective-permute-start | bytes 983048 | tf_op jit(solution)/shard_map/ppermute | solution.py:1123
  685.2 26.0 %collective-permute-start.44 = (bf16[6,64,1280]{2,1,0:T(8,128)(2,1)}, bf16[6,64,1280]{2,1,0:T(8,128)(2,1)}, u32[]{:S(2)}, u32[]{:S(2)}) collective-permute-start(bf16[6,64,1280]{2,1,0:T(8,128)(2,1)} %bitcast.40), channel_id=1, source_target_pairs={{2,0},{4,2},{6,4},{3,1},{5,3},{7,5},{10,8},{12,10},{14,12},{11,9},... | collective-permute-start | bytes 2949128 | tf_op jit(solution)/shard_map/ppermute | solution.py:1121
  696.1 13.9 %collective-permute-start.42 = (bf16[2,40,1920]{2,1,0:T(8,128)(2,1)}, bf16[2,40,1920]{2,1,0:T(8,128)(2,1)}, u32[]{:S(2)}, u32[]{:S(2)}) collective-permute-start(bf16[2,40,1920]{2,1,0:T(8,128)(2,1)} %add_convert_fusion.14), channel_id=1, source_target_pairs={{0,2},{1,3},{2,0},{3,1},{4,6},{5,7},{6,4},{7,5},{8,9},{9,8},{10,11... | collective-permute-start | bytes 921608 | tf_op jit(solution)/shard_map/ppermute | solution.py:882
  700.9 9.2 %collective-permute-start.43 = (f32[19680]{0:T(1024)S(1)}, f32[19680]{0:T(1024)S(1)}, u32[]{:S(2)}, u32[]{:S(2)}) collective-permute-start(f32[19680]{0:T(1024)S(1)} %add.705), channel_id=1, source_target_pairs={{0,16},{8,24},{16,0},{24,8},{1,17},{9,25},{17,1},{25,9},{2,18},{10... | collective-permute-start | bytes 236168 | tf_op jit(solution)/shard_map/ppermute | solution.py:782
  714.2 22.9 %collective-permute-start.51 = (bf16[8,32,1280]{2,1,0:T(8,128)(2,1)S(1)}, bf16[8,32,1280]{2,1,0:T(8,128)(2,1)S(1)}, u32[]{:S(2)}, u32[]{:S(2)}) collective-permute-start(bf16[8,32,1280]{2,1,0:T(8,128)(2,1)S(1)} %get-tuple-element.435), channel_id=1, source_target_pairs={{0,1},{1,0},{2,3},{3,2},{4,5},{5,4},{6,7},{7,6},{8,9},{9,8},{10,11... | collective-permute-start | bytes 1966088 | tf_op jit(solution)/shard_map/ppermute | solution.py:1024
  716.3 20.8 %collective-permute-start.49 = (bf16[1,40,1920]{2,1,0:T(8,128)(2,1)S(1)}, bf16[1,40,1920]{2,1,0:T(8,128)(2,1)S(1)}, u32[]{:S(2)}, u32[]{:S(2)}) collective-permute-start(bf16[1,40,1920]{2,1,0:T(8,128)(2,1)S(1)} %add_convert_fusion.16), channel_id=1, source_target_pairs={{0,4},{1,5},{2,6},{3,7},{4,0},{5,1},{6,2},{7,3},{8,12},{9,13},{10,... | collective-permute-start | bytes 460808 | tf_op jit(solution)/shard_map/ppermute | solution.py:882
  (78 other events, 777.7 us)
Sparse Core Ops, SparseCore 0:
  13.0 106.2 all-gather.3
  122.7 123.5 all-gather.5
  249.1 99.2 all-gather.7

commit v5 on v4

--- a/solution.py
+++ b/solution.py
@@ -105,13 +105,10 @@
     scale = HD**-0.5
     zeros = jnp.zeros((DEPTH - HD - 2 * SIDE, TOK), jnp.bfloat16)
 
-    def place_of(head):
-        return head // HALF * 3 * model // 2 + head % HALF * HD
-
     def wide(head):
-        place = place_of(head)
+        place = head * HD
         query = project_ref[place : place + HD]
-        key = project_ref[model // 2 + place : model // 2 + place + HD]
+        key = project_ref[model + place : model + place + HD]
         rows, cols = query_offsets(query, tab_ref, lane)
         rows = (rows * HD**0.5).astype(jnp.bfloat16)
         cols = jnp.where(sub < WIN, cols * HD**0.5, NEG).astype(jnp.bfloat16)
@@ -131,7 +128,7 @@
         results = [softmax(one) for one in scores]
         for head, (weights, inverse) in zip(heads, results):
             low = head * HD
-            place = model + place_of(head)
+            place = 2 * model + head * HD
             weights_ref[0, head] = weights
             inverse_ref[0, head : head + 1] = inverse
             attended = dot(project_ref[place : place + HD, :KEYS], weights)
@@ -171,7 +168,7 @@
 
 
 def attention_backward_kernel(
-    project_ref, weights_ref, inverse_ref, grad_ref, tab_ref, ind_ref, out_ref, dtab_ref, turned_ref
+    query_ref, key_ref, value_ref, weights_ref, inverse_ref, grad_ref, tab_ref, ind_ref, out_ref, dtab_ref, turned_ref
 ):
     model = turned_ref.shape[0]
     lane = lax.broadcasted_iota(jnp.int32, (SIDE, TOK), 1)
@@ -187,7 +184,7 @@
     total = jnp.zeros(dtab_ref.shape, jnp.float32)
     def products(head):
         low = head * HD
-        value = project_ref[2 * model + low : 2 * model + low + HD]
+        value = value_ref[low : low + HD]
         grad = (turned_ref[low : low + HD] * inverse_ref[0, head : head + 1]).astype(jnp.bfloat16)
         return grad, dot_tn(value, grad)[:KEYS]
 
@@ -199,8 +196,8 @@
 
     def wide_grads(head, grad, grad_scores):
         low = head * HD
-        query = project_ref[low : low + HD]
-        key = project_ref[model + low : model + low + HD]
+        query = query_ref[low : low + HD]
+        key = key_ref[low : low + HD]
         key = jnp.concatenate([key, ind], axis=0)
         grad_wide = dot(key[:, :KEYS], grad_scores)
         grad_value = dot_nt(grad, weights_ref[0, head])
@@ -211,7 +208,7 @@
 
     def offset_grads(head, grad_wide, total):
         low = head * HD
-        query = project_ref[low : low + HD]
+        query = query_ref[low : low + HD]
         rows = grad_wide[HD : HD + SIDE]
         cols = grad_wide[HD + SIDE : HD + 2 * SIDE]
         spread = jnp.concatenate(
@@ -243,7 +240,9 @@
         attention_backward_kernel,
         grid=(slots,),
         in_specs=[
-            pl.BlockSpec((3 * model, TOK), lambda i: (half, i)),
+            pl.BlockSpec((model, TOK), lambda i: (half, i)),
+            pl.BlockSpec((model, TOK), lambda i: (2 + half, i)),
+            pl.BlockSpec((model, TOK), lambda i: (4 + half, i)),
             pl.BlockSpec((1, HALF, KEYS, TOK), lambda i: (i, half, 0, 0)),
             pl.BlockSpec((1, HALF, TOK), lambda i: (i, half, 0)),
             pl.BlockSpec((TOK, model), lambda i: (i, half)),
@@ -263,7 +262,7 @@
         cost_estimate=pl.CostEstimate(
             flops=slots * 2_500_000_000, bytes_accessed=slots * 4 * MIB, transcendentals=0
         ),
-    )(project, weights, inverse, grad, tab, ind)
+    )(project, project, project, weights, inverse, grad, tab, ind)
 
 
 def write_placed(table_ref, kept_ref, sent_ref, core_stride, write):
@@ -430,8 +429,13 @@
     return mixed, grad, parts, grad_shift
 
 
-def token_gradient_kernel(grad_ref, weight_ref, out_ref):
-    out_ref[...] = dot(weight_ref[...], grad_ref[...]).astype(jnp.bfloat16).T
+def token_gradient_kernel(grad_ref, *refs):
+    *weight_refs, out_ref = refs
+    total = 0
+    for n, weight_ref in enumerate(weight_refs):
+        wide = weight_ref.shape[1]
+        total = total + dot(weight_ref[...], grad_ref[n * wide : (n + 1) * wide])
+    out_ref[...] = total.astype(jnp.bfloat16).T
 
 
 def token_gradient(grad, weight, half):
@@ -442,7 +446,14 @@
         grid=(tokens // TOK,),
         in_specs=[
             pl.BlockSpec((wide, TOK), lambda i: (0, i)),
-            pl.BlockSpec((model, wide), lambda i: (0, half), pipeline_mode=pl.Buffered(1)),
+            *[
+                pl.BlockSpec(
+                    (model, wide // 3),
+                    lambda i, n=n: (0, 2 * n + half),
+                    pipeline_mode=pl.Buffered(1),
+                )
+                for n in range(3)
+            ],
         ],
         out_specs=pl.BlockSpec((TOK, model), lambda i: (i, 0)),
         out_shape=jax.ShapeDtypeStruct((tokens, model), jnp.bfloat16),
@@ -452,7 +463,7 @@
             bytes_accessed=2 * (wide * tokens + model * wide + tokens * model),
             transcendentals=0,
         ),
-    )(grad, weight)
+    )(grad, weight, weight, weight)
 
 
 def window_gradient_kernel(own, core_stride, table_ref, *refs):
@@ -1220,8 +1231,7 @@
     up_shift = vectors[:, 8 * share :].reshape(devices, PARTS, share)
     up_shift = up_shift.transpose(1, 0, 2).reshape(1, devices * unit)
     half = model // 2
-    thirds = [w_qkv[:, n * half : (n + 1) * half] for n in (0, 2, 4, 1, 3, 5)]
-    qkv_full = gathered(jnp.concatenate(thirds, axis=1))
+    qkv_full = gathered(w_qkv)
     up_shard = w_fc1.reshape(share, devices, PARTS, share).transpose(0, 2, 1, 3)
     down_shard = [w_fc2[n * share : (n + 1) * share] for n in range(PARTS)]
     up_shard = up_shard.reshape(share, devices * unit)
@@ -1234,12 +1244,7 @@
     norm_vectors = sync(norm_vectors, [rows])
     rows = rows.finish()
     window_tokens = layout.to_windows(row_norm(rows, norm_vectors))
-    nothing = jnp.zeros((1, half), jnp.float32)
-    shift_qkv = jnp.concatenate(
-        [query_shift[:, :half], nothing, value_shift[:, :half]]
-        + [query_shift[:, half:], nothing, value_shift[:, half:]],
-        axis=1,
-    )
+    shift_qkv = jnp.concatenate([query_shift, jnp.zeros((1, model), jnp.float32), value_shift], 1)
     window_tokens = launch(window_tokens, [cot])
     project = lax.dot_general(
         qkv_full, window_tokens, (((0,), (1,)), ((), ())), preferred_element_type=jnp.float32
@@ -1354,10 +1359,14 @@
     flat = [one.finish() for one in sums[:-3]]
     flat, output.arrived = sync((flat, output.arrived), sums)
     launch(flat, sums)
+    norm_sums = sync(norm_sums, [small])
+    launch(norm_sums, [small])
     grad_fc1, grad_fc2 = formatted(*zip(*flat))
     done = output.finish()
     grad_fc1, grad_fc2, done = sync((grad_fc1, grad_fc2, done), sums + [grad_in])
     launch(grad_fc1, [grad_in] + sums)
+    norm_sums = sync(norm_sums, [small])
+    launch(norm_sums, [small])
     first_qkv, sum_proj = sums[-3].finish()
     first_qkv, sum_proj = sync((first_qkv, sum_proj), sums + [grad_in])
     launch(first_qkv, [grad_in] + sums)

time: 770 us -> 773 us (level)
  local copies, waits for them, and re-layouts: 101 us -> 109 us
    unnamed x157 -> x153, local copies, waits for them, and re-layouts: 35.7 us -> 32.5 us
  transfers between devices with their start and end apart: 57 -> 57, of which waited for: 15 -> 12; matrix products, arithmetic and copies ran while one was open for 21% -> 23% of each run, Pallas kernels for 41% -> 41%
where the time goes in v5:
time: 773 us; the launch traced here: 764 us
  Pallas kernels  317 us (41%)
  local copies, waits for them, and re-layouts  109 us (14%)
  waiting for transfers between devices  103 us (13%)
  other arithmetic  98.2 us (13%)
  starting transfers between devices  95.4 us (12%)
  matrix products  25.6 us (3%)
  between operations  15.5 us (2%)
    pallas_call x2, Pallas kernels, mlp(): pl.pallas_call(functools.partial(mlp_kernel, tokens // 2, begins, ends, p...  142 us
    all_gather x3, waiting for transfers between devices, gathered(): return lax.all_gather(shard, ALL, axis=0, tiled=True)  57 us
    convert_element_type x16, other arithmetic, summed(): sent = sent.astype(jnp.bfloat16)  49 us
    ppermute x20, starting transfers between devices, partner_permute(): return lax.ppermute(value, ALL, pairs)  38.4 us
    pallas_call x2, Pallas kernels, window_gradient(): pl.pallas_call(functools.partial(window_gradient_kernel, own, core_stride...  35.6 us
    pallas_call x2, Pallas kernels, attention_backward(): pl.pallas_call(attention_backward_kernel, grid=(slots,), in_specs=[pl.Blo...  35.1 us
    unnamed x153, local copies, waits for them, and re-layouts  32.5 us
    pallas_call x2, Pallas kernels, token_gradient(): pl.pallas_call(token_gradient_kernel, grid=(tokens // TOK,), in_specs=[pl...  30.4 us
  transfers between devices with their start and end apart: 57, of which 12 were waited for; matrix products, arithmetic and copies ran while one was open for 23% of the time, Pallas kernels for 41%

profile of v5, /device:TPU:1, one launch (start us, length us, event | category | flops | bytes accessed | tf_op | source)
XLA Modules:
  0.0 763.6 jit_solution(11744262376105233314)
XLA Ops:
  8.7 4.8 concatenate.139
  19.2 2.5 collective-permute-start.2
  23.7 3.2 collective-permute-start.3
  32.3 14.3 %collective-permute-done.5 = bf16[8,32,1280]{2,1,0:T(8,128)(2,1)S(1)} collective-permute-done((bf16[8,32,1280]{2,1,0:T(8,128)(2,1)}, bf16[8,32,1280]{2,1,0:T(8,128)(2,1)S(1)}, u32[]{:S(2)}, u32[]{:S(2)}) %collective-permute-start.5) | collective-permute-done | bytes 655392 | tf_op jit(solution)/shard_map/ppermute | solution.py:1019
  52.0 5.7 reshape.332
  59.3 3.3 reshape.333
  71.1 3.0 fusion.45
  74.1 4.1 collective-permute-start.7
  78.8 2.4 dynamic-slice_bitcast_fusion.4
  90.3 4.2 collective-permute-done.8
  96.5 3.8 collective-permute-done.6
  100.3 13.9 %collective-permute-done.7 = bf16[6,64,1280]{2,1,0:T(8,128)(2,1)} collective-permute-done((bf16[6,64,1280]{2,1,0:T(8,128)(2,1)}, bf16[6,64,1280]{2,1,0:T(8,128)(2,1)}, u32[]{:S(2)}, u32[]{:S(2)}) %collective-permute-start.7) | collective-permute-done | bytes 983072 | tf_op jit(solution)/shard_map/ppermute | solution.py:1104
  120.1 4.9 shard_map.378.rows_ref
  131.5 24.4 %fusion.project_ref.query_ref.key_ref.value_ref = bf16[3840,1792]{1,0:T(8,128)(2,1)} fusion(f32[3840]{0:T(1024)S(1)} %fusion.31, bf16[1792,1280]{1,0:T(8,128)(2,1)} %copy-done.14, bf16[1280,3840]{1,0:T(8,128)(2,1)} %all-gather.4.cloned.1.call-done.refs_0_.refs_1_.refs_2_), kind=kOutput, calls=%fused_computation.1 | convolution fusion | flops 17629839360 | bytes 28195840 | tf_op jit(solution)/shard_map/dot_general | solution.py:1249
  163.6 5.4 collective-permute-start.12
  171.2 19.9 %shard_map.380 = (bf16[1792,1280]{1,0:T(8,128)(2,1)}, bf16[7,16,224,256]{3,2,1,0:T(8,128)(2,1)}, f32[7,16,256]{2,1,0:T(8,128)}) custom-call(bf16[3840,1792]{1,0:T(8,128)(2,1)} %fusion.project_ref.query_ref.key_ref.value_ref, bf16[448,80]{1,0:T(8,128)(2,1)} %pad_maximum_fusion.6.tab_ref, bf16[48,256]{1,0:T(8,128)(2,1)} %fusion.26.ind_ref), custom_call_target="tpu_custom_call" | custom-call | flops 24500000768 | bytes 44040192 | tf_op jit(solution)/shard_map/pallas_call | solution.py:142
  200.7 37.4 %all-gather.6.cloned.1.call-done.proj_ref.refs_3_.refs_4_ = bf16[1280,6400]{1,0:T(8,128)(2,1)} async-done(((bf16[40,6400]{1,0:T(8,128)(2,1)}), bf16[1280,6400]{1,0:T(8,128)(2,1)}) %all-gather.6.cloned.1.call-update) | async-done | bytes 16384016 | tf_op jit(solution)/shard_map/all_gather | solution.py:1218
  239.8 7.8 %shard_map.382 = (f32[1088,1280]{1,0:T(8,128)S(1)}, bf16[1088,1280]{1,0:T(8,128)(2,1)S(1)}) custom-call(bf16[1088,1280]{1,0:T(8,128)(2,1)S(1)} %copy-done.4, bf16[1280,6400]{1,0:T(8,128)(2,1)} %all-gather.6.cloned.1.call-done.proj_ref.refs_3_.refs_4_, bf16[1088,1280]{1,0:T(8,128)(2,1)S(1)} %copy-done.2, f32[8,1280]{1,0:T(8,128)S(1)} %select_maximum_fusion.vectors_ref), custom_call_target="tpu_custom_call" | custom-call | flops 3565158400 | bytes 16711680 | tf_op jit(solution)/shard_map/pallas_call | solution.py:595
  252.1 70.3 %shard_map.383 = (f32[1088,1280]{1,0:T(8,128)}, f32[1088,1280]{1,0:T(8,128)}, bf16[16,320,640]{2,1,0:T(8,128)(2,1)}, bf16[16,320,640]{2,1,0:T(8,128)(2,1)}, f32[1,2560]{1,0:T(1,128)}) custom-call(s32[33]{0:T(128)} %pad_add_fusion.1.refs_0_.table_ref, bf16[1088,1280]{1,0:T(8,128)(2,1)} %copy-done.19, bf16[1088,1280]{1,0:T(8,128)(2,1)} %pad_maximum_fusion.1.refs_2_.cot_ref, ...), custom_call_target="tpu_custom_call" | custom-call | flops 57042534400 | bytes 59637760 | tf_op jit(solution)/shard_map/pallas_call | solution.py:386
  322.7 19.6 %all-gather.8.cloned.1.call-done.refs_3_.refs_4_ = bf16[1280,5120]{1,0:T(8,128)(2,1)} async-done(((bf16[40,5120]{1,0:T(8,128)(2,1)}), bf16[1280,5120]{1,0:T(8,128)(2,1)}) %all-gather.8.cloned.1.call-update) | async-done | bytes 13107216 | tf_op jit(solution)/shard_map/all_gather | solution.py:1218
  342.4 5.4 add_convert_fusion.2
  349.0 71.8 %shard_map.384 = (bf16[1088,1280]{1,0:T(8,128)(2,1)}, f32[1088,1280]{1,0:T(8,128)}, bf16[16,320,640]{2,1,0:T(8,128)(2,1)}, bf16[16,320,640]{2,1,0:T(8,128)(2,1)}, f32[1,2560]{1,0:T(1,128)}) custom-call(s32[33]{0:T(128)} %pad_add_fusion.1.refs_0_.table_ref, bf16[1088,1280]{1,0:T(8,128)(2,1)} %copy-done.19, ...), custom_call_target="tpu_custom_call" | custom-call | flops 57042534400 | bytes 59637760 | tf_op jit(solution)/shard_map/pallas_call | solution.py:386
  421.3 4.4 add_convert_fusion.5
  427.7 20.9 %shard_map.385 = (f32[1088,1280]{1,0:T(8,128)}, bf16[1088,1280]{1,0:T(8,128)(2,1)}, bf16[1280,1280]{1,0:T(8,128)(2,1)}, f32[8,1280]{1,0:T(8,128)}) custom-call(f32[1088,1280]{1,0:T(8,128)} %get-tuple-element.262.grad_ref, f32[1088,1280]{1,0:T(8,128)} %copy-done.13, bf16[1088,1280]{1,0:T(8,128)(2,1)} %pad_maximum_fusion.1.refs_2_.cot_ref, ...), custom_call_target="tpu_custom_call" | custom-call | flops 7130316800 | bytes 33423360 | tf_op jit(solution)/shard_map/pallas_call | solution.py:650
  448.6 4.8 add_convert_fusion.1
  453.9 4.1 collective-permute-start.24
  468.8 17.4 %shard_map.387 = (bf16[1920,1792]{1,0:T(8,128)(2,1)}, f32[448,80]{1,0:T(8,128)}) custom-call(bf16[3840,1792]{1,0:T(8,128)(2,1)} %fusion.project_ref.query_ref.key_ref.value_ref, bf16[3840,1792]{1,0:T(8,128)(2,1)} %fusion.project_ref.query_ref.key_ref.value_ref, bf16[3840,1792]{1,0:T(8,128)(2,1)} %fusion.project_ref.query_ref.key_ref.value_ref, ...), custom_call_target="tpu_custom_call" | custom-call | flops 17500000256 | bytes 29360128 | tf_op jit(solution)/shard_map/pallas_call | solution.py:239
  487.5 2.4 add_convert_fusion.13
  489.9 19.7 %shard_map.388 = (bf16[16,40,3200]{2,1,0:T(8,128)(2,1)}, bf16[16,40,3200]{2,1,0:T(8,128)(2,1)}, f32[1920,128]{1,0:T(8,128)}) custom-call(s32[33]{0:T(128)} %pad_add_fusion.1.refs_0_.table_ref, bf16[1792,1280]{1,0:T(8,128)(2,1)} %copy-done.14, bf16[1920,1792]{1,0:T(8,128)(2,1)} %get-tuple-element.298.refs_1_.grad_ref, ...), custom_call_target="tpu_custom_call" | custom-call | flops 8808038400 | bytes 19660800 | tf_op jit(solution)/shard_map/pallas_call | solution.py:507
  525.6 3.3 collective-permute-start.27
  528.9 4.2 add_convert_fusion.4
  533.2 2.7 collective-permute-start.29
  540.2 15.1 %shard_map.389.windows_ref = bf16[1792,1280]{1,0:T(8,128)(2,1)S(1)} custom-call(bf16[1920,1792]{1,0:T(8,128)(2,1)S(1)} %bitcast.114, bf16[1280,3840]{1,0:T(8,128)(2,1)} %all-gather.4.cloned.1.call-done.refs_0_.refs_1_.refs_2_, bf16[1280,3840]{1,0:T(8,128)(2,1)} %all-gather.4.cloned.1.call-done.refs_0_.refs_1_.refs_2_, ...), custom_call_target="tpu_custom_call" | custom-call | flops 8808038400 | bytes 16384000 | tf_op jit(solution)/shard_map/pallas_call | solution.py:444
  564.8 2.9 add_convert_fusion.3
  569.0 17.7 %shard_map.391 = (bf16[1920,1792]{1,0:T(8,128)(2,1)}, f32[448,80]{1,0:T(8,128)}) custom-call(bf16[3840,1792]{1,0:T(8,128)(2,1)} %fusion.project_ref.query_ref.key_ref.value_ref, bf16[3840,1792]{1,0:T(8,128)(2,1)} %fusion.project_ref.query_ref.key_ref.value_ref, bf16[3840,1792]{1,0:T(8,128)(2,1)} %fusion.project_ref.query_ref.key_ref.value_ref, ...), custom_call_target="tpu_custom_call" | custom-call | flops 17500000256 | bytes 29360128 | tf_op jit(solution)/shard_map/pallas_call | solution.py:239
  591.8 3.2 add_convert_fusion.8
  596.8 15.9 %shard_map.392 = (bf16[16,40,1920]{2,1,0:T(8,128)(2,1)}, bf16[16,40,1920]{2,1,0:T(8,128)(2,1)}, f32[1920,128]{1,0:T(8,128)}) custom-call(s32[33]{0:T(128)} %pad_add_fusion.1.refs_0_.table_ref, bf16[1792,1280]{1,0:T(8,128)(2,1)} %copy-done.14, bf16[1920,1792]{1,0:T(8,128)(2,1)} %get-tuple-element.330.refs_1_.grad_ref), custom_call_target="tpu_custom_call" | custom-call | flops 8808038400 | bytes 16384000 | tf_op jit(solution)/shard_map/pallas_call | solution.py:507
  616.9 3.3 add_convert_fusion.7
  620.6 2.9 copy-done.12
  623.5 15.3 %shard_map.393.windows_ref = bf16[1792,1280]{1,0:T(8,128)(2,1)S(1)} custom-call(bf16[1920,1792]{1,0:T(8,128)(2,1)S(1)} %copy-done.12, bf16[1280,3840]{1,0:T(8,128)(2,1)} %all-gather.4.cloned.1.call-done.refs_0_.refs_1_.refs_2_, bf16[1280,3840]{1,0:T(8,128)(2,1)} %all-gather.4.cloned.1.call-done.refs_0_.refs_1_.refs_2_, ...), custom_call_target="tpu_custom_call" | custom-call | flops 8808038400 | bytes 16384000 | tf_op jit(solution)/shard_map/pallas_call | solution.py:444
  642.5 3.0 add_convert_fusion.6
  659.4 9.3 %shard_map.395 = (bf16[1088,1280]{1,0:T(8,128)(2,1)}, f32[8,1280]{1,0:T(8,128)}) custom-call(bf16[1088,1280]{1,0:T(8,128)(2,1)} %pad_maximum_fusion.rows_ref.image_ref, bf16[1088,1280]{1,0:T(8,128)(2,1)} %copy-done.9, bf16[1088,1280]{1,0:T(8,128)(2,1)} %copy-done.10, f32[1088,1280]{1,0:T(8,128)} %get-tuple-element.349.grad_middle_ref, ...), custom_call_target="tpu_custom_call" | custom-call | flops 16711680 | bytes 13926400 | tf_op jit(solution)/shard_map/pallas_call | solution.py:693
  686.8 3.2 collective-permute-start.47
  698.2 2.5 add_bitcast_fusion
  715.1 4.2 reshape.358
  724.7 17.6 %collective-permute-start.50 = (bf16[1,40,1920]{2,1,0:T(8,128)(2,1)S(1)}, bf16[1,40,1920]{2,1,0:T(8,128)(2,1)S(1)}, u32[]{:S(2)}, u32[]{:S(2)}) collective-permute-start(bf16[1,40,1920]{2,1,0:T(8,128)(2,1)S(1)} %add_convert_fusion.16), channel_id=1, source_target_pairs={{0,4},{1,5},{2,6},{3,7},{4,0},{5,1},{6,2},{7,3},{8,12},{9,13},{10,... | collective-permute-start | bytes 460808 | tf_op jit(solution)/shard_map/ppermute | solution.py:893
  743.9 2.6 collective-permute-done.50
  752.4 2.7 maximum_convert_fusion
  (432 shorter events, 210.3 us)
Async XLA Ops:
  7.2 124.3 %all-gather.4.cloned.1.call-start = ((), (), s32[]{:S(2)}) async-start(), calls=%async_computation | async-start | bytes 10137600 | tf_op jit(solution)/shard_map/all_gather | solution.py:1218
  7.9 230.1 %all-gather.6.cloned.1.call-start = ((), (), s32[]{:S(2)}) async-start(), calls=%async_computation.1 | async-start | bytes 16896000 | tf_op jit(solution)/shard_map/all_gather | solution.py:1218
  27.9 18.6 %collective-permute-start.5 = (bf16[8,32,1280]{2,1,0:T(8,128)(2,1)}, bf16[8,32,1280]{2,1,0:T(8,128)(2,1)S(1)}, u32[]{:S(2)}, u32[]{:S(2)}) collective-permute-start(bf16[8,32,1280]{2,1,0:T(8,128)(2,1)} %get-tuple-element.457), channel_id=1, source_target_pairs={{0,1},{1,0},{2,3},{3,2},{4,5},{5,4},{6,7},{7,6},{8,9},{9,8},{10,11... | collective-permute-start | bytes 1966088 | tf_op jit(solution)/shard_map/ppermute | solution.py:1019
  65.4 276.9 %all-gather.8.cloned.1.call-start = ((), (), s32[]{:S(2)}) async-start(), calls=%async_computation.2 | async-start | bytes 13516800 | tf_op jit(solution)/shard_map/all_gather | solution.py:1218
  74.1 40.1 %collective-permute-start.7 = (bf16[6,64,1280]{2,1,0:T(8,128)(2,1)}, bf16[6,64,1280]{2,1,0:T(8,128)(2,1)}, u32[]{:S(2)}, u32[]{:S(2)}) collective-permute-start(bf16[6,64,1280]{2,1,0:T(8,128)(2,1)} %slice.704), channel_id=1, source_target_pairs={{0,2},{2,4},{4,6},{1,3},{3,5},{5,7},{8,10},{10,12},{12,14},{9,11},... | collective-permute-start | bytes 2949128 | tf_op jit(solution)/shard_map/ppermute | solution.py:1104
  81.2 19.1 %collective-permute-start.6 = (bf16[8,32,1280]{2,1,0:T(8,128)(2,1)}, bf16[8,32,1280]{2,1,0:T(8,128)(2,1)}, u32[]{:S(2)}, u32[]{:S(2)}) collective-permute-start(bf16[8,32,1280]{2,1,0:T(8,128)(2,1)} %get-tuple-element.452), channel_id=1, source_target_pairs={{0,1},{1,0},{2,3},{3,2},{4,5},{5,4},{6,7},{7,6},{8,9},{9,8},{10,11... | collective-permute-start | bytes 1966088 | tf_op jit(solution)/shard_map/ppermute | solution.py:1019
  83.3 11.2 %collective-permute-start.8 = (bf16[8,16,1280]{2,1,0:T(8,128)(2,1)}, bf16[8,16,1280]{2,1,0:T(8,128)(2,1)}, u32[]{:S(2)}, u32[]{:S(2)}) collective-permute-start(bf16[8,16,1280]{2,1,0:T(8,128)(2,1)} %get-tuple-element.455), channel_id=1, source_target_pairs={{6,0},{7,1},{14,8},{15,9},{22,16},{23,17},{30,24},{31,25}} | collective-permute-start | bytes 983048 | tf_op jit(solution)/shard_map/ppermute | solution.py:1107
  84.6 11.9 %collective-permute-start.9 = (bf16[8,16,1280]{2,1,0:T(8,128)(2,1)}, bf16[8,16,1280]{2,1,0:T(8,128)(2,1)}, u32[]{:S(2)}, u32[]{:S(2)}) collective-permute-start(bf16[8,16,1280]{2,1,0:T(8,128)(2,1)} %get-tuple-element.454), channel_id=1, source_target_pairs={{6,2},{7,3},{14,10},{15,11},{22,18},{23,19},{30,26},{31,27}} | collective-permute-start | bytes 983048 | tf_op jit(solution)/shard_map/ppermute | solution.py:1107
  94.5 61.4 %collective-permute-start.11 = (bf16[8,32,1280]{2,1,0:T(8,128)(2,1)}, bf16[8,32,1280]{2,1,0:T(8,128)(2,1)}, u32[]{:S(2)}, u32[]{:S(2)}) collective-permute-start(bf16[8,32,1280]{2,1,0:T(8,128)(2,1)} %get-tuple-element.450), channel_id=1, source_target_pairs={{0,1},{1,0},{2,3},{3,2},{4,5},{5,4},{6,7},{7,6},{8,9},{9,8},{10,11... | collective-permute-start | bytes 1966088 | tf_op jit(solution)/shard_map/ppermute | solution.py:1019
  159.6 35.9 %collective-permute-start.16 = (bf16[8,16,1280]{2,1,0:T(8,128)(2,1)}, bf16[8,16,1280]{2,1,0:T(8,128)(2,1)S(1)}, u32[]{:S(2)}, u32[]{:S(2)}) collective-permute-start(bf16[8,16,1280]{2,1,0:T(8,128)(2,1)} %get-tuple-element.448), channel_id=1, source_target_pairs={{6,0},{7,1},{14,8},{15,9},{22,16},{23,17},{30,24},{31,25}} | collective-permute-start | bytes 983048 | tf_op jit(solution)/shard_map/ppermute | solution.py:1107
  160.8 34.6 %collective-permute-start.15 = (bf16[8,16,1280]{2,1,0:T(8,128)(2,1)}, bf16[8,16,1280]{2,1,0:T(8,128)(2,1)}, u32[]{:S(2)}, u32[]{:S(2)}) collective-permute-start(bf16[8,16,1280]{2,1,0:T(8,128)(2,1)} %get-tuple-element.447), channel_id=1, source_target_pairs={{6,2},{7,3},{14,10},{15,11},{22,18},{23,19},{30,26},{31,27}} | collective-permute-start | bytes 983048 | tf_op jit(solution)/shard_map/ppermute | solution.py:1107
  162.2 33.2 %collective-permute-start.14 = (bf16[8,16,1280]{2,1,0:T(8,128)(2,1)}, bf16[8,16,1280]{2,1,0:T(8,128)(2,1)}, u32[]{:S(2)}, u32[]{:S(2)}) collective-permute-start(bf16[8,16,1280]{2,1,0:T(8,128)(2,1)} %get-tuple-element.446), channel_id=1, source_target_pairs={{6,4},{7,5},{14,12},{15,13},{22,20},{23,21},{30,28},{31,29}} | collective-permute-start | bytes 983048 | tf_op jit(solution)/shard_map/ppermute | solution.py:1107
  163.6 34.2 %collective-permute-start.12 = (bf16[6,64,1280]{2,1,0:T(8,128)(2,1)}, bf16[6,64,1280]{2,1,0:T(8,128)(2,1)}, u32[]{:S(2)}, u32[]{:S(2)}) collective-permute-start(bf16[6,64,1280]{2,1,0:T(8,128)(2,1)} %slice.713), channel_id=1, source_target_pairs={{0,2},{2,4},{4,6},{1,3},{3,5},{5,7},{8,10},{10,12},{12,14},{9,11},... | collective-permute-start | bytes 2949128 | tf_op jit(solution)/shard_map/ppermute | solution.py:1104
  170.0 27.3 %collective-permute-start.13 = (bf16[8,32,1280]{2,1,0:T(8,128)(2,1)}, bf16[8,32,1280]{2,1,0:T(8,128)(2,1)S(1)}, u32[]{:S(2)}, u32[]{:S(2)}) collective-permute-start(bf16[8,32,1280]{2,1,0:T(8,128)(2,1)} %get-tuple-element.445), channel_id=1, source_target_pairs={{0,1},{1,0},{2,3},{3,2},{4,5},{5,4},{6,7},{7,6},{8,9},{9,8},{10,11... | collective-permute-start | bytes 1966088 | tf_op jit(solution)/shard_map/ppermute | solution.py:1019
  322.4 19.9 %collective-permute-start.17 = (bf16[16,320,640]{2,1,0:T(8,128)(2,1)}, bf16[16,320,640]{2,1,0:T(8,128)(2,1)}, u32[]{:S(2)}, u32[]{:S(2)}) collective-permute-start(bf16[16,320,640]{2,1,0:T(8,128)(2,1)} %get-tuple-element.243), channel_id=1, source_target_pairs={{0,8},{1,9},{2,10},{3,11},{4,12},{5,13},{6,14},{7,15},{8,0},{9,1},... | collective-permute-start | bytes 19660808 | tf_op jit(solution)/shard_map/ppermute | solution.py:893
  347.8 73.0 %collective-permute-start.18 = (bf16[8,320,640]{2,1,0:T(8,128)(2,1)}, bf16[8,320,640]{2,1,0:T(8,128)(2,1)}, u32[]{:S(2)}, u32[]{:S(2)}) collective-permute-start(bf16[8,320,640]{2,1,0:T(8,128)(2,1)} %add_convert_fusion.2), channel_id=1, source_target_pairs={{0,1},{1,0},{2,3},{3,2},{4,5},{5,4},{6,7},{7,6},{8,24},{9,25},{10,... | collective-permute-start | bytes 9830408 | tf_op jit(solution)/shard_map/ppermute | solution.py:893
  420.8 27.8 %collective-permute-start.20 = (bf16[16,320,640]{2,1,0:T(8,128)(2,1)}, bf16[16,320,640]{2,1,0:T(8,128)(2,1)}, u32[]{:S(2)}, u32[]{:S(2)}) collective-permute-start(bf16[16,320,640]{2,1,0:T(8,128)(2,1)} %get-tuple-element.261), channel_id=1, source_target_pairs={{0,8},{1,9},{2,10},{3,11},{4,12},{5,13},{6,14},{7,15},{8,0},{9,1},... | collective-permute-start | bytes 19660808 | tf_op jit(solution)/shard_map/ppermute | solution.py:893
  425.7 22.9 %collective-permute-start.19 = (bf16[4,320,640]{2,1,0:T(8,128)(2,1)}, bf16[4,320,640]{2,1,0:T(8,128)(2,1)}, u32[]{:S(2)}, u32[]{:S(2)}) collective-permute-start(bf16[4,320,640]{2,1,0:T(8,128)(2,1)} %add_convert_fusion.5), channel_id=1, source_target_pairs={{0,16},{1,17},{2,18},{3,19},{4,20},{5,21},{6,22},{7,23},{8,10},{9,... | collective-permute-start | bytes 4915208 | tf_op jit(solution)/shard_map/ppermute | solution.py:893
  453.4 57.1 %collective-permute-start.22 = (bf16[8,320,640]{2,1,0:T(8,128)(2,1)}, bf16[8,320,640]{2,1,0:T(8,128)(2,1)}, u32[]{:S(2)}, u32[]{:S(2)}) collective-permute-start(bf16[8,320,640]{2,1,0:T(8,128)(2,1)} %add_convert_fusion.1), channel_id=1, source_target_pairs={{0,1},{1,0},{2,3},{3,2},{4,5},{5,4},{6,7},{7,6},{8,24},{9,25},{10,... | collective-permute-start | bytes 9830408 | tf_op jit(solution)/shard_map/ppermute | solution.py:893
  453.9 55.8 %collective-permute-start.24 = (bf16[8,16,1280]{2,1,0:T(8,128)(2,1)S(1)}, bf16[8,16,1280]{2,1,0:T(8,128)(2,1)S(1)}, u32[]{:S(2)}, u32[]{:S(2)}) collective-permute-start(bf16[8,16,1280]{2,1,0:T(8,128)(2,1)S(1)} %slice.725), channel_id=1, source_target_pairs={{0,6},{1,7},{8,14},{9,15},{16,22},{17,23},{24,30},{25,31}} | collective-permute-start | bytes 983048 | tf_op jit(solution)/shard_map/ppermute | solution.py:1134
  458.0 51.7 %collective-permute-start.25 = (bf16[8,16,1280]{2,1,0:T(8,128)(2,1)S(1)}, bf16[8,16,1280]{2,1,0:T(8,128)(2,1)}, u32[]{:S(2)}, u32[]{:S(2)}) collective-permute-start(bf16[8,16,1280]{2,1,0:T(8,128)(2,1)S(1)} %slice.725), channel_id=1, source_target_pairs={{2,6},{3,7},{10,14},{11,15},{18,22},{19,23},{26,30},{27,31}} | collective-permute-start | bytes 983048 | tf_op jit(solution)/shard_map/ppermute | solution.py:1134
  459.4 50.3 %collective-permute-start.26 = (bf16[8,16,1280]{2,1,0:T(8,128)(2,1)S(1)}, bf16[8,16,1280]{2,1,0:T(8,128)(2,1)}, u32[]{:S(2)}, u32[]{:S(2)}) collective-permute-start(bf16[8,16,1280]{2,1,0:T(8,128)(2,1)S(1)} %slice.725), channel_id=1, source_target_pairs={{4,6},{5,7},{12,14},{13,15},{20,22},{21,23},{28,30},{29,31}} | collective-permute-start | bytes 983048 | tf_op jit(solution)/shard_map/ppermute | solution.py:1134
  463.1 23.1 %collective-permute-start.21 = (bf16[2,320,640]{2,1,0:T(8,128)(2,1)S(1)}, bf16[2,320,640]{2,1,0:T(8,128)(2,1)S(1)}, u32[]{:S(2)}, u32[]{:S(2)}) collective-permute-start(bf16[2,320,640]{2,1,0:T(8,128)(2,1)S(1)} %add_convert_fusion.9), channel_id=1, source_target_pairs={{0,2},{1,3},{2,0},{3,1},{4,6},{5,7},{6,4},{7,5},{8,9},{9,8},{10,11... | collective-permute-start | bytes 2457608 | tf_op jit(solution)/shard_map/ppermute | solution.py:893
  486.2 24.3 %collective-permute-start.23 = (bf16[6,64,1280]{2,1,0:T(8,128)(2,1)S(1)}, bf16[6,64,1280]{2,1,0:T(8,128)(2,1)}, u32[]{:S(2)}, u32[]{:S(2)}) collective-permute-start(bf16[6,64,1280]{2,1,0:T(8,128)(2,1)S(1)} %bitcast.136), channel_id=1, source_target_pairs={{2,0},{4,2},{6,4},{3,1},{5,3},{7,5},{10,8},{12,10},{14,12},{11,9},... | collective-permute-start | bytes 2949128 | tf_op jit(solution)/shard_map/ppermute | solution.py:1132
  510.5 54.0 %collective-permute-start.28 = (bf16[16,40,3200]{2,1,0:T(8,128)(2,1)}, bf16[16,40,3200]{2,1,0:T(8,128)(2,1)}, u32[]{:S(2)}, u32[]{:S(2)}) collective-permute-start(bf16[16,40,3200]{2,1,0:T(8,128)(2,1)} %get-tuple-element.293), channel_id=1, source_target_pairs={{0,8},{1,9},{2,10},{3,11},{4,12},{5,13},{6,14},{7,15},{8,0},{9,1},... | collective-permute-start | bytes 12288008 | tf_op jit(solution)/shard_map/ppermute | solution.py:893
  515.8 75.2 %collective-permute-start.30 = (bf16[8,32,1280]{2,1,0:T(8,128)(2,1)}, bf16[8,32,1280]{2,1,0:T(8,128)(2,1)}, u32[]{:S(2)}, u32[]{:S(2)}) collective-permute-start(bf16[8,32,1280]{2,1,0:T(8,128)(2,1)} %get-tuple-element.443), channel_id=1, source_target_pairs={{0,1},{1,0},{2,3},{3,2},{4,5},{5,4},{6,7},{7,6},{8,9},{9,8},{10,11... | collective-permute-start | bytes 1966088 | tf_op jit(solution)/shard_map/ppermute | solution.py:1035
  525.6 39.0 %collective-permute-start.27 = (bf16[1,320,640]{2,1,0:T(8,128)(2,1)}, bf16[1,320,640]{2,1,0:T(8,128)(2,1)}, u32[]{:S(2)}, u32[]{:S(2)}) collective-permute-start(bf16[1,320,640]{2,1,0:T(8,128)(2,1)} %add_convert_fusion.13), channel_id=1, source_target_pairs={{0,4},{1,5},{2,6},{3,7},{4,0},{5,1},{6,2},{7,3},{8,12},{9,13},{10,... | collective-permute-start | bytes 1228808 | tf_op jit(solution)/shard_map/ppermute | solution.py:893
  533.2 57.8 %collective-permute-start.29 = (bf16[4,320,640]{2,1,0:T(8,128)(2,1)}, bf16[4,320,640]{2,1,0:T(8,128)(2,1)}, u32[]{:S(2)}, u32[]{:S(2)}) collective-permute-start(bf16[4,320,640]{2,1,0:T(8,128)(2,1)} %add_convert_fusion.4), channel_id=1, source_target_pairs={{0,16},{1,17},{2,18},{3,19},{4,20},{5,21},{6,22},{7,23},{8,10},{9,... | collective-permute-start | bytes 4915208 | tf_op jit(solution)/shard_map/ppermute | solution.py:893
  539.8 51.1 %collective-permute-start.31 = (bf16[8,32,1280]{2,1,0:T(8,128)(2,1)}, bf16[8,32,1280]{2,1,0:T(8,128)(2,1)S(1)}, u32[]{:S(2)}, u32[]{:S(2)}) collective-permute-start(bf16[8,32,1280]{2,1,0:T(8,128)(2,1)} %get-tuple-element.439), channel_id=1, source_target_pairs={{0,1},{1,0},{2,3},{3,2},{4,5},{5,4},{6,7},{7,6},{8,9},{9,8},{10,11... | collective-permute-start | bytes 1966088 | tf_op jit(solution)/shard_map/ppermute | solution.py:1035
  567.7 45.0 %collective-permute-start.33 = (bf16[8,40,3200]{2,1,0:T(8,128)(2,1)S(1)}, bf16[8,40,3200]{2,1,0:T(8,128)(2,1)}, u32[]{:S(2)}, u32[]{:S(2)}) collective-permute-start(bf16[8,40,3200]{2,1,0:T(8,128)(2,1)S(1)} %add_convert_fusion.3), channel_id=1, source_target_pairs={{0,1},{1,0},{2,3},{3,2},{4,5},{5,4},{6,7},{7,6},{8,24},{9,25},{10,... | collective-permute-start | bytes 6144008 | tf_op jit(solution)/shard_map/ppermute | solution.py:893
  595.0 17.7 %collective-permute-start.32 = (bf16[2,320,640]{2,1,0:T(8,128)(2,1)}, bf16[2,320,640]{2,1,0:T(8,128)(2,1)S(1)}, u32[]{:S(2)}, u32[]{:S(2)}) collective-permute-start(bf16[2,320,640]{2,1,0:T(8,128)(2,1)} %add_convert_fusion.8), channel_id=1, source_target_pairs={{0,2},{1,3},{2,0},{3,1},{4,6},{5,7},{6,4},{7,5},{8,9},{9,8},{10,11... | collective-permute-start | bytes 2457608 | tf_op jit(solution)/shard_map/ppermute | solution.py:893
  612.7 29.8 %collective-permute-start.36 = (bf16[16,40,1920]{2,1,0:T(8,128)(2,1)}, bf16[16,40,1920]{2,1,0:T(8,128)(2,1)}, u32[]{:S(2)}, u32[]{:S(2)}) collective-permute-start(bf16[16,40,1920]{2,1,0:T(8,128)(2,1)} %get-tuple-element.329), channel_id=1, source_target_pairs={{0,8},{1,9},{2,10},{3,11},{4,12},{5,13},{6,14},{7,15},{8,0},{9,1},... | collective-permute-start | bytes 7372808 | tf_op jit(solution)/shard_map/ppermute | solution.py:893
  616.9 25.6 %collective-permute-start.34 = (bf16[1,320,640]{2,1,0:T(8,128)(2,1)}, bf16[1,320,640]{2,1,0:T(8,128)(2,1)}, u32[]{:S(2)}, u32[]{:S(2)}) collective-permute-start(bf16[1,320,640]{2,1,0:T(8,128)(2,1)} %add_convert_fusion.12), channel_id=1, source_target_pairs={{0,4},{1,5},{2,6},{3,7},{4,0},{5,1},{6,2},{7,3},{8,12},{9,13},{10,... | collective-permute-start | bytes 1228808 | tf_op jit(solution)/shard_map/ppermute | solution.py:893
  620.2 22.3 %collective-permute-start.35 = (bf16[4,40,3200]{2,1,0:T(8,128)(2,1)}, bf16[4,40,3200]{2,1,0:T(8,128)(2,1)S(1)}, u32[]{:S(2)}, u32[]{:S(2)}) collective-permute-start(bf16[4,40,3200]{2,1,0:T(8,128)(2,1)} %add_convert_fusion.7), channel_id=1, source_target_pairs={{0,16},{1,17},{2,18},{3,19},{4,20},{5,21},{6,22},{7,23},{8,10},{9,... | collective-permute-start | bytes 3072008 | tf_op jit(solution)/shard_map/ppermute | solution.py:893
  645.6 23.1 %collective-permute-start.38 = (bf16[8,40,1920]{2,1,0:T(8,128)(2,1)}, bf16[8,40,1920]{2,1,0:T(8,128)(2,1)S(1)}, u32[]{:S(2)}, u32[]{:S(2)}) collective-permute-start(bf16[8,40,1920]{2,1,0:T(8,128)(2,1)} %add_convert_fusion.6), channel_id=1, source_target_pairs={{0,1},{1,0},{2,3},{3,2},{4,5},{5,4},{6,7},{7,6},{8,24},{9,25},{10,... | collective-permute-start | bytes 3686408 | tf_op jit(solution)/shard_map/ppermute | solution.py:893
  649.1 19.6 %collective-permute-start.37 = (bf16[2,40,3200]{2,1,0:T(8,128)(2,1)}, bf16[2,40,3200]{2,1,0:T(8,128)(2,1)}, u32[]{:S(2)}, u32[]{:S(2)}) collective-permute-start(bf16[2,40,3200]{2,1,0:T(8,128)(2,1)} %add_convert_fusion.11), channel_id=1, source_target_pairs={{0,2},{1,3},{2,0},{3,1},{4,6},{5,7},{6,4},{7,5},{8,9},{9,8},{10,11... | collective-permute-start | bytes 1536008 | tf_op jit(solution)/shard_map/ppermute | solution.py:893
  676.0 15.3 %collective-permute-start.39 = (bf16[1,40,3200]{2,1,0:T(8,128)(2,1)}, bf16[1,40,3200]{2,1,0:T(8,128)(2,1)}, u32[]{:S(2)}, u32[]{:S(2)}) collective-permute-start(bf16[1,40,3200]{2,1,0:T(8,128)(2,1)} %add_convert_fusion.15), channel_id=1, source_target_pairs={{0,4},{1,5},{2,6},{3,7},{4,0},{5,1},{6,2},{7,3},{8,12},{9,13},{10,... | collective-permute-start | bytes 768008 | tf_op jit(solution)/shard_map/ppermute | solution.py:893
  680.7 13.8 %collective-permute-start.40 = (bf16[4,40,1920]{2,1,0:T(8,128)(2,1)}, bf16[4,40,1920]{2,1,0:T(8,128)(2,1)}, u32[]{:S(2)}, u32[]{:S(2)}) collective-permute-start(bf16[4,40,1920]{2,1,0:T(8,128)(2,1)} %add_convert_fusion.10), channel_id=1, source_target_pairs={{0,16},{1,17},{2,18},{3,19},{4,20},{5,21},{6,22},{7,23},{8,10},{9,... | collective-permute-start | bytes 1843208 | tf_op jit(solution)/shard_map/ppermute | solution.py:893
  686.4 32.9 %collective-permute-start.46 = (bf16[8,32,1280]{2,1,0:T(8,128)(2,1)}, bf16[8,32,1280]{2,1,0:T(8,128)(2,1)}, u32[]{:S(2)}, u32[]{:S(2)}) collective-permute-start(bf16[8,32,1280]{2,1,0:T(8,128)(2,1)} %get-tuple-element.441), channel_id=1, source_target_pairs={{0,1},{1,0},{2,3},{3,2},{4,5},{5,4},{6,7},{7,6},{8,9},{9,8},{10,11... | collective-permute-start | bytes 1966088 | tf_op jit(solution)/shard_map/ppermute | solution.py:1035
  686.8 17.1 %collective-permute-start.47 = (bf16[8,16,1280]{2,1,0:T(8,128)(2,1)}, bf16[8,16,1280]{2,1,0:T(8,128)(2,1)S(1)}, u32[]{:S(2)}, u32[]{:S(2)}) collective-permute-start(bf16[8,16,1280]{2,1,0:T(8,128)(2,1)} %slice.730), channel_id=1, source_target_pairs={{0,6},{1,7},{8,14},{9,15},{16,22},{17,23},{24,30},{25,31}} | collective-permute-start | bytes 983048 | tf_op jit(solution)/shard_map/ppermute | solution.py:1134
  690.0 19.8 %collective-permute-start.48 = (bf16[8,16,1280]{2,1,0:T(8,128)(2,1)}, bf16[8,16,1280]{2,1,0:T(8,128)(2,1)}, u32[]{:S(2)}, u32[]{:S(2)}) collective-permute-start(bf16[8,16,1280]{2,1,0:T(8,128)(2,1)} %slice.730), channel_id=1, source_target_pairs={{2,6},{3,7},{10,14},{11,15},{18,22},{19,23},{26,30},{27,31}} | collective-permute-start | bytes 983048 | tf_op jit(solution)/shard_map/ppermute | solution.py:1134
  691.4 28.0 %collective-permute-start.45 = (bf16[6,64,1280]{2,1,0:T(8,128)(2,1)}, bf16[6,64,1280]{2,1,0:T(8,128)(2,1)}, u32[]{:S(2)}, u32[]{:S(2)}) collective-permute-start(bf16[6,64,1280]{2,1,0:T(8,128)(2,1)} %bitcast.41), channel_id=1, source_target_pairs={{2,0},{4,2},{6,4},{3,1},{5,3},{7,5},{10,8},{12,10},{14,12},{11,9},... | collective-permute-start | bytes 2949128 | tf_op jit(solution)/shard_map/ppermute | solution.py:1132
  694.5 10.9 %collective-permute-start.43 = (f32[19680]{0:T(1024)S(1)}, f32[19680]{0:T(1024)S(1)}, u32[]{:S(2)}, u32[]{:S(2)}) collective-permute-start(f32[19680]{0:T(1024)S(1)} %add.706), channel_id=1, source_target_pairs={{0,16},{8,24},{16,0},{24,8},{1,17},{9,25},{17,1},{25,9},{2,18},{10... | collective-permute-start | bytes 236168 | tf_op jit(solution)/shard_map/ppermute | solution.py:793
  703.9 15.4 %collective-permute-start.49 = (bf16[8,16,1280]{2,1,0:T(8,128)(2,1)}, bf16[8,16,1280]{2,1,0:T(8,128)(2,1)}, u32[]{:S(2)}, u32[]{:S(2)}) collective-permute-start(bf16[8,16,1280]{2,1,0:T(8,128)(2,1)} %slice.730), channel_id=1, source_target_pairs={{4,6},{5,7},{12,14},{13,15},{20,22},{21,23},{28,30},{29,31}} | collective-permute-start | bytes 983048 | tf_op jit(solution)/shard_map/ppermute | solution.py:1134
  705.4 14.0 %collective-permute-start.42 = (bf16[2,40,1920]{2,1,0:T(8,128)(2,1)}, bf16[2,40,1920]{2,1,0:T(8,128)(2,1)}, u32[]{:S(2)}, u32[]{:S(2)}) collective-permute-start(bf16[2,40,1920]{2,1,0:T(8,128)(2,1)} %add_convert_fusion.14), channel_id=1, source_target_pairs={{0,2},{1,3},{2,0},{3,1},{4,6},{5,7},{6,4},{7,5},{8,9},{9,8},{10,11... | collective-permute-start | bytes 921608 | tf_op jit(solution)/shard_map/ppermute | solution.py:893
  719.4 22.9 %collective-permute-start.51 = (f32[19680]{0:T(1024)S(1)}, f32[19680]{0:T(1024)S(1)}, u32[]{:S(2)}, u32[]{:S(2)}) collective-permute-start(f32[19680]{0:T(1024)S(1)} %add.721), channel_id=1, source_target_pairs={{0,2},{2,0},{4,6},{6,4},{1,3},{3,1},{5,7},{7,5},{8,10},{10,8},{12,... | collective-permute-start | bytes 236168 | tf_op jit(solution)/shard_map/ppermute | solution.py:793
  722.7 25.6 %collective-permute-start.53 = (bf16[8,32,1280]{2,1,0:T(8,128)(2,1)S(1)}, bf16[8,32,1280]{2,1,0:T(8,128)(2,1)S(1)}, u32[]{:S(2)}, u32[]{:S(2)}) collective-permute-start(bf16[8,32,1280]{2,1,0:T(8,128)(2,1)S(1)} %get-tuple-element.437), channel_id=1, source_target_pairs={{0,1},{1,0},{2,3},{3,2},{4,5},{5,4},{6,7},{7,6},{8,9},{9,8},{10,11... | collective-permute-start | bytes 1966088 | tf_op jit(solution)/shard_map/ppermute | solution.py:1035
  724.7 21.9 %collective-permute-start.50 = (bf16[1,40,1920]{2,1,0:T(8,128)(2,1)S(1)}, bf16[1,40,1920]{2,1,0:T(8,128)(2,1)S(1)}, u32[]{:S(2)}, u32[]{:S(2)}) collective-permute-start(bf16[1,40,1920]{2,1,0:T(8,128)(2,1)S(1)} %add_convert_fusion.16), channel_id=1, source_target_pairs={{0,4},{1,5},{2,6},{3,7},{4,0},{5,1},{6,2},{7,3},{8,12},{9,13},{10,... | collective-permute-start | bytes 460808 | tf_op jit(solution)/shard_map/ppermute | solution.py:893
  (81 other events, 1245.1 us)
Sparse Core Ops, SparseCore 0:
  11.0 102.2 all-gather.3
  116.8 121.2 all-gather.5
  240.9 101.4 all-gather.7
